TPU v7x, 32 devices: a whole 2x2x4 slice. The times are simulated.
32 devices in a mesh: seq: 8 (over y, x, core), rank: 4 (over z).
Axes of the slice: x: 2, y: 2, z: 4, core: 2. Of those that a mesh axis runs over, the one named last changes fastest.
Arguments:
- tokens_in: bfloat16 [4608, 2048], P('seq'), may hold values from -6 to 6
- norm1_gain: float32 [2048], replicated, may hold values from 0.5 to 1.5
- q_down: bfloat16 [2048, 1024], P(None, 'rank'), may hold values from -1 to 1
- latent_gain: float32 [1024], P('rank'), may hold values from 0.5 to 1.5
- q_up: bfloat16 [1024, 4096], P('rank'), may hold values from -1 to 1
- kv_weight: bfloat16 [2048, 512], replicated, may hold values from -0.125 to 0.125
- out_weight: bfloat16 [4096, 2048], P('rank'), may hold values from -0.375 to 0.375
- norm2_gain: float32 [2048], replicated, may hold values from 0.5 to 1.5
- gate_weight: bfloat16 [2048, 5632], P(None, 'rank'), may hold values from -0.125 to 0.125
- up_weight: bfloat16 [2048, 5632], P(None, 'rank'), may hold values from -0.125 to 0.125
- down_weight: bfloat16 [5632, 2048], P('rank'), may hold values from -0.15625 to 0.15625
- doc_ids: int32 [4608], replicated, may hold values from 0 to 8, as said below
- out_grad: bfloat16 [4608, 2048], P('seq'), may hold values from -6 to 6
Outputs:
- layer_out: bfloat16 [4608, 2048], P('seq')
- grad_in: float32 [4608, 2048], P('seq', 'rank')
- grad_norm1: float32 [2048], P('rank')
- grad_q_down: float32 [2048, 1024], P(None, 'rank')
- grad_latent_gain: float32 [1024], P('rank')
- grad_q_up: float32 [1024, 4096], P('rank')
- grad_kv_weight: float32 [2048, 512], P('rank')
- grad_out: float32 [4096, 2048], P('rank')
- grad_norm2: float32 [2048], replicated
- grad_gate: float32 [2048, 5632], P(None, 'rank')
- grad_up: float32 [2048, 5632], P(None, 'rank')
- grad_down: float32 [5632, 2048], P('rank')
Inputs may be any that keep to these rules, and one draw needn't show every extreme that they name: `doc_ids`: document numbers never fall along the row; equal numbers in a run mark one document.
All inputs are finite; a program needn't handle non-finite values.
Results may differ from a plain program's by a relative error of at most 0.022.
Values may be sent and summed in bfloat16 or wider, within the bound.
No kernel may reach another device: no remote copies, remote signals or barrier semaphores. Data moves between devices by JAX's collectives and lax.ppermute only.
A program may use at most 320 MiB of HBM per device.

v0:
```python
import jax
import jax.numpy as jnp
from jax import lax
from jax.sharding import PartitionSpec as P

EPS = 1e-05
BASE = 10000.0
NEG = -1e30


def norm_rows(values, gain):
    recip = lax.rsqrt(jnp.mean(values * values, -1, keepdims=True) + EPS)
    return (values * recip * gain, recip)


def rotate(values, cosine_rows, sine_rows):
    half_dim = values.shape[-1] // 2
    front_half = values[..., :half_dim]
    back_half = values[..., half_dim:]
    return jnp.concatenate(
        [
            front_half * cosine_rows - back_half * sine_rows,
            front_half * sine_rows + back_half * cosine_rows,
        ],
        -1,
    )


def rope_tables(doc_ids, head_dim):
    index_all = jnp.arange(doc_ids.shape[0], dtype=jnp.int32)
    changed = jnp.concatenate([jnp.ones((1,), dtype=bool), doc_ids[1:] != doc_ids[:-1]])
    starts = lax.cummax(jnp.where(changed, index_all, 0), axis=0)
    position = (index_all - starts).astype(jnp.float32)
    half_dim = head_dim // 2
    freqs = BASE ** (-jnp.arange(half_dim, dtype=jnp.float32) / half_dim)
    angle = position[:, None] * freqs[None, :]
    return (jnp.cos(angle), jnp.sin(angle))


def dense(left, right):
    return jnp.dot(left, right, preferred_element_type=jnp.float32)


def dense_tn(left, right):
    return lax.dot_general(
        left, right, (((0,), (0,)), ((), ())), preferred_element_type=jnp.float32
    )


def dense_nt(left, right):
    return lax.dot_general(
        left, right, (((1,), (1,)), ((), ())), preferred_element_type=jnp.float32
    )


def finish_kv(summed, cosine_rows, sine_rows, head_dim):
    rounded = summed.astype(jnp.bfloat16).astype(jnp.float32)
    key_back = rotate(rounded[:, :head_dim], cosine_rows, -sine_rows)
    return jnp.concatenate([key_back, rounded[:, head_dim:]], -1).astype(jnp.bfloat16)


def per_device(
    tokens_in,
    norm1_gain,
    q_down,
    latent_gain,
    q_up,
    kv_weight,
    out_weight,
    norm2_gain,
    gate_weight,
    up_weight,
    down_weight,
    doc_ids,
    out_grad,
):
    row_count = tokens_in.shape[0]
    model_width = tokens_in.shape[1]
    rank_count = lax.axis_size("rank")
    rank_ix = lax.axis_index("rank")
    seq_ix = lax.axis_index("seq")
    head_dim = kv_weight.shape[1] // 2
    local_heads = out_weight.shape[0] // head_dim
    key_count = doc_ids.shape[0]
    score_scale = head_dim ** (-0.5)
    cosine_all, sine_all = rope_tables(doc_ids, head_dim)
    first_row = seq_ix * row_count
    cosine_rows = lax.dynamic_slice_in_dim(cosine_all, first_row, row_count, 0)
    sine_rows = lax.dynamic_slice_in_dim(sine_all, first_row, row_count, 0)
    ids_local = lax.dynamic_slice_in_dim(doc_ids, first_row, row_count, 0)
    query_index = first_row + jnp.arange(row_count, dtype=jnp.int32)
    key_index = jnp.arange(key_count, dtype=jnp.int32)
    allowed = (ids_local[:, None] == doc_ids[None, :]) & (
        key_index[None, :] <= query_index[:, None]
    )
    tokens = tokens_in.astype(jnp.float32)
    normed_in, recip1 = norm_rows(tokens, norm1_gain)
    normed_low = normed_in.astype(jnp.bfloat16)
    latent = dense(normed_low, q_down)
    latent_sq = lax.psum(jnp.sum(latent * latent, -1), "rank")
    rank_width = latent.shape[1] * rank_count
    recip_c = lax.rsqrt(latent_sq / rank_width + EPS)[:, None]
    latent_low = (latent * recip_c * latent_gain).astype(jnp.bfloat16)
    query_pre = lax.psum_scatter(dense(latent_low, q_up), "rank", scatter_dimension=1, tiled=True)
    query_pre = query_pre.reshape(row_count, local_heads, head_dim)
    query = rotate(query_pre, cosine_rows[:, None, :], sine_rows[:, None, :]).astype(jnp.bfloat16)
    kv_pre = dense(normed_low, kv_weight)
    key_local = rotate(kv_pre[:, :head_dim], cosine_rows, sine_rows)
    kv_local = jnp.concatenate([key_local, kv_pre[:, head_dim:]], -1).astype(jnp.bfloat16)
    kv_all = lax.all_gather(kv_local, "seq", axis=0, tiled=True)
    keys = kv_all[:, :head_dim]
    values = kv_all[:, head_dim:]

    def scores_of():
        raw = jnp.einsum("thd,nd->htn", query, keys, preferred_element_type=jnp.float32)
        return jnp.where(allowed[None], raw * score_scale, NEG)

    scores = scores_of()
    row_max = jnp.max(scores, -1, keepdims=True)
    log_total = row_max + jnp.log(jnp.sum(jnp.exp(scores - row_max), -1, keepdims=True))
    attn_probs = jnp.exp(scores - log_total)
    probs_low = attn_probs.astype(jnp.bfloat16)
    attn_vals = jnp.einsum("htn,nd->thd", probs_low, values, preferred_element_type=jnp.float32)
    attn_low = attn_vals.reshape(row_count, local_heads * head_dim).astype(jnp.bfloat16)
    branch = lax.psum(dense(attn_low, out_weight), "rank")
    residual = tokens + branch
    normed_mid, recip2 = norm_rows(residual, norm2_gain)
    mid_low = normed_mid.astype(jnp.bfloat16)
    gate_pre = dense(mid_low, gate_weight)
    up_pre = dense(mid_low, up_weight)
    sigmoid_gate = jax.nn.sigmoid(gate_pre)
    activated = gate_pre * sigmoid_gate
    hidden_low = (activated * up_pre).astype(jnp.bfloat16)
    feed_out = lax.psum(dense(hidden_low, down_weight).astype(jnp.bfloat16), "rank").astype(
        jnp.float32
    )
    layer_out = (residual + feed_out).astype(jnp.bfloat16)
    grad_hidden = dense_nt(out_grad, down_weight)
    grad_down = dense_tn(hidden_low, out_grad)
    grad_gate_pre = (
        grad_hidden * up_pre * sigmoid_gate * (1.0 + gate_pre * (1.0 - sigmoid_gate))
    ).astype(jnp.bfloat16)
    grad_up_pre = (grad_hidden * activated).astype(jnp.bfloat16)
    grad_gate = dense_tn(mid_low, grad_gate_pre)
    grad_up = dense_tn(mid_low, grad_up_pre)
    grad_mid = lax.psum(
        dense_nt(grad_gate_pre, gate_weight) + dense_nt(grad_up_pre, up_weight), "rank"
    )
    gained_mid = grad_mid * norm2_gain
    stat_mid = jnp.sum(residual * gained_mid, -1, keepdims=True)
    grad_residual = (
        out_grad.astype(jnp.float32)
        + recip2 * gained_mid
        - residual * recip2**3 * stat_mid / model_width
    )
    grad_norm2 = jnp.sum(grad_mid * residual * recip2, 0)
    grad_branch = grad_residual.astype(jnp.bfloat16)
    grad_out = dense_tn(attn_low, grad_branch)
    grad_attn = (
        dense_nt(grad_branch, out_weight)
        .astype(jnp.bfloat16)
        .reshape(row_count, local_heads, head_dim)
    )
    scores = scores_of()
    attn_probs = jnp.exp(scores - log_total)
    probs_low = attn_probs.astype(jnp.bfloat16)
    grad_probs = jnp.einsum("thd,nd->htn", grad_attn, values, preferred_element_type=jnp.float32)
    grad_dot = jnp.sum(attn_probs * grad_probs, -1, keepdims=True)
    grad_scores = (attn_probs * (grad_probs - grad_dot)).astype(jnp.bfloat16)
    grad_query = (
        jnp.einsum("htn,nd->thd", grad_scores, keys, preferred_element_type=jnp.float32)
        * score_scale
    )
    grad_keys = (
        jnp.einsum("htn,thd->nd", grad_scores, query, preferred_element_type=jnp.float32)
        * score_scale
    )
    grad_values = jnp.einsum(
        "htn,thd->nd", probs_low, grad_attn, preferred_element_type=jnp.float32
    )
    grad_kv_part = jnp.concatenate([grad_keys, grad_values], -1)
    grad_query_pre = rotate(
        grad_query.astype(jnp.bfloat16).astype(jnp.float32),
        cosine_rows[:, None, :],
        -sine_rows[:, None, :],
    )
    grad_query_pre = grad_query_pre.astype(jnp.bfloat16).reshape(row_count, local_heads * head_dim)
    grad_query_all = lax.all_gather(grad_query_pre, "rank", axis=1, tiled=True)
    grad_latent_in = dense_nt(grad_query_all, q_up)
    grad_q_up = dense_tn(latent_low, grad_query_all)
    gained_latent = grad_latent_in * latent_gain
    stat_latent = lax.psum(jnp.sum(latent * gained_latent, -1), "rank")[:, None]
    grad_latent = (
        recip_c * gained_latent - latent * recip_c**3 * stat_latent / rank_width
    ).astype(jnp.bfloat16)
    grad_latent_gain = jnp.sum(grad_latent_in * latent * recip_c, 0)
    grad_q_down = dense_tn(normed_low, grad_latent)
    grad_input_part = dense_nt(grad_latent, q_down)
    partial_rows = lax.psum_scatter(
        grad_kv_part.astype(jnp.bfloat16), "seq", scatter_dimension=0, tiled=True
    )
    summed = lax.psum(partial_rows, "rank").astype(jnp.float32)
    grad_kv_pre = finish_kv(summed, cosine_rows, sine_rows, head_dim)
    col_count = model_width // rank_count
    col_start = rank_ix * col_count
    kv_rows = lax.dynamic_slice_in_dim(kv_weight, col_start, col_count, 0)
    kv_term = dense_nt(grad_kv_pre, kv_rows)
    grad_kv_weight = dense_tn(
        lax.dynamic_slice_in_dim(normed_low, col_start, col_count, 1), grad_kv_pre
    )
    own_part = lax.dynamic_slice_in_dim(grad_input_part, col_start, col_count, 1)
    grad_input_part = lax.dynamic_update_slice_in_dim(
        grad_input_part, own_part + kv_term, col_start, 1
    )
    stat_part = jnp.sum(tokens * norm1_gain * grad_input_part, -1)
    stat_spread = jnp.broadcast_to(stat_part[:, None], (row_count, rank_count))
    grad_normed, norm1_stat = (
        lax.psum_scatter(
            grad_input_part.astype(jnp.bfloat16), "rank", scatter_dimension=1, tiled=True
        ).astype(jnp.float32),
        lax.psum_scatter(
            stat_spread.astype(jnp.bfloat16), "rank", scatter_dimension=1, tiled=True
        ).astype(jnp.float32),
    )
    tokens_own = lax.dynamic_slice_in_dim(tokens, col_start, col_count, 1)
    gain_own = lax.dynamic_slice_in_dim(norm1_gain, col_start, col_count, 0)
    resid_own = lax.dynamic_slice_in_dim(grad_residual, col_start, col_count, 1)
    grad_in = (
        resid_own
        + recip1 * gain_own * grad_normed
        - tokens_own * recip1**3 * norm1_stat / model_width
    )
    grad_norm1 = jnp.sum(grad_normed * tokens_own * recip1, 0)
    totals = (
        lax.psum(grad_norm1.astype(jnp.bfloat16), "seq").astype(jnp.float32),
        lax.psum(grad_q_down.astype(jnp.bfloat16), "seq").astype(jnp.float32),
        lax.psum(grad_latent_gain.astype(jnp.bfloat16), "seq").astype(jnp.float32),
        lax.psum(grad_q_up.astype(jnp.bfloat16), "seq").astype(jnp.float32),
        lax.psum(grad_kv_weight.astype(jnp.bfloat16), "seq").astype(jnp.float32),
        lax.psum(grad_out.astype(jnp.bfloat16), "seq").astype(jnp.float32),
        lax.psum(grad_norm2.astype(jnp.bfloat16), "seq").astype(jnp.float32),
        lax.psum(grad_gate.astype(jnp.bfloat16), "seq").astype(jnp.float32),
        lax.psum(grad_up.astype(jnp.bfloat16), "seq").astype(jnp.float32),
        lax.psum(grad_down.astype(jnp.bfloat16), "seq").astype(jnp.float32),
    )
    return (
        layer_out,
        grad_in,
        totals[0],
        totals[1],
        totals[2],
        totals[3],
        totals[4],
        totals[5],
        totals[6],
        totals[7],
        totals[8],
        totals[9],
    )


def solution(mesh):
    return jax.shard_map(
        per_device,
        mesh=mesh,
        in_specs=(
            P("seq", None),
            P(),
            P(None, "rank"),
            P("rank"),
            P("rank", None),
            P(),
            P("rank", None),
            P(),
            P(None, "rank"),
            P(None, "rank"),
            P("rank", None),
            P(),
            P("seq", None),
        ),
        out_specs=(
            P("seq", None),
            P("seq", "rank"),
            P("rank"),
            P(None, "rank"),
            P("rank"),
            P("rank", None),
            P("rank", None),
            P("rank", None),
            P(),
            P(None, "rank"),
            P(None, "rank"),
            P("rank", None),
        ),
        check_vma=False,
    )
```

profile of v0, /device:TPU:25, one launch (start us, length us, event | category | flops | bytes accessed | tf_op | source)
XLA Modules:
  0.0 1377.1 jit_solution(12448989819479679796)
XLA Ops:
  14.7 6.4 psum.112
  22.3 5.2 fusion.37
  28.8 3.7 fusion.42
  38.2 5.1 fusion.5
  43.3 149.0 %reduce-scatter.4.cloned.1.call-done = f32[576,1024]{1,0:T(8,128)} async-done(((f32[576,4096]{1,0:T(8,128)}), f32[576,1024]{1,0:T(8,128)}) %reduce-scatter.4.cloned.1.call-update) | async-done | bytes 2359312 | tf_op jit(solution)/shard_map/reduce_scatter | solution.py:104
  192.3 3.8 reshape.175
  199.1 19.6 %fusion.4 = (f32[4,576]{1,0:T(4,128)S(1)}, f32[4608,576,4]{0,1,2:T(8,128)}) fusion(pred[576,4608]{1,0:T(8,128)(4,1)} %fusion.5, bf16[576,4,128]{2,0,1:T(8,128)(2,1)} %get-tuple-element.44, bf16[576,4,128]{2,0,1:T(8,128)(2,1)S(1)} %get-tuple-element.43, bf16[4608,512]{1,0:T(8,128)(2,1)} %all-gather.3.cloned.1.call-done), kind=kOutput, calls=%fused_computation.9 | convolution fusion | flops 5470025728 | bytes 48669696 | tf_op jit(solution)/shard_map/thd,nd->htn/dot_general | solution.py:115
  218.6 20.3 %exponential_reduce_fusion = f32[4,576]{1,0:T(4,128)S(1)} fusion(f32[4608,576,4]{0,1,2:T(8,128)} %get-tuple-element.58, f32[4,576]{1,0:T(4,128)S(1)} %get-tuple-element.57, pred[576,4608]{1,0:T(8,128)(4,1)} %fusion.5), kind=kLoop, calls=%fused_computation.7 | loop fusion | flops 42465024 | bytes 45139968 | tf_op jit(solution)/shard_map/reduce_sum | solution.py:120
  238.9 17.8 %fusion.15 = bf16[4,72,8,256]{3,2,1,0:T(8,128)(2,1)S(1)} fusion(bf16[4608,512]{1,0:T(8,128)(2,1)} %all-gather.3.cloned.1.call-done, f32[4608,576,4]{0,1,2:T(8,128)} %get-tuple-element.58, f32[4,576]{1,0:T(4,128)S(1)} %log_add_fusion, pred[576,4608]{1,0:T(8,128)(4,1)} %fusion.5), kind=kOutput, calls=%fused_computation.53 | convolution fusion | flops 5478875136 | bytes 48669696 | tf_op jit(solution)/shard_map/htn,nd->thd/dot_general | solution.py:123
  258.0 6.4 fusion.43
  264.6 170.9 %all-reduce.9.cloned.1.call-done = f32[576,2048]{1,0:T(8,128)} async-done(((f32[576,2048]{1,0:T(8,128)}), f32[576,2048]{1,0:T(8,128)}) %all-reduce.9.cloned.1.call-update) | async-done | bytes 4718608 | tf_op jit(solution)/shard_map/psum | solution.py:125
  435.5 3.8 multiply_reduce_fusion.3
  441.7 7.6 fusion.44
  449.4 5.5 fusion.45
  454.9 9.8 multiply_convert_fusion.2
  464.7 5.4 fusion.46
  470.2 5.5 convolution_add_fusion
  475.8 171.1 %all-reduce.11.cloned.1.call-done = f32[576,2048]{1,0:T(8,128)} async-done(((f32[576,2048]{1,0:T(8,128)}), f32[576,2048]{1,0:T(8,128)}) %all-reduce.11.cloned.1.call-update) | async-done | bytes 4718608 | tf_op jit(solution)/shard_map/psum | solution.py:146
  646.8 5.6 multiply_reduce_fusion
  652.7 3.9 multiply_subtract_fusion
  660.3 20.0 %fusion.8 = bf16[4608,256]{1,0:T(8,128)(2,1)} fusion(bf16[72,4,8,256]{3,2,1,0:T(8,128)(2,1)S(1)} %bitcast.128, f32[4608,576,4]{0,1,2:T(8,128)} %get-tuple-element.58, f32[4,576]{1,0:T(4,128)S(1)} %log_add_fusion, pred[576,4608]{1,0:T(8,128)(4,1)S(1)} %copy-done.4), kind=kOutput, calls=%fused_computation.19 | convolution fusion | flops 5479464960 | bytes 48669696 | tf_op jit(solution)/shard_map/htn,thd->nd/dot_general | solution.py:178
  680.3 33.9 %fusion = (f32[4,576]{1,0:T(4,128)S(1)}, f32[4608,576,4]{0,1,2:T(8,128)}) fusion(f32[4608,576,4]{0,1,2:T(8,128)} %get-tuple-element.58, f32[4,576]{1,0:T(4,128)S(1)} %log_add_fusion, pred[576,4608]{1,0:T(8,128)(4,1)} %fusion.5, bf16[72,4,8,256]{3,2,1,0:T(8,128)(2,1)} %bitcast.129, bf16[4608,512]{1,0:T(8,128)(2,1)} %all-gather.3.cloned.1.call-done), kind=kOutput, calls=%fused_computation.2 | convolution fusion | flops 5488900096 | bytes 91146240 | tf_op jit(solution)/shard_map/thd,nd->htn/dot_general | solution.py:167
  714.2 35.1 %fusion.2 = bf16[4,576,4608]{2,1,0:T(8,128)(2,1)} fusion(f32[4608,576,4]{0,1,2:T(8,128)} %get-tuple-element.60, f32[4608,576,4]{0,1,2:T(8,128)} %get-tuple-element.58, f32[4,576]{1,0:T(4,128)S(1)} %get-tuple-element.59, f32[4,576]{1,0:T(4,128)S(1)} %log_add_fusion, pred[576,4608]{1,0:T(8,128)(4,1)} %fusion.5), kind=kLoop, calls=%fused_computation.4 | loop fusion | flops 63700992 | bytes 108840960 | tf_op jit(solution)/shard_map/convert_element_type | solution.py:169
  749.3 10.2 fusion.7
  762.2 11.1 convert_bitcast_fusion
  775.0 9.0 convolution_convert_fusion.5
  784.0 32.9 %reduce-scatter.6.cloned.1.call-done = bf16[576,512]{1,0:T(8,128)(2,1)} async-done(((bf16[4608,512]{1,0:T(8,128)(2,1)}), bf16[576,512]{1,0:T(8,128)(2,1)}) %reduce-scatter.6.cloned.1.call-update) | async-done | bytes 589840 | tf_op jit(solution)/shard_map/reduce_scatter | solution.py:199
  817.0 46.2 %all-gather.5.cloned.1.call-done = bf16[576,4096]{1,0:T(8,128)(2,1)} async-done(((bf16[576,1024]{1,0:T(8,128)(2,1)}), bf16[576,4096]{1,0:T(8,128)(2,1)}) %all-gather.5.cloned.1.call-update) | async-done | bytes 4718608 | tf_op jit(solution)/shard_map/all_gather | solution.py:188
  863.2 4.6 multiply_reduce_fusion.5
  867.8 10.6 psum.116
  880.5 4.3 fusion.47
  884.8 95.7 %all-reduce.15.cloned.1.call-done = (bf16[576,2048]{1,0:T(8,128)(2,1)}, bf16[576,512]{1,0:T(8,128)(2,1)}) async-done(((bf16[576,2048]{1,0:T(8,128)(2,1)}, bf16[576,512]{1,0:T(8,128)(2,1)}), (bf16[576,2048]{1,0:T(8,128)(2,1)}, bf16[576,512]{1,0:T(8,128)(2,1)})) %all-reduce.15.cloned.1.call-update) | async-done | bytes 2949136 | tf_op jit(solution)/shard_map/psum | solution.py:134
  986.6 6.3 multiply_reduce_fusion.1
  992.9 8.7 convolution_convert_fusion.1
  1001.7 6.8 convolution_convert_fusion.2
  1008.5 6.5 convolution_convert_fusion
  1015.1 5.3 convolution_convert_fusion.4
  1022.4 3.3 convolution_convert_fusion.3
  1027.3 4.5 convert_element_type.160
  1032.3 8.5 all-reduce
  1041.5 5.5 add_convert_fusion
  1047.1 3.4 fusion.20
  1050.5 14.1 %all-reduce.1 = (bf16[512]{0:T(512)(128)(2,1)S(1)}, bf16[256]{0:T(256)(128)(2,1)S(1)}, bf16[2048]{0:T(1024)(128)(2,1)S(1)}) all-reduce(bf16[512]{0:T(512)(128)(2,1)S(1)} %get-tuple-element.37, bf16[256]{0:T(256)(128)(2,1)S(1)} %get-tuple-element.14, bf16[2048]{0:T(1024)(128)(2,1)S(1)} %copy-done.51), channel_id=1, replica_groups=mesh['seq'=8,'rank'=4] {'seq'}, use_global_device_ids=true, to_apply=%region_22.23 | all-reduce | flops 2816 | bytes 11264 | tf_op jit(solution)/shard_map/psum | solution.py:235
  1066.3 273.4 %all-reduce.13.cloned.1.call-done = (bf16[2048,256]{1,0:T(8,128)(2,1)}, bf16[256,4096]{1,0:T(8,128)(2,1)}, bf16[512,512]{1,0:T(8,128)(2,1)}, bf16[1024,2048]{1,0...) async-done(((bf16[2048,256]{1,0:T(8,128)(2,1)}, bf16[256,4096]{1,0:T(8,128)(2,1)}, bf16[512,512]{1,0:T(8,128)(2,1)}, ...) | async-done | bytes 25165840 | tf_op jit(solution)/shard_map/psum | solution.py:236
  1339.7 8.6 convert_element_type.203
  1348.3 5.2 convert_element_type.205
  1353.5 6.0 convert_element_type.207
  1359.5 4.5 convert_element_type.199
  (212 shorter events, 49.9 us)
Async XLA Ops:
  8.0 14.3 %copy-start = (bf16[256,4096]{1,0:T(8,128)(2,1)S(1)}, bf16[256,4096]{1,0:T(8,128)(2,1)}, u32[]{:S(2)}) copy-start(bf16[256,4096]{1,0:T(8,128)(2,1)} %param.17) | copy-start | bytes 6291460
  8.0 184.3 %reduce-scatter.4.cloned.1.call-start = ((), (), s32[]{:S(2)}) async-start(), calls=%async_computation.4 | async-start | bytes 11796480 | tf_op jit(solution)/shard_map/reduce_scatter | solution.py:104
  8.1 5.7 copy-start.33
  13.8 8.5 copy-start.46
  14.7 12.8 copy-start.6
  27.5 171.6 %all-gather.3.cloned.1.call-start = ((), (), s32[]{:S(2)}) async-start(), calls=%async_computation.3 | async-start | bytes 5308416 | tf_op jit(solution)/shard_map/all_gather | solution.py:110
  36.1 161.8 %copy-start.10 = (f32[576,128]{1,0:T(8,128)}, f32[576,128]{1,0:T(8,128)S(1)}, u32[]{:S(2)}) copy-start(f32[576,128]{1,0:T(8,128)S(1)} %get-tuple-element.29) | copy-start | bytes 884740
  37.1 160.8 %copy-start.8 = (f32[576,128]{1,0:T(8,128)}, f32[576,128]{1,0:T(8,128)S(1)}, u32[]{:S(2)}) copy-start(f32[576,128]{1,0:T(8,128)S(1)} %get-tuple-element.33) | copy-start | bytes 884740
  38.1 397.4 %all-reduce.9.cloned.1.call-start = ((), (), s32[]{:S(2)}) async-start(), calls=%async_computation.5 | async-start | bytes 9437184 | tf_op jit(solution)/shard_map/psum | solution.py:125
  199.1 19.6 %copy-start.39 = (bf16[576,4,128]{2,0,1:T(8,128)(2,1)}, bf16[576,4,128]{2,0,1:T(8,128)(2,1)S(1)}, u32[]{:S(2)}) copy-start(bf16[576,4,128]{2,0,1:T(8,128)(2,1)S(1)} %get-tuple-element.43) | copy-start | bytes 1769476
  264.4 175.0 %copy-start.44 = (f32[2048]{0:T(1024)S(1)}, f32[2048]{0:T(1024)}, u32[]{:S(2)}) copy-start(f32[2048]{0:T(1024)} %param.20) | copy-start | bytes 24580
  264.4 382.5 %all-reduce.11.cloned.1.call-start = ((), (), s32[]{:S(2)}) async-start(), calls=%async_computation.6 | async-start | bytes 9437184 | tf_op jit(solution)/shard_map/psum | solution.py:146
  439.3 10.0 slice-start.8
  441.7 7.6 copy-start.20
  441.7 7.7 slice-start.9
  449.4 15.3 %slice-start.6 = ((s8[5767168]{0:T(1024)(128)(4,1)}), s8[4194304]{0:T(1024)(128)(4,1)S(1)}, s32[]{:S(2)}) async-start(s8[5767168]{0:T(1024)(128)(4,1)} %bitcast.124), calls=%async_computation.18 | async-start | bytes 8388608
  454.9 9.8 slice-start.7
  475.7 341.2 %reduce-scatter.6.cloned.1.call-start = ((), (), s32[]{:S(2)}) async-start(), calls=%async_computation.8 | async-start | bytes 5308416 | tf_op jit(solution)/shard_map/reduce_scatter | solution.py:199
  646.8 5.6 copy-start.5
  646.8 5.9 copy-start.18
  714.2 35.1 %copy-start.40 = (bf16[576,4,128]{2,0,1:T(8,128)(2,1)S(1)}, bf16[576,4,128]{2,0,1:T(8,128)(2,1)}, u32[]{:S(2)}) copy-start(bf16[576,4,128]{2,0,1:T(8,128)(2,1)} %copy-done.39) | copy-start | bytes 1769476
  714.2 35.1 %copy-start.41 = (bf16[576,4,128]{2,0,1:T(8,128)(2,1)S(1)}, bf16[576,4,128]{2,0,1:T(8,128)(2,1)}, u32[]{:S(2)}) copy-start(bf16[576,4,128]{2,0,1:T(8,128)(2,1)} %get-tuple-element.44) | copy-start | bytes 1769476
  749.3 10.2 copy-start.22
  762.1 11.2 copy-start.9
  762.1 11.2 copy-start.28
  762.1 101.1 %all-gather.5.cloned.1.call-start = ((), (), s32[]{:S(2)}) async-start(), calls=%async_computation.7 | async-start | bytes 5898240 | tf_op jit(solution)/shard_map/all_gather | solution.py:188
  775.0 205.5 %all-reduce.15.cloned.1.call-start = ((), (), s32[]{:S(2)}) async-start(), calls=%async_computation.11 | async-start | bytes 5898240 | tf_op jit(solution)/shard_map/psum | solution.py:134
  775.0 88.2 %copy-start.7 = (f32[576,256]{1,0:T(8,128)S(1)}, f32[576,256]{1,0:T(8,128)}, u32[]{:S(2)}) copy-start(f32[576,256]{1,0:T(8,128)} %copy-done.6) | copy-start | bytes 1769476
  775.0 88.2 %copy-start.36 = (f32[576]{0:T(1024)S(1)}, f32[576]{0:T(1024)}, u32[]{:S(2)}) copy-start(f32[576]{0:T(1024)} %copy-done.35) | copy-start | bytes 6916
  775.0 88.2 %copy-start.47 = (f32[256]{0:T(256)S(1)}, f32[256]{0:T(256)}, u32[]{:S(2)}) copy-start(f32[256]{0:T(256)} %param.16) | copy-start | bytes 3076
  817.0 230.1 %reduce-scatter.8.cloned.1.call-start = ((), (), s32[]{:S(2)}) async-start(), calls=%async_computation.9 | async-start | bytes 2949120 | tf_op jit(solution)/shard_map/reduce_scatter | solution.py:218
  817.0 61.4 %copy-start.50 = (f32[576]{0:T(1024)S(1)}, f32[576]{0:T(1024)}, u32[]{:S(2)}) copy-start(f32[576]{0:T(1024)} %get-tuple-element.51) | copy-start | bytes 6916
  880.5 102.3 %copy-start.11 = (f32[576,128]{1,0:T(8,128)S(1)}, f32[576,128]{1,0:T(8,128)}, u32[]{:S(2)}) copy-start(f32[576,128]{1,0:T(8,128)} %copy-done.10) | copy-start | bytes 884740
  980.4 6.1 copy-start.3
  980.4 6.1 copy-start.45
  992.8 346.8 %all-reduce.13.cloned.1.call-start = ((), (), s32[]{:S(2)}) async-start(), calls=%async_computation.10 | async-start | bytes 50331648 | tf_op jit(solution)/shard_map/psum | solution.py:236
  992.9 8.8 copy-start.21
  992.9 8.8 copy-start.56
  992.9 22.1 %slice-start.2 = ((s8[4718592]{0:T(1024)(128)(4,1)}), s8[4194304]{0:T(1024)(128)(4,1)S(1)}, s32[]{:S(2)}) async-start(s8[4718592]{0:T(1024)(128)(4,1)} %bitcast.117), calls=%async_computation.14 | async-start | bytes 8388608
  1001.7 6.8 copy-start.19
  1001.7 6.8 copy-start.58
  1001.7 13.4 slice-start.3
  1008.5 6.5 copy-start.32
  1008.5 13.9 %slice-start = ((s8[4718592]{0:T(1024)(128)(4,1)}), s8[524288]{0:T(1024)(128)(4,1)S(1)}, s32[]{:S(2)}) async-start(s8[4718592]{0:T(1024)(128)(4,1)} %bitcast.115), calls=%async_computation.12 | async-start | bytes 1048576
  1015.1 7.3 slice-start.1
  1339.7 8.6 copy-start.13
  1339.7 13.8 slice-start.4
  1353.5 6.0 copy-start.14
  (30 other events, 93.0 us)
Sparse Core Ops, SparseCore 0:
  27.6 164.6 reduce-scatter.3
  264.5 170.9 all-reduce.8
  475.9 170.9 all-reduce.10
  775.1 88.0 all-gather.4
  866.2 114.1 all-reduce.14
  993.0 47.8 reduce-scatter.7
Sparse Core Ops, SparseCore 1:
  38.1 42.7 all-gather.2
  762.2 54.7 reduce-scatter.5
  1027.3 312.3 all-reduce.12
where the time goes:
time: 1390 us; the launch traced here: 1380 us
  waiting for transfers between devices  939 us (68%)
  matrix products  220 us (16%)
  other arithmetic  142 us (10%)
  blocking collectives  39.5 us (3%)
  local copies, waits for them, and re-layouts  18.4 us (1%)
  between operations  17 us (1%)
    psum x1, waiting for transfers between devices, per_device(): lax.psum(grad_q_down.astype(jnp.bfloat16), 'seq').astype(jnp.float32)  273 us
    psum x1, waiting for transfers between devices, per_device(): lax.psum(dense_nt(grad_gate_pre, gate_weight) + dense_nt(grad_up_pre, up_...  171 us
    psum x1, waiting for transfers between devices, per_device(): branch = lax.psum(dense(attn_low, out_weight), 'rank')  171 us
    reduce_scatter x1, waiting for transfers between devices, per_device(): lax.psum_scatter(dense(latent_low, q_up), 'rank', scatter_dimension=1, ti...  149 us
    psum x1, waiting for transfers between devices, per_device(): lax.psum(dense(hidden_low, down_weight).astype(jnp.bfloat16), 'rank')  95.7 us
    all_gather x1, waiting for transfers between devices, per_device(): grad_query_all = lax.all_gather(grad_query_pre, 'rank', axis=1, tiled=True)  46.2 us
    dot_general x7, matrix products, dense(): return jnp.dot(left, right, preferred_element_type=jnp.float32)  38.2 us
    dot_general x7, matrix products, dense_nt(): lax.dot_general(left, right, (((1,), (1,)), ((), ())), preferred_element_...  35.2 us
  transfers between devices with their start and end apart: 9, of which 7 were waited for; matrix products, arithmetic and copies ran while one was open for 7% of the time, Pallas kernels for 0%

commit v1 on v0

v1 whole, which is shorter than its diff:
```python
import functools

import jax
import jax.numpy as jnp
from jax import lax
from jax.experimental import pallas as pl
from jax.experimental.pallas import tpu as pltpu
from jax.sharding import PartitionSpec as P

EPS = 1e-05
BASE = 10000.0
NEG = -1e30
LOG2E = 1.4426950408889634
BF = jnp.bfloat16
F32 = jnp.float32
I32 = jnp.int32


def norm_rows(values, gain):
    recip = lax.rsqrt(jnp.mean(values * values, -1, keepdims=True) + EPS)
    return (values * recip * gain, recip)


def rotate(values, cosine_rows, sine_rows):
    half_dim = values.shape[-1] // 2
    front_half = values[..., :half_dim]
    back_half = values[..., half_dim:]
    return jnp.concatenate(
        [
            front_half * cosine_rows - back_half * sine_rows,
            front_half * sine_rows + back_half * cosine_rows,
        ],
        -1,
    )


def dense(left, right):
    return jnp.dot(left, right, preferred_element_type=F32)


def dense_tn(left, right):
    return lax.dot_general(left, right, (((0,), (0,)), ((), ())), preferred_element_type=F32)


def dense_nt(left, right):
    return lax.dot_general(left, right, (((1,), (1,)), ((), ())), preferred_element_type=F32)


def key_block(key_count):
    for size in (512, 256, 128):
        if key_count % size == 0:
            return size
    return key_count


def row_tile(rows):
    for parts in (3, 2):
        if rows % (parts * 128) == 0:
            return rows // parts
    return rows


def over_key_blocks(info_ref, size, tokens, run):
    first, low, high = info_ref[0], info_ref[1], info_ref[2]
    begin = low // size
    whole_end = jnp.maximum(first // size, begin)
    whole_begin = jnp.clip((high + size - 1) // size, begin, whole_end)
    end = (first + tokens + size - 1) // size
    lax.fori_loop(begin, whole_begin, lambda j, c: run(j, True), None)
    lax.fori_loop(whole_begin, whole_end, lambda j, c: run(j, False), None)
    lax.fori_loop(whole_end, end, lambda j, c: run(j, True), None)


def attend_kernel(
    size, tile, heads, info_ref, pre_ref, cos_ref, sin_ref, kv_ref, start_ref, index_ref,
    query_ref, out_ref, log_ref, max_ref, sum_ref, acc_ref,
):
    tokens = pre_ref.shape[0]
    width = kv_ref.shape[1] // 2
    half = width // 2
    scale = width**-0.5 * LOG2E
    cosine, sine = cos_ref[...], sin_ref[...]
    for h in range(heads):
        front = pre_ref[:, h * width : h * width + half]
        back = pre_ref[:, h * width + half : (h + 1) * width]
        rows = slice(h * tokens, (h + 1) * tokens)
        query_ref[rows, :half] = (front * cosine - back * sine).astype(BF)
        query_ref[rows, half:] = (front * sine + back * cosine).astype(BF)
    max_ref[...] = jnp.full(max_ref.shape, NEG, F32)
    sum_ref[...] = jnp.zeros(sum_ref.shape, F32)
    acc_ref[...] = jnp.zeros(acc_ref.shape, F32)

    def run(j, masked):
        base = pl.multiple_of(j * size, size)
        keys = kv_ref[pl.ds(base, size), :width]
        values = kv_ref[pl.ds(base, size), width:]
        for i in range(heads * tokens // tile):
            r = slice(i * tile, (i + 1) * tile)
            scores = dense_nt(keys, query_ref[r, :])
            if masked:
                at = base + lax.broadcasted_iota(I32, (size, tile), 0)
                allowed = (at >= start_ref[:, r]) & (at <= index_ref[:, r])
                scores = jnp.where(allowed, scores, NEG)
            old = max_ref[:, r]
            new = jnp.maximum(old, jnp.max(scores, 0, keepdims=True) * scale)
            probs = jnp.exp2(scores * scale - new)
            if masked:
                probs = jnp.where(allowed, probs, 0.0)
            fade = jnp.exp2(old - new)
            max_ref[:, r] = new
            sum_ref[:, r] = fade * sum_ref[:, r] + jnp.sum(probs, 0, keepdims=True)
            acc_ref[:, r] = fade * acc_ref[:, r] + dense_tn(values, probs.astype(BF))
        return None

    over_key_blocks(info_ref, size, tokens, run)
    total = sum_ref[...]
    log_ref[...] = max_ref[...] + jnp.log2(total)
    out = (acc_ref[...] * (1.0 / total)).T
    for h in range(heads):
        out_ref[:, h * width : (h + 1) * width] = out[h * tokens : (h + 1) * tokens, :]


def in_vmem(count):
    return [pl.BlockSpec(memory_space=pltpu.VMEM) for _ in range(count)]


def attend(info, query_pre, cosine, sine, kv, start, index):
    tokens, all_heads = query_pre.shape
    keys, width = kv.shape[0], kv.shape[1] // 2
    rows = tokens * (all_heads // width)
    return pl.pallas_call(
        functools.partial(attend_kernel, key_block(keys), row_tile(rows), all_heads // width),
        out_shape=(
            jax.ShapeDtypeStruct((rows, width), BF),
            jax.ShapeDtypeStruct((tokens, all_heads), F32),
            jax.ShapeDtypeStruct((1, rows), F32),
        ),
        in_specs=[pl.BlockSpec(memory_space=pltpu.SMEM)] + in_vmem(6),
        out_specs=tuple(in_vmem(3)),
        scratch_shapes=[
            pltpu.VMEM((1, rows), F32),
            pltpu.VMEM((1, rows), F32),
            pltpu.VMEM((width, rows), F32),
        ],
        compiler_params=pltpu.CompilerParams(vmem_limit_bytes=48 * 2**20),
        cost_estimate=pl.CostEstimate(
            flops=4 * rows * keys * width,
            bytes_accessed=12 * rows * width + 4 * keys * width,
            transcendentals=rows * keys,
        ),
        name="attend",
    )(info, query_pre, cosine, sine, kv, start, index)


def attend_back_kernel(
    size, tile, heads, info_ref, query_ref, grad_ref, delta_ref, log_ref, cos_ref, sin_ref, kv_ref, start_ref, index_ref,
    gq_ref, near_ref, far_ref, gout_ref, gk_ref, gv_ref, gqt_ref,
):
    tokens = grad_ref.shape[0]
    width = kv_ref.shape[1] // 2
    half = width // 2
    scale = width**-0.5
    for h in range(heads):
        gout_ref[h * tokens : (h + 1) * tokens, :] = grad_ref[:, h * width : (h + 1) * width]
    gk_ref[...] = jnp.zeros(gk_ref.shape, F32)
    gv_ref[...] = jnp.zeros(gv_ref.shape, F32)
    gqt_ref[...] = jnp.zeros(gqt_ref.shape, F32)

    def run(j, masked):
        base = pl.multiple_of(j * size, size)
        at_keys = pl.ds(base, size)
        keys = kv_ref[at_keys, :width]
        values = kv_ref[at_keys, width:]
        for i in range(heads * tokens // tile):
            r = slice(i * tile, (i + 1) * tile)
            query, gout = query_ref[r, :], gout_ref[r, :]
            probs = jnp.exp2(dense_nt(keys, query) * (scale * LOG2E) - log_ref[:, r])
            if masked:
                at = base + lax.broadcasted_iota(I32, (size, tile), 0)
                allowed = (at >= start_ref[:, r]) & (at <= index_ref[:, r])
                probs = jnp.where(allowed, probs, 0.0)
            gscores = (probs * (dense_nt(values, gout) - delta_ref[:, r])).astype(BF)
            gv_ref[at_keys, :] += dense(probs.astype(BF), gout)
            gk_ref[at_keys, :] += dense(gscores, query)
            gqt_ref[:, r] += dense_tn(keys, gscores)
        return None

    over_key_blocks(info_ref, size, tokens, run)
    mine = info_ref[3]
    for s in range(kv_ref.shape[0] // tokens):
        rows = slice(s * tokens, (s + 1) * tokens)
        gk = (gk_ref[rows, :] * scale).astype(BF)
        gv = gv_ref[rows, :].astype(BF)

        @pl.when(mine == s % 2)
        def _(s=s, gk=gk, gv=gv):
            near_ref[s // 2, :, :width] = gk
            near_ref[s // 2, :, width:] = gv

        @pl.when(mine != s % 2)
        def _(s=s, gk=gk, gv=gv):
            far_ref[s // 2, :, :width] = gk
            far_ref[s // 2, :, width:] = gv

    gq = (gqt_ref[...] * scale).T.astype(BF).astype(F32)
    cosine, sine = cos_ref[...], sin_ref[...]
    for h in range(heads):
        front = gq[h * tokens : (h + 1) * tokens, :half]
        back = gq[h * tokens : (h + 1) * tokens, half:]
        gq_ref[:, h * width : h * width + half] = (front * cosine + back * sine).astype(BF)
        gq_ref[:, h * width + half : (h + 1) * width] = (back * cosine - front * sine).astype(BF)


def attend_back(info, query, grad, delta, log, cosine, sine, kv, start, index):
    tokens, all_heads = grad.shape
    keys, width = kv.shape[0], kv.shape[1] // 2
    rows = tokens * (all_heads // width)
    blocks = keys // tokens
    return pl.pallas_call(
        functools.partial(attend_back_kernel, key_block(keys), row_tile(rows), all_heads // width),
        out_shape=(
            jax.ShapeDtypeStruct((tokens, all_heads), BF),
            jax.ShapeDtypeStruct((blocks // 2, tokens, 2 * width), BF),
            jax.ShapeDtypeStruct((blocks // 2, tokens, 2 * width), BF),
        ),
        in_specs=[pl.BlockSpec(memory_space=pltpu.SMEM)] + in_vmem(9),
        out_specs=tuple(in_vmem(3)),
        scratch_shapes=[
            pltpu.VMEM((rows, width), BF),
            pltpu.VMEM((keys, width), F32),
            pltpu.VMEM((keys, width), F32),
            pltpu.VMEM((width, rows), F32),
        ],
        compiler_params=pltpu.CompilerParams(vmem_limit_bytes=56 * 2**20),
        cost_estimate=pl.CostEstimate(
            flops=10 * rows * keys * width,
            bytes_accessed=6 * rows * width + 8 * keys * width,
            transcendentals=rows * keys,
        ),
        name="attend_back",
    )(info, query, grad, delta, log, cosine, sine, kv, start, index)


def swap(value, bit):
    count = lax.axis_size("seq")
    return lax.ppermute(value, "seq", [(i, i ^ (1 << bit)) for i in range(count)])


def bit_of(index, bit):
    return (index >> bit) & 1


def add_low(left, right):
    return (left.astype(F32) + right.astype(F32)).astype(BF)


def halve(value, axis, bit, seq_ix):
    own = bit_of(seq_ix, bit)
    keep = lax.dynamic_index_in_dim(value, own, axis, keepdims=False)
    send = lax.dynamic_index_in_dim(value, 1 - own, axis, keepdims=False)
    return add_low(keep, swap(send, bit))


def scatter_chips(value, seq_ix):
    bits = value.shape[0].bit_length() - 1
    shape = (2,) * bits + value.shape[2:]
    first, last = value[:, 0].reshape(shape), value[:, 1].reshape(shape)
    first_axes = list(range(bits))
    last_axes = list(range(bits))
    for step in range(bits):
        bit = step + 1
        axis = first_axes.index(bits - bit)
        first = halve(first, axis, bit, seq_ix)
        del first_axes[axis]
        bit = bits - step
        axis = last_axes.index(bits - bit)
        last = halve(last, axis, bit, seq_ix)
        del last_axes[axis]
    return jnp.stack([first, last])


def scatter_rows(near, far, seq_ix):
    return scatter_chips(add_low(near, swap(far, 0)), seq_ix)


def split_product(left, right, seq_ix):
    chips = lax.axis_size("seq") // 2
    rows = left.shape[1] // 2
    own = bit_of(seq_ix, 0)
    parts = []
    for core in (own, 1 - own):
        piece = lax.dynamic_slice_in_dim(left, core * rows, rows, 1)
        parts.append(dense_tn(piece, right).astype(BF))
    shape = (2, chips, rows // (2 * chips), right.shape[1])
    return [jnp.swapaxes(part.reshape(shape), 0, 1) for part in parts]


def gather_rows(piece):
    seq = lax.axis_size("seq")
    whole = lax.all_gather(piece, "seq", axis=0, tiled=False)
    whole = whole.reshape((seq // 2, 2) + piece.shape)
    whole = jnp.transpose(whole, (1, 2, 0, 3, 4))
    return whole.reshape(seq * piece.shape[0] * piece.shape[1], piece.shape[2])


def reduce_product(left, right, seq_ix):
    near, far = split_product(left, right, seq_ix)
    return gather_rows(scatter_rows(near, far, seq_ix)).astype(F32)


def gather_kv(local, seq_ix):
    seq = lax.axis_size("seq")
    if seq != 8:
        return lax.all_gather(local, "seq", axis=0, tiled=True)
    half = local.shape[0] // 2
    by_x = swap(local, 1)
    by_y = swap(local, 2)
    across = jnp.concatenate([swap(by_x[:half], 2), swap(by_y[half:], 1)], 0)
    blocks = {0: local, 2: by_x, 4: by_y, 6: across}
    for mask in (0, 2, 4, 6):
        blocks[mask + 1] = swap(blocks[mask], 0)
    whole = jnp.zeros((seq * local.shape[0], local.shape[1]), local.dtype)
    for mask, block in blocks.items():
        whole = lax.dynamic_update_slice_in_dim(
            whole, block, (seq_ix ^ mask) * local.shape[0], 0
        )
    return whole


def high_low(values):
    high = values.astype(BF)
    return [high, (values - high.astype(F32)).astype(BF)]


def per_device(
    tokens_in,
    norm1_gain,
    q_down,
    latent_gain,
    q_up,
    kv_weight,
    out_weight,
    norm2_gain,
    gate_weight,
    up_weight,
    down_weight,
    doc_ids,
    out_grad,
):
    row_count, model_width = tokens_in.shape
    rank_count = lax.axis_size("rank")
    seq_count = lax.axis_size("seq")
    rank_ix = lax.axis_index("rank")
    seq_ix = lax.axis_index("seq")
    head_dim = kv_weight.shape[1] // 2
    local_heads = out_weight.shape[0] // head_dim
    first_row = seq_ix * row_count
    core = bit_of(seq_ix, 0)
    own_rows = row_count // rank_count
    rank_cols = q_down.shape[1]
    rank_width = rank_cols * rank_count

    half_rows = q_up.shape[0] // 2
    up_half = lax.dynamic_slice_in_dim(q_up, core * half_rows, half_rows, 0)
    up_half = lax.all_to_all(up_half, "rank", 1, 0, tiled=True)
    up_other = swap(up_half, 0)
    up_half = up_half.reshape(rank_count, 1, half_rows, -1)
    up_other = up_other.reshape(rank_count, 1, half_rows, -1)
    q_up_own = jnp.concatenate(
        [jnp.where(core == 0, up_half, up_other), jnp.where(core == 0, up_other, up_half)], 1
    ).reshape(rank_width, -1)

    ids_local = lax.dynamic_slice_in_dim(doc_ids, first_row, row_count, 0)
    start = jnp.sum((doc_ids[None, :] < ids_local[:, None]).astype(I32), 1)
    query_index = first_row + jnp.arange(row_count, dtype=I32)
    position = (query_index - start).astype(F32)
    half_dim = head_dim // 2
    freqs = BASE ** (-jnp.arange(half_dim, dtype=F32) / half_dim)
    angle = position[:, None] * freqs[None, :]
    cosine_rows, sine_rows = jnp.cos(angle), jnp.sin(angle)
    start_rows = jnp.tile(start, local_heads)[None]
    index_rows = jnp.tile(query_index, local_heads)[None]
    info = jnp.stack([first_row, start[0], start[-1], core]).astype(I32)

    tokens = tokens_in.astype(F32)
    normed_in, recip1 = norm_rows(tokens, norm1_gain)
    normed_low = normed_in.astype(BF)
    kv_pre = dense(normed_low, kv_weight)
    key_local = rotate(kv_pre[:, :head_dim], cosine_rows, sine_rows)
    kv_local = jnp.concatenate([key_local, kv_pre[:, head_dim:]], -1).astype(BF)
    kv_all = gather_kv(kv_local, seq_ix)

    latent = dense(normed_low, q_down)
    high, rest = high_low(latent_gain)
    low = (latent_gain - high.astype(F32) - rest.astype(F32)).astype(BF)
    gain_rows = jnp.stack([high, rest, low] + [jnp.zeros_like(high)] * 13)
    gathered = lax.all_gather(
        jnp.concatenate([latent.astype(BF), gain_rows], 0), "rank", axis=1, tiled=True
    ).astype(F32)
    latent_all = gathered[:row_count]
    gain_all = gathered[row_count] + gathered[row_count + 1] + gathered[row_count + 2]
    recip_c = lax.rsqrt(jnp.mean(latent_all * latent_all, -1, keepdims=True) + EPS)
    latent_low = (latent_all * recip_c * gain_all).astype(BF)
    query_pre = dense(latent_low, q_up_own)

    query, attn_vals, log_total = attend(
        info, query_pre, cosine_rows, sine_rows, kv_all, start_rows, index_rows
    )
    attn_low = attn_vals.astype(BF)
    branch = lax.psum_scatter(
        dense(attn_low, out_weight).astype(BF), "rank", scatter_dimension=0, tiled=True
    )
    tokens_rows = lax.dynamic_slice_in_dim(tokens_in, rank_ix * own_rows, own_rows, 0)
    residual = tokens_rows.astype(F32) + branch.astype(F32)
    normed_mid, recip2 = norm_rows(residual, norm2_gain)
    mid_low = lax.all_gather(normed_mid.astype(BF), "rank", axis=0, tiled=True)

    grad_hidden = dense_nt(out_grad, down_weight)
    gate_pre = dense(mid_low, gate_weight)
    up_pre = dense(mid_low, up_weight)
    sigmoid_gate = jax.nn.sigmoid(gate_pre)
    activated = gate_pre * sigmoid_gate
    hidden_low = (activated * up_pre).astype(BF)
    grad_gate_pre = (
        grad_hidden * up_pre * sigmoid_gate * (1.0 + gate_pre * (1.0 - sigmoid_gate))
    ).astype(BF)
    grad_up_pre = (grad_hidden * activated).astype(BF)
    grad_mid = lax.psum_scatter(
        (dense_nt(grad_gate_pre, gate_weight) + dense_nt(grad_up_pre, up_weight)).astype(BF),
        "rank",
        scatter_dimension=0,
        tiled=True,
    ).astype(F32)
    feed_out = lax.psum_scatter(
        dense(hidden_low, down_weight).astype(BF), "rank", scatter_dimension=0, tiled=True
    )
    layer_out = lax.all_gather(
        (residual + feed_out.astype(F32)).astype(BF), "rank", axis=0, tiled=True
    )
    grad_gate = reduce_product(mid_low, grad_gate_pre, seq_ix)
    grad_up = reduce_product(mid_low, grad_up_pre, seq_ix)
    grad_down = reduce_product(hidden_low, out_grad, seq_ix)

    gained_mid = grad_mid * norm2_gain
    stat_mid = jnp.sum(residual * gained_mid, -1, keepdims=True)
    out_grad_rows = lax.dynamic_slice_in_dim(out_grad, rank_ix * own_rows, own_rows, 0)
    grad_residual = (
        out_grad_rows.astype(F32)
        + recip2 * gained_mid
        - residual * recip2**3 * stat_mid / model_width
    )
    grad_norm2 = jnp.sum(grad_mid * residual * recip2, 0)
    grad_branch = lax.all_gather(grad_residual.astype(BF), "rank", axis=0, tiled=True)
    grad_attn_wide = dense_nt(grad_branch, out_weight)
    grad_attn = grad_attn_wide.astype(BF)
    grad_out = reduce_product(attn_low, grad_branch, seq_ix)
    delta = jnp.sum(
        (grad_attn.astype(F32) * attn_vals).reshape(row_count, local_heads, head_dim), -1
    ).T.reshape(1, -1)

    grad_query, near, far = attend_back(
        info, query, grad_attn, delta, log_total, cosine_rows, sine_rows, kv_all, start_rows, index_rows
    )

    chips = seq_count // 2
    kv_shape = (chips, 2, row_count // 2, 2 * head_dim)
    summed = scatter_rows(near.reshape(kv_shape), far.reshape(kv_shape), seq_ix)
    summed = lax.psum(summed.reshape(row_count, 2 * head_dim), "rank").astype(F32)
    key_back = rotate(summed[:, :head_dim], cosine_rows, -sine_rows)
    grad_kv = jnp.concatenate([key_back, summed[:, head_dim:]], -1).astype(BF)

    grad_latent_part = dense_nt(grad_query, q_up_own).astype(BF)
    norm2_rows = jnp.concatenate(high_low(grad_norm2)).reshape(-1, rank_width)
    extra = norm2_rows.shape[0]
    norm2_rows = jnp.pad(norm2_rows, ((0, -extra % 16), (0, 0)))
    over_ranks = lax.psum(jnp.concatenate([grad_latent_part, norm2_rows], 0), "rank").astype(F32)
    grad_latent_in = over_ranks[:row_count]
    grad_norm2 = jnp.sum(
        over_ranks[row_count : row_count + extra].reshape(2, model_width), 0
    )
    gained_latent = grad_latent_in * gain_all
    stat_latent = jnp.sum(latent_all * gained_latent, -1, keepdims=True)
    grad_latent = (
        recip_c * gained_latent - latent_all * recip_c**3 * stat_latent / rank_width
    ).astype(BF)
    own_latent = lambda v: lax.dynamic_slice_in_dim(v, rank_ix * rank_cols, rank_cols, 1)
    grad_latent_gain = jnp.sum(own_latent(grad_latent_in) * latent * recip_c, 0)

    near, far = split_product(grad_query, latent_low, seq_ix)
    piece = scatter_rows(near, far, seq_ix)
    piece = lax.all_to_all(piece, "rank", 2, 0, tiled=True)
    piece = piece.reshape(rank_count * 2, piece.shape[1], rank_cols)
    whole = lax.all_gather(piece, "seq", axis=0, tiled=False)
    whole = whole.reshape(chips, 2, rank_count, 2, piece.shape[1], rank_cols)
    grad_q_up = jnp.transpose(whole, (5, 2, 1, 3, 0, 4)).reshape(rank_cols, -1).astype(F32)

    col_count = model_width // rank_count
    col_start = rank_ix * col_count
    cols = lambda v: lax.dynamic_slice_in_dim(v, col_start, col_count, v.ndim - 1)
    q_down_rows = lax.all_to_all(q_down, "rank", 0, 1, tiled=True)
    kv_rows = lax.dynamic_slice_in_dim(kv_weight, col_start, col_count, 0)
    grad_normed = dense_nt(grad_latent, q_down_rows) + dense_nt(grad_kv, kv_rows)
    norm1_stat = (
        jnp.sum(grad_latent.astype(F32) * latent_all, -1, keepdims=True)
        + jnp.sum(grad_kv.astype(F32) * kv_pre, -1, keepdims=True)
    ) / recip1
    tokens_own = cols(tokens_in).astype(F32)
    grad_in = (
        cols(grad_branch).astype(F32)
        + recip1 * cols(norm1_gain) * grad_normed
        - tokens_own * recip1**3 * norm1_stat / model_width
    )
    grad_norm1 = jnp.sum(grad_normed * tokens_own * recip1, 0)

    grad_q_down = lax.psum(
        dense_tn(normed_low, own_latent(grad_latent)).astype(BF), "seq"
    ).astype(F32)
    grad_kv_weight = dense_tn(cols(normed_low), grad_kv).astype(BF)
    small = jnp.concatenate([grad_norm1, grad_latent_gain, grad_norm2])
    small = jnp.concatenate(high_low(small)).reshape(2, -1)
    count = small.shape[1]
    kv_cols = grad_kv_weight.shape[1]
    small_rows = jnp.pad(small.reshape(-1), (0, -2 * count % (16 * kv_cols))).reshape(-1, kv_cols)
    last = lax.psum(jnp.concatenate([grad_kv_weight, small_rows], 0), "seq").astype(F32)
    grad_kv_weight = last[:col_count]
    small = jnp.sum(last[col_count:].reshape(-1)[: 2 * count].reshape(2, count), 0)
    grad_norm1 = small[:col_count]
    grad_latent_gain = small[col_count : col_count + rank_cols]
    grad_norm2 = small[col_count + rank_cols :]
    return (
        layer_out,
        grad_in,
        grad_norm1,
        grad_q_down,
        grad_latent_gain,
        grad_q_up,
        grad_kv_weight,
        grad_out,
        grad_norm2,
        grad_gate,
        grad_up,
        grad_down,
    )


def solution(mesh):
    return jax.shard_map(
        per_device,
        mesh=mesh,
        in_specs=(
            P("seq", None),
            P(),
            P(None, "rank"),
            P("rank"),
            P("rank", None),
            P(),
            P("rank", None),
            P(),
            P(None, "rank"),
            P(None, "rank"),
            P("rank", None),
            P(),
            P("seq", None),
        ),
        out_specs=(
            P("seq", None),
            P("seq", "rank"),
            P("rank"),
            P(None, "rank"),
            P("rank"),
            P("rank", None),
            P("rank", None),
            P("rank", None),
            P(),
            P(None, "rank"),
            P(None, "rank"),
            P("rank", None),
        ),
        check_vma=False,
    )
```

time: 1390 us -> 965 us (0.69)
  waiting for transfers between devices: 939 us -> 479 us
  matrix products: 220 us -> 117 us
  local copies, waits for them, and re-layouts: 18.4 us -> 114 us
  starting transfers between devices: 0.59 us -> 95.2 us
  other arithmetic: 142 us -> 97.9 us
  blocking collectives: 39.5 us -> 0 us
  Pallas kernels: 0 us -> 34.1 us
    psum x4 -> x2, waiting for transfers between devices: 711 us -> 44.2 us  [the longest x1 44.2 us: per_device(): lax.psum(jnp.concatenate([grad_kv_weight, small_rows], 0), 'seq')]
    dot_general x13 -> x7, matrix products: 151 us -> 37.3 us  [dense(): return jnp.dot(left, right, preferred_element_type=F32)]
    ppermute x0 -> x39, waiting for transfers between devices: none -> 107 us  [swap(): return lax.ppermute(value, 'seq', [(i, i ^ 1 << bit) for i in range(count)])]
    all_gather x2 -> x9, waiting for transfers between devices: 46.2 us -> 141 us  [the longest x1 49.4 us: per_device(): lax.all_gather(grad_residual.astype(BF), 'rank', axis=0, tiled=True)]
    ppermute x0 -> x39, starting transfers between devices: none -> 78.2 us  [swap(): return lax.ppermute(value, 'seq', [(i, i ^ 1 << bit) for i in range(count)])]
    convert_element_type x2 -> x5, local copies, waits for them, and re-layouts: 1.32 us -> 38.1 us  [the longest x4 35.8 us: reduce_product(): return gather_rows(scatter_rows(near, far, seq_ix)).astype(F32)]
    pallas_call x0 -> x2, Pallas kernels: none -> 34.1 us  [the longest x1 18.6 us: attend_back(): pl.pallas_call(functools.partial(attend_back_kernel, key_block(keys), row...]
    psum x3 -> x0, blocking collectives: 31 us -> none  [the longest x1 14.1 us: per_device(): lax.psum(grad_norm1.astype(jnp.bfloat16), 'seq').astype(jnp.float32)]
  transfers between devices with their start and end apart: 9 -> 56, of which waited for: 7 -> 31; matrix products, arithmetic and copies ran while one was open for 7% -> 23% of each run, Pallas kernels for 0% -> 0%
where the time goes in v1:
time: 965 us; the launch traced here: 954 us
  waiting for transfers between devices  479 us (50%)
  matrix products  117 us (12%)
  local copies, waits for them, and re-layouts  114 us (12%)
  other arithmetic  97.9 us (10%)
  starting transfers between devices  95.2 us (10%)
  Pallas kernels  34.1 us (4%)
  between operations  15.8 us (2%)
    ppermute x39, waiting for transfers between devices, swap(): return lax.ppermute(value, 'seq', [(i, i ^ 1 << bit) for i in range(count)])  107 us
    ppermute x39, starting transfers between devices, swap(): return lax.ppermute(value, 'seq', [(i, i ^ 1 << bit) for i in range(count)])  78.2 us
    reduce_scatter x1, waiting for transfers between devices, per_device(): lax.psum_scatter(dense(attn_low, out_weight).astype(BF), 'rank', scatter_...  68.7 us
    all_gather x1, waiting for transfers between devices, per_device(): lax.all_gather(grad_residual.astype(BF), 'rank', axis=0, tiled=True)  49.4 us
    all_gather x1, waiting for transfers between devices, per_device(): mid_low = lax.all_gather(normed_mid.astype(BF), 'rank', axis=0, tiled=True)  49 us
    reduce_scatter x1, waiting for transfers between devices, per_device(): lax.psum_scatter(dense(hidden_low, down_weight).astype(BF), 'rank', scatt...  48.6 us
    dot_general x12, matrix products, dense_tn(): lax.dot_general(left, right, (((0,), (0,)), ((), ())), preferred_element_...  46.9 us
    psum x1, waiting for transfers between devices, per_device(): lax.psum(jnp.concatenate([grad_kv_weight, small_rows], 0), 'seq')  44.2 us
  transfers between devices with their start and end apart: 56, of which 31 were waited for; matrix products, arithmetic and copies ran while one was open for 23% of the time, Pallas kernels for 0%

profile of v1, /device:TPU:25, one launch (start us, length us, event | category | flops | bytes accessed | tf_op | source)
XLA Modules:
  0.0 953.7 jit_solution(10558809694065911661)
XLA Ops:
  30.4 4.5 all-to-all-start
  58.0 17.7 %all-to-all-done = bf16[128,4,1024]{0,2,1:T(8,128)(2,1)} async-done(((bf16[128,4,1024]{0,2,1:T(8,128)(2,1)}), bf16[128,4,1024]{0,2,1:T(8,128)(2,1)}, u32[]{:S(2)}, u32[]{:S(2)}) %all-to-all-start) | async-done | bytes 1048608 | tf_op jit(solution)/shard_map/all_to_all | solution.py:365
  94.5 4.7 fusion.125.pre_ref
  99.3 15.5 %attend.1 = (bf16[2304,256]{1,0:T(8,128)(2,1)S(1)}, f32[576,1024]{1,0:T(8,128)S(1)}, f32[1,2304]{1,0:T(1,128)S(1)}) custom-call(s32[4]{0:T(128)S(1)} %pad_add_fusion.info_ref, f32[576,1024]{1,0:T(8,128)} %fusion.125.pre_ref, f32[576,128]{1,0:T(8,128)S(1)} %get-tuple-element.122.cos_ref, f32[576,128]{1,0:T(8,128)S(1)} %get-tuple-element.121.sin_ref, ...), custom_call_target="tpu_custom_call" | custom-call | flops 10871635968 | bytes 11796480 | tf_op jit(solution)/shard_map/attend/pallas_call | solution.py:131
  121.6 68.7 %reduce-scatter.4.cloned.1.call-done = bf16[144,2048]{1,0:T(8,128)(2,1)} async-done(((bf16[576,2048]{1,0:T(8,128)(2,1)}), bf16[144,2048]{1,0:T(8,128)(2,1)}) %reduce-scatter.4.cloned.1.call-update) | async-done | bytes 589840 | tf_op jit(solution)/shard_map/reduce_scatter | solution.py:410
  194.6 49.0 %all-gather.16.cloned.1.call-done = bf16[576,2048]{1,0:T(8,128)(2,1)} async-done(((bf16[144,2048]{1,0:T(8,128)(2,1)}), bf16[576,2048]{1,0:T(8,128)(2,1)}) %all-gather.16.cloned.1.call-update) | async-done | bytes 2359312 | tf_op jit(solution)/shard_map/all_gather | solution.py:416
  243.6 9.0 fusion.128
  252.6 8.3 fusion.127
  260.9 9.7 %multiply_convert_fusion = (bf16[576,1408]{1,0:T(8,128)(2,1)S(1)}, bf16[576,1408]{1,0:T(8,128)(2,1)S(1)}, bf16[576,1408]{1,0:T(8,128)(2,1)}) fusion(f32[576,1408]{1,0:T(8,128)} %fusion.127, f32[576,1408]{1,0:T(8,128)} %fusion.128, bf16[576,2048]{1,0:T(8,128)(2,1)S(1)} %copy-done.38, bf16[1408,2048]{1,0:T(8,128)(2,1)} %param.23), kind=kOutput, calls=%fused_computation.32 | convolution fusion | flops 3334053888 | bytes 19480576 | tf_op jit(solution)/shard_map/dot_general | solution.py:46
  274.6 5.1 add_convert_fusion
  279.9 8.4 convolution_convert_fusion.6
  288.4 39.0 %reduce-scatter.8.cloned.1.call-done = bf16[144,2048]{1,0:T(8,128)(2,1)} async-done(((bf16[576,2048]{1,0:T(8,128)(2,1)}), bf16[144,2048]{1,0:T(8,128)(2,1)}) %reduce-scatter.8.cloned.1.call-update) | async-done | bytes 589840 | tf_op jit(solution)/shard_map/reduce_scatter | solution.py:428
  329.1 48.6 %reduce-scatter.6.cloned.1.call-done = bf16[144,2048]{1,0:T(8,128)(2,1)} async-done(((bf16[576,2048]{1,0:T(8,128)(2,1)}), bf16[144,2048]{1,0:T(8,128)(2,1)}) %reduce-scatter.6.cloned.1.call-update) | async-done | bytes 589840 | tf_op jit(solution)/shard_map/reduce_scatter | solution.py:434
  381.0 49.4 %all-gather.20.cloned.1.call-done = bf16[576,2048]{1,0:T(8,128)(2,1)} async-done(((bf16[144,2048]{1,0:T(8,128)(2,1)}), bf16[576,2048]{1,0:T(8,128)(2,1)}) %all-gather.20.cloned.1.call-update) | async-done | bytes 2359312 | tf_op jit(solution)/shard_map/all_gather | solution.py:453
  430.4 8.1 convert_multiply_fusion.2
  445.3 18.6 %attend_back.1 = (bf16[576,1024]{1,0:T(8,128)(2,1)}, bf16[4,576,512]{2,1,0:T(8,128)(2,1)}, bf16[4,576,512]{2,1,0:T(8,128)(2,1)}) custom-call(s32[4]{0:T(128)} %copy-done.6, bf16[2304,256]{1,0:T(8,128)(2,1)} %copy-done.7, bf16[576,1024]{1,0:T(8,128)(2,1)} %get-tuple-element.137.grad_ref, f32[1,2304]{1,0:T(1,128)} %reshape.265.delta_ref, f32[1,2304]{1,0:T(1,128)} %copy-done.8, ...), custom_call_target="tpu_custom_call" | custom-call | flops 27179089920 | bytes 12976128 | tf_op jit(solution)/shard_map/attend_back/pallas_call | solution.py:219
  467.2 4.8 collective-permute-done.9
  475.4 8.2 collective-permute-start.10
  483.7 16.4 %collective-permute-start.12 = (bf16[2,288,512]{2,1,0:T(8,128)(2,1)S(1)}, bf16[2,288,512]{2,1,0:T(8,128)(2,1)S(1)}, u32[]{:S(2)}, u32[]{:S(2)}) collective-permute-start(bf16[2,288,512]{2,1,0:T(8,128)(2,1)S(1)} %dynamic-slice_bitcast_fusion.6), channel_id=1, source_target_pairs={{0,16},{4,20},{8,24},{12,28},{16,0},{20,4},{24,8},{28,12},{1,17},{... | collective-permute-start | bytes 1769480 | tf_op jit(solution)/shard_map/ppermute | solution.py:246
  501.8 12.0 %collective-permute-start.11 = (bf16[288,512]{1,0:T(8,128)(2,1)S(1)}, bf16[288,512]{1,0:T(8,128)(2,1)S(1)}, u32[]{:S(2)}, u32[]{:S(2)}) collective-permute-start(bf16[288,512]{1,0:T(8,128)(2,1)S(1)} %dynamic-slice_bitcast_fusion.17), channel_id=1, source_target_pairs={{0,16},{4,20},{8,24},{12,28},{16,0},{20,4},{24,8},{28,12},{1,17},{... | collective-permute-start | bytes 884744 | tf_op jit(solution)/shard_map/ppermute | solution.py:246
  528.0 6.2 convolution_convert_fusion.4
  546.8 4.3 collective-permute-done.17
  557.1 5.6 all-to-all-start.2
  562.7 5.7 fusion.1
  573.7 9.2 collective-permute-done.35
  586.6 7.2 collective-permute-done.36
  597.1 6.0 convolution_convert_fusion
  603.0 9.1 collective-permute-start.29
  612.1 4.4 convolution_convert_fusion.1
  622.2 15.7 %collective-permute-done.30 = bf16[2,128,1408]{2,1,0:T(8,128)(2,1)S(1)} collective-permute-done((bf16[2,128,1408]{2,1,0:T(8,128)(2,1)S(1)}, bf16[2,128,1408]{2,1,0:T(8,128)(2,1)S(1)}, u32[]{:S(2)}, u32[]{:S(2)}) %collective-permute-start.30) | collective-permute-done | bytes 720928 | tf_op jit(solution)/shard_map/ppermute | solution.py:246
  640.4 7.1 collective-permute-done.31
  650.1 4.5 convolution_convert_fusion.2
  664.2 22.5 %collective-permute-done.25 = bf16[2,128,1408]{2,1,0:T(8,128)(2,1)S(1)} collective-permute-done((bf16[2,128,1408]{2,1,0:T(8,128)(2,1)S(1)}, bf16[2,128,1408]{2,1,0:T(8,128)(2,1)S(1)}, u32[]{:S(2)}, u32[]{:S(2)}) %collective-permute-start.25) | collective-permute-done | bytes 720928 | tf_op jit(solution)/shard_map/ppermute | solution.py:246
  688.8 7.0 collective-permute-done.26
  698.0 5.1 convolution_convert_fusion.8
  705.3 4.5 all-to-all-start.1
  720.3 12.9 %all-to-all-done.1 = bf16[4,512,256]{2,1,0:T(8,128)(2,1)S(1)} async-done(((bf16[4,512,256]{2,1,0:T(8,128)(2,1)}), bf16[4,512,256]{2,1,0:T(8,128)(2,1)S(1)}, u32[]{:S(2)}, u32[]{:S(2)}) %all-to-all-start.1) | async-done | bytes 1048608 | tf_op jit(solution)/shard_map/all_to_all | solution.py:500
  736.4 7.1 collective-permute-done.20
  782.2 5.6 copy.101
  787.8 8.8 convert_bitcast_fusion
  796.6 10.9 %copy.100 = f32[2,2,4,88,2048]{4,3,2,1,0:T(8,128)} copy(f32[2,2,4,88,2048]{4,3,1,0,2:T(8,128)} %convert_bitcast_fusion) | data formatting | bytes 23068672 | tf_op jit(solution)/shard_map/convert_element_type | solution.py:308
  807.5 8.3 convert_bitcast_fusion.1
  815.8 10.8 %copy.99 = f32[2,2,4,128,1408]{4,3,2,1,0:T(8,128)} copy(f32[2,2,4,128,1408]{4,3,1,0,2:T(8,128)} %convert_bitcast_fusion.1) | data formatting | bytes 23068672 | tf_op jit(solution)/shard_map/convert_element_type | solution.py:308
  826.6 10.0 %all-gather.26.cloned.1.call-done = bf16[16,128,1408]{2,1,0:T(8,128)(2,1)} async-done(((bf16[2,128,1408]{2,1,0:T(8,128)(2,1)}), bf16[16,128,1408]{2,1,0:T(8,128)(2,1)}) %all-gather.26.cloned.1.call-update) | async-done | bytes 5767184 | tf_op jit(solution)/shard_map/all_gather | solution.py:300
  836.5 8.1 convert_bitcast_fusion.2
  844.6 10.1 %copy.98 = f32[2,2,4,128,1408]{4,3,2,1,0:T(8,128)} copy(f32[2,2,4,128,1408]{4,3,1,0,2:T(8,128)} %convert_bitcast_fusion.2) | data formatting | bytes 23068672 | tf_op jit(solution)/shard_map/convert_element_type | solution.py:308
  854.8 44.2 %all-reduce.7.cloned.1.call-done = (bf16[528,512]{1,0:T(8,128)(2,1)}, bf16[2048,256]{1,0:T(8,128)(2,1)}) async-done(((bf16[528,512]{1,0:T(8,128)(2,1)}, bf16[2048,256]{1,0:T(8,128)(2,1)}), (bf16[528,512]{1,0:T(8,128)(2,1)}, bf16[2048,256]{1,0:T(8,128)(2,1)})) %all-reduce.7.cloned.1.call-update) | async-done | bytes 1589264 | tf_op jit(solution)/shard_map/psum | solution.py:524
  905.2 32.8 %all-gather.24.cloned.1.call-done = bf16[16,64,2048]{2,1,0:T(8,128)(2,1)} async-done(((bf16[2,64,2048]{2,1,0:T(8,128)(2,1)}), bf16[16,64,2048]{2,1,0:T(8,128)(2,1)}) %all-gather.24.cloned.1.call-update) | async-done | bytes 4194320 | tf_op jit(solution)/shard_map/all_gather | solution.py:300
  (420 shorter events, 238.5 us)
Async XLA Ops:
  7.2 73.9 %all-gather.14.cloned.1.call-start = ((), (), s32[]{:S(2)}) async-start(), calls=%async_computation.6 | async-start | bytes 1515520 | tf_op jit(solution)/shard_map/all_gather | solution.py:397
  17.9 21.4 %collective-permute-start.2 = (bf16[576,512]{1,0:T(8,128)(2,1)}, bf16[576,512]{1,0:T(8,128)(2,1)S(1)}, u32[]{:S(2)}, u32[]{:S(2)}) collective-permute-start(bf16[576,512]{1,0:T(8,128)(2,1)} %get-tuple-element.119), channel_id=1, source_target_pairs={{0,16},{4,20},{8,24},{12,28},{16,0},{20,4},{24,8},{28,12},{1,17},{... | collective-permute-start | bytes 1769480 | tf_op jit(solution)/shard_map/ppermute | solution.py:246
  19.2 17.6 %collective-permute-start.1 = (bf16[576,512]{1,0:T(8,128)(2,1)}, bf16[576,512]{1,0:T(8,128)(2,1)}, u32[]{:S(2)}, u32[]{:S(2)}) collective-permute-start(bf16[576,512]{1,0:T(8,128)(2,1)} %get-tuple-element.119), channel_id=1, source_target_pairs={{0,8},{4,12},{8,0},{12,4},{16,24},{20,28},{24,16},{28,20},{1,9},{5... | collective-permute-start | bytes 1769480 | tf_op jit(solution)/shard_map/ppermute | solution.py:246
  30.4 45.2 %all-to-all-start = ((bf16[128,4,1024]{0,2,1:T(8,128)(2,1)}), bf16[128,4,1024]{0,2,1:T(8,128)(2,1)}, u32[]{:S(2)}, u32[]{:S(2)}) async-start(bf16[128,4,1024]{0,2,1:T(8,128)(2,1)} %bitcast.325), calls=%async_computation | async-start | bytes 2097152 | tf_op jit(solution)/shard_map/all_to_all | solution.py:365
  35.0 155.3 %reduce-scatter.4.cloned.1.call-start = ((), (), s32[]{:S(2)}) async-start(), calls=%async_computation.7 | async-start | bytes 2949120 | tf_op jit(solution)/shard_map/reduce_scatter | solution.py:410
  35.0 19.4 %collective-permute-start.5 = (bf16[576,512]{1,0:T(8,128)(2,1)}, bf16[576,512]{1,0:T(8,128)(2,1)}, u32[]{:S(2)}, u32[]{:S(2)}) collective-permute-start(bf16[576,512]{1,0:T(8,128)(2,1)} %get-tuple-element.119), channel_id=1, source_target_pairs={{0,4},{4,0},{8,12},{12,8},{16,20},{20,16},{24,28},{28,24},{1,5},{5... | collective-permute-start | bytes 1769480 | tf_op jit(solution)/shard_map/ppermute | solution.py:246
  38.5 9.0 collective-permute-start.3
  40.0 9.1 collective-permute-start.4
  41.9 15.3 %collective-permute-start.7 = (bf16[576,512]{1,0:T(8,128)(2,1)S(1)}, bf16[576,512]{1,0:T(8,128)(2,1)S(1)}, u32[]{:S(2)}, u32[]{:S(2)}) collective-permute-start(bf16[576,512]{1,0:T(8,128)(2,1)S(1)} %collective-permute-done.2), channel_id=1, source_target_pairs={{0,4},{4,0},{8,12},{12,8},{16,20},{20,16},{24,28},{28,24},{1,5},{5... | collective-permute-start | bytes 1769480 | tf_op jit(solution)/shard_map/ppermute | solution.py:246
  42.5 13.8 %collective-permute-start.6 = (bf16[576,512]{1,0:T(8,128)(2,1)}, bf16[576,512]{1,0:T(8,128)(2,1)S(1)}, u32[]{:S(2)}, u32[]{:S(2)}) collective-permute-start(bf16[576,512]{1,0:T(8,128)(2,1)} %collective-permute-done.1), channel_id=1, source_target_pairs={{0,4},{4,0},{8,12},{12,8},{16,20},{20,16},{24,28},{28,24},{1,5},{5... | collective-permute-start | bytes 1769480 | tf_op jit(solution)/shard_map/ppermute | solution.py:246
  50.8 28.4 %collective-permute-start.8 = (bf16[576,512]{1,0:T(8,128)(2,1)}, bf16[576,512]{1,0:T(8,128)(2,1)}, u32[]{:S(2)}, u32[]{:S(2)}) collective-permute-start(bf16[576,512]{1,0:T(8,128)(2,1)} %constant_dynamic-update-slice_fusion.8), channel_id=1, source_target_pairs={{0,4},{4,0},{8,12},{12,8},{16,20},{20,16},{24,28},{28,24},{1,5},{5... | collective-permute-start | bytes 1769480 | tf_op jit(solution)/shard_map/ppermute | solution.py:246
  121.6 122.0 %all-gather.16.cloned.1.call-start = ((), (), s32[]{:S(2)}) async-start(), calls=%async_computation.8 | async-start | bytes 2949120 | tf_op jit(solution)/shard_map/all_gather | solution.py:416
  194.2 133.3 %reduce-scatter.8.cloned.1.call-start = ((), (), s32[]{:S(2)}) async-start(), calls=%async_computation.11 | async-start | bytes 2949120 | tf_op jit(solution)/shard_map/reduce_scatter | solution.py:428
  279.7 98.0 %reduce-scatter.6.cloned.1.call-start = ((), (), s32[]{:S(2)}) async-start(), calls=%async_computation.9 | async-start | bytes 2949120 | tf_op jit(solution)/shard_map/reduce_scatter | solution.py:434
  288.3 142.0 %all-gather.20.cloned.1.call-start = ((), (), s32[]{:S(2)}) async-start(), calls=%async_computation.12 | async-start | bytes 2949120 | tf_op jit(solution)/shard_map/all_gather | solution.py:453
  380.9 368.7 %all-reduce.9.cloned.1.call-start = ((), (), s32[]{:S(2)}) async-start(), calls=%async_computation.19 | async-start | bytes 3604480 | tf_op jit(solution)/shard_map/psum | solution.py:476
  475.4 26.1 %collective-permute-start.10 = (bf16[2,288,512]{2,1,0:T(8,128)(2,1)S(1)}, bf16[2,288,512]{2,1,0:T(8,128)(2,1)S(1)}, u32[]{:S(2)}, u32[]{:S(2)}) collective-permute-start(bf16[2,288,512]{2,1,0:T(8,128)(2,1)S(1)} %dynamic-slice_bitcast_fusion.7), channel_id=1, source_target_pairs={{0,8},{4,12},{8,0},{12,4},{16,24},{20,28},{24,16},{28,20},{1,9},{5... | collective-permute-start | bytes 1769480 | tf_op jit(solution)/shard_map/ppermute | solution.py:246
  483.7 30.1 %collective-permute-start.12 = (bf16[2,288,512]{2,1,0:T(8,128)(2,1)S(1)}, bf16[2,288,512]{2,1,0:T(8,128)(2,1)S(1)}, u32[]{:S(2)}, u32[]{:S(2)}) collective-permute-start(bf16[2,288,512]{2,1,0:T(8,128)(2,1)S(1)} %dynamic-slice_bitcast_fusion.6), channel_id=1, source_target_pairs={{0,16},{4,20},{8,24},{12,28},{16,0},{20,4},{24,8},{28,12},{1,17},{... | collective-permute-start | bytes 1769480 | tf_op jit(solution)/shard_map/ppermute | solution.py:246
  501.8 18.7 %collective-permute-start.11 = (bf16[288,512]{1,0:T(8,128)(2,1)S(1)}, bf16[288,512]{1,0:T(8,128)(2,1)S(1)}, u32[]{:S(2)}, u32[]{:S(2)}) collective-permute-start(bf16[288,512]{1,0:T(8,128)(2,1)S(1)} %dynamic-slice_bitcast_fusion.17), channel_id=1, source_target_pairs={{0,16},{4,20},{8,24},{12,28},{16,0},{20,4},{24,8},{28,12},{1,17},{... | collective-permute-start | bytes 884744 | tf_op jit(solution)/shard_map/ppermute | solution.py:246
  522.6 255.0 %all-gather.18.cloned.1.call-start = ((), (), s32[]{:S(2)}) async-start(), calls=%async_computation.10 | async-start | bytes 2949120 | tf_op jit(solution)/shard_map/all_gather | solution.py:437
  526.1 10.2 %collective-permute-start.14 = (bf16[4,2,64,1024]{3,2,0,1:T(8,128)(2,1)}, bf16[4,2,64,1024]{3,2,0,1:T(8,128)(2,1)}, u32[]{:S(2)}, u32[]{:S(2)}) collective-permute-start(bf16[4,2,64,1024]{3,2,0,1:T(8,128)(2,1)} %bitcast.32), channel_id=1, source_target_pairs={{0,4},{4,0},{8,12},{12,8},{16,20},{20,16},{24,28},{28,24},{1,5},{5... | collective-permute-start | bytes 3145736 | tf_op jit(solution)/shard_map/ppermute | solution.py:246
  534.2 28.4 %collective-permute-start.34 = (bf16[4,2,88,2048]{3,2,0,1:T(8,128)(2,1)}, bf16[4,2,88,2048]{3,2,0,1:T(8,128)(2,1)}, u32[]{:S(2)}, u32[]{:S(2)}) collective-permute-start(bf16[4,2,88,2048]{3,2,0,1:T(8,128)(2,1)} %bitcast.111), channel_id=1, source_target_pairs={{0,4},{4,0},{8,12},{12,8},{16,20},{20,16},{24,28},{28,24},{1,5},{5... | collective-permute-start | bytes 8650760 | tf_op jit(solution)/shard_map/ppermute | solution.py:246
  557.1 11.3 %all-to-all-start.2 = ((bf16[4,2,16384]{2,1,0:T(2,128)(2,1)}), bf16[4,2,16384]{2,1,0:T(2,128)(2,1)S(1)}, u32[]{:S(2)}, u32[]{:S(2)}) async-start(bf16[4,2,16384]{2,1,0:T(2,128)(2,1)} %reshape.328), calls=%async_computation.5 | async-start | bytes 524288 | tf_op jit(solution)/shard_map/all_to_all | solution.py:491
  562.7 215.0 %all-gather.22.cloned.1.call-start = ((), (), s32[]{:S(2)}) async-start(), calls=%async_computation.13 | async-start | bytes 2359296 | tf_op jit(solution)/shard_map/all_gather | solution.py:493
  569.9 217.9 %all-gather.30.cloned.1.call-start = ((), (), s32[]{:S(2)}) async-start(), calls=%async_computation.17 | async-start | bytes 6488064 | tf_op jit(solution)/shard_map/all_gather | solution.py:300
  572.3 10.6 %collective-permute-start.35 = (bf16[2,88,2048]{2,1,0:T(8,128)(2,1)S(1)}, bf16[2,88,2048]{2,1,0:T(8,128)(2,1)S(1)}, u32[]{:S(2)}, u32[]{:S(2)}) collective-permute-start(bf16[2,88,2048]{2,1,0:T(8,128)(2,1)S(1)} %dynamic-slice_bitcast_fusion.1), channel_id=1, source_target_pairs={{0,8},{4,12},{8,0},{12,4},{16,24},{20,28},{24,16},{28,20},{1,9},{5... | collective-permute-start | bytes 2162696 | tf_op jit(solution)/shard_map/ppermute | solution.py:246
  573.2 10.9 %collective-permute-start.37 = (bf16[2,88,2048]{2,1,0:T(8,128)(2,1)S(1)}, bf16[2,88,2048]{2,1,0:T(8,128)(2,1)S(1)}, u32[]{:S(2)}, u32[]{:S(2)}) collective-permute-start(bf16[2,88,2048]{2,1,0:T(8,128)(2,1)S(1)} %dynamic-slice_bitcast_fusion), channel_id=1, source_target_pairs={{0,16},{4,20},{8,24},{12,28},{16,0},{20,4},{24,8},{28,12},{1,17},{... | collective-permute-start | bytes 2162696 | tf_op jit(solution)/shard_map/ppermute | solution.py:246
  583.2 10.6 %collective-permute-start.36 = (bf16[88,2048]{1,0:T(8,128)(2,1)S(1)}, bf16[88,2048]{1,0:T(8,128)(2,1)S(1)}, u32[]{:S(2)}, u32[]{:S(2)}) collective-permute-start(bf16[88,2048]{1,0:T(8,128)(2,1)S(1)} %dynamic-slice_bitcast_fusion.11), channel_id=1, source_target_pairs={{0,16},{4,20},{8,24},{12,28},{16,0},{20,4},{24,8},{28,12},{1,17},{... | collective-permute-start | bytes 1081352 | tf_op jit(solution)/shard_map/ppermute | solution.py:246
  584.4 11.4 %collective-permute-start.38 = (bf16[88,2048]{1,0:T(8,128)(2,1)S(1)}, bf16[88,2048]{1,0:T(8,128)(2,1)S(1)}, u32[]{:S(2)}, u32[]{:S(2)}) collective-permute-start(bf16[88,2048]{1,0:T(8,128)(2,1)S(1)} %dynamic-slice_bitcast_fusion.10), channel_id=1, source_target_pairs={{0,8},{4,12},{8,0},{12,4},{16,24},{20,28},{24,16},{28,20},{1,9},{5... | collective-permute-start | bytes 1081352 | tf_op jit(solution)/shard_map/ppermute | solution.py:246
  596.8 210.7 %all-gather.28.cloned.1.call-start = ((), (), s32[]{:S(2)}) async-start(), calls=%async_computation.16 | async-start | bytes 6488064 | tf_op jit(solution)/shard_map/all_gather | solution.py:300
  603.0 14.4 %collective-permute-start.29 = (bf16[4,2,128,1408]{3,2,0,1:T(8,128)(2,1)}, bf16[4,2,128,1408]{3,2,0,1:T(8,128)(2,1)}, u32[]{:S(2)}, u32[]{:S(2)}) collective-permute-start(bf16[4,2,128,1408]{3,2,0,1:T(8,128)(2,1)} %bitcast.92), channel_id=1, source_target_pairs={{0,4},{4,0},{8,12},{12,8},{16,20},{20,16},{24,28},{28,24},{1,5},{5... | collective-permute-start | bytes 8650760 | tf_op jit(solution)/shard_map/ppermute | solution.py:246
  620.2 17.6 %collective-permute-start.30 = (bf16[2,128,1408]{2,1,0:T(8,128)(2,1)S(1)}, bf16[2,128,1408]{2,1,0:T(8,128)(2,1)S(1)}, u32[]{:S(2)}, u32[]{:S(2)}) collective-permute-start(bf16[2,128,1408]{2,1,0:T(8,128)(2,1)S(1)} %dynamic-slice_bitcast_fusion.3), channel_id=1, source_target_pairs={{0,8},{4,12},{8,0},{12,4},{16,24},{20,28},{24,16},{28,20},{1,9},{5... | collective-permute-start | bytes 2162696 | tf_op jit(solution)/shard_map/ppermute | solution.py:246
  621.8 17.9 %collective-permute-start.32 = (bf16[2,128,1408]{2,1,0:T(8,128)(2,1)S(1)}, bf16[2,128,1408]{2,1,0:T(8,128)(2,1)S(1)}, u32[]{:S(2)}, u32[]{:S(2)}) collective-permute-start(bf16[2,128,1408]{2,1,0:T(8,128)(2,1)S(1)} %dynamic-slice_bitcast_fusion.2), channel_id=1, source_target_pairs={{0,16},{4,20},{8,24},{12,28},{16,0},{20,4},{24,8},{28,12},{1,17},{... | collective-permute-start | bytes 2162696 | tf_op jit(solution)/shard_map/ppermute | solution.py:246
  638.1 9.4 collective-permute-start.31
  640.0 8.7 collective-permute-start.33
  649.8 186.7 %all-gather.26.cloned.1.call-start = ((), (), s32[]{:S(2)}) async-start(), calls=%async_computation.15 | async-start | bytes 6488064 | tf_op jit(solution)/shard_map/all_gather | solution.py:300
  662.8 24.0 %collective-permute-start.25 = (bf16[2,128,1408]{2,1,0:T(8,128)(2,1)S(1)}, bf16[2,128,1408]{2,1,0:T(8,128)(2,1)S(1)}, u32[]{:S(2)}, u32[]{:S(2)}) collective-permute-start(bf16[2,128,1408]{2,1,0:T(8,128)(2,1)S(1)} %dynamic-slice_bitcast_fusion.5), channel_id=1, source_target_pairs={{0,8},{4,12},{8,0},{12,4},{16,24},{20,28},{24,16},{28,20},{1,9},{5... | collective-permute-start | bytes 2162696 | tf_op jit(solution)/shard_map/ppermute | solution.py:246
  663.2 24.9 %collective-permute-start.27 = (bf16[2,128,1408]{2,1,0:T(8,128)(2,1)S(1)}, bf16[2,128,1408]{2,1,0:T(8,128)(2,1)S(1)}, u32[]{:S(2)}, u32[]{:S(2)}) collective-permute-start(bf16[2,128,1408]{2,1,0:T(8,128)(2,1)S(1)} %dynamic-slice_bitcast_fusion.4), channel_id=1, source_target_pairs={{0,16},{4,20},{8,24},{12,28},{16,0},{20,4},{24,8},{28,12},{1,17},{... | collective-permute-start | bytes 2162696 | tf_op jit(solution)/shard_map/ppermute | solution.py:246
  687.0 8.8 collective-permute-start.26
  688.4 8.4 collective-permute-start.28
  703.0 10.7 %collective-permute-start.19 = (bf16[4,2,64,2048]{3,2,0,1:T(8,128)(2,1)}, bf16[4,2,64,2048]{3,2,0,1:T(8,128)(2,1)}, u32[]{:S(2)}, u32[]{:S(2)}) collective-permute-start(bf16[4,2,64,2048]{3,2,0,1:T(8,128)(2,1)} %bitcast.54), channel_id=1, source_target_pairs={{0,4},{4,0},{8,12},{12,8},{16,20},{20,16},{24,28},{28,24},{1,5},{5... | collective-permute-start | bytes 6291464 | tf_op jit(solution)/shard_map/ppermute | solution.py:246
  705.3 28.0 %all-to-all-start.1 = ((bf16[4,512,256]{2,1,0:T(8,128)(2,1)}), bf16[4,512,256]{2,1,0:T(8,128)(2,1)S(1)}, u32[]{:S(2)}, u32[]{:S(2)}) async-start(bf16[4,512,256]{2,1,0:T(8,128)(2,1)} %bitcast.350), calls=%async_computation.4 | async-start | bytes 2097152 | tf_op jit(solution)/shard_map/all_to_all | solution.py:500
  709.8 189.2 %all-reduce.7.cloned.1.call-start = ((), (), s32[]{:S(2)}) async-start(), calls=%async_computation.18 | async-start | bytes 3178496 | tf_op jit(solution)/shard_map/psum | solution.py:524
  719.0 24.5 %collective-permute-start.20 = (bf16[2,64,2048]{2,1,0:T(8,128)(2,1)}, bf16[2,64,2048]{2,1,0:T(8,128)(2,1)}, u32[]{:S(2)}, u32[]{:S(2)}) collective-permute-start(bf16[2,64,2048]{2,1,0:T(8,128)(2,1)} %dynamic-slice_bitcast_fusion.9), channel_id=1, source_target_pairs={{0,8},{4,12},{8,0},{12,4},{16,24},{20,28},{24,16},{28,20},{1,9},{5... | collective-permute-start | bytes 1572872 | tf_op jit(solution)/shard_map/ppermute | solution.py:246
  735.8 12.4 %collective-permute-start.22 = (bf16[2,64,2048]{2,1,0:T(8,128)(2,1)S(1)}, bf16[2,64,2048]{2,1,0:T(8,128)(2,1)S(1)}, u32[]{:S(2)}, u32[]{:S(2)}) collective-permute-start(bf16[2,64,2048]{2,1,0:T(8,128)(2,1)S(1)} %dynamic-slice_bitcast_fusion.8), channel_id=1, source_target_pairs={{0,16},{4,20},{8,24},{12,28},{16,0},{20,4},{24,8},{28,12},{1,17},{... | collective-permute-start | bytes 1572872 | tf_op jit(solution)/shard_map/ppermute | solution.py:246
  745.7 29.0 %collective-permute-start.21 = (bf16[64,2048]{1,0:T(8,128)(2,1)}, bf16[64,2048]{1,0:T(8,128)(2,1)}, u32[]{:S(2)}, u32[]{:S(2)}) collective-permute-start(bf16[64,2048]{1,0:T(8,128)(2,1)} %dynamic-slice_bitcast_fusion.19), channel_id=1, source_target_pairs={{0,16},{4,20},{8,24},{12,28},{16,0},{20,4},{24,8},{28,12},{1,17},{... | collective-permute-start | bytes 786440 | tf_op jit(solution)/shard_map/ppermute | solution.py:246
  749.2 26.5 %collective-permute-start.23 = (bf16[64,2048]{1,0:T(8,128)(2,1)}, bf16[64,2048]{1,0:T(8,128)(2,1)}, u32[]{:S(2)}, u32[]{:S(2)}) collective-permute-start(bf16[64,2048]{1,0:T(8,128)(2,1)} %dynamic-slice_bitcast_fusion.18), channel_id=1, source_target_pairs={{0,8},{4,12},{8,0},{12,4},{16,24},{20,28},{24,16},{28,20},{1,9},{5... | collective-permute-start | bytes 786440 | tf_op jit(solution)/shard_map/ppermute | solution.py:246
  774.3 163.7 %all-gather.24.cloned.1.call-start = ((), (), s32[]{:S(2)}) async-start(), calls=%async_computation.14 | async-start | bytes 4718592 | tf_op jit(solution)/shard_map/all_gather | solution.py:300
  (77 other events, 838.6 us)
Sparse Core Ops, SparseCore 0:
  26.0 51.0 all-gather.13
  121.7 68.5 reduce-scatter.3
  194.3 49.2 all-gather.15
  279.8 47.5 reduce-scatter.7
  330.1 47.5 reduce-scatter.5
  381.0 49.2 all-gather.19
  522.7 78.3 all-reduce.8
  602.8 47.2 all-gather.17
  652.2 36.9 all-gather.21
  691.1 53.6 all-gather.29
  747.4 43.8 all-gather.27
  793.2 43.3 all-gather.25
  840.8 58.1 all-reduce.6
  900.7 37.2 all-gather.23

commit v2 on v1

--- a/solution.py
+++ b/solution.py
@@ -14,7 +14,7 @@
 BF = jnp.bfloat16
 F32 = jnp.float32
 I32 = jnp.int32
-
+LANES = 128
 
 def norm_rows(values, gain):
     recip = lax.rsqrt(jnp.mean(values * values, -1, keepdims=True) + EPS)
@@ -46,9 +46,9 @@
     return lax.dot_general(left, right, (((1,), (1,)), ((), ())), preferred_element_type=F32)
 
 
-def key_block(key_count):
-    for size in (512, 256, 128):
-        if key_count % size == 0:
+def key_block(key_count, most):
+    for size in (1536, 1024, 512, 256, 128):
+        if size <= most and key_count % size == 0:
             return size
     return key_count
 
@@ -72,12 +72,22 @@
 
 
 def attend_kernel(
-    size, tile, heads, info_ref, pre_ref, cos_ref, sin_ref, kv_ref, start_ref, index_ref,
-    query_ref, out_ref, log_ref, max_ref, sum_ref, acc_ref,
+    size, tile, heads, places, info_ref, pre_ref, cos_ref, sin_ref, first_ref, *refs
 ):
+    pieces_in = refs[: len(places)]
+    query_ref, out_ref, low_ref, log_ref, kv_ref = refs[len(places) : len(places) + 5]
+    max_ref, sum_ref, acc_ref, scores_ref, start_ref, index_ref, sems = refs[len(places) + 5 :]
     tokens = pre_ref.shape[0]
+    copies = []
+    for n, (mask, offset) in enumerate(places):
+        at = lax.bitwise_xor(info_ref[5], mask) * tokens + offset if mask is not None else 0
+        rows = pl.ds(pl.multiple_of(at, 16), pieces_in[n].shape[0])
+        copies.append(pltpu.make_async_copy(pieces_in[n], kv_ref.at[rows, :], sems.at[n]))
+    for copy in copies:
+        copy.start()
     width = kv_ref.shape[1] // 2
     half = width // 2
+    lanes = max_ref.shape[1]
     scale = width**-0.5 * LOG2E
     cosine, sine = cos_ref[...], sin_ref[...]
     for h in range(heads):
@@ -86,82 +96,120 @@
         rows = slice(h * tokens, (h + 1) * tokens)
         query_ref[rows, :half] = (front * cosine - back * sine).astype(BF)
         query_ref[rows, half:] = (front * sine + back * cosine).astype(BF)
-    max_ref[...] = jnp.full(max_ref.shape, NEG, F32)
-    sum_ref[...] = jnp.zeros(sum_ref.shape, F32)
-    acc_ref[...] = jnp.zeros(acc_ref.shape, F32)
-
-    def run(j, masked):
-        base = pl.multiple_of(j * size, size)
-        keys = kv_ref[pl.ds(base, size), :width]
-        values = kv_ref[pl.ds(base, size), width:]
-        for i in range(heads * tokens // tile):
-            r = slice(i * tile, (i + 1) * tile)
-            scores = dense_nt(keys, query_ref[r, :])
-            if masked:
-                at = base + lax.broadcasted_iota(I32, (size, tile), 0)
-                allowed = (at >= start_ref[:, r]) & (at <= index_ref[:, r])
-                scores = jnp.where(allowed, scores, NEG)
-            old = max_ref[:, r]
-            new = jnp.maximum(old, jnp.max(scores, 0, keepdims=True) * scale)
-            probs = jnp.exp2(scores * scale - new)
-            if masked:
-                probs = jnp.where(allowed, probs, 0.0)
-            fade = jnp.exp2(old - new)
-            max_ref[:, r] = new
-            sum_ref[:, r] = fade * sum_ref[:, r] + jnp.sum(probs, 0, keepdims=True)
-            acc_ref[:, r] = fade * acc_ref[:, r] + dense_tn(values, probs.astype(BF))
-        return None
-
-    over_key_blocks(info_ref, size, tokens, run)
-    total = sum_ref[...]
-    log_ref[...] = max_ref[...] + jnp.log2(total)
-    out = (acc_ref[...] * (1.0 / total)).T
-    for h in range(heads):
-        out_ref[:, h * width : (h + 1) * width] = out[h * tokens : (h + 1) * tokens, :]
+        start_ref[rows, :] = first_ref[...]
+        index_ref[rows, :] = info_ref[0] + lax.broadcasted_iota(I32, (tokens, lanes), 0)
+    for copy in copies:
+        copy.wait()
+    pieces = [slice(n * lanes, (n + 1) * lanes) for n in range(size // lanes)]
+    for i in range(heads * tokens // tile):
+        r = slice(i * tile, (i + 1) * tile)
+        max_ref[...] = jnp.full(max_ref.shape, NEG, F32)
+        sum_ref[...] = jnp.zeros(sum_ref.shape, F32)
+        acc_ref[...] = jnp.zeros(acc_ref.shape, F32)
+
+        def score(j, masked, r=r):
+            base = pl.multiple_of(j * size, size)
+            scores = dense_nt(query_ref[r, :], kv_ref[pl.ds(base, size), :width])
+            most = max_ref[...]
+            lane = lax.broadcasted_iota(I32, max_ref.shape, 1)
+            for n, piece in enumerate(pieces):
+                part = scores[:, piece]
+                if masked:
+                    at = lane + (base + n * lanes)
+                    allowed = (at >= start_ref[r, :]) & (at <= index_ref[r, :])
+                    part = jnp.where(allowed, part, NEG)
+                scores_ref[j, :, piece] = part
+                most = jnp.maximum(most, part)
+            max_ref[...] = most
+            return None
+
+        over_key_blocks(info_ref, size, tokens, score)
+        most = jnp.max(max_ref[...], 1, keepdims=True) * scale
+        max_ref[...] = jnp.broadcast_to(most, max_ref.shape)
+
+        def mix(j, carry):
+            base = pl.multiple_of(j * size, size)
+            most, total = max_ref[...], sum_ref[...]
+            probs = []
+            for piece in pieces:
+                prob = jnp.exp2(scores_ref[j, :, piece] * scale - most)
+                total = total + prob
+                probs.append(prob.astype(BF))
+            sum_ref[...] = total
+            acc_ref[...] += dense(jnp.concatenate(probs, 1), kv_ref[pl.ds(base, size), width:])
+            return carry
+
+        end = (info_ref[0] + tokens + size - 1) // size
+        lax.fori_loop(info_ref[1] // size, end, mix, None)
+        total = jnp.sum(sum_ref[...], 1, keepdims=True)
+        log_ref[:, r] = jnp.broadcast_to(most + jnp.log2(total), max_ref.shape).T[0:1, :]
+        out = acc_ref[...] * (1.0 / total)
+        at = i * tile
+        while at < (i + 1) * tile:
+            h = at // tokens
+            stop = min((i + 1) * tile, (h + 1) * tokens)
+            rows, cols = slice(at - h * tokens, stop - h * tokens), slice(h * width, (h + 1) * width)
+            part = out[at - i * tile : stop - i * tile, :]
+            out_ref[rows, cols] = part
+            low_ref[rows, cols] = part.astype(BF)
+            at = stop
 
 
 def in_vmem(count):
     return [pl.BlockSpec(memory_space=pltpu.VMEM) for _ in range(count)]
 
 
-def attend(info, query_pre, cosine, sine, kv, start, index):
+def attend(info, query_pre, cosine, sine, start, pieces):
     tokens, all_heads = query_pre.shape
-    keys, width = kv.shape[0], kv.shape[1] // 2
+    width = pieces[0][0].shape[1] // 2
+    keys = sum(piece[0].shape[0] for piece in pieces)
     rows = tokens * (all_heads // width)
+    size, tile = key_block(keys, 1536), row_tile(rows)
+    start = jnp.broadcast_to(start[:, None], (tokens, LANES))
     return pl.pallas_call(
-        functools.partial(attend_kernel, key_block(keys), row_tile(rows), all_heads // width),
+        functools.partial(
+            attend_kernel, size, tile, all_heads // width, [piece[1:] for piece in pieces]
+        ),
         out_shape=(
             jax.ShapeDtypeStruct((rows, width), BF),
             jax.ShapeDtypeStruct((tokens, all_heads), F32),
+            jax.ShapeDtypeStruct((tokens, all_heads), BF),
             jax.ShapeDtypeStruct((1, rows), F32),
+            jax.ShapeDtypeStruct((keys, 2 * width), BF),
         ),
-        in_specs=[pl.BlockSpec(memory_space=pltpu.SMEM)] + in_vmem(6),
-        out_specs=tuple(in_vmem(3)),
+        in_specs=[pl.BlockSpec(memory_space=pltpu.SMEM)]
+        + in_vmem(4)
+        + [pl.BlockSpec(memory_space=pl.ANY)] * len(pieces),
+        out_specs=tuple(in_vmem(5)),
         scratch_shapes=[
-            pltpu.VMEM((1, rows), F32),
-            pltpu.VMEM((1, rows), F32),
-            pltpu.VMEM((width, rows), F32),
+            pltpu.VMEM((tile, LANES), F32),
+            pltpu.VMEM((tile, LANES), F32),
+            pltpu.VMEM((tile, width), F32),
+            pltpu.VMEM((keys // size, tile, size), F32),
+            pltpu.VMEM((rows, LANES), I32),
+            pltpu.VMEM((rows, LANES), I32),
+            pltpu.SemaphoreType.DMA((len(pieces),)),
         ],
-        compiler_params=pltpu.CompilerParams(vmem_limit_bytes=48 * 2**20),
-        cost_estimate=pl.CostEstimate(
-            flops=4 * rows * keys * width,
-            bytes_accessed=12 * rows * width + 4 * keys * width,
-            transcendentals=rows * keys,
-        ),
+        compiler_params=pltpu.CompilerParams(vmem_limit_bytes=56 * 2**20),
+        cost_estimate=brief(0),
         name="attend",
-    )(info, query_pre, cosine, sine, kv, start, index)
+    )(info, query_pre, cosine, sine, start, *[piece[0] for piece in pieces])
 
 
 def attend_back_kernel(
-    size, tile, heads, info_ref, query_ref, grad_ref, delta_ref, log_ref, cos_ref, sin_ref, kv_ref, start_ref, index_ref,
-    gq_ref, near_ref, far_ref, gout_ref, gk_ref, gv_ref, gqt_ref,
+    size, tile, heads, by_axis, info_ref, query_ref, grad_ref, out_ref, log_ref, cos_ref, sin_ref, kv_ref, start_ref, index_ref,
+    gq_ref, near_ref, far_ref, gout_ref, gk_ref, gv_ref, gqt_ref, dots_ref,
 ):
     tokens = grad_ref.shape[0]
     width = kv_ref.shape[1] // 2
     half = width // 2
     scale = width**-0.5
     for h in range(heads):
-        gout_ref[h * tokens : (h + 1) * tokens, :] = grad_ref[:, h * width : (h + 1) * width]
+        gout = grad_ref[:, h * width : (h + 1) * width]
+        gout_ref[h * tokens : (h + 1) * tokens, :] = gout
+        dots = gout.astype(F32) * out_ref[:, h * width : (h + 1) * width]
+        dots_ref[h * tokens : (h + 1) * tokens, :] = dots[:, :half] + dots[:, half:]
+    delta = jnp.sum(dots_ref[...].T, 0, keepdims=True)
     gk_ref[...] = jnp.zeros(gk_ref.shape, F32)
     gv_ref[...] = jnp.zeros(gv_ref.shape, F32)
     gqt_ref[...] = jnp.zeros(gqt_ref.shape, F32)
@@ -179,7 +227,7 @@
                 at = base + lax.broadcasted_iota(I32, (size, tile), 0)
                 allowed = (at >= start_ref[:, r]) & (at <= index_ref[:, r])
                 probs = jnp.where(allowed, probs, 0.0)
-            gscores = (probs * (dense_nt(values, gout) - delta_ref[:, r])).astype(BF)
+            gscores = (probs * (dense_nt(values, gout) - delta[:, r])).astype(BF)
             gv_ref[at_keys, :] += dense(probs.astype(BF), gout)
             gk_ref[at_keys, :] += dense(gscores, query)
             gqt_ref[:, r] += dense_tn(keys, gscores)
@@ -187,20 +235,24 @@
 
     over_key_blocks(info_ref, size, tokens, run)
     mine = info_ref[3]
-    for s in range(kv_ref.shape[0] // tokens):
-        rows = slice(s * tokens, (s + 1) * tokens)
+    part = tokens // 2
+    for s in range(kv_ref.shape[0] // part):
+        rows = slice(s * part, (s + 1) * part)
+        chip = s // 4
+        if by_axis and s % 2 == 0:
+            chip = chip % 2 * 2 + chip // 2
         gk = (gk_ref[rows, :] * scale).astype(BF)
         gv = gv_ref[rows, :].astype(BF)
 
-        @pl.when(mine == s % 2)
-        def _(s=s, gk=gk, gv=gv):
-            near_ref[s // 2, :, :width] = gk
-            near_ref[s // 2, :, width:] = gv
-
-        @pl.when(mine != s % 2)
-        def _(s=s, gk=gk, gv=gv):
-            far_ref[s // 2, :, :width] = gk
-            far_ref[s // 2, :, width:] = gv
+        @pl.when(mine == s // 2 % 2)
+        def _(s=s, chip=chip, gk=gk, gv=gv):
+            near_ref[s % 2, chip, :, :width] = gk
+            near_ref[s % 2, chip, :, width:] = gv
+
+        @pl.when(mine != s // 2 % 2)
+        def _(s=s, chip=chip, gk=gk, gv=gv):
+            far_ref[s % 2, chip, :, :width] = gk
+            far_ref[s % 2, chip, :, width:] = gv
 
     gq = (gqt_ref[...] * scale).T.astype(BF).astype(F32)
     cosine, sine = cos_ref[...], sin_ref[...]
@@ -211,17 +263,19 @@
         gq_ref[:, h * width + half : (h + 1) * width] = (back * cosine - front * sine).astype(BF)
 
 
-def attend_back(info, query, grad, delta, log, cosine, sine, kv, start, index):
+def attend_back(info, query, grad, out, log, cosine, sine, kv, start, index, by_axis):
     tokens, all_heads = grad.shape
     keys, width = kv.shape[0], kv.shape[1] // 2
     rows = tokens * (all_heads // width)
     blocks = keys // tokens
     return pl.pallas_call(
-        functools.partial(attend_back_kernel, key_block(keys), row_tile(rows), all_heads // width),
+        functools.partial(
+            attend_back_kernel, key_block(keys, 512), row_tile(rows), all_heads // width, by_axis
+        ),
         out_shape=(
             jax.ShapeDtypeStruct((tokens, all_heads), BF),
-            jax.ShapeDtypeStruct((blocks // 2, tokens, 2 * width), BF),
-            jax.ShapeDtypeStruct((blocks // 2, tokens, 2 * width), BF),
+            jax.ShapeDtypeStruct((2, blocks // 2, tokens // 2, 2 * width), BF),
+            jax.ShapeDtypeStruct((2, blocks // 2, tokens // 2, 2 * width), BF),
         ),
         in_specs=[pl.BlockSpec(memory_space=pltpu.SMEM)] + in_vmem(9),
         out_specs=tuple(in_vmem(3)),
@@ -230,24 +284,1021 @@
             pltpu.VMEM((keys, width), F32),
             pltpu.VMEM((keys, width), F32),
             pltpu.VMEM((width, rows), F32),
+            pltpu.VMEM((rows, width // 2), F32),
         ],
         compiler_params=pltpu.CompilerParams(vmem_limit_bytes=56 * 2**20),
-        cost_estimate=pl.CostEstimate(
-            flops=10 * rows * keys * width,
-            bytes_accessed=6 * rows * width + 8 * keys * width,
-            transcendentals=rows * keys,
+        cost_estimate=brief(0),
+        name="attend_back",
+    )(info, query, grad, out, log, cosine, sine, kv, start, index)
+
+
+def feed_kernel(tile, mid_ref, grad_ref, gate_ref, up_ref, hidden_ref, both_ref, part_ref):
+    width = gate_ref.shape[1]
+
+    def run(i, carry):
+        rows = pl.ds(pl.multiple_of(i * tile, tile), tile)
+        mid = mid_ref[rows, :]
+        gate = dense(mid, gate_ref[...])
+        up = dense(mid, up_ref[...])
+        grad = grad_ref[rows, :]
+        sigmoid = 1.0 / (1.0 + jnp.exp(-gate))
+        active = gate * sigmoid
+        hidden_ref[rows, :] = (active * up).astype(BF)
+        grad_gate = (grad * up * sigmoid * (1.0 + gate * (1.0 - sigmoid))).astype(BF)
+        grad_up = (grad * active).astype(BF)
+        both_ref[rows, :width] = grad_gate
+        both_ref[rows, width:] = grad_up
+        part = dense_nt(grad_gate, gate_ref[...]) + dense_nt(grad_up, up_ref[...])
+        part_ref[rows, :] = part.astype(BF)
+        return carry
+
+    lax.fori_loop(0, mid_ref.shape[0] // tile, run, None)
+
+
+def feed_forward(mid, grad, gate, up):
+    rows, model = mid.shape
+    width = gate.shape[1]
+    tile = next(t for t in (288, 192, 144, 96, 64, 48, 32, 16, rows) if rows % t == 0)
+    return pl.pallas_call(
+        functools.partial(feed_kernel, tile),
+        out_shape=(
+            jax.ShapeDtypeStruct((rows, width), BF),
+            jax.ShapeDtypeStruct((rows, 2 * width), BF),
+            jax.ShapeDtypeStruct((rows, model), BF),
         ),
-        name="attend_back",
-    )(info, query, grad, delta, log, cosine, sine, kv, start, index)
-
-
-def swap(value, bit):
-    count = lax.axis_size("seq")
-    return lax.ppermute(value, "seq", [(i, i ^ (1 << bit)) for i in range(count)])
+        in_specs=in_vmem(4),
+        out_specs=tuple(in_vmem(3)),
+        compiler_params=pltpu.CompilerParams(vmem_limit_bytes=40 * 2**20),
+        cost_estimate=brief(20),
+        name="feed_forward",
+    )(mid, grad, gate, up)
+
+
+class Order:
+    last = None
+
+
+def brief(micros):
+    return pl.CostEstimate(flops=int(micros * 1e8), bytes_accessed=0, transcendentals=0)
+
+
+def call(kernel, outs, args, name, micros=0, scratch=(), grid=None, in_specs=None, out_specs=None, prefetch=None):
+    out_shape = tuple(jax.ShapeDtypeStruct(*out) for out in outs)
+    prefetch = in_order(prefetch)
+    params = dict(
+        out_shape=out_shape,
+        compiler_params=pltpu.CompilerParams(vmem_limit_bytes=56 * 2**20),
+        cost_estimate=brief(micros),
+        name=name,
+    )
+    outs = placed_call(kernel, out_shape, args, params, scratch, grid, in_specs, out_specs, prefetch)
+    Order.last = outs[0]
+    return outs
+
+
+def in_order(info):
+    return info if Order.last is None else after(info, Order.last)
+
+
+def placed_call(kernel, out_shape, args, params, scratch, grid, in_specs, out_specs, prefetch):
+    if grid is None:
+        return pl.pallas_call(
+            kernel,
+            in_specs=[pl.BlockSpec(memory_space=pltpu.SMEM)] + in_vmem(len(args)),
+            out_specs=tuple(in_vmem(len(out_shape))),
+            scratch_shapes=list(scratch),
+            **params,
+        )(prefetch, *args)
+    return pl.pallas_call(
+        kernel,
+        grid_spec=pltpu.PrefetchScalarGridSpec(
+            num_scalar_prefetch=1,
+            grid=grid,
+            in_specs=in_specs,
+            out_specs=tuple(out_specs),
+            scratch_shapes=list(scratch),
+        ),
+        **params,
+    )(prefetch, *args)
+
+
+def once(shape, index):
+    return pl.BlockSpec(shape, index, pipeline_mode=pl.Buffered(1))
+
+
+def at_block(index, size):
+    return pl.ds(pl.multiple_of(index * size, size), size)
+
+
+CORE, RANK, SEQ = 3, 4, 5
+
+
+def ahead(info_ref, shift, ranks):
+    return lax.rem(info_ref[RANK] + shift, ranks)
+
+
+def behind(info_ref, shift, ranks):
+    return lax.rem(info_ref[RANK] + ranks - shift, ranks)
+
+
+def chip_of(info_ref):
+    return lax.div(info_ref[SEQ], 2)
+
+
+def rank_blocks(info, index):
+    return lambda i, info_ref: index(info_ref[RANK])
+
+
+def project_kernel(
+    info_ref, tokens_ref, gain_ref, down_ref, kv_weight_ref, latent_gain_ref, normed_ref, recip_ref, kv_ref, low_ref
+):
+    values = tokens_ref[...].astype(F32)
+    normed, recip = norm_rows(values, gain_ref[...])
+    normed_ref[...] = normed.astype(BF)
+    recip_ref[...] = jnp.broadcast_to(recip, recip_ref.shape)
+    rows = normed_ref.shape[0]
+    low_ref[at_block(pl.program_id(0), rows), :] = dense(normed_ref[...], down_ref[...]).astype(BF)
+
+    @pl.when(pl.program_id(0) == 0)
+    def _():
+        rest = latent_gain_ref[...]
+        parts = []
+        for _ in range(3):
+            parts.append(rest.astype(BF))
+            rest = rest - parts[-1].astype(F32)
+        parts.append(jnp.zeros((EXTRA - 3, rest.shape[1]), BF))
+        low_ref[low_ref.shape[0] - EXTRA :, :] = jnp.concatenate(parts, 0)
+
+    kv_ref[...] = dense(normed_ref[...], kv_weight_ref[...])
+
+
+EXTRA = 16
+
+
+def project(info, tokens, gain, q_down, kv_weight, latent_gain):
+    rows, model = tokens.shape
+    tile = rows // 2
+    widths = ((model, BF), (LANES, F32), (kv_weight.shape[1], F32))
+    low = (rows + EXTRA, q_down.shape[1])
+    return call(
+        project_kernel,
+        [((rows, width), dtype) for width, dtype in widths] + [(low, BF)],
+        (tokens, gain.reshape(1, -1), q_down, kv_weight, latent_gain.reshape(1, -1)),
+        "project",
+        grid=(2,),
+        in_specs=[
+            pl.BlockSpec((tile, model), lambda i, w: (i, 0)),
+            once((1, model), lambda i, w: (0, 0)),
+            once(q_down.shape, lambda i, w: (0, 0)),
+            once(kv_weight.shape, lambda i, w: (0, 0)),
+            once((1, q_down.shape[1]), lambda i, w: (0, 0)),
+        ],
+        out_specs=[pl.BlockSpec((tile, width), lambda i, w: (i, 0)) for width, _ in widths]
+        + [pl.BlockSpec(low, lambda i, w: (0, 0))],
+        prefetch=info,
+    )
+
+
+def turn_kernel(info_ref, kv_ref, cos_ref, sin_ref, out_ref):
+    half = cos_ref.shape[1]
+    front, back = kv_ref[:, :half], kv_ref[:, half : 2 * half]
+    cosine, sine = cos_ref[...], sin_ref[...]
+    out_ref[:, :half] = (front * cosine - back * sine).astype(BF)
+    out_ref[:, half : 2 * half] = (front * sine + back * cosine).astype(BF)
+    out_ref[:, 2 * half :] = kv_ref[:, 2 * half :].astype(BF)
+
+
+def turn(info, kv_pre, cosine, sine):
+    return call(turn_kernel, [(kv_pre.shape, BF)], (kv_pre, cosine, sine), "turn", prefetch=info)[0]
+
+
+def query_kernel(info_ref, latent_ref, own_ref, other_ref, low_ref, recip_ref, gain_ref, query_ref):
+    rows = low_ref.shape[0]
+    parts = latent_ref[rows:, :].astype(F32)
+    gain_ref[...] = parts[0:1] + parts[1:2] + parts[2:3]
+    normed, recip = norm_rows(latent_ref[:rows, :].astype(F32), gain_ref[...])
+    low_ref[...] = normed.astype(BF)
+    recip_ref[...] = jnp.broadcast_to(recip, recip_ref.shape)
+    half = own_ref.shape[1]
+    ranks = 4
+    cols = latent_ref.shape[1] // ranks
+    totals = [0.0, 0.0]
+    for s in range(ranks):
+        left = low_ref[:, at_block(behind(info_ref, s, ranks), cols)]
+        for n, ref in enumerate((own_ref, other_ref)):
+            totals[n] = totals[n] + dense(left, ref[s * cols : (s + 1) * cols, :])
+    core = info_ref[CORE]
+    query_ref[:, at_block(core, half)] = totals[0]
+    query_ref[:, at_block(1 - core, half)] = totals[1]
+
+
+def queries(info, latent, own, other):
+    rows, width = latent.shape[0] - EXTRA, latent.shape[1]
+    return call(
+        query_kernel,
+        [((rows, width), BF), ((rows, LANES), F32), ((1, width), F32), ((rows, 2 * own.shape[1]), F32)],
+        (latent, own, other),
+        "queries",
+        prefetch=info,
+    )
+
+
+def latent_part_kernel(info_ref, grad_ref, own_ref, other_ref, *refs):
+    outs, all_ref = refs[:-1], refs[-1]
+    ranks, rows = len(outs), outs[0].shape[0]
+    half, cols = own_ref.shape[1], own_ref.shape[0] // ranks
+    core = info_ref[CORE]
+    own_grad = grad_ref[:, at_block(core, half)]
+    other_grad = grad_ref[:, at_block(1 - core, half)]
+    for s in range(ranks):
+        part = slice(s * cols, (s + 1) * cols)
+        out = dense_nt(own_grad, own_ref[part, :]) + dense_nt(other_grad, other_ref[part, :])
+        all_ref[:, at_block(behind(info_ref, s, ranks), cols)] = out.astype(BF)
+    for s in range(ranks):
+        outs[s][...] = all_ref[at_block(ahead(info_ref, s, ranks), rows), :]
+
+
+def latent_parts(info, grad, own, other, ranks):
+    rows, width = grad.shape[0], own.shape[0]
+    return call(
+        latent_part_kernel,
+        [((rows // ranks, width), BF)] * ranks,
+        (grad, own, other),
+        "latent_parts",
+        scratch=[pltpu.VMEM((rows, width), BF)],
+        prefetch=info,
+    )
+
+
+def latent_back_kernel(info_ref, latent_ref, recip_ref, gain_ref, *refs):
+    parts, (grad_ref, gain_grad_ref) = refs[:-2], refs[-2:]
+    grad_in = sum(part[...].astype(F32) for part in parts)
+    latent = latent_ref[...].astype(F32)
+    recip = recip_ref[:, 0:1]
+    gained = grad_in * gain_ref[...]
+    stat = jnp.sum(latent * gained, -1, keepdims=True)
+    grad = recip * gained - latent * (recip * recip * recip * stat / latent.shape[1])
+    grad_ref[...] = grad.astype(BF)
+    gain_grad_ref[...] = jnp.sum(grad_in * latent * recip, 0, keepdims=True)
+
+
+def latent_back(info, latent, recip, gain, parts):
+    rows, width = parts[0].shape
+    return call(
+        latent_back_kernel,
+        [((rows, width), BF), ((1, width), F32)],
+        (latent, recip, gain, *parts),
+        "latent_back",
+        grid=(1,),
+        in_specs=[
+            pl.BlockSpec((rows, width), lambda i, w: (w[RANK], 0)),
+            pl.BlockSpec((rows, LANES), lambda i, w: (w[RANK], 0)),
+            pl.BlockSpec((1, width), lambda i, w: (0, 0)),
+        ]
+        + [pl.BlockSpec((rows, width), lambda i, w: (0, 0)) for _ in parts],
+        out_specs=[
+            pl.BlockSpec((rows, width), lambda i, w: (0, 0)),
+            pl.BlockSpec((1, width), lambda i, w: (0, 0)),
+        ],
+        prefetch=info,
+    )
+
+
+def kv_back_kernel(info_ref, cos_ref, sin_ref, *refs):
+    parts, out_ref = refs[:-1], refs[-1]
+    total = sum(part[...].astype(F32) for part in parts).astype(BF).astype(F32)
+    half = cos_ref.shape[1]
+    front, back = total[:, :half], total[:, half : 2 * half]
+    cosine, sine = cos_ref[...], sin_ref[...]
+    out_ref[:, :half] = (front * cosine + back * sine).astype(BF)
+    out_ref[:, half : 2 * half] = (back * cosine - front * sine).astype(BF)
+    out_ref[:, 2 * half :] = total[:, 2 * half :].astype(BF)
+
+
+def kv_back(info, cosine, sine, parts):
+    rows, width = parts[0].shape
+    return call(
+        kv_back_kernel,
+        [((rows, width), BF)],
+        (cosine, sine, *parts),
+        "kv_back",
+        grid=(1,),
+        in_specs=[pl.BlockSpec((rows, cosine.shape[1]), lambda i, w: (w[RANK], 0))] * 2
+        + [pl.BlockSpec((rows, width), lambda i, w: (0, 0)) for _ in parts],
+        out_specs=[pl.BlockSpec((rows, width), lambda i, w: (0, 0))],
+        prefetch=info,
+    )[0]
+
+
+def mid_kernel(info_ref, branch_ref, tokens_ref, gain_ref, residual_ref, mid_ref, recip_ref):
+    residual = tokens_ref[...].astype(F32) + branch_ref[...].astype(F32)
+    normed, recip = norm_rows(residual, gain_ref[...])
+    residual_ref[...] = residual
+    mid_ref[...] = normed.astype(BF)
+    recip_ref[...] = jnp.broadcast_to(recip, recip_ref.shape)
+
+
+def mid_norm(info, branch, tokens, gain):
+    rows, model = branch.shape
+    whole = pl.BlockSpec((rows, model), lambda i, w: (0, 0))
+    return call(
+        mid_kernel,
+        [((rows, model), F32), ((rows, model), BF), ((rows, LANES), F32)],
+        (branch, tokens, gain.reshape(1, -1)),
+        "mid_norm",
+        grid=(1,),
+        in_specs=[
+            whole,
+            pl.BlockSpec((rows, model), lambda i, w: (w[RANK], 0)),
+            pl.BlockSpec((1, model), lambda i, w: (0, 0)),
+        ],
+        out_specs=[whole, whole, pl.BlockSpec((rows, LANES), lambda i, w: (0, 0))],
+        prefetch=info,
+    )
+
+
+def mid_back_kernel(info_ref, grad_ref, residual_ref, recip_ref, gain_ref, out_grad_ref, branch_ref, gain_grad_ref):
+    grad = grad_ref[...].astype(F32)
+    residual = residual_ref[...]
+    recip = recip_ref[:, 0:1]
+    gained = grad * gain_ref[...]
+    stat = jnp.sum(residual * gained, -1, keepdims=True)
+    out = out_grad_ref[...].astype(F32) + recip * gained
+    out = out - residual * (recip * recip * recip * stat / residual.shape[1])
+    branch_ref[...] = out.astype(BF)
+    gain_grad_ref[...] = jnp.sum(grad * residual * recip, 0, keepdims=True)
+
+
+def mid_back(info, grad, residual, recip, gain, out_grad):
+    rows, model = grad.shape
+    whole = pl.BlockSpec((rows, model), lambda i, w: (0, 0))
+    return call(
+        mid_back_kernel,
+        [((rows, model), BF), ((1, model), F32)],
+        (grad, residual, recip, gain.reshape(1, -1), out_grad),
+        "mid_back",
+        grid=(1,),
+        in_specs=[
+            whole,
+            whole,
+            pl.BlockSpec((rows, LANES), lambda i, w: (0, 0)),
+            pl.BlockSpec((1, model), lambda i, w: (0, 0)),
+            pl.BlockSpec((rows, model), lambda i, w: (w[RANK], 0)),
+        ],
+        out_specs=[whole, pl.BlockSpec((1, model), lambda i, w: (0, 0))],
+        prefetch=info,
+    )
+
+
+def matmul_kernel(dims, info_ref, left_ref, right_ref, *refs):
+    out = lax.dot_general(left_ref[...], right_ref[...], (dims, ((), ())), preferred_element_type=F32)
+    if len(refs) == 1:
+        refs[0][...] = out.astype(BF)
+        return
+    outs, all_ref = refs[:-1], refs[-1]
+    all_ref[...] = out.astype(BF)
+    for s, out_ref in enumerate(outs):
+        out_ref[...] = all_ref[at_block(ahead(info_ref, s, len(outs)), out_ref.shape[0]), :]
+
+
+def matmul(info, left, right, transposed=False, parts=1):
+    rows, depth = left.shape
+    cols = right.shape[0 if transposed else 1]
+    tile = next(t for t in ((512, 256, LANES) if transposed else (1024, 512, 256, LANES)) if cols % t == 0)
+    if transposed:
+        dims, spec = ((1,), (1,)), pl.BlockSpec((tile, depth), lambda i, w: (i, 0))
+    else:
+        dims, spec = ((1,), (0,)), pl.BlockSpec((depth, tile), lambda i, w: (0, i))
+    outs = call(
+        functools.partial(matmul_kernel, dims),
+        [((rows // parts, cols), BF)] * parts,
+        (left, right),
+        "matmul",
+        scratch=[pltpu.VMEM((rows, tile), BF)] if parts > 1 else [],
+        grid=(cols // tile,),
+        in_specs=[once((rows, depth), lambda i, w: (0, 0)), spec],
+        out_specs=[pl.BlockSpec((rows // parts, tile), lambda i, w: (0, i))] * parts,
+        prefetch=info,
+    )
+    return outs if parts > 1 else outs[0]
+
+
+def quarter_order(info_ref):
+    bit_x = lax.rem(chip_of(info_ref), 2)
+    bit_y = lax.div(chip_of(info_ref), 2)
+    return 1 - bit_x, 3 - bit_y, bit_x, 2 + bit_y
+
+
+def product_kernel(counts, info_ref, *refs):
+    outs, all_ref = refs[4 * len(counts) : 4 * len(counts) + 4], refs[-1]
+    order = quarter_order(info_ref)
+    rows = outs[0].shape[0]
+    first = 0
+    for n, count in enumerate(counts):
+        own, other, own_right, other_right = refs[4 * n : 4 * n + 4]
+        step = pl.program_id(0)
+
+        def mixed(cols):
+            out = dense_tn(own[:, cols], own_right[...])
+            return (out + dense_tn(other[:, cols], other_right[...])).astype(BF)
+
+        @pl.when((step >= first) & (step < first + count))
+        def _():
+            if rows >= 256:
+                for out_ref, at in zip(outs, order):
+                    out_ref[...] = mixed(at_block(at, rows))
+            else:
+                all_ref[...] = mixed(slice(None))
+                for out_ref, at in zip(outs, order):
+                    out_ref[...] = all_ref[at_block(at, rows), :]
+
+        first += count
+
+
+def pair_products(info, terms, tile):
+    tokens, rows = terms[0][0].shape[0], terms[0][0].shape[1] // 2
+    counts = [term[2].shape[1] // tile for term in terms]
+    specs, args, first = [], [], 0
+    for term, count in zip(terms, counts):
+        specs += [once((tokens, rows), lambda i, w: (0, w[CORE]))] * 2
+        place = lambda i, w, first=first, count=count: (0, jnp.clip(i - first, 0, count - 1))
+        specs += [pl.BlockSpec((tokens, tile), place)] * 2
+        args += term
+        first += count
+    return call(
+        functools.partial(product_kernel, counts),
+        [((rows // 4, first * tile), BF)] * 4,
+        args,
+        "pair_products",
+        scratch=[pltpu.VMEM((rows, tile) if rows < 1024 else (16, LANES), BF)],
+        grid=(first,),
+        in_specs=specs,
+        out_specs=[pl.BlockSpec((rows // 4, tile), lambda i, w: (0, i))] * 4,
+        prefetch=info,
+    )
+
+
+def add_low(left, right):
+    return (left.astype(F32) + right.astype(F32)).astype(BF)
+
+
+def fold_near_kernel(info_ref, near_ref, got_ref, *outs):
+    for out_ref, at in zip(outs, quarter_order(info_ref)):
+        p, bit = lax.div(at, 2), lax.rem(at, 2)
+        for other in range(2):
+            chip = bit * 2 + other
+            out_ref[other] = add_low(near_ref[p, chip], got_ref[p, chip])
+
+
+def fold_near(info, near, got):
+    _, chips, rows, cols = near.shape
+    tile = rows // 3
+    return call(
+        fold_near_kernel,
+        [((2, rows, cols), BF)] * 4,
+        (near, got),
+        "fold_near",
+        grid=(3,),
+        in_specs=[pl.BlockSpec((2, chips, tile, cols), lambda i, w: (0, 0, i, 0))] * 2,
+        out_specs=[pl.BlockSpec((2, tile, cols), lambda i, w: (0, i, 0))] * 4,
+        prefetch=info,
+    )
+
+
+def fold_first_kernel(info_ref, keep_first, got_first, keep_last, got_last, *outs):
+    bit_x = lax.rem(chip_of(info_ref), 2)
+    bit_y = lax.div(chip_of(info_ref), 2)
+    outs[0][...] = add_low(keep_first[1 - bit_y], got_first[1 - bit_y])
+    outs[1][...] = add_low(keep_last[1 - bit_x], got_last[1 - bit_x])
+    outs[2][...] = add_low(keep_first[bit_y], got_first[bit_y])
+    outs[3][...] = add_low(keep_last[bit_x], got_last[bit_x])
+
+
+def fold_first(info, arrays, steps, micros=0):
+    rows, cols = arrays[0].shape[1:]
+    tile = rows // steps
+    return call(
+        fold_first_kernel,
+        [((rows, cols), BF)] * 4,
+        arrays,
+        "fold_first",
+        micros,
+        grid=(steps,),
+        in_specs=[pl.BlockSpec((2, tile, cols), lambda i, w: (0, i, 0))] * 4,
+        out_specs=[pl.BlockSpec((tile, cols), lambda i, w: (i, 0))] * 4,
+        prefetch=info,
+    )
+
+
+def fold_last_kernel(info_ref, keep_first, got_first, keep_last, got_last, out_ref):
+    out_ref[0] = add_low(keep_first[...], got_first[...])
+    out_ref[1] = add_low(keep_last[...], got_last[...])
+
+
+def fold_last(info, arrays, steps):
+    rows, cols = arrays[0].shape
+    tile = rows // steps
+    return call(
+        fold_last_kernel,
+        [((2, rows, cols), BF)],
+        arrays,
+        "fold_last",
+        grid=(steps,),
+        in_specs=[pl.BlockSpec((tile, cols), lambda i, w: (i, 0))] * 4,
+        out_specs=[pl.BlockSpec((2, tile, cols), lambda i, w: (0, i, 0))],
+        prefetch=info,
+    )[0]
+
+
+def fold_kv_kernel(info_ref, keep_first, got_first, keep_last, got_last, *refs):
+    outs, all_ref = refs[:-1], refs[-1]
+    half = keep_first.shape[0]
+    all_ref[:half, :] = add_low(keep_first[...], got_first[...])
+    all_ref[half:, :] = add_low(keep_last[...], got_last[...])
+    for s, out_ref in enumerate(outs):
+        out_ref[...] = all_ref[at_block(ahead(info_ref, s, len(outs)), out_ref.shape[0]), :]
+
+
+def fold_kv(info, arrays, ranks):
+    rows, cols = arrays[0].shape
+    return call(
+        fold_kv_kernel,
+        [((2 * rows // ranks, cols), BF)] * ranks,
+        arrays,
+        "fold_kv",
+        scratch=[pltpu.VMEM((2 * rows, cols), BF)],
+        prefetch=info,
+    )
+
+
+def fold_heads_kernel(info_ref, keep_first, got_first, keep_last, got_last, out_ref, *refs):
+    ups, all_ref = refs[:-1], refs[-1]
+    width = out_ref.shape[2]
+    all_ref[0] = add_low(keep_first[...], got_first[...])
+    all_ref[1] = add_low(keep_last[...], got_last[...])
+    out_ref[...] = all_ref[:, :, :width]
+    for s, up_ref in enumerate(ups):
+        up_ref[...] = all_ref[:, at_block(ahead(info_ref, s, len(ups)), up_ref.shape[1]), width:]
+
+
+def fold_heads(info, arrays, width, ranks):
+    rows, cols = arrays[0].shape
+    return call(
+        fold_heads_kernel,
+        [((2, rows, width), BF)] + [((2, rows // ranks, cols - width), BF)] * ranks,
+        arrays,
+        "fold_heads",
+        scratch=[pltpu.VMEM((2, rows, cols), BF)],
+        prefetch=info,
+    )
+
+
+def pack_heads_kernel(info_ref, out_ref, *refs):
+    ups, all_ref = refs[:-1], refs[-1]
+    width = out_ref.shape[2]
+    all_ref[:, :, :width] = out_ref[...]
+    for s, up_ref in enumerate(ups):
+        all_ref[:, at_block(behind(info_ref, s, len(ups)), up_ref.shape[1]), width:] = up_ref[...]
+
+
+def pack_heads(info, out, ups):
+    shape = out.shape[:2] + (out.shape[2] + ups[0].shape[2],)
+    return call(pack_heads_kernel, [(shape, BF)], (out, *ups), "pack_heads", prefetch=info)[0]
+
+
+def layer_kernel(info_ref, residual_ref, *refs):
+    parts, out_ref = refs[:-1], refs[-1]
+    out_ref[...] = (residual_ref[...] + sum(part[...].astype(F32) for part in parts)).astype(BF)
+
+
+def place_kernel(info_ref, *refs):
+    parts, out_ref = refs[:-1], refs[-1]
+    for s, part in enumerate(parts):
+        pl.when(pl.program_id(0) == s)(lambda part=part: out_ref.__setitem__(..., part[...]))
+
+
+def place(info, parts):
+    rows, cols = parts[0].shape
+    ranks = len(parts)
+    return call(
+        place_kernel,
+        [((ranks * rows, cols), BF)],
+        parts,
+        "place",
+        grid=(ranks,),
+        in_specs=[once((rows, cols), lambda i, w: (0, 0))] * ranks,
+        out_specs=[pl.BlockSpec((rows, cols), lambda i, w: (behind(w, i, ranks), 0))],
+        prefetch=info,
+    )[0]
+
+
+def input_back_kernel(
+    ranks, info_ref, tokens_ref, branch_ref, gain_ref, kv_weight_ref, recip_ref, latent_ref, kv_pre_ref, *refs
+):
+    latents, kvs, downs = refs[:ranks], refs[ranks : 2 * ranks], refs[2 * ranks : 3 * ranks]
+    grad_in_ref, norm_ref, own_ref, kv_ref, all_ref = refs[3 * ranks :]
+    rows = latents[0].shape[0]
+    cols = own_ref.shape[1]
+    for s in range(ranks):
+        at = at_block(behind(info_ref, s, ranks), rows)
+        all_ref[at, :] = latents[s][...]
+        kv_ref[at, :] = kvs[s][...]
+    grad = dense_nt(kv_ref[...], kv_weight_ref[...])
+    for s in range(ranks):
+        at = at_block(behind(info_ref, s, ranks), cols)
+        grad = grad + dense_nt(all_ref[:, at], downs[s][...])
+    own_ref[...] = all_ref[:, at_block(info_ref[RANK], cols)]
+    recip = recip_ref[:, 0:1]
+    latent = latent_ref[: all_ref.shape[0], :].astype(F32)
+    stat = jnp.sum(all_ref[...].astype(F32) * latent, -1, keepdims=True)
+    stat = stat + jnp.sum(kv_ref[...].astype(F32) * kv_pre_ref[...], -1, keepdims=True)
+    tokens = tokens_ref[...].astype(F32)
+    model = tokens.shape[1] * ranks
+    out = branch_ref[...].astype(F32) + recip * gain_ref[...] * grad
+    grad_in_ref[...] = out - tokens * (recip * recip * stat / model)
+    norm_ref[...] = jnp.sum(grad * tokens * recip, 0, keepdims=True)
+
+
+def input_back(info, tokens, branch, gain, kv_weight, recip, latent, kv_pre, latents, kvs, downs):
+    ranks = len(latents)
+    rows, model = tokens.shape
+    cols = model // ranks
+    width, down = kv_weight.shape[1], downs[0].shape[1]
+    whole = lambda array: pl.BlockSpec(array.shape, lambda i, w: (0, 0))
+    wide = pl.BlockSpec((rows, cols), lambda i, w: (0, w[RANK]))
+    outs = [((rows, cols), F32), ((1, cols), F32), ((rows, down), BF), ((rows, width), BF)]
+    return call(
+        functools.partial(input_back_kernel, ranks),
+        outs,
+        (tokens, branch, gain.reshape(1, -1), kv_weight, recip, latent, kv_pre, *latents, *kvs, *downs),
+        "input_back",
+        scratch=[pltpu.VMEM((rows, latent.shape[1]), BF)],
+        grid=(1,),
+        in_specs=[
+            wide,
+            wide,
+            pl.BlockSpec((1, cols), lambda i, w: (0, w[RANK])),
+            pl.BlockSpec((cols, width), lambda i, w: (w[RANK], 0)),
+        ]
+        + [whole(array) for array in (recip, latent, kv_pre, *latents, *kvs, *downs)],
+        out_specs=[pl.BlockSpec(shape, lambda i, w: (0, 0)) for shape, _ in outs],
+        prefetch=info,
+    )
+
+
+def last_products_kernel(info_ref, normed_ref, latent_ref, kv_ref, near_ref, far_ref, down_ref, wide_ref):
+    down_ref[...] = dense_tn(normed_ref[...], latent_ref[...]).astype(BF)
+    cols = wide_ref.shape[0]
+    wide_ref[...] = dense_tn(normed_ref[:, at_block(info_ref[RANK], cols)], kv_ref[...]).astype(BF)
+    chips, width = near_ref.shape[0], near_ref.shape[2]
+    for out_ref, core in ((near_ref, info_ref[CORE]), (far_ref, 1 - info_ref[CORE])):
+        for chip in range(chips):
+            rows = down_ref.shape[0] // (2 * chips)
+            out_ref[chip, :rows, :] = down_ref[at_block(core * chips + chip, rows), :]
+            more = wide_ref.shape[0] // (2 * chips)
+            part = wide_ref[at_block(core * chips + chip, more), :]
+            out_ref[chip, rows : rows + more, :] = part[:, :width]
+            out_ref[chip, rows + more :, :] = part[:, width:]
+
+
+def last_products(info, normed, latent, kv, ranks):
+    model, down, width = normed.shape[1], latent.shape[1], kv.shape[1]
+    cols = model // ranks
+    rows = (model + cols * width // down) // 8
+    return call(
+        last_products_kernel,
+        [((4, rows, down), BF)] * 2,
+        (normed, latent, kv),
+        "last_products",
+        scratch=[pltpu.VMEM((model, down), BF), pltpu.VMEM((cols, width), BF)],
+        prefetch=info,
+    )
+
+
+def fold_direct_kernel(info_ref, near_ref, got_ref, *outs):
+    for mask, out_ref in enumerate(outs):
+        chip = lax.bitwise_xor(chip_of(info_ref), mask)
+        out_ref[...] = add_low(near_ref[chip], got_ref[chip])
+
+
+def fold_direct(info, near, got):
+    return call(fold_direct_kernel, [(near.shape[1:], BF)] * 4, (near, got), "fold_direct", prefetch=info)
+
+
+def sum_kernel(info_ref, *refs):
+    refs[-1][...] = sum(part[...].astype(F32) for part in refs[:-1]).astype(BF)
+
+
+def sum_parts(info, parts):
+    return call(sum_kernel, [(parts[0].shape, BF)], parts, "sum_parts", prefetch=info)[0]
+
+
+def stack_kernel(info_ref, *refs):
+    for mask, part in enumerate(refs[:-1]):
+        refs[-1][lax.bitwise_xor(chip_of(info_ref), mask)] = part[...]
+
+
+def stack_chips(info, parts):
+    return call(stack_kernel, [((4,) + parts[0].shape, BF)], parts, "stack_chips", prefetch=info)[0]
+
+
+def last_kernel(info_ref, own_ref, other_ref, down_ref, kv_ref):
+    chips, width = own_ref.shape[0], own_ref.shape[2]
+    rows, more = down_ref.shape[0] // (2 * chips), kv_ref.shape[0] // (2 * chips)
+    for in_ref, core in ((own_ref, info_ref[CORE]), (other_ref, 1 - info_ref[CORE])):
+        for chip in range(chips):
+            part = in_ref[chip].astype(F32)
+            down_ref[at_block(core * chips + chip, rows), :] = part[:rows]
+            kv_ref[at_block(core * chips + chip, more), :width] = part[rows : rows + more]
+            kv_ref[at_block(core * chips + chip, more), width:] = part[rows + more :]
+
+
+def store_feed(part, gate_ref, up_ref, down_ref):
+    width = gate_ref.shape[1]
+    gate_ref[...] = part[:, :width].astype(F32)
+    up_ref[...] = part[:, width : 2 * width].astype(F32)
+    down_ref[...] = part[:, 2 * width :].astype(F32).T
+
+
+def store_heads(part, out_ref, up_ref):
+    width = out_ref.shape[1]
+    rows, cols = up_ref.shape[0], part.shape[1] - width
+    out_ref[...] = part[:, :width].astype(F32)
+    for r in range(part.shape[0] // rows):
+        up_ref[:, r * cols : (r + 1) * cols] = part[r * rows : (r + 1) * rows, width:].astype(F32)
+
+
+def unpack_kernel(store, info_ref, in_ref, *out_refs):
+    store(in_ref[...], *out_refs)
+
+
+def unpack(info, whole, store, shapes, along):
+    def where(i):
+        source, p = i // 2, i % 2
+        chip = source // 2
+        return source % 2 * 8 + p * 4 + jnp.where(p == 0, chip % 2 * 2 + chip // 2, chip)
+
+    out_specs = []
+    for (rows, cols), dim in zip(shapes, along):
+        if dim == 0:
+            out_specs.append(pl.BlockSpec((rows // 16, cols), lambda i, w: (where(i), 0)))
+        else:
+            out_specs.append(pl.BlockSpec((rows, cols // 16), lambda i, w: (0, where(i))))
+    return call(
+        functools.partial(unpack_kernel, store),
+        [(shape, F32) for shape in shapes],
+        (whole,),
+        "unpack",
+        grid=(16,),
+        in_specs=[pl.BlockSpec((None, None) + whole.shape[2:], lambda i, w: (i // 2, i % 2, 0, 0))],
+        out_specs=out_specs,
+        prefetch=info,
+    )
 
 
 def bit_of(index, bit):
     return (index >> bit) & 1
+
+
+def exchange(value, mask):
+    count = lax.axis_size("seq")
+    return lax.ppermute(value, "seq", [(i, i ^ mask) for i in range(count)])
+
+
+def swap(value, bit):
+    return exchange(value, 1 << bit)
+
+
+def ring(value, shift):
+    if not shift:
+        return value
+    ranks = lax.axis_size("rank")
+    return lax.ppermute(value, "rank", [(i, (i + shift) % ranks) for i in range(ranks)])
+
+
+def rings(values):
+    return [ring(value, s) for s, value in enumerate(values)]
+
+
+def sum_over(value, axis):
+    count = lax.axis_size(axis)
+    mask = 1
+    while mask < count:
+        value = value + lax.ppermute(value, axis, [(i, i ^ mask) for i in range(count)])
+        mask *= 2
+    return value
+
+
+def after(value, *others):
+    return lax.optimization_barrier((value, others))[0]
+
+
+def per_device_fast(
+    tokens_in,
+    norm1_gain,
+    q_down,
+    latent_gain,
+    q_up,
+    kv_weight,
+    out_weight,
+    norm2_gain,
+    gate_weight,
+    up_weight,
+    down_weight,
+    doc_ids,
+    out_grad,
+):
+    Order.last = None
+    row_count, model_width = tokens_in.shape
+    ranks = lax.axis_size("rank")
+    rank_ix = lax.axis_index("rank")
+    seq_ix = lax.axis_index("seq")
+    head_dim = kv_weight.shape[1] // 2
+    local_heads = out_weight.shape[0] // head_dim
+    first_row = seq_ix * row_count
+    core = bit_of(seq_ix, 0)
+    rank_cols = q_down.shape[1]
+    rank_width = rank_cols * ranks
+    col_count = model_width // ranks
+
+    up_cols = q_up.shape[1] // ranks
+    half_cols = up_cols // 2
+    blocks = [
+        lax.dynamic_slice_in_dim(
+            q_up, lax.rem(rank_ix + s, ranks) * up_cols + core * half_cols, half_cols, 1
+        )
+        for s in range(ranks)
+    ]
+    tokens_late = after(tokens_in, blocks)
+    up_own = jnp.concatenate(rings(blocks), 0)
+    up_other = swap(up_own, 0)
+
+    ids_local = lax.dynamic_slice_in_dim(doc_ids, first_row, row_count, 0)
+    start = jnp.sum((doc_ids[None, :] < ids_local[:, None]).astype(I32), 1)
+    query_index = first_row + jnp.arange(row_count, dtype=I32)
+    position = (query_index - start).astype(F32)
+    half_dim = head_dim // 2
+    freqs = BASE ** (-jnp.arange(half_dim, dtype=F32) / half_dim)
+    angle = position[:, None] * freqs[None, :]
+    cosine, sine = jnp.cos(angle), jnp.sin(angle)
+    start_rows = jnp.tile(start, local_heads)[None]
+    index_rows = jnp.tile(query_index, local_heads)[None]
+    place_info = jnp.stack([first_row, first_row, first_row, core, rank_ix, seq_ix]).astype(I32)
+    info = jnp.stack([first_row, start[0], start[-1], core, rank_ix, seq_ix]).astype(I32)
+
+    normed_low, recip1, kv_pre, latent = project(
+        place_info, tokens_late, norm1_gain, q_down, kv_weight, latent_gain
+    )
+    latent_all = lax.all_gather(latent, "rank", axis=1, tiled=True)
+
+    kv_local = turn(place_info, kv_pre, cosine, sine)
+    half_rows = row_count // 2
+    by_x, by_y = swap(kv_local, 1), swap(kv_local, 2)
+    top, bottom = swap(by_x[:half_rows], 2), swap(by_y[half_rows:], 1)
+    pieces = [(kv_local, 0, 0), (by_x, 2, 0), (by_y, 4, 0), (top, 6, 0), (bottom, 6, half_rows)]
+    pieces += [(swap(array, 0), mask ^ 1, offset) for array, mask, offset in pieces]
+
+    latent_low, recip_c, gain_all, query_pre = queries(place_info, latent_all, up_own, up_other)
+    query, attn_vals, attn_low, log_total, kv_all = attend(
+        in_order(info), query_pre, cosine, sine, start, pieces
+    )
+    Order.last = attn_low
+
+    branch_part = matmul(info, attn_low, out_weight)
+    branch = lax.psum_scatter(branch_part, "rank", scatter_dimension=0, tiled=True)
+    grad_hidden = dense_nt(after(out_grad, branch_part), down_weight)
+    out_grad_pair = swap(after(out_grad, branch_part), 0)
+    attn_pair = swap(attn_low, 0)
+    piece_cols = rank_cols // 16
+    latent_cut = jnp.transpose(
+        after(latent_low, branch_part).reshape(row_count, ranks, 16, piece_cols), (0, 2, 1, 3)
+    ).reshape(row_count, rank_width)
+    latent_pair = swap(latent_cut, 0)
+    down_blocks = [
+        lax.dynamic_slice_in_dim(
+            after(q_down, branch_part), lax.rem(rank_ix + s, ranks) * col_count, col_count, 0
+        )
+        for s in range(ranks)
+    ]
+    branch = after(
+        branch, grad_hidden, out_grad_pair, attn_pair, latent_pair, latent_cut, down_blocks
+    )
+    residual, mid_own, recip2 = mid_norm(info, branch, tokens_in, norm2_gain)
+    mid_low = lax.all_gather(mid_own, "rank", axis=0, tiled=True)
+
+    downs = rings(after(down_blocks, mid_low))
+    mid_pair = swap(mid_low, 0)
+    hidden_low, grad_both, grad_mid_part = feed_forward(
+        mid_low, grad_hidden, gate_weight, up_weight
+    )
+    Order.last = hidden_low
+    hidden_low, grad_both, grad_mid_part = after((hidden_low, grad_both, grad_mid_part), downs)
+    grad_mid = lax.psum_scatter(grad_mid_part, "rank", scatter_dimension=0, tiled=True)
+    both_pair, hidden_pair = swap(grad_both, 0), swap(hidden_low, 0)
+    feed_parts = matmul(info, hidden_low, down_weight, parts=ranks)
+    feed_width = gate_weight.shape[1]
+    send_first, send_last, keep_first, keep_last = pair_products(
+        info,
+        [
+            (mid_low, mid_pair, grad_both, both_pair),
+            (out_grad, out_grad_pair, hidden_low, hidden_pair),
+        ],
+        feed_width,
+    )
+    grad_mid = after(grad_mid, send_first)
+    branch_own, norm2_part = mid_back(info, grad_mid, residual, recip2, norm2_gain, out_grad)
+    grad_branch = lax.all_gather(branch_own, "rank", axis=0, tiled=True)
+
+    two = lambda array: array.reshape((2, -1) + array.shape[1:])
+    arrays = (keep_first, swap(send_first, 1), keep_last, swap(send_last, 2))
+    arrays = fold_first(info, [two(array) for array in arrays], 4, 10000)
+    arrays = (arrays[2], swap(arrays[0], 2), arrays[3], swap(arrays[1], 1))
+    feed_piece = fold_last(info, arrays, 4)
+    branch_pair = swap(grad_branch, 0)
+    grad_attn = matmul(info, grad_branch, out_weight, True)
+    feed_whole = lax.all_gather(feed_piece, "seq", axis=0, tiled=False)
+    feed_sums = rings(after(feed_parts, grad_branch))
+    grad_query, near, far = attend_back(
+        in_order(info), query, grad_attn, attn_vals, log_total, cosine, sine, kv_all,
+        start_rows, index_rows, True,
+    )
+    grad_query, near, far = after((grad_query, near, far), feed_sums, branch_pair)
+    Order.last = grad_query
+
+    latent_grads = rings(latent_parts(info, grad_query, up_own, up_other, ranks))
+    query_pair = swap(grad_query, 0)
+    arrays = fold_near(info, near, swap(far, 0))
+    heads = pair_products(
+        info,
+        [
+            (attn_low, attn_pair, grad_branch, branch_pair),
+            (latent_cut, latent_pair, grad_query, query_pair),
+        ],
+        up_cols,
+    )
+    arrays = (arrays[2], swap(arrays[0], 1), arrays[3], swap(arrays[1], 2))
+    arrays = fold_first(info, after(arrays, latent_grads), 1)
+    arrays = (arrays[2], swap(arrays[0], 2), arrays[3], swap(arrays[1], 1))
+    latent_own, gain_part = latent_back(info, latent_all, recip_c, gain_all, latent_grads)
+    latent_blocks = rings([latent_own] * ranks)
+    kv_sums = rings(fold_kv(info, arrays, ranks))
+    arrays = (heads[2], swap(heads[0], 1), heads[3], swap(heads[1], 2))
+    arrays = fold_first(info, [two(array) for array in arrays], 1)
+    kv_own = kv_back(info, cosine, sine, kv_sums)
+    kv_blocks = rings([kv_own] * ranks)
+    arrays = (arrays[2], swap(arrays[0], 2), arrays[3], swap(arrays[1], 1))
+    arrays = after(arrays, latent_blocks)
+    out_piece, *up_pieces = fold_heads(info, arrays, model_width, ranks)
+    heads_piece = pack_heads(info, out_piece, rings(up_pieces))
+    heads_whole = lax.all_gather(heads_piece, "seq", axis=0, tiled=False)
+    layer_own = call(
+        layer_kernel, [(residual.shape, BF)], (residual, *feed_sums), "layer", prefetch=info
+    )[0]
+    shape = gate_weight.shape
+    grad_gate, grad_up, grad_down = unpack(
+        info, after(feed_whole, kv_blocks), store_feed, (shape, shape, shape[::-1]), (0, 0, 1)
+    )
+    gains = jnp.concatenate([norm2_part[0], gain_part[0]])
+    gains = sum_over(sum_over(gains, "rank"), "seq")
+    layer_blocks = rings([after(layer_own, kv_blocks, latent_blocks, gains)] * ranks)
+
+    grad_in, norm1_part, latent_cols, grad_kv = input_back(
+        info, tokens_in, grad_branch, norm1_gain, kv_weight, recip1, latent_all, kv_pre,
+        latent_blocks, kv_blocks, downs,
+    )
+    near, far = last_products(info, normed_low, latent_cols, grad_kv, ranks)
+    own, *others = fold_direct(info, near, swap(far, 0))
+    norm1 = sum_over(norm1_part[0], "seq")
+    piece = sum_parts(info, [own] + [exchange(part, 2 * m) for m, part in enumerate(others, 1)])
+    last = stack_chips(info, after([piece] + [exchange(piece, 2 * m) for m in (1, 2, 3)], norm1))
+    grad_q_down, grad_kv_weight = call(
+        last_kernel,
+        [(q_down.shape, F32), ((col_count, 2 * head_dim), F32)],
+        (last, swap(last, 0)),
+        "last",
+        prefetch=info,
+    )
+    grad_out, grad_q_up = unpack(
+        info, heads_whole, store_heads, (out_weight.shape, q_up.shape), (0, 0)
+    )
+    layer_out = place(info, after(layer_blocks, grad_out))
+
+    grad_norm2 = gains[:model_width]
+    grad_latent_gain = lax.dynamic_slice_in_dim(gains, model_width + rank_ix * rank_cols, rank_cols, 0)
+    return (
+        layer_out,
+        grad_in,
+        norm1,
+        grad_q_down,
+        grad_latent_gain,
+        grad_q_up,
+        grad_kv_weight,
+        grad_out,
+        grad_norm2,
+        grad_gate,
+        grad_up,
+        grad_down,
+    )
 
 
 def add_low(left, right):
@@ -308,31 +1359,12 @@
     return gather_rows(scatter_rows(near, far, seq_ix)).astype(F32)
 
 
-def gather_kv(local, seq_ix):
-    seq = lax.axis_size("seq")
-    if seq != 8:
-        return lax.all_gather(local, "seq", axis=0, tiled=True)
-    half = local.shape[0] // 2
-    by_x = swap(local, 1)
-    by_y = swap(local, 2)
-    across = jnp.concatenate([swap(by_x[:half], 2), swap(by_y[half:], 1)], 0)
-    blocks = {0: local, 2: by_x, 4: by_y, 6: across}
-    for mask in (0, 2, 4, 6):
-        blocks[mask + 1] = swap(blocks[mask], 0)
-    whole = jnp.zeros((seq * local.shape[0], local.shape[1]), local.dtype)
-    for mask, block in blocks.items():
-        whole = lax.dynamic_update_slice_in_dim(
-            whole, block, (seq_ix ^ mask) * local.shape[0], 0
-        )
-    return whole
-
-
 def high_low(values):
     high = values.astype(BF)
     return [high, (values - high.astype(F32)).astype(BF)]
 
 
-def per_device(
+def per_device_general(
     tokens_in,
     norm1_gain,
     q_down,
@@ -388,7 +1420,7 @@
     kv_pre = dense(normed_low, kv_weight)
     key_local = rotate(kv_pre[:, :head_dim], cosine_rows, sine_rows)
     kv_local = jnp.concatenate([key_local, kv_pre[:, head_dim:]], -1).astype(BF)
-    kv_all = gather_kv(kv_local, seq_ix)
+    kv_all = lax.all_gather(kv_local, "seq", axis=0, tiled=True)
 
     latent = dense(normed_low, q_down)
     high, rest = high_low(latent_gain)
@@ -403,10 +1435,9 @@
     latent_low = (latent_all * recip_c * gain_all).astype(BF)
     query_pre = dense(latent_low, q_up_own)
 
-    query, attn_vals, log_total = attend(
-        info, query_pre, cosine_rows, sine_rows, kv_all, start_rows, index_rows
-    )
-    attn_low = attn_vals.astype(BF)
+    query, attn_vals, attn_low, log_total, kv_all = attend(
+        info, query_pre, cosine_rows, sine_rows, start, [(kv_all, None, 0)]
+    )
     branch = lax.psum_scatter(
         dense(attn_low, out_weight).astype(BF), "rank", scatter_dimension=0, tiled=True
     )
@@ -451,20 +1482,15 @@
     )
     grad_norm2 = jnp.sum(grad_mid * residual * recip2, 0)
     grad_branch = lax.all_gather(grad_residual.astype(BF), "rank", axis=0, tiled=True)
-    grad_attn_wide = dense_nt(grad_branch, out_weight)
-    grad_attn = grad_attn_wide.astype(BF)
+    grad_attn = dense_nt(grad_branch, out_weight).astype(BF)
     grad_out = reduce_product(attn_low, grad_branch, seq_ix)
-    delta = jnp.sum(
-        (grad_attn.astype(F32) * attn_vals).reshape(row_count, local_heads, head_dim), -1
-    ).T.reshape(1, -1)
-
     grad_query, near, far = attend_back(
-        info, query, grad_attn, delta, log_total, cosine_rows, sine_rows, kv_all, start_rows, index_rows
+        info, query, grad_attn, attn_vals, log_total, cosine_rows, sine_rows, kv_all,
+        start_rows, index_rows, False,
     )
 
     chips = seq_count // 2
-    kv_shape = (chips, 2, row_count // 2, 2 * head_dim)
-    summed = scatter_rows(near.reshape(kv_shape), far.reshape(kv_shape), seq_ix)
+    summed = scatter_rows(jnp.swapaxes(near, 0, 1), jnp.swapaxes(far, 0, 1), seq_ix)
     summed = lax.psum(summed.reshape(row_count, 2 * head_dim), "rank").astype(F32)
     key_back = rotate(summed[:, :head_dim], cosine_rows, -sine_rows)
     grad_kv = jnp.concatenate([key_back, summed[:, head_dim:]], -1).astype(BF)
@@ -541,6 +1567,21 @@
         grad_up,
         grad_down,
     )
+
+
+def per_device(*args):
+    tokens, out_weight = args[0], args[6]
+    fits = (
+        lax.axis_size("seq") == 8
+        and lax.axis_size("rank") == 4
+        and tokens.shape[0] % 64 == 0
+        and tokens.shape[1] % 2048 == 0
+        and args[2].shape[1] % 256 == 0
+        and out_weight.shape[0] % 1024 == 0
+        and args[8].shape[1] % LANES == 0
+        and args[11].shape[0] % 512 == 0
+    )
+    return (per_device_fast if fits else per_device_general)(*args)
 
 
 def solution(mesh):

time: 965 us -> 732 us (0.76)
  Pallas kernels: 34.1 us -> 236 us
  waiting for transfers between devices: 479 us -> 326 us
  matrix products: 117 us -> 6.97 us
  other arithmetic: 97.9 us -> 5.45 us
  local copies, waits for them, and re-layouts: 114 us -> 35.2 us
    pallas_call x2 -> x34, Pallas kernels: 34.1 us -> 236 us  [the longest x19 144 us: placed_call(): pl.pallas_call(kernel, grid_spec=pltpu.PrefetchScalarGridSpec(num_scalar_...]
    ppermute x39 -> x74, waiting for transfers between devices: 107 us -> 203 us  [the longest x39 105 us: exchange(): return lax.ppermute(value, 'seq', [(i, i ^ mask) for i in range(count)])]
    all_gather x9 -> x5, waiting for transfers between devices: 141 us -> 49.4 us  [the longest x1 49.4 us: per_device_fast(): mid_low = lax.all_gather(mid_own, 'rank', axis=0, tiled=True)]
    dot_general x19 -> x0, matrix products: 84.3 us -> none  [the longest x12 46.9 us: dense_tn(): lax.dot_general(left, right, (((0,), (0,)), ((), ())), preferred_element_...]
    reduce_scatter x3 -> x2, waiting for transfers between devices: 156 us -> 73.7 us  [the longest x1 62.3 us: per_device_fast(): lax.psum_scatter(branch_part, 'rank', scatter_dimension=0, tiled=True)]
    convert_element_type x37 -> x1, other arithmetic: 66.2 us -> 0.6 us  [per_device_fast(): position = (query_index - start).astype(F32)]
    psum x2 -> x0, waiting for transfers between devices: 44.2 us -> none  [the longest x1 44.2 us: per_device(): lax.psum(jnp.concatenate([grad_kv_weight, small_rows], 0), 'seq')]
    convert_element_type x5 -> x0, local copies, waits for them, and re-layouts: 38.1 us -> none  [the longest x4 35.8 us: reduce_product(): return gather_rows(scatter_rows(near, far, seq_ix)).astype(F32)]
  transfers between devices with their start and end apart: 56 -> 81, of which waited for: 31 -> 36; matrix products, arithmetic and copies ran while one was open for 23% -> 3% of each run, Pallas kernels for 0% -> 29%
where the time goes in v2:
time: 732 us; the launch traced here: 718 us
  waiting for transfers between devices  326 us (45%)
  Pallas kernels  236 us (32%)
  starting transfers between devices  93.3 us (13%)
  local copies, waits for them, and re-layouts  35.2 us (5%)
  between operations  15.2 us (2%)
    pallas_call x19, Pallas kernels, placed_call(): pl.pallas_call(kernel, grid_spec=pltpu.PrefetchScalarGridSpec(num_scalar_...  144 us
    ppermute x39, waiting for transfers between devices, exchange(): return lax.ppermute(value, 'seq', [(i, i ^ mask) for i in range(count)])  105 us
    ppermute x27, waiting for transfers between devices, ring(): lax.ppermute(value, 'rank', [(i, (i + shift) % ranks) for i in range(rank...  86 us
    reduce_scatter x1, waiting for transfers between devices, per_device_fast(): lax.psum_scatter(branch_part, 'rank', scatter_dimension=0, tiled=True)  62.3 us
    all_gather x1, waiting for transfers between devices, per_device_fast(): mid_low = lax.all_gather(mid_own, 'rank', axis=0, tiled=True)  49.4 us
    ppermute x39, starting transfers between devices, exchange(): return lax.ppermute(value, 'seq', [(i, i ^ mask) for i in range(count)])  43.1 us
    ppermute x27, starting transfers between devices, ring(): lax.ppermute(value, 'rank', [(i, (i + shift) % ranks) for i in range(rank...  41 us
    pallas_call x12, Pallas kernels, placed_call(): pl.pallas_call(kernel, in_specs=[pl.BlockSpec(memory_space=pltpu.SMEM)] +...  36.4 us
  transfers between devices with their start and end apart: 81, of which 36 were waited for; matrix products, arithmetic and copies ran while one was open for 3% of the time, Pallas kernels for 29%

profile of v2, /device:TPU:25, one launch (start us, length us, event | category | flops | bytes accessed | tf_op | source)
XLA Modules:
  0.0 717.7 jit_solution(16112857040982085570)
XLA Ops:
  12.5 7.2 %project.1 = (bf16[576,2048]{1,0:T(8,128)(2,1)}, f32[576,128]{1,0:T(8,128)}, f32[576,512]{1,0:T(8,128)}, bf16[592,256]{1,0:T(8,128)(2,1)}) custom-call(s32[6]{0:T(128)} %stack.29.info_ref, bf16[576,2048]{1,0:T(8,128)(2,1)} %tokens_ref.4, f32[1,2048]{1,0:T(1,128)} %bitcast.38, bf16[2048,256]{1,0:T(8,128)(2,1)} %down_ref.1, bf16[2048,512]{1,0:T(8,128)(2,1)} %kv_weight_ref.3, ...), custom_call_target="tpu_custom_call" | custom-call | tf_op jit(solution)/shard_map/project/pallas_call | solution.py:372
  33.7 6.1 collective-permute-done.4.refs_1_
  43.5 4.2 collective-permute-done.5.refs_2_
  60.9 5.1 queries.1
  66.9 15.8 %attend.1 = (bf16[2304,256]{1,0:T(8,128)(2,1)}, f32[576,1024]{1,0:T(8,128)}, bf16[576,1024]{1,0:T(8,128)(2,1)}, f32[1,2304]{1,0:T(1,128)}, bf16[4608,512]{1,0:T(8,128)(2,1)}) custom-call(s32[6]{0:T(128)} %stack.28.info_ref, f32[576,1024]{1,0:T(8,128)} %get-tuple-element.174.pre_ref, f32[576,128]{1,0:T(8,128)} %get-tuple-element.329.cos_ref, ...), custom_call_target="tpu_custom_call" | custom-call | tf_op jit(solution)/shard_map/attend/pallas_call | solution.py:169
  82.7 6.4 matmul.3
  93.9 7.0 fusion.2.grad_ref
  100.9 62.3 %reduce-scatter.3.cloned.1.call-done.branch_ref = bf16[144,2048]{1,0:T(8,128)(2,1)} async-done(((bf16[576,2048]{1,0:T(8,128)(2,1)}), bf16[144,2048]{1,0:T(8,128)(2,1)}) %reduce-scatter.3.cloned.1.call-update) | async-done | bytes 589840 | tf_op jit(solution)/shard_map/reduce_scatter | solution.py:1168
  163.2 3.3 mid_norm.1
  166.6 49.4 %all-gather.10.cloned.1.call-done.mid_ref.refs_0_ = bf16[576,2048]{1,0:T(8,128)(2,1)} async-done(((bf16[144,2048]{1,0:T(8,128)(2,1)}), bf16[576,2048]{1,0:T(8,128)(2,1)}) %all-gather.10.cloned.1.call-update) | async-done | bytes 2359312 | tf_op jit(solution)/shard_map/all_gather | solution.py:1187
  220.4 19.7 %feed_forward.1 = (bf16[576,1408]{1,0:T(8,128)(2,1)S(1)}, bf16[576,2816]{1,0:T(8,128)(2,1)S(1)}, bf16[576,2048]{1,0:T(8,128)(2,1)S(1)}) custom-call(bf16[576,2048]{1,0:T(8,128)(2,1)S(1)} %copy-done, f32[576,1408]{1,0:T(8,128)S(1)} %fusion.2.grad_ref, bf16[2048,1408]{1,0:T(8,128)(2,1)} %gate_ref.1, bf16[2048,1408]{1,0:T(8,128)(2,1)} %up_ref.1), custom_call_target="tpu_custom_call" | custom-call | flops 2000000000 | tf_op jit(solution)/shard_map/feed_forward/pallas_call | solution.py:322
  247.3 8.2 %matmul.4 = (bf16[144,2048]{1,0:T(8,128)(2,1)}, bf16[144,2048]{1,0:T(8,128)(2,1)}, bf16[144,2048]{1,0:T(8,128)(2,1)}, bf16[144,2048]{1,0:T(8,128)(2,1)}) custom-call(s32[6]{0:T(128)} %stack.28.info_ref, bf16[576,1408]{1,0:T(8,128)(2,1)} %copy-done.2, bf16[1408,2048]{1,0:T(8,128)(2,1)} %right_ref.4), custom_call_target="tpu_custom_call" | custom-call | tf_op jit(solution)/shard_map/matmul/pallas_call | solution.py:372
  258.3 22.2 %pair_products.2 = (bf16[256,4224]{1,0:T(8,128)(2,1)}, bf16[256,4224]{1,0:T(8,128)(2,1)}, bf16[256,4224]{1,0:T(8,128)(2,1)}, bf16[256,4224]{1,0:T(8,128)(2,1)}) custom-call(s32[6]{0:T(128)} %stack.28.info_ref, bf16[576,2048]{1,0:T(8,128)(2,1)} %all-gather.10.cloned.1.call-done.mid_ref.refs_0_, bf16[576,2048]{1,0:T(8,128)(2,1)} %copy-done.12, ...), custom_call_target="tpu_custom_call" | custom-call | tf_op jit(solution)/shard_map/pair_products/pallas_call | solution.py:372
  282.8 11.4 %reduce-scatter.5.cloned.1.call-done.grad_ref = bf16[144,2048]{1,0:T(8,128)(2,1)} async-done(((bf16[576,2048]{1,0:T(8,128)(2,1)}), bf16[144,2048]{1,0:T(8,128)(2,1)}) %reduce-scatter.5.cloned.1.call-update) | async-done | bytes 589840 | tf_op jit(solution)/shard_map/reduce_scatter | solution.py:1196
  294.3 3.7 mid_back.1
  298.0 31.0 %collective-permute-done.22 = bf16[256,4224]{1,0:T(8,128)(2,1)S(1)} collective-permute-done((bf16[256,4224]{1,0:T(8,128)(2,1)}, bf16[256,4224]{1,0:T(8,128)(2,1)S(1)}, u32[]{:S(2)}, u32[]{:S(2)}) %collective-permute-start.22) | collective-permute-done | bytes 2162720 | tf_op jit(solution)/shard_map/ppermute | solution.py:1065
  330.3 6.6 fold_first.3
  339.3 22.0 %collective-permute-done.24.got_first = bf16[128,4224]{1,0:T(8,128)(2,1)S(1)} collective-permute-done((bf16[128,4224]{1,0:T(8,128)(2,1)}, bf16[128,4224]{1,0:T(8,128)(2,1)S(1)}, u32[]{:S(2)}, u32[]{:S(2)}) %collective-permute-start.24) | collective-permute-done | bytes 1081376 | tf_op jit(solution)/shard_map/ppermute | solution.py:1065
  363.3 5.1 fold_last.1
  370.9 3.3 collective-permute-start.26
  377.0 7.3 %matmul.5.grad_ref = bf16[576,1024]{1,0:T(8,128)(2,1)} custom-call(s32[6]{0:T(128)} %stack.28.info_ref, bf16[576,2048]{1,0:T(8,128)(2,1)} %all-gather.12.cloned.1.call-done.left_ref.refs_2_.branch_ref, bf16[1024,2048]{1,0:T(8,128)(2,1)} %right_ref.5), custom_call_target="tpu_custom_call" | custom-call | tf_op jit(solution)/shard_map/matmul/pallas_call | solution.py:372
  384.3 19.4 %attend_back.1 = (bf16[576,1024]{1,0:T(8,128)(2,1)}, bf16[2,4,288,512]{3,2,1,0:T(8,128)(2,1)}, bf16[2,4,288,512]{3,2,1,0:T(8,128)(2,1)}) custom-call(s32[6]{0:T(128)} %stack.28.info_ref, bf16[2304,256]{1,0:T(8,128)(2,1)} %get-tuple-element.213.query_ref, bf16[576,1024]{1,0:T(8,128)(2,1)} %matmul.5.grad_ref, f32[576,1024]{1,0:T(8,128)} %get-tuple-element.214.out_ref, ...), custom_call_target="tpu_custom_call" | custom-call | tf_op jit(solution)/shard_map/attend_back/pallas_call | solution.py:271
  403.7 22.6 %collective-permute-done.27.refs_2_ = bf16[144,2048]{1,0:T(8,128)(2,1)S(1)} collective-permute-done((bf16[144,2048]{1,0:T(8,128)(2,1)}, bf16[144,2048]{1,0:T(8,128)(2,1)S(1)}, u32[]{:S(2)}, u32[]{:S(2)}) %collective-permute-start.27) | collective-permute-done | bytes 589856 | tf_op jit(solution)/shard_map/ppermute | solution.py:1076
  427.3 4.7 latent_parts.1
  434.2 5.3 fold_near.1
  443.9 10.9 %pair_products.3 = (bf16[128,3072]{1,0:T(8,128)(2,1)}, bf16[128,3072]{1,0:T(8,128)(2,1)}, bf16[128,3072]{1,0:T(8,128)(2,1)}, bf16[128,3072]{1,0:T(8,128)(2,1)}) custom-call(s32[6]{0:T(128)} %stack.28.info_ref, bf16[576,1024]{1,0:T(8,128)(2,1)} %get-tuple-element.175.left_ref.refs_0_, bf16[576,1024]{1,0:T(8,128)(2,1)} %collective-permute-done.14.refs_1_, ...), custom_call_target="tpu_custom_call" | custom-call | tf_op jit(solution)/shard_map/pair_products/pallas_call | solution.py:372
  456.3 7.4 %collective-permute-done.36.refs_3_ = bf16[144,1024]{1,0:T(8,128)(2,1)S(1)} collective-permute-done((bf16[144,1024]{1,0:T(8,128)(2,1)S(1)}, bf16[144,1024]{1,0:T(8,128)(2,1)S(1)}, u32[]{:S(2)}, u32[]{:S(2)}) %collective-permute-start.36) | collective-permute-done | bytes 294944 | tf_op jit(solution)/shard_map/ppermute | solution.py:1076
  463.7 3.7 collective-permute-done.32.got_first
  470.1 3.5 fold_first.4
  475.5 3.2 latent_back.1
  478.7 18.2 %collective-permute-done.37.got_first = bf16[288,512]{1,0:T(8,128)(2,1)S(1)} collective-permute-done((bf16[288,512]{1,0:T(8,128)(2,1)}, bf16[288,512]{1,0:T(8,128)(2,1)S(1)}, u32[]{:S(2)}, u32[]{:S(2)}) %collective-permute-start.37) | collective-permute-done | bytes 294944 | tf_op jit(solution)/shard_map/ppermute | solution.py:1065
  503.2 3.9 fold_first.5
  513.5 13.8 %collective-permute-start.48 = (bf16[144,1024]{1,0:T(8,128)(2,1)S(1)}, bf16[144,1024]{1,0:T(8,128)(2,1)S(1)}, u32[]{:S(2)}, u32[]{:S(2)}) collective-permute-start(bf16[144,1024]{1,0:T(8,128)(2,1)S(1)} %copy-done.33), channel_id=1, source_target_pairs={{0,3},{1,0},{2,1},{3,2},{4,7},{5,4},{6,5},{7,6},{8,11},{9,8},{10,9... | collective-permute-start | bytes 884744 | tf_op jit(solution)/shard_map/ppermute | solution.py:1076
  529.9 9.1 %collective-permute-done.47.refs_2_ = bf16[144,1024]{1,0:T(8,128)(2,1)S(1)} collective-permute-done((bf16[144,1024]{1,0:T(8,128)(2,1)S(1)}, bf16[144,1024]{1,0:T(8,128)(2,1)S(1)}, u32[]{:S(2)}, u32[]{:S(2)}) %collective-permute-start.47) | collective-permute-done | bytes 294944 | tf_op jit(solution)/shard_map/ppermute | solution.py:1076
  542.5 3.6 collective-permute-start.49
  547.8 5.2 collective-permute-done.50.refs_2_
  561.5 7.7 %collective-permute-done.53.refs_6_ = bf16[144,512]{1,0:T(8,128)(2,1)S(1)} collective-permute-done((bf16[144,512]{1,0:T(8,128)(2,1)S(1)}, bf16[144,512]{1,0:T(8,128)(2,1)S(1)}, u32[]{:S(2)}, u32[]{:S(2)}) %collective-permute-start.53) | collective-permute-done | bytes 147488 | tf_op jit(solution)/shard_map/ppermute | solution.py:1076
  569.3 21.4 %unpack.2 = (f32[2048,1408]{1,0:T(8,128)}, f32[2048,1408]{1,0:T(8,128)}, f32[1408,2048]{1,0:T(8,128)}) custom-call(s32[6]{0:T(128)} %stack.28.info_ref, bf16[8,2,128,4224]{3,2,1,0:T(8,128)(2,1)} %bitcast.26), custom_call_target="tpu_custom_call" | custom-call | tf_op jit(solution)/shard_map/unpack/pallas_call | solution.py:372
  590.7 6.6 input_back.1
  597.3 4.5 last_products.1
  611.4 3.7 collective-permute-done.56.refs_1_
  616.0 4.5 collective-permute-done.58.refs_3_
  625.9 3.1 collective-permute-start.62
  639.4 3.3 collective-permute-start.65
  659.3 3.2 last.1
  662.5 12.7 %unpack.3 = (f32[1024,2048]{1,0:T(8,128)}, f32[256,4096]{1,0:T(8,128)}) custom-call(s32[6]{0:T(128)} %stack.28.info_ref, bf16[8,2,64,3072]{3,2,1,0:T(8,128)(2,1)} %bitcast.27), custom_call_target="tpu_custom_call" | custom-call | tf_op jit(solution)/shard_map/unpack/pallas_call | solution.py:372
  675.3 29.3 %collective-permute-done.72.refs_2_ = bf16[144,2048]{1,0:T(8,128)(2,1)S(1)} collective-permute-done((bf16[144,2048]{1,0:T(8,128)(2,1)S(1)}, bf16[144,2048]{1,0:T(8,128)(2,1)S(1)}, u32[]{:S(2)}, u32[]{:S(2)}) %collective-permute-start.72) | collective-permute-done | bytes 589856 | tf_op jit(solution)/shard_map/ppermute | solution.py:1076
  706.2 4.2 place.1
  (320 shorter events, 156.3 us)
Async XLA Ops:
  7.2 53.7 %all-gather.8.cloned.1.call-start = ((), (), s32[]{:S(2)}) async-start(), calls=%async_computation.2 | async-start | bytes 1515520 | tf_op jit(solution)/shard_map/all_gather | solution.py:1152
  8.5 18.6 %collective-permute-start.2 = (bf16[256,512]{1,0:T(8,128)(2,1)S(1)}, bf16[256,512]{1,0:T(8,128)(2,1)S(1)}, u32[]{:S(2)}, u32[]{:S(2)}) collective-permute-start(bf16[256,512]{1,0:T(8,128)(2,1)S(1)} %get-tuple-element.320), channel_id=1, source_target_pairs={{0,3},{1,0},{2,1},{3,2},{4,7},{5,4},{6,5},{7,6},{8,11},{9,8},{10,9... | collective-permute-start | bytes 786440 | tf_op jit(solution)/shard_map/ppermute | solution.py:1076
  8.8 19.6 %collective-permute-start.1 = (bf16[256,512]{1,0:T(8,128)(2,1)S(1)}, bf16[256,512]{1,0:T(8,128)(2,1)S(1)}, u32[]{:S(2)}, u32[]{:S(2)}) collective-permute-start(bf16[256,512]{1,0:T(8,128)(2,1)S(1)} %get-tuple-element.323), channel_id=1, source_target_pairs={{0,2},{1,3},{2,0},{3,1},{4,6},{5,7},{6,4},{7,5},{8,10},{9,11},{10,... | collective-permute-start | bytes 786440 | tf_op jit(solution)/shard_map/ppermute | solution.py:1076
  8.8 20.3 %collective-permute-start = (bf16[256,512]{1,0:T(8,128)(2,1)S(1)}, bf16[256,512]{1,0:T(8,128)(2,1)}, u32[]{:S(2)}, u32[]{:S(2)}) collective-permute-start(bf16[256,512]{1,0:T(8,128)(2,1)S(1)} %get-tuple-element.321), channel_id=1, source_target_pairs={{0,1},{1,2},{2,3},{3,0},{4,5},{5,6},{6,7},{7,4},{8,9},{9,10},{10,1... | collective-permute-start | bytes 786440 | tf_op jit(solution)/shard_map/ppermute | solution.py:1076
  19.7 143.6 %reduce-scatter.3.cloned.1.call-start = ((), (), s32[]{:S(2)}) async-start(), calls=%async_computation.3 | async-start | bytes 2949120 | tf_op jit(solution)/shard_map/reduce_scatter | solution.py:1168
  25.9 13.9 %collective-permute-start.4 = (bf16[576,512]{1,0:T(8,128)(2,1)}, bf16[576,512]{1,0:T(8,128)(2,1)S(1)}, u32[]{:S(2)}, u32[]{:S(2)}) collective-permute-start(bf16[576,512]{1,0:T(8,128)(2,1)} %turn.1.refs_0_), channel_id=1, source_target_pairs={{0,8},{4,12},{8,0},{12,4},{16,24},{20,28},{24,16},{28,20},{1,9},{5... | collective-permute-start | bytes 1769480 | tf_op jit(solution)/shard_map/ppermute | solution.py:1065
  30.2 28.0 %collective-permute-start.3 = (bf16[1024,512]{1,0:T(8,128)(2,1)S(1)}, bf16[1024,512]{1,0:T(8,128)(2,1)S(1)}, u32[]{:S(2)}, u32[]{:S(2)}) collective-permute-start(bf16[1024,512]{1,0:T(8,128)(2,1)S(1)} %pad_maximum_fusion.own_ref), channel_id=1, source_target_pairs={{0,4},{4,0},{8,12},{12,8},{16,20},{20,16},{24,28},{28,24},{1,5},{5... | collective-permute-start | bytes 3145736 | tf_op jit(solution)/shard_map/ppermute | solution.py:1065
  32.4 15.2 %collective-permute-start.5 = (bf16[576,512]{1,0:T(8,128)(2,1)}, bf16[576,512]{1,0:T(8,128)(2,1)}, u32[]{:S(2)}, u32[]{:S(2)}) collective-permute-start(bf16[576,512]{1,0:T(8,128)(2,1)} %turn.1.refs_0_), channel_id=1, source_target_pairs={{0,16},{4,20},{8,24},{12,28},{16,0},{20,4},{24,8},{28,12},{1,17},{... | collective-permute-start | bytes 1769480 | tf_op jit(solution)/shard_map/ppermute | solution.py:1065
  39.8 14.1 %collective-permute-start.6 = (bf16[288,512]{1,0:T(8,128)(2,1)S(1)}, bf16[288,512]{1,0:T(8,128)(2,1)}, u32[]{:S(2)}, u32[]{:S(2)}) collective-permute-start(bf16[288,512]{1,0:T(8,128)(2,1)S(1)} %slice.20), channel_id=1, source_target_pairs={{0,16},{4,20},{8,24},{12,28},{16,0},{20,4},{24,8},{28,12},{1,17},{... | collective-permute-start | bytes 884744 | tf_op jit(solution)/shard_map/ppermute | solution.py:1065
  41.1 24.8 %collective-permute-start.8 = (bf16[576,512]{1,0:T(8,128)(2,1)S(1)}, bf16[576,512]{1,0:T(8,128)(2,1)}, u32[]{:S(2)}, u32[]{:S(2)}) collective-permute-start(bf16[576,512]{1,0:T(8,128)(2,1)S(1)} %copy-done.9), channel_id=1, source_target_pairs={{0,4},{4,0},{8,12},{12,8},{16,20},{20,16},{24,28},{28,24},{1,5},{5... | collective-permute-start | bytes 1769480 | tf_op jit(solution)/shard_map/ppermute | solution.py:1065
  49.9 16.1 %collective-permute-start.9 = (bf16[576,512]{1,0:T(8,128)(2,1)S(1)}, bf16[576,512]{1,0:T(8,128)(2,1)}, u32[]{:S(2)}, u32[]{:S(2)}) collective-permute-start(bf16[576,512]{1,0:T(8,128)(2,1)S(1)} %collective-permute-done.4.refs_1_), channel_id=1, source_target_pairs={{0,4},{4,0},{8,12},{12,8},{16,20},{20,16},{24,28},{28,24},{1,5},{5... | collective-permute-start | bytes 1769480 | tf_op jit(solution)/shard_map/ppermute | solution.py:1065
  89.1 126.9 %all-gather.10.cloned.1.call-start = ((), (), s32[]{:S(2)}) async-start(), calls=%async_computation.4 | async-start | bytes 2949120 | tf_op jit(solution)/shard_map/all_gather | solution.py:1187
  166.6 127.7 %reduce-scatter.5.cloned.1.call-start = ((), (), s32[]{:S(2)}) async-start(), calls=%async_computation.5 | async-start | bytes 2949120 | tf_op jit(solution)/shard_map/reduce_scatter | solution.py:1196
  216.0 28.4 %collective-permute-start.16 = (bf16[512,256]{1,0:T(8,128)(2,1)}, bf16[512,256]{1,0:T(8,128)(2,1)}, u32[]{:S(2)}, u32[]{:S(2)}) collective-permute-start(bf16[512,256]{1,0:T(8,128)(2,1)} %get-tuple-element.188), channel_id=1, source_target_pairs={{0,1},{1,2},{2,3},{3,0},{4,5},{5,6},{6,7},{7,4},{8,9},{9,10},{10,1... | collective-permute-start | bytes 786440 | tf_op jit(solution)/shard_map/ppermute | solution.py:1076
  218.4 26.0 %collective-permute-start.17 = (bf16[512,256]{1,0:T(8,128)(2,1)}, bf16[512,256]{1,0:T(8,128)(2,1)}, u32[]{:S(2)}, u32[]{:S(2)}) collective-permute-start(bf16[512,256]{1,0:T(8,128)(2,1)} %get-tuple-element.189), channel_id=1, source_target_pairs={{0,2},{1,3},{2,0},{3,1},{4,6},{5,7},{6,4},{7,5},{8,10},{9,11},{10,... | collective-permute-start | bytes 786440 | tf_op jit(solution)/shard_map/ppermute | solution.py:1076
  218.5 25.9 %collective-permute-start.18 = (bf16[512,256]{1,0:T(8,128)(2,1)S(1)}, bf16[512,256]{1,0:T(8,128)(2,1)}, u32[]{:S(2)}, u32[]{:S(2)}) collective-permute-start(bf16[512,256]{1,0:T(8,128)(2,1)S(1)} %get-tuple-element.190), channel_id=1, source_target_pairs={{0,3},{1,0},{2,1},{3,2},{4,7},{5,4},{6,5},{7,6},{8,11},{9,8},{10,9... | collective-permute-start | bytes 786440 | tf_op jit(solution)/shard_map/ppermute | solution.py:1076
  245.8 122.7 %all-gather.12.cloned.1.call-start = ((), (), s32[]{:S(2)}) async-start(), calls=%async_computation.6 | async-start | bytes 2949120 | tf_op jit(solution)/shard_map/all_gather | solution.py:1210
  280.4 48.5 %collective-permute-start.22 = (bf16[256,4224]{1,0:T(8,128)(2,1)}, bf16[256,4224]{1,0:T(8,128)(2,1)S(1)}, u32[]{:S(2)}, u32[]{:S(2)}) collective-permute-start(bf16[256,4224]{1,0:T(8,128)(2,1)} %get-tuple-element.195), channel_id=1, source_target_pairs={{0,8},{4,12},{8,0},{12,4},{16,24},{20,28},{24,16},{28,20},{1,9},{5... | collective-permute-start | bytes 6488072 | tf_op jit(solution)/shard_map/ppermute | solution.py:1065
  281.6 48.2 %collective-permute-start.23 = (bf16[256,4224]{1,0:T(8,128)(2,1)}, bf16[256,4224]{1,0:T(8,128)(2,1)}, u32[]{:S(2)}, u32[]{:S(2)}) collective-permute-start(bf16[256,4224]{1,0:T(8,128)(2,1)} %get-tuple-element.205), channel_id=1, source_target_pairs={{0,16},{4,20},{8,24},{12,28},{16,0},{20,4},{24,8},{28,12},{1,17},{... | collective-permute-start | bytes 6488072 | tf_op jit(solution)/shard_map/ppermute | solution.py:1065
  297.9 271.3 %all-gather.14.cloned.1.call-start = ((), (), s32[]{:S(2)}) async-start(), calls=%async_computation.7 | async-start | bytes 19464192 | tf_op jit(solution)/shard_map/all_gather | solution.py:1219
  337.0 24.4 %collective-permute-start.24 = (bf16[128,4224]{1,0:T(8,128)(2,1)}, bf16[128,4224]{1,0:T(8,128)(2,1)S(1)}, u32[]{:S(2)}, u32[]{:S(2)}) collective-permute-start(bf16[128,4224]{1,0:T(8,128)(2,1)} %get-tuple-element.206), channel_id=1, source_target_pairs={{0,16},{4,20},{8,24},{12,28},{16,0},{20,4},{24,8},{28,12},{1,17},{... | collective-permute-start | bytes 3244040 | tf_op jit(solution)/shard_map/ppermute | solution.py:1065
  338.2 24.1 %collective-permute-start.25 = (bf16[128,4224]{1,0:T(8,128)(2,1)}, bf16[128,4224]{1,0:T(8,128)(2,1)S(1)}, u32[]{:S(2)}, u32[]{:S(2)}) collective-permute-start(bf16[128,4224]{1,0:T(8,128)(2,1)} %get-tuple-element.210), channel_id=1, source_target_pairs={{0,8},{4,12},{8,0},{12,4},{16,24},{20,28},{24,16},{28,20},{1,9},{5... | collective-permute-start | bytes 3244040 | tf_op jit(solution)/shard_map/ppermute | solution.py:1065
  368.4 294.1 %all-gather.16.cloned.1.call-start = ((), (), s32[]{:S(2)}) async-start(), calls=%async_computation.8 | async-start | bytes 7077888 | tf_op jit(solution)/shard_map/all_gather | solution.py:1253
  368.5 57.8 %collective-permute-start.29 = (bf16[576,2048]{1,0:T(8,128)(2,1)}, bf16[576,2048]{1,0:T(8,128)(2,1)S(1)}, u32[]{:S(2)}, u32[]{:S(2)}) collective-permute-start(bf16[576,2048]{1,0:T(8,128)(2,1)} %all-gather.12.cloned.1.call-done.left_ref.refs_2_.branch_ref), channel_id=1, source_target_pairs={{0,4},{4,0},{8,12},{12,8},{16,20},{20,16},{24,28},{28,24},{1,5},{5... | collective-permute-start | bytes 7077896 | tf_op jit(solution)/shard_map/ppermute | solution.py:1065
  370.9 32.8 %collective-permute-start.26 = (bf16[144,2048]{1,0:T(8,128)(2,1)}, bf16[144,2048]{1,0:T(8,128)(2,1)S(1)}, u32[]{:S(2)}, u32[]{:S(2)}) collective-permute-start(bf16[144,2048]{1,0:T(8,128)(2,1)} %get-tuple-element.224), channel_id=1, source_target_pairs={{0,1},{1,2},{2,3},{3,0},{4,5},{5,6},{6,7},{7,4},{8,9},{9,10},{10,1... | collective-permute-start | bytes 1769480 | tf_op jit(solution)/shard_map/ppermute | solution.py:1076
  374.3 52.1 %collective-permute-start.27 = (bf16[144,2048]{1,0:T(8,128)(2,1)}, bf16[144,2048]{1,0:T(8,128)(2,1)S(1)}, u32[]{:S(2)}, u32[]{:S(2)}) collective-permute-start(bf16[144,2048]{1,0:T(8,128)(2,1)} %get-tuple-element.225), channel_id=1, source_target_pairs={{0,2},{1,3},{2,0},{3,1},{4,6},{5,7},{6,4},{7,5},{8,10},{9,11},{10,... | collective-permute-start | bytes 1769480 | tf_op jit(solution)/shard_map/ppermute | solution.py:1076
  374.8 51.6 %collective-permute-start.28 = (bf16[144,2048]{1,0:T(8,128)(2,1)}, bf16[144,2048]{1,0:T(8,128)(2,1)}, u32[]{:S(2)}, u32[]{:S(2)}) collective-permute-start(bf16[144,2048]{1,0:T(8,128)(2,1)} %get-tuple-element.226), channel_id=1, source_target_pairs={{0,3},{1,0},{2,1},{3,2},{4,7},{5,4},{6,5},{7,6},{8,11},{9,8},{10,9... | collective-permute-start | bytes 1769480 | tf_op jit(solution)/shard_map/ppermute | solution.py:1076
  427.3 15.6 %collective-permute-start.31 = (bf16[576,1024]{1,0:T(8,128)(2,1)}, bf16[576,1024]{1,0:T(8,128)(2,1)S(1)}, u32[]{:S(2)}, u32[]{:S(2)}) collective-permute-start(bf16[576,1024]{1,0:T(8,128)(2,1)} %get-tuple-element.227.grad_ref.refs_6_), channel_id=1, source_target_pairs={{0,4},{4,0},{8,12},{12,8},{16,20},{20,16},{24,28},{28,24},{1,5},{5... | collective-permute-start | bytes 3538952 | tf_op jit(solution)/shard_map/ppermute | solution.py:1065
  432.0 23.1 %collective-permute-start.34 = (bf16[144,1024]{1,0:T(8,128)(2,1)}, bf16[144,1024]{1,0:T(8,128)(2,1)S(1)}, u32[]{:S(2)}, u32[]{:S(2)}) collective-permute-start(bf16[144,1024]{1,0:T(8,128)(2,1)} %get-tuple-element.240), channel_id=1, source_target_pairs={{0,1},{1,2},{2,3},{3,0},{4,5},{5,6},{6,7},{7,4},{8,9},{9,10},{10,1... | collective-permute-start | bytes 884744 | tf_op jit(solution)/shard_map/ppermute | solution.py:1076
  432.0 23.1 %collective-permute-start.35 = (bf16[144,1024]{1,0:T(8,128)(2,1)}, bf16[144,1024]{1,0:T(8,128)(2,1)S(1)}, u32[]{:S(2)}, u32[]{:S(2)}) collective-permute-start(bf16[144,1024]{1,0:T(8,128)(2,1)} %get-tuple-element.241), channel_id=1, source_target_pairs={{0,2},{1,3},{2,0},{3,1},{4,6},{5,7},{6,4},{7,5},{8,10},{9,11},{10,... | collective-permute-start | bytes 884744 | tf_op jit(solution)/shard_map/ppermute | solution.py:1076
  439.5 27.8 %collective-permute-start.32 = (bf16[2,288,512]{2,1,0:T(8,128)(2,1)}, bf16[2,288,512]{2,1,0:T(8,128)(2,1)S(1)}, u32[]{:S(2)}, u32[]{:S(2)}) collective-permute-start(bf16[2,288,512]{2,1,0:T(8,128)(2,1)} %get-tuple-element.233), channel_id=1, source_target_pairs={{0,8},{4,12},{8,0},{12,4},{16,24},{20,28},{24,16},{28,20},{1,9},{5... | collective-permute-start | bytes 1769480 | tf_op jit(solution)/shard_map/ppermute | solution.py:1065
  440.8 28.5 %collective-permute-start.33 = (bf16[2,288,512]{2,1,0:T(8,128)(2,1)}, bf16[2,288,512]{2,1,0:T(8,128)(2,1)S(1)}, u32[]{:S(2)}, u32[]{:S(2)}) collective-permute-start(bf16[2,288,512]{2,1,0:T(8,128)(2,1)} %get-tuple-element.239), channel_id=1, source_target_pairs={{0,16},{4,20},{8,24},{12,28},{16,0},{20,4},{24,8},{28,12},{1,17},{... | collective-permute-start | bytes 1769480 | tf_op jit(solution)/shard_map/ppermute | solution.py:1065
  454.8 47.2 %collective-permute-start.39 = (bf16[128,3072]{1,0:T(8,128)(2,1)}, bf16[128,3072]{1,0:T(8,128)(2,1)S(1)}, u32[]{:S(2)}, u32[]{:S(2)}) collective-permute-start(bf16[128,3072]{1,0:T(8,128)(2,1)} %get-tuple-element.235), channel_id=1, source_target_pairs={{0,8},{4,12},{8,0},{12,4},{16,24},{20,28},{24,16},{28,20},{1,9},{5... | collective-permute-start | bytes 2359304 | tf_op jit(solution)/shard_map/ppermute | solution.py:1065
  455.1 47.0 %collective-permute-start.40 = (bf16[128,3072]{1,0:T(8,128)(2,1)}, bf16[128,3072]{1,0:T(8,128)(2,1)S(1)}, u32[]{:S(2)}, u32[]{:S(2)}) collective-permute-start(bf16[128,3072]{1,0:T(8,128)(2,1)} %get-tuple-element.260), channel_id=1, source_target_pairs={{0,16},{4,20},{8,24},{12,28},{16,0},{20,4},{24,8},{28,12},{1,17},{... | collective-permute-start | bytes 2359304 | tf_op jit(solution)/shard_map/ppermute | solution.py:1065
  473.6 23.3 %collective-permute-start.37 = (bf16[288,512]{1,0:T(8,128)(2,1)}, bf16[288,512]{1,0:T(8,128)(2,1)S(1)}, u32[]{:S(2)}, u32[]{:S(2)}) collective-permute-start(bf16[288,512]{1,0:T(8,128)(2,1)} %get-tuple-element.247), channel_id=1, source_target_pairs={{0,16},{4,20},{8,24},{12,28},{16,0},{20,4},{24,8},{28,12},{1,17},{... | collective-permute-start | bytes 884744 | tf_op jit(solution)/shard_map/ppermute | solution.py:1065
  475.2 21.7 %collective-permute-start.38 = (bf16[288,512]{1,0:T(8,128)(2,1)}, bf16[288,512]{1,0:T(8,128)(2,1)S(1)}, u32[]{:S(2)}, u32[]{:S(2)}) collective-permute-start(bf16[288,512]{1,0:T(8,128)(2,1)} %get-tuple-element.255), channel_id=1, source_target_pairs={{0,8},{4,12},{8,0},{12,4},{16,24},{20,28},{24,16},{28,20},{1,9},{5... | collective-permute-start | bytes 884744 | tf_op jit(solution)/shard_map/ppermute | solution.py:1065
  500.1 13.4 %collective-permute-start.42 = (bf16[144,512]{1,0:T(8,128)(2,1)}, bf16[144,512]{1,0:T(8,128)(2,1)S(1)}, u32[]{:S(2)}, u32[]{:S(2)}) collective-permute-start(bf16[144,512]{1,0:T(8,128)(2,1)} %get-tuple-element.264), channel_id=1, source_target_pairs={{0,2},{1,3},{2,0},{3,1},{4,6},{5,7},{6,4},{7,5},{8,10},{9,11},{10,... | collective-permute-start | bytes 442376 | tf_op jit(solution)/shard_map/ppermute | solution.py:1076
  507.1 31.9 %collective-permute-start.44 = (bf16[64,3072]{1,0:T(8,128)(2,1)}, bf16[64,3072]{1,0:T(8,128)(2,1)S(1)}, u32[]{:S(2)}, u32[]{:S(2)}) collective-permute-start(bf16[64,3072]{1,0:T(8,128)(2,1)} %get-tuple-element.261), channel_id=1, source_target_pairs={{0,16},{4,20},{8,24},{12,28},{16,0},{20,4},{24,8},{28,12},{1,17},{... | collective-permute-start | bytes 1179656 | tf_op jit(solution)/shard_map/ppermute | solution.py:1065
  508.4 30.7 %collective-permute-start.45 = (bf16[64,3072]{1,0:T(8,128)(2,1)}, bf16[64,3072]{1,0:T(8,128)(2,1)S(1)}, u32[]{:S(2)}, u32[]{:S(2)}) collective-permute-start(bf16[64,3072]{1,0:T(8,128)(2,1)} %get-tuple-element.269), channel_id=1, source_target_pairs={{0,8},{4,12},{8,0},{12,4},{16,24},{20,28},{24,16},{28,20},{1,9},{5... | collective-permute-start | bytes 1179656 | tf_op jit(solution)/shard_map/ppermute | solution.py:1065
  508.7 21.3 %collective-permute-start.46 = (bf16[144,1024]{1,0:T(8,128)(2,1)S(1)}, bf16[144,1024]{1,0:T(8,128)(2,1)S(1)}, u32[]{:S(2)}, u32[]{:S(2)}) collective-permute-start(bf16[144,1024]{1,0:T(8,128)(2,1)S(1)} %copy-done.33), channel_id=1, source_target_pairs={{0,1},{1,2},{2,3},{3,0},{4,5},{5,6},{6,7},{7,4},{8,9},{9,10},{10,1... | collective-permute-start | bytes 884744 | tf_op jit(solution)/shard_map/ppermute | solution.py:1076
  513.5 25.6 %collective-permute-start.47 = (bf16[144,1024]{1,0:T(8,128)(2,1)S(1)}, bf16[144,1024]{1,0:T(8,128)(2,1)S(1)}, u32[]{:S(2)}, u32[]{:S(2)}) collective-permute-start(bf16[144,1024]{1,0:T(8,128)(2,1)S(1)} %copy-done.33), channel_id=1, source_target_pairs={{0,2},{1,3},{2,0},{3,1},{4,6},{5,7},{6,4},{7,5},{8,10},{9,11},{10,... | collective-permute-start | bytes 884744 | tf_op jit(solution)/shard_map/ppermute | solution.py:1076
  513.5 25.6 %collective-permute-start.48 = (bf16[144,1024]{1,0:T(8,128)(2,1)S(1)}, bf16[144,1024]{1,0:T(8,128)(2,1)S(1)}, u32[]{:S(2)}, u32[]{:S(2)}) collective-permute-start(bf16[144,1024]{1,0:T(8,128)(2,1)S(1)} %copy-done.33), channel_id=1, source_target_pairs={{0,3},{1,0},{2,1},{3,2},{4,7},{5,4},{6,5},{7,6},{8,11},{9,8},{10,9... | collective-permute-start | bytes 884744 | tf_op jit(solution)/shard_map/ppermute | solution.py:1076
  556.2 13.1 %collective-permute-start.53 = (bf16[144,512]{1,0:T(8,128)(2,1)S(1)}, bf16[144,512]{1,0:T(8,128)(2,1)S(1)}, u32[]{:S(2)}, u32[]{:S(2)}) collective-permute-start(bf16[144,512]{1,0:T(8,128)(2,1)S(1)} %copy-done.30), channel_id=1, source_target_pairs={{0,2},{1,3},{2,0},{3,1},{4,6},{5,7},{6,4},{7,5},{8,10},{9,11},{10,... | collective-permute-start | bytes 442376 | tf_op jit(solution)/shard_map/ppermute | solution.py:1076
  625.8 16.9 %collective-permute-start.66 = (f32[3072]{0:T(1024)S(1)}, f32[3072]{0:T(1024)S(1)}, u32[]{:S(2)}, u32[]{:S(2)}) collective-permute-start(f32[3072]{0:T(1024)S(1)} %pad_maximum_fusion.1), channel_id=1, source_target_pairs={{0,1},{1,0},{2,3},{3,2},{4,5},{5,4},{6,7},{7,6},{8,9},{9,8},{10,11... | collective-permute-start | bytes 36872 | tf_op jit(solution)/shard_map/ppermute | solution.py:1087
  639.4 19.0 %collective-permute-start.65 = (bf16[4,384,256]{2,1,0:T(8,128)(2,1)}, bf16[4,384,256]{2,1,0:T(8,128)(2,1)S(1)}, u32[]{:S(2)}, u32[]{:S(2)}) collective-permute-start(bf16[4,384,256]{2,1,0:T(8,128)(2,1)} %stack_chips.1.own_ref), channel_id=1, source_target_pairs={{0,4},{4,0},{8,12},{12,8},{16,20},{20,16},{24,28},{28,24},{1,5},{5... | collective-permute-start | bytes 2359304 | tf_op jit(solution)/shard_map/ppermute | solution.py:1065
  653.3 21.9 %collective-permute-start.71 = (bf16[144,2048]{1,0:T(8,128)(2,1)S(1)}, bf16[144,2048]{1,0:T(8,128)(2,1)S(1)}, u32[]{:S(2)}, u32[]{:S(2)}) collective-permute-start(bf16[144,2048]{1,0:T(8,128)(2,1)S(1)} %copy-done.8), channel_id=1, source_target_pairs={{0,1},{1,2},{2,3},{3,0},{4,5},{5,6},{6,7},{7,4},{8,9},{9,10},{10,1... | collective-permute-start | bytes 1769480 | tf_op jit(solution)/shard_map/ppermute | solution.py:1076
  654.9 49.7 %collective-permute-start.72 = (bf16[144,2048]{1,0:T(8,128)(2,1)S(1)}, bf16[144,2048]{1,0:T(8,128)(2,1)S(1)}, u32[]{:S(2)}, u32[]{:S(2)}) collective-permute-start(bf16[144,2048]{1,0:T(8,128)(2,1)S(1)} %copy-done.8), channel_id=1, source_target_pairs={{0,2},{1,3},{2,0},{3,1},{4,6},{5,7},{6,4},{7,5},{8,10},{9,11},{10,... | collective-permute-start | bytes 1769480 | tf_op jit(solution)/shard_map/ppermute | solution.py:1076
  655.8 48.8 %collective-permute-start.73 = (bf16[144,2048]{1,0:T(8,128)(2,1)S(1)}, bf16[144,2048]{1,0:T(8,128)(2,1)S(1)}, u32[]{:S(2)}, u32[]{:S(2)}) collective-permute-start(bf16[144,2048]{1,0:T(8,128)(2,1)S(1)} %copy-done.8), channel_id=1, source_target_pairs={{0,3},{1,0},{2,1},{3,2},{4,7},{5,4},{6,5},{7,6},{8,11},{9,8},{10,9... | collective-permute-start | bytes 1769480 | tf_op jit(solution)/shard_map/ppermute | solution.py:1076
  (99 other events, 1093.7 us)
Sparse Core Ops, SparseCore 0:
  19.8 36.1 all-gather.7
  89.2 74.0 reduce-scatter.2
  166.7 49.2 all-gather.9
  245.9 48.3 reduce-scatter.4
  298.1 49.2 all-gather.11
  368.5 113.6 all-gather.13
  555.9 46.3 all-gather.15

commit v3 on v2

--- a/solution.py
+++ b/solution.py
@@ -356,8 +356,12 @@
     return outs
 
 
-def in_order(info):
-    return info if Order.last is None else after(info, Order.last)
+def in_order(value):
+    return value if Order.last is None else after(value, Order.last)
+
+
+def wait(*values):
+    Order.last = (Order.last, values)
 
 
 def placed_call(kernel, out_shape, args, params, scratch, grid, in_specs, out_specs, prefetch):
@@ -530,38 +534,42 @@
     )
 
 
-def latent_back_kernel(info_ref, latent_ref, recip_ref, gain_ref, *refs):
-    parts, (grad_ref, gain_grad_ref) = refs[:-2], refs[-2:]
+def latent_back_kernel(info_ref, latent_ref, recip_ref, gain_ref, norm2_ref, *refs):
+    parts, grad_ref = refs[:-1], refs[-1]
     grad_in = sum(part[...].astype(F32) for part in parts)
     latent = latent_ref[...].astype(F32)
     recip = recip_ref[:, 0:1]
     gained = grad_in * gain_ref[...]
     stat = jnp.sum(latent * gained, -1, keepdims=True)
     grad = recip * gained - latent * (recip * recip * recip * stat / latent.shape[1])
-    grad_ref[...] = grad.astype(BF)
-    gain_grad_ref[...] = jnp.sum(grad_in * latent * recip, 0, keepdims=True)
-
-
-def latent_back(info, latent, recip, gain, parts):
+    rows, width = grad.shape
+    grad_ref[:rows, :] = grad.astype(BF)
+    sums = [norm2_ref[:, i * width : (i + 1) * width] for i in range(norm2_ref.shape[1] // width)]
+    sums = jnp.concatenate(sums + [jnp.sum(grad_in * latent * recip, 0, keepdims=True)], 0)
+    high = sums.astype(BF)
+    low = (sums - high.astype(F32)).astype(BF)
+    fill = jnp.zeros((EXTRA - 2 * sums.shape[0], width), BF)
+    grad_ref[rows:, :] = jnp.concatenate([high, low, fill], 0)
+
+
+def latent_back(info, latent, recip, gain, norm2, parts):
     rows, width = parts[0].shape
     return call(
         latent_back_kernel,
-        [((rows, width), BF), ((1, width), F32)],
-        (latent, recip, gain, *parts),
+        [((rows + EXTRA, width), BF)],
+        (latent, recip, gain, norm2, *parts),
         "latent_back",
         grid=(1,),
         in_specs=[
             pl.BlockSpec((rows, width), lambda i, w: (w[RANK], 0)),
             pl.BlockSpec((rows, LANES), lambda i, w: (w[RANK], 0)),
             pl.BlockSpec((1, width), lambda i, w: (0, 0)),
+            pl.BlockSpec(norm2.shape, lambda i, w: (0, 0)),
         ]
         + [pl.BlockSpec((rows, width), lambda i, w: (0, 0)) for _ in parts],
-        out_specs=[
-            pl.BlockSpec((rows, width), lambda i, w: (0, 0)),
-            pl.BlockSpec((1, width), lambda i, w: (0, 0)),
-        ],
-        prefetch=info,
-    )
+        out_specs=[pl.BlockSpec((rows + EXTRA, width), lambda i, w: (0, 0))],
+        prefetch=info,
+    )[0]
 
 
 def kv_back_kernel(info_ref, cos_ref, sin_ref, *refs):
@@ -831,39 +839,35 @@
     )
 
 
-def fold_heads_kernel(info_ref, keep_first, got_first, keep_last, got_last, out_ref, *refs):
+def fold_up_kernel(info_ref, keep_first, got_first, keep_last, got_last, *refs):
     ups, all_ref = refs[:-1], refs[-1]
-    width = out_ref.shape[2]
     all_ref[0] = add_low(keep_first[...], got_first[...])
     all_ref[1] = add_low(keep_last[...], got_last[...])
-    out_ref[...] = all_ref[:, :, :width]
     for s, up_ref in enumerate(ups):
-        up_ref[...] = all_ref[:, at_block(ahead(info_ref, s, len(ups)), up_ref.shape[1]), width:]
-
-
-def fold_heads(info, arrays, width, ranks):
+        up_ref[...] = all_ref[:, at_block(ahead(info_ref, s, len(ups)), up_ref.shape[1]), :]
+
+
+def fold_up(info, arrays, ranks):
     rows, cols = arrays[0].shape
     return call(
-        fold_heads_kernel,
-        [((2, rows, width), BF)] + [((2, rows // ranks, cols - width), BF)] * ranks,
+        fold_up_kernel,
+        [((2, rows // ranks, cols), BF)] * ranks,
         arrays,
-        "fold_heads",
+        "fold_up",
         scratch=[pltpu.VMEM((2, rows, cols), BF)],
         prefetch=info,
     )
 
 
-def pack_heads_kernel(info_ref, out_ref, *refs):
+def pack_up_kernel(info_ref, *refs):
     ups, all_ref = refs[:-1], refs[-1]
-    width = out_ref.shape[2]
-    all_ref[:, :, :width] = out_ref[...]
     for s, up_ref in enumerate(ups):
-        all_ref[:, at_block(behind(info_ref, s, len(ups)), up_ref.shape[1]), width:] = up_ref[...]
-
-
-def pack_heads(info, out, ups):
-    shape = out.shape[:2] + (out.shape[2] + ups[0].shape[2],)
-    return call(pack_heads_kernel, [(shape, BF)], (out, *ups), "pack_heads", prefetch=info)[0]
+        all_ref[:, at_block(behind(info_ref, s, len(ups)), up_ref.shape[1]), :] = up_ref[...]
+
+
+def pack_up(info, ups):
+    _, rows, cols = ups[0].shape
+    return call(pack_up_kernel, [((2, rows * len(ups), cols), BF)], ups, "pack_up", prefetch=info)[0]
 
 
 def layer_kernel(info_ref, residual_ref, *refs):
@@ -896,12 +900,14 @@
     ranks, info_ref, tokens_ref, branch_ref, gain_ref, kv_weight_ref, recip_ref, latent_ref, kv_pre_ref, *refs
 ):
     latents, kvs, downs = refs[:ranks], refs[ranks : 2 * ranks], refs[2 * ranks : 3 * ranks]
-    grad_in_ref, norm_ref, own_ref, kv_ref, all_ref = refs[3 * ranks :]
-    rows = latents[0].shape[0]
+    grad_in_ref, small_ref, own_ref, kv_ref, all_ref, sums_ref = refs[3 * ranks :]
+    rows = kvs[0].shape[0]
     cols = own_ref.shape[1]
+    sums = 0.0
     for s in range(ranks):
         at = at_block(behind(info_ref, s, ranks), rows)
-        all_ref[at, :] = latents[s][...]
+        all_ref[at, :] = latents[s][:rows, :]
+        sums = sums + latents[s][rows:, :].astype(F32)
         kv_ref[at, :] = kvs[s][...]
     grad = dense_nt(kv_ref[...], kv_weight_ref[...])
     for s in range(ranks):
@@ -916,7 +922,15 @@
     model = tokens.shape[1] * ranks
     out = branch_ref[...].astype(F32) + recip * gain_ref[...] * grad
     grad_in_ref[...] = out - tokens * (recip * recip * stat / model)
-    norm_ref[...] = jnp.sum(grad * tokens * recip, 0, keepdims=True)
+    count = sums.shape[0] // 16 * 3
+    sums = sums[:count] + sums[count : 2 * count]
+    sums_ref[...] = sums[count - 1 :]
+    norm1 = jnp.sum(grad * tokens * recip, 0, keepdims=True)
+    lines = [sums[r : r + 1, i * cols : (i + 1) * cols] for r in range(count - 1) for i in range(sums.shape[1] // cols)]
+    lines += [norm1[:, i * cols : (i + 1) * cols] for i in range(norm1.shape[1] // cols)]
+    lines.append(sums_ref[:, at_block(info_ref[RANK], cols)])
+    lines += [jnp.zeros_like(lines[0])] * (small_ref.shape[0] - len(lines))
+    small_ref[...] = jnp.concatenate(lines, 0).astype(BF)
 
 
 def input_back(info, tokens, branch, gain, kv_weight, recip, latent, kv_pre, latents, kvs, downs):
@@ -926,13 +940,13 @@
     width, down = kv_weight.shape[1], downs[0].shape[1]
     whole = lambda array: pl.BlockSpec(array.shape, lambda i, w: (0, 0))
     wide = pl.BlockSpec((rows, cols), lambda i, w: (0, w[RANK]))
-    outs = [((rows, cols), F32), ((1, cols), F32), ((rows, down), BF), ((rows, width), BF)]
+    outs = [((rows, cols), F32), ((16, down), BF), ((rows, down), BF), ((rows, width), BF)]
     return call(
         functools.partial(input_back_kernel, ranks),
         outs,
         (tokens, branch, gain.reshape(1, -1), kv_weight, recip, latent, kv_pre, *latents, *kvs, *downs),
         "input_back",
-        scratch=[pltpu.VMEM((rows, latent.shape[1]), BF)],
+        scratch=[pltpu.VMEM((rows, latent.shape[1]), BF), pltpu.VMEM((1, latent.shape[1]), F32)],
         grid=(1,),
         in_specs=[
             wide,
@@ -946,111 +960,91 @@
     )
 
 
-def last_products_kernel(info_ref, normed_ref, latent_ref, kv_ref, near_ref, far_ref, down_ref, wide_ref):
-    down_ref[...] = dense_tn(normed_ref[...], latent_ref[...]).astype(BF)
-    cols = wide_ref.shape[0]
-    wide_ref[...] = dense_tn(normed_ref[:, at_block(info_ref[RANK], cols)], kv_ref[...]).astype(BF)
-    chips, width = near_ref.shape[0], near_ref.shape[2]
-    for out_ref, core in ((near_ref, info_ref[CORE]), (far_ref, 1 - info_ref[CORE])):
-        for chip in range(chips):
-            rows = down_ref.shape[0] // (2 * chips)
-            out_ref[chip, :rows, :] = down_ref[at_block(core * chips + chip, rows), :]
-            more = wide_ref.shape[0] // (2 * chips)
-            part = wide_ref[at_block(core * chips + chip, more), :]
-            out_ref[chip, rows : rows + more, :] = part[:, :width]
-            out_ref[chip, rows + more :, :] = part[:, width:]
-
-
-def last_products(info, normed, latent, kv, ranks):
-    model, down, width = normed.shape[1], latent.shape[1], kv.shape[1]
-    cols = model // ranks
-    rows = (model + cols * width // down) // 8
+def last_products_kernel(info_ref, normed_ref, latent_ref, kv_ref, small_ref, out_ref):
+    rows, width = normed_ref.shape[1], latent_ref.shape[1]
+    out_ref[:rows, :] = dense_tn(normed_ref[...], latent_ref[...]).astype(BF)
+    count = (out_ref.shape[0] - rows - small_ref.shape[0]) // 2
+    wide = dense_tn(normed_ref[:, at_block(info_ref[RANK], count)], kv_ref[...]).astype(BF)
+    out_ref[rows : rows + count, :] = wide[:, :width]
+    out_ref[rows + count : rows + 2 * count, :] = wide[:, width:]
+    out_ref[rows + 2 * count :, :] = small_ref[...]
+
+
+def last_products(info, normed, latent, kv, small, ranks):
+    model, width = normed.shape[1], latent.shape[1]
+    shape = (model + 2 * model // ranks + small.shape[0], width)
     return call(
-        last_products_kernel,
-        [((4, rows, down), BF)] * 2,
-        (normed, latent, kv),
-        "last_products",
-        scratch=[pltpu.VMEM((model, down), BF), pltpu.VMEM((cols, width), BF)],
-        prefetch=info,
-    )
-
-
-def fold_direct_kernel(info_ref, near_ref, got_ref, *outs):
-    for mask, out_ref in enumerate(outs):
-        chip = lax.bitwise_xor(chip_of(info_ref), mask)
-        out_ref[...] = add_low(near_ref[chip], got_ref[chip])
-
-
-def fold_direct(info, near, got):
-    return call(fold_direct_kernel, [(near.shape[1:], BF)] * 4, (near, got), "fold_direct", prefetch=info)
-
-
-def sum_kernel(info_ref, *refs):
-    refs[-1][...] = sum(part[...].astype(F32) for part in refs[:-1]).astype(BF)
-
-
-def sum_parts(info, parts):
-    return call(sum_kernel, [(parts[0].shape, BF)], parts, "sum_parts", prefetch=info)[0]
-
-
-def stack_kernel(info_ref, *refs):
-    for mask, part in enumerate(refs[:-1]):
-        refs[-1][lax.bitwise_xor(chip_of(info_ref), mask)] = part[...]
-
-
-def stack_chips(info, parts):
-    return call(stack_kernel, [((4,) + parts[0].shape, BF)], parts, "stack_chips", prefetch=info)[0]
-
-
-def last_kernel(info_ref, own_ref, other_ref, down_ref, kv_ref):
-    chips, width = own_ref.shape[0], own_ref.shape[2]
-    rows, more = down_ref.shape[0] // (2 * chips), kv_ref.shape[0] // (2 * chips)
-    for in_ref, core in ((own_ref, info_ref[CORE]), (other_ref, 1 - info_ref[CORE])):
-        for chip in range(chips):
-            part = in_ref[chip].astype(F32)
-            down_ref[at_block(core * chips + chip, rows), :] = part[:rows]
-            kv_ref[at_block(core * chips + chip, more), :width] = part[rows : rows + more]
-            kv_ref[at_block(core * chips + chip, more), width:] = part[rows + more :]
-
-
-def store_feed(part, gate_ref, up_ref, down_ref):
-    width = gate_ref.shape[1]
-    gate_ref[...] = part[:, :width].astype(F32)
-    up_ref[...] = part[:, width : 2 * width].astype(F32)
-    down_ref[...] = part[:, 2 * width :].astype(F32).T
-
-
-def store_heads(part, out_ref, up_ref):
-    width = out_ref.shape[1]
-    rows, cols = up_ref.shape[0], part.shape[1] - width
-    out_ref[...] = part[:, :width].astype(F32)
-    for r in range(part.shape[0] // rows):
-        up_ref[:, r * cols : (r + 1) * cols] = part[r * rows : (r + 1) * rows, width:].astype(F32)
+        last_products_kernel, [(shape, BF)], (normed, latent, kv, small), "last_products", prefetch=info
+    )[0]
+
+
+def last_kernel(info_ref, in_ref, down_ref, kv_ref, small_ref):
+    rows, width = down_ref.shape
+    count = kv_ref.shape[0]
+    down_ref[...] = in_ref[:rows, :].astype(F32)
+    kv_ref[:, :width] = in_ref[rows : rows + count, :].astype(F32)
+    kv_ref[:, width:] = in_ref[rows + count : rows + 2 * count, :].astype(F32)
+    small_ref[...] = in_ref[rows + 2 * count :, :].astype(F32)
+
+
+def store_feed(part, at, gate_ref, up_ref, down_ref):
+    rows, width = part.shape[0], gate_ref.shape[1]
+    block = slice(at * rows, (at + 1) * rows)
+    gate_ref[block, :] = part[:, :width].astype(F32)
+    up_ref[block, :] = part[:, width : 2 * width].astype(F32)
+    down_ref[:, block] = part[:, 2 * width :].astype(F32).T
+
+
+def store_same(part, at, out_ref):
+    rows = part.shape[0]
+    out_ref[at * rows : (at + 1) * rows, :] = part.astype(F32)
+
+
+def unpack_up_kernel(info_ref, *refs):
+    out_ref = refs[-1]
+    for mask, ref in enumerate(refs[:-1]):
+        source = lax.bitwise_xor(info_ref[SEQ], mask)
+        core, chip = lax.rem(source, 2), lax.div(source, 2)
+        _, rows, cols = ref.shape
+        rows = rows // (out_ref.shape[1] // cols)
+        for p in range(2):
+            place = lax.rem(chip, 2) * 2 + lax.div(chip, 2) if p == 0 else chip
+            at = at_block(core * 8 + p * 4 + place, rows)
+            for r in range(out_ref.shape[1] // cols):
+                block = ref[p, r * rows : (r + 1) * rows, :].astype(F32)
+                out_ref[at, r * cols : (r + 1) * cols] = block
+
+
+def unpack_up(info, pieces, shape):
+    return call(unpack_up_kernel, [(shape, F32)], pieces, "unpack_up", prefetch=info)[0]
 
 
 def unpack_kernel(store, info_ref, in_ref, *out_refs):
-    store(in_ref[...], *out_refs)
+    part = lax.rem(pl.program_id(0), 2)
+    for chip in range(4):
+        turned = chip % 2 * 2 + chip // 2
+        pl.when(part == 0)(lambda chip=chip, at=turned: store(in_ref[chip], at, *out_refs))
+        pl.when(part == 1)(lambda chip=chip: store(in_ref[chip], chip, *out_refs))
 
 
 def unpack(info, whole, store, shapes, along):
-    def where(i):
-        source, p = i // 2, i % 2
-        chip = source // 2
-        return source % 2 * 8 + p * 4 + jnp.where(p == 0, chip % 2 * 2 + chip // 2, chip)
-
+    _, _, rows, cols = whole.shape
+    whole = whole.reshape(4, 2, 2, rows, cols)
     out_specs = []
-    for (rows, cols), dim in zip(shapes, along):
+    for (height, width), dim in zip(shapes, along):
         if dim == 0:
-            out_specs.append(pl.BlockSpec((rows // 16, cols), lambda i, w: (where(i), 0)))
+            out_specs.append(pl.BlockSpec((height // 4, width), lambda i, w: (i, 0)))
         else:
-            out_specs.append(pl.BlockSpec((rows, cols // 16), lambda i, w: (0, where(i))))
+            out_specs.append(pl.BlockSpec((height, width // 4), lambda i, w: (0, i)))
     return call(
         functools.partial(unpack_kernel, store),
         [(shape, F32) for shape in shapes],
         (whole,),
         "unpack",
-        grid=(16,),
-        in_specs=[pl.BlockSpec((None, None) + whole.shape[2:], lambda i, w: (i // 2, i % 2, 0, 0))],
+        grid=(4,),
+        in_specs=[
+            pl.BlockSpec((4, None, None, rows, cols), lambda i, w: (0, i // 2, i % 2, 0, 0))
+        ],
         out_specs=out_specs,
         prefetch=info,
     )
@@ -1078,6 +1072,10 @@
 
 def rings(values):
     return [ring(value, s) for s, value in enumerate(values)]
+
+
+def both(first, last):
+    return swap(first, 1), swap(last, 2)
 
 
 def sum_over(value, axis):
@@ -1153,7 +1151,7 @@
 
     kv_local = turn(place_info, kv_pre, cosine, sine)
     half_rows = row_count // 2
-    by_x, by_y = swap(kv_local, 1), swap(kv_local, 2)
+    by_x, by_y = lax.optimization_barrier(both(kv_local, kv_local))
     top, bottom = swap(by_x[:half_rows], 2), swap(by_y[half_rows:], 1)
     pieces = [(kv_local, 0, 0), (by_x, 2, 0), (by_y, 4, 0), (top, 6, 0), (bottom, 6, half_rows)]
     pieces += [(swap(array, 0), mask ^ 1, offset) for array, mask, offset in pieces]
@@ -1210,81 +1208,84 @@
     grad_branch = lax.all_gather(branch_own, "rank", axis=0, tiled=True)
 
     two = lambda array: array.reshape((2, -1) + array.shape[1:])
-    arrays = (keep_first, swap(send_first, 1), keep_last, swap(send_last, 2))
-    arrays = fold_first(info, [two(array) for array in arrays], 4, 10000)
-    arrays = (arrays[2], swap(arrays[0], 2), arrays[3], swap(arrays[1], 1))
-    feed_piece = fold_last(info, arrays, 4)
+    first, last = both(send_first, send_last)
+    arrays = [two(array) for array in (keep_first, first, keep_last, last)]
+    arrays = fold_first(info, arrays, 4, 10000)
+    last, first = both(arrays[1], arrays[0])
+    grad_branch = after(grad_branch, arrays[0])
+    grad_attn = matmul(info, grad_branch, out_weight, True)
     branch_pair = swap(grad_branch, 0)
-    grad_attn = matmul(info, grad_branch, out_weight, True)
+    outs = pair_products(info, [(attn_low, attn_pair, grad_branch, branch_pair)], up_cols)
+    feed_piece = fold_last(info, (arrays[2], first, arrays[3], last), 4)
     feed_whole = lax.all_gather(feed_piece, "seq", axis=0, tiled=False)
     feed_sums = rings(after(feed_parts, grad_branch))
+    first, last = both(outs[0], outs[1])
     grad_query, near, far = attend_back(
         in_order(info), query, grad_attn, attn_vals, log_total, cosine, sine, kv_all,
         start_rows, index_rows, True,
     )
-    grad_query, near, far = after((grad_query, near, far), feed_sums, branch_pair)
+    grad_query, near, far = after((grad_query, near, far), feed_sums, first, last)
     Order.last = grad_query
 
     latent_grads = rings(latent_parts(info, grad_query, up_own, up_other, ranks))
     query_pair = swap(grad_query, 0)
     arrays = fold_near(info, near, swap(far, 0))
-    heads = pair_products(
-        info,
-        [
-            (attn_low, attn_pair, grad_branch, branch_pair),
-            (latent_cut, latent_pair, grad_query, query_pair),
-        ],
-        up_cols,
-    )
-    arrays = (arrays[2], swap(arrays[0], 1), arrays[3], swap(arrays[1], 2))
-    arrays = fold_first(info, after(arrays, latent_grads), 1)
-    arrays = (arrays[2], swap(arrays[0], 2), arrays[3], swap(arrays[1], 1))
-    latent_own, gain_part = latent_back(info, latent_all, recip_c, gain_all, latent_grads)
+    kv_first, kv_last = both(arrays[0], arrays[1])
+    outs = [two(array) for array in (outs[2], first, outs[3], last)]
+    outs = fold_first(info, outs, 1)
+    ups = pair_products(info, [(latent_cut, latent_pair, grad_query, query_pair)], up_cols)
+    wait(latent_grads, kv_first, kv_last)
+
+    latent_own = latent_back(info, latent_all, recip_c, gain_all, norm2_part, latent_grads)
     latent_blocks = rings([latent_own] * ranks)
-    kv_sums = rings(fold_kv(info, arrays, ranks))
-    arrays = (heads[2], swap(heads[0], 1), heads[3], swap(heads[1], 2))
-    arrays = fold_first(info, [two(array) for array in arrays], 1)
-    kv_own = kv_back(info, cosine, sine, kv_sums)
-    kv_blocks = rings([kv_own] * ranks)
-    arrays = (arrays[2], swap(arrays[0], 2), arrays[3], swap(arrays[1], 1))
-    arrays = after(arrays, latent_blocks)
-    out_piece, *up_pieces = fold_heads(info, arrays, model_width, ranks)
-    heads_piece = pack_heads(info, out_piece, rings(up_pieces))
-    heads_whole = lax.all_gather(heads_piece, "seq", axis=0, tiled=False)
+    arrays = fold_first(info, (arrays[2], kv_first, arrays[3], kv_last), 1)
+    kv_last, kv_first = both(arrays[1], arrays[0])
+    last, first = both(*in_order((outs[1], outs[0])))
+    kv_sums = rings(fold_kv(info, (arrays[2], kv_first, arrays[3], kv_last), ranks))
+    ups_first, ups_last = both(*in_order(ups[:2]))
+    ups = fold_first(info, [two(array) for array in (ups[2], ups_first, ups[3], ups_last)], 1)
+    ups_last, ups_first = both(ups[1], ups[0])
     layer_own = call(
         layer_kernel, [(residual.shape, BF)], (residual, *feed_sums), "layer", prefetch=info
     )[0]
+    joined, *latent_blocks = lax.optimization_barrier((info, *latent_blocks))
+
+    ups = rings(fold_up(joined, (ups[2], ups_first, ups[3], ups_last), ranks))
+    kv_own = kv_back(info, cosine, sine, kv_sums)
+    kv_blocks = rings([kv_own] * ranks)
+    out_piece = fold_last(info, (outs[2], first, outs[3], last), 1)
+    out_whole = lax.all_gather(out_piece, "seq", axis=0, tiled=False)
+    wait(kv_blocks)
+
+    grad_in, small, latent_cols, grad_kv = input_back(
+        info, tokens_in, grad_branch, norm1_gain, kv_weight, recip1, latent_all, kv_pre,
+        latent_blocks, kv_blocks, downs,
+    )
+    last = last_products(info, normed_low, latent_cols, grad_kv, small, ranks)
+    last = lax.psum(last, "seq")
+    up_piece = pack_up(info, ups)
+    layer_blocks = rings([in_order(layer_own)] * ranks)
+    up_pieces = [up_piece] + [exchange(in_order(up_piece), mask) for mask in (1, 2)]
     shape = gate_weight.shape
     grad_gate, grad_up, grad_down = unpack(
-        info, after(feed_whole, kv_blocks), store_feed, (shape, shape, shape[::-1]), (0, 0, 1)
-    )
-    gains = jnp.concatenate([norm2_part[0], gain_part[0]])
-    gains = sum_over(sum_over(gains, "rank"), "seq")
-    layer_blocks = rings([after(layer_own, kv_blocks, latent_blocks, gains)] * ranks)
-
-    grad_in, norm1_part, latent_cols, grad_kv = input_back(
-        info, tokens_in, grad_branch, norm1_gain, kv_weight, recip1, latent_all, kv_pre,
-        latent_blocks, kv_blocks, downs,
-    )
-    near, far = last_products(info, normed_low, latent_cols, grad_kv, ranks)
-    own, *others = fold_direct(info, near, swap(far, 0))
-    norm1 = sum_over(norm1_part[0], "seq")
-    piece = sum_parts(info, [own] + [exchange(part, 2 * m) for m, part in enumerate(others, 1)])
-    last = stack_chips(info, after([piece] + [exchange(piece, 2 * m) for m in (1, 2, 3)], norm1))
-    grad_q_down, grad_kv_weight = call(
+        info, feed_whole, store_feed, (shape, shape, shape[::-1]), (0, 0, 1)
+    )
+    up_pieces += [exchange(in_order(up_piece), mask) for mask in range(3, 8)]
+    grad_out = unpack(info, out_whole, store_same, [out_weight.shape], [0])[0]
+    layer_out = place(info, layer_blocks)
+    grad_q_up = unpack_up(info, up_pieces, q_up.shape)
+    grad_q_down, grad_kv_weight, small = call(
         last_kernel,
-        [(q_down.shape, F32), ((col_count, 2 * head_dim), F32)],
-        (last, swap(last, 0)),
+        [(q_down.shape, F32), ((col_count, 2 * head_dim), F32), (small.shape, F32)],
+        (last,),
         "last",
         prefetch=info,
     )
-    grad_out, grad_q_up = unpack(
-        info, heads_whole, store_heads, (out_weight.shape, q_up.shape), (0, 0)
-    )
-    layer_out = place(info, after(layer_blocks, grad_out))
-
-    grad_norm2 = gains[:model_width]
-    grad_latent_gain = lax.dynamic_slice_in_dim(gains, model_width + rank_ix * rank_cols, rank_cols, 0)
+
+    small = small.reshape(-1)
+    norm1 = small[model_width : model_width + col_count]
+    grad_latent_gain = small[model_width + col_count : model_width + col_count + rank_cols]
+    grad_norm2 = small[:model_width]
     return (
         layer_out,
         grad_in,

time: 732 us -> 658 us (0.90)
  waiting for transfers between devices: 326 us -> 291 us
  starting transfers between devices: 93.3 us -> 68.4 us
  Pallas kernels: 236 us -> 227 us
    ppermute x39 -> x42, waiting for transfers between devices: 105 us -> 66.1 us  [exchange(): return lax.ppermute(value, 'seq', [(i, i ^ mask) for i in range(count)])]
    ppermute x27, waiting for transfers between devices: 86 us -> 107 us  [ring(): lax.ppermute(value, 'rank', [(i, (i + shift) % ranks) for i in range(rank...]
    reduce_scatter x1, waiting for transfers between devices: 62.3 us -> 46.6 us  [per_device_fast(): lax.psum_scatter(branch_part, 'rank', scatter_dimension=0, tiled=True)]
    ppermute x27, starting transfers between devices: 41 us -> 26.4 us  [ring(): lax.ppermute(value, 'rank', [(i, (i + shift) % ranks) for i in range(rank...]
    ppermute x8 -> x0, waiting for transfers between devices: 11.6 us -> none  [sum_over(): lax.ppermute(value, axis, [(i, i ^ mask) for i in range(count)])]
    all_gather x1, waiting for transfers between devices: 0.02 us -> 10.4 us  [per_device_fast(): grad_branch = lax.all_gather(branch_own, 'rank', axis=0, tiled=True)]
    ppermute x8 -> x0, starting transfers between devices: 8.35 us -> none  [sum_over(): lax.ppermute(value, axis, [(i, i ^ mask) for i in range(count)])]
    pallas_call x12 -> x10, Pallas kernels: 36.4 us -> 32.4 us  [placed_call(): pl.pallas_call(kernel, in_specs=[pl.BlockSpec(memory_space=pltpu.SMEM)] +...]
  transfers between devices with their start and end apart: 81 -> 77, of which waited for: 36 -> 24; matrix products, arithmetic and copies ran while one was open for 3% -> 3% of each run, Pallas kernels for 29% -> 30%
where the time goes in v3:
time: 658 us; the launch traced here: 648 us
  waiting for transfers between devices  291 us (44%)
  Pallas kernels  227 us (34%)
  starting transfers between devices  68.4 us (10%)
  local copies, waits for them, and re-layouts  34.9 us (5%)
  between operations  15.2 us (2%)
  matrix products  6.97 us (1%)
    pallas_call x22, Pallas kernels, placed_call(): pl.pallas_call(kernel, grid_spec=pltpu.PrefetchScalarGridSpec(num_scalar_...  142 us
    ppermute x27, waiting for transfers between devices, ring(): lax.ppermute(value, 'rank', [(i, (i + shift) % ranks) for i in range(rank...  107 us
    ppermute x42, waiting for transfers between devices, exchange(): return lax.ppermute(value, 'seq', [(i, i ^ mask) for i in range(count)])  66.1 us
    all_gather x1, waiting for transfers between devices, per_device_fast(): mid_low = lax.all_gather(mid_own, 'rank', axis=0, tiled=True)  49.4 us
    reduce_scatter x1, waiting for transfers between devices, per_device_fast(): lax.psum_scatter(branch_part, 'rank', scatter_dimension=0, tiled=True)  46.6 us
    ppermute x42, starting transfers between devices, exchange(): return lax.ppermute(value, 'seq', [(i, i ^ mask) for i in range(count)])  40.9 us
    pallas_call x10, Pallas kernels, placed_call(): pl.pallas_call(kernel, in_specs=[pl.BlockSpec(memory_space=pltpu.SMEM)] +...  32.4 us
    ppermute x27, starting transfers between devices, ring(): lax.ppermute(value, 'rank', [(i, (i + shift) % ranks) for i in range(rank...  26.4 us
  transfers between devices with their start and end apart: 77, of which 24 were waited for; matrix products, arithmetic and copies ran while one was open for 3% of the time, Pallas kernels for 30%

profile of v3, /device:TPU:25, one launch (start us, length us, event | category | flops | bytes accessed | tf_op | source)
XLA Modules:
  0.0 648.1 jit_solution(13669118266330473246)
XLA Ops:
  10.7 7.2 %project.1 = (bf16[576,2048]{1,0:T(8,128)(2,1)}, f32[576,128]{1,0:T(8,128)}, f32[576,512]{1,0:T(8,128)}, bf16[592,256]{1,0:T(8,128)(2,1)}) custom-call(s32[6]{0:T(128)} %stack.29.info_ref, bf16[576,2048]{1,0:T(8,128)(2,1)} %tokens_ref.4, f32[1,2048]{1,0:T(1,128)} %bitcast.48, bf16[2048,256]{1,0:T(8,128)(2,1)} %down_ref.1, bf16[2048,512]{1,0:T(8,128)(2,1)} %kv_weight_ref.3, ...), custom_call_target="tpu_custom_call" | custom-call | tf_op jit(solution)/shard_map/project/pallas_call | solution.py:376
  26.6 15.4 %collective-permute-done.1 = bf16[256,512]{1,0:T(8,128)(2,1)S(1)} collective-permute-done((bf16[256,512]{1,0:T(8,128)(2,1)S(1)}, bf16[256,512]{1,0:T(8,128)(2,1)S(1)}, u32[]{:S(2)}, u32[]{:S(2)}) %collective-permute-start.1) | collective-permute-done | bytes 262176 | tf_op jit(solution)/shard_map/ppermute | solution.py:1070
  43.8 3.9 collective-permute-start.3
  51.8 4.8 collective-permute-done.6.refs_3_
  62.1 5.1 queries.1
  68.1 15.8 %attend.1 = (bf16[2304,256]{1,0:T(8,128)(2,1)}, f32[576,1024]{1,0:T(8,128)}, bf16[576,1024]{1,0:T(8,128)(2,1)}, f32[1,2304]{1,0:T(1,128)}, bf16[4608,512]{1,0:T(8,128)(2,1)}) custom-call(s32[6]{0:T(128)} %stack.28.info_ref, f32[576,1024]{1,0:T(8,128)} %get-tuple-element.170.pre_ref, f32[576,128]{1,0:T(8,128)} %get-tuple-element.321.cos_ref, ...), custom_call_target="tpu_custom_call" | custom-call | tf_op jit(solution)/shard_map/attend/pallas_call | solution.py:169
  83.9 6.4 matmul.3
  95.3 7.0 %fusion.1.grad_ref = f32[576,1408]{1,0:T(8,128)S(1)} fusion(bf16[576,2048]{1,0:T(8,128)(2,1)} %out_grad_ref.1, bf16[1408,2048]{1,0:T(8,128)(2,1)} %right_ref.4), kind=kOutput, calls=%fused_computation.18 | convolution fusion | flops 3321888768 | bytes 11370496 | tf_op jit(solution)/shard_map/dot_general | solution.py:46
  102.4 46.6 %reduce-scatter.3.cloned.1.call-done.branch_ref = bf16[144,2048]{1,0:T(8,128)(2,1)} async-done(((bf16[576,2048]{1,0:T(8,128)(2,1)}), bf16[144,2048]{1,0:T(8,128)(2,1)}) %reduce-scatter.3.cloned.1.call-update) | async-done | bytes 589840 | tf_op jit(solution)/shard_map/reduce_scatter | solution.py:1166
  149.0 3.3 mid_norm.1
  152.4 49.4 %all-gather.10.cloned.1.call-done.mid_ref.refs_0_ = bf16[576,2048]{1,0:T(8,128)(2,1)} async-done(((bf16[144,2048]{1,0:T(8,128)(2,1)}), bf16[576,2048]{1,0:T(8,128)(2,1)}) %all-gather.10.cloned.1.call-update) | async-done | bytes 2359312 | tf_op jit(solution)/shard_map/all_gather | solution.py:1185
  206.1 19.7 %feed_forward.1 = (bf16[576,1408]{1,0:T(8,128)(2,1)S(1)}, bf16[576,2816]{1,0:T(8,128)(2,1)S(1)}, bf16[576,2048]{1,0:T(8,128)(2,1)S(1)}) custom-call(bf16[576,2048]{1,0:T(8,128)(2,1)S(1)} %copy-done, f32[576,1408]{1,0:T(8,128)S(1)} %fusion.1.grad_ref, bf16[2048,1408]{1,0:T(8,128)(2,1)} %gate_ref.1, bf16[2048,1408]{1,0:T(8,128)(2,1)} %up_ref.1), custom_call_target="tpu_custom_call" | custom-call | flops 2000000000 | tf_op jit(solution)/shard_map/feed_forward/pallas_call | solution.py:322
  233.1 8.2 %matmul.4 = (bf16[144,2048]{1,0:T(8,128)(2,1)}, bf16[144,2048]{1,0:T(8,128)(2,1)}, bf16[144,2048]{1,0:T(8,128)(2,1)}, bf16[144,2048]{1,0:T(8,128)(2,1)}) custom-call(s32[6]{0:T(128)} %stack.28.info_ref, bf16[576,1408]{1,0:T(8,128)(2,1)} %copy-done.2, bf16[1408,2048]{1,0:T(8,128)(2,1)} %right_ref.4), custom_call_target="tpu_custom_call" | custom-call | tf_op jit(solution)/shard_map/matmul/pallas_call | solution.py:376
  244.0 22.2 %pair_products.3 = (bf16[256,4224]{1,0:T(8,128)(2,1)}, bf16[256,4224]{1,0:T(8,128)(2,1)}, bf16[256,4224]{1,0:T(8,128)(2,1)}, bf16[256,4224]{1,0:T(8,128)(2,1)}) custom-call(s32[6]{0:T(128)} %stack.28.info_ref, bf16[576,2048]{1,0:T(8,128)(2,1)} %all-gather.10.cloned.1.call-done.mid_ref.refs_0_, bf16[576,2048]{1,0:T(8,128)(2,1)} %copy-done.12, ...), custom_call_target="tpu_custom_call" | custom-call | tf_op jit(solution)/shard_map/pair_products/pallas_call | solution.py:376
  268.6 11.5 %reduce-scatter.5.cloned.1.call-done.grad_ref = bf16[144,2048]{1,0:T(8,128)(2,1)} async-done(((bf16[576,2048]{1,0:T(8,128)(2,1)}), bf16[144,2048]{1,0:T(8,128)(2,1)}) %reduce-scatter.5.cloned.1.call-update) | async-done | bytes 589840 | tf_op jit(solution)/shard_map/reduce_scatter | solution.py:1194
  280.0 3.6 mid_back.1
  283.9 30.8 %collective-permute-done.22 = bf16[256,4224]{1,0:T(8,128)(2,1)S(1)} collective-permute-done((bf16[256,4224]{1,0:T(8,128)(2,1)}, bf16[256,4224]{1,0:T(8,128)(2,1)S(1)}, u32[]{:S(2)}, u32[]{:S(2)}) %collective-permute-start.22) | collective-permute-done | bytes 2162720 | tf_op jit(solution)/shard_map/ppermute | solution.py:1059
  316.1 6.6 %fold_first.4 = (bf16[128,4224]{1,0:T(8,128)(2,1)}, bf16[128,4224]{1,0:T(8,128)(2,1)}, bf16[128,4224]{1,0:T(8,128)(2,1)}, bf16[128,4224]{1,0:T(8,128)(2,1)}) custom-call(s32[6]{0:T(128)} %stack.28.info_ref, bf16[2,128,4224]{2,1,0:T(8,128)(2,1)} %bitcast.54, bf16[2,128,4224]{2,1,0:T(8,128)(2,1)} %bitcast.56, bf16[2,128,4224]{2,1,0:T(8,128)(2,1)} %bitcast.55, ...), custom_call_target="tpu_custom_call" | custom-call | flops 999999995904 | tf_op jit(solution)/shard_map/fold_first/pallas_call | solution.py:376
  322.7 10.4 %all-gather.12.cloned.1.call-done.left_ref.refs_2_.branch_ref = bf16[576,2048]{1,0:T(8,128)(2,1)} async-done(((bf16[144,2048]{1,0:T(8,128)(2,1)}), bf16[576,2048]{1,0:T(8,128)(2,1)}) %all-gather.12.cloned.1.call-update) | async-done | bytes 2359312 | tf_op jit(solution)/shard_map/all_gather | solution.py:1208
  336.2 6.6 %matmul.5.grad_ref = bf16[576,1024]{1,0:T(8,128)(2,1)} custom-call(s32[6]{0:T(128)} %stack.28.info_ref, bf16[576,2048]{1,0:T(8,128)(2,1)} %all-gather.12.cloned.1.call-done.left_ref.refs_2_.branch_ref, bf16[1024,2048]{1,0:T(8,128)(2,1)} %right_ref.5), custom_call_target="tpu_custom_call" | custom-call | tf_op jit(solution)/shard_map/matmul/pallas_call | solution.py:376
  344.3 7.6 %pair_products.4 = (bf16[128,2048]{1,0:T(8,128)(2,1)}, bf16[128,2048]{1,0:T(8,128)(2,1)}, bf16[128,2048]{1,0:T(8,128)(2,1)}, bf16[128,2048]{1,0:T(8,128)(2,1)}) custom-call(s32[6]{0:T(128)} %stack.28.info_ref, bf16[576,1024]{1,0:T(8,128)(2,1)} %get-tuple-element.173.left_ref.refs_0_, bf16[576,1024]{1,0:T(8,128)(2,1)} %collective-permute-done.14.refs_1_, ...), custom_call_target="tpu_custom_call" | custom-call | tf_op jit(solution)/shard_map/pair_products/pallas_call | solution.py:376
  351.8 7.4 %collective-permute-done.25.got_first = bf16[128,4224]{1,0:T(8,128)(2,1)S(1)} collective-permute-done((bf16[128,4224]{1,0:T(8,128)(2,1)}, bf16[128,4224]{1,0:T(8,128)(2,1)S(1)}, u32[]{:S(2)}, u32[]{:S(2)}) %collective-permute-start.25) | collective-permute-done | bytes 1081376 | tf_op jit(solution)/shard_map/ppermute | solution.py:1059
  361.3 5.0 fold_last.2
  372.6 17.1 %attend_back.1 = (bf16[576,1024]{1,0:T(8,128)(2,1)}, bf16[2,4,288,512]{3,2,1,0:T(8,128)(2,1)}, bf16[2,4,288,512]{3,2,1,0:T(8,128)(2,1)}) custom-call(s32[6]{0:T(128)} %stack.28.info_ref, bf16[2304,256]{1,0:T(8,128)(2,1)} %get-tuple-element.214.query_ref, bf16[576,1024]{1,0:T(8,128)(2,1)} %matmul.5.grad_ref, f32[576,1024]{1,0:T(8,128)} %get-tuple-element.215.out_ref, ...), custom_call_target="tpu_custom_call" | custom-call | tf_op jit(solution)/shard_map/attend_back/pallas_call | solution.py:271
  389.6 29.7 %collective-permute-done.28.refs_2_ = bf16[144,2048]{1,0:T(8,128)(2,1)S(1)} collective-permute-done((bf16[144,2048]{1,0:T(8,128)(2,1)}, bf16[144,2048]{1,0:T(8,128)(2,1)S(1)}, u32[]{:S(2)}, u32[]{:S(2)}) %collective-permute-start.28) | collective-permute-done | bytes 589856 | tf_op jit(solution)/shard_map/ppermute | solution.py:1070
  421.6 4.5 latent_parts.1
  427.5 5.3 fold_near.1
  437.7 3.3 fold_first.5
  441.0 5.6 pair_products.5
  446.6 15.1 %collective-permute-done.35.refs_2_ = bf16[144,1024]{1,0:T(8,128)(2,1)S(1)} collective-permute-done((bf16[144,1024]{1,0:T(8,128)(2,1)S(1)}, bf16[144,1024]{1,0:T(8,128)(2,1)S(1)}, u32[]{:S(2)}, u32[]{:S(2)}) %collective-permute-start.35) | collective-permute-done | bytes 294944 | tf_op jit(solution)/shard_map/ppermute | solution.py:1070
  462.6 3.4 latent_back.1.refs_0_
  466.0 3.6 fold_first.6
  472.6 8.1 %collective-permute-done.42.got_first = bf16[288,512]{1,0:T(8,128)(2,1)S(1)} collective-permute-done((bf16[288,512]{1,0:T(8,128)(2,1)}, bf16[288,512]{1,0:T(8,128)(2,1)S(1)}, u32[]{:S(2)}, u32[]{:S(2)}) %collective-permute-start.42) | collective-permute-done | bytes 294944 | tf_op jit(solution)/shard_map/ppermute | solution.py:1059
  485.9 4.7 collective-permute-done.44
  496.7 4.0 collective-permute-done.40.refs_2_
  509.1 6.4 collective-permute-done.49.refs_2_
  529.8 10.0 %collective-permute-done.54.refs_6_ = bf16[144,512]{1,0:T(8,128)(2,1)S(1)} collective-permute-done((bf16[144,512]{1,0:T(8,128)(2,1)}, bf16[144,512]{1,0:T(8,128)(2,1)S(1)}, u32[]{:S(2)}, u32[]{:S(2)}) %collective-permute-start.54) | collective-permute-done | bytes 147488 | tf_op jit(solution)/shard_map/ppermute | solution.py:1070
  540.5 6.6 %input_back.1 = (f32[576,512]{1,0:T(8,128)}, bf16[16,256]{1,0:T(8,128)(2,1)}, bf16[576,256]{1,0:T(8,128)(2,1)}, bf16[576,512]{1,0:T(8,128)(2,1)}) custom-call(s32[6]{0:T(128)} %stack.28.info_ref, bf16[576,2048]{1,0:T(8,128)(2,1)} %tokens_ref.4, bf16[576,2048]{1,0:T(8,128)(2,1)} %all-gather.12.cloned.1.call-done.left_ref.refs_2_.branch_ref, ...), custom_call_target="tpu_custom_call" | custom-call | tf_op jit(solution)/shard_map/input_back/pallas_call | solution.py:376
  547.1 4.6 last_products.1
  554.6 4.0 collective-permute-start.60
  562.0 18.4 %unpack.2 = (f32[2048,1408]{1,0:T(8,128)}, f32[2048,1408]{1,0:T(8,128)}, f32[1408,2048]{1,0:T(8,128)}) custom-call(s32[6]{0:T(128)} %stack.28.info_ref, bf16[4,2,2,128,4224]{4,3,2,1,0:T(8,128)(2,1)} %bitcast.34), custom_call_target="tpu_custom_call" | custom-call | tf_op jit(solution)/shard_map/unpack/pallas_call | solution.py:376
  583.6 25.9 %collective-permute-done.60.refs_2_ = bf16[144,2048]{1,0:T(8,128)(2,1)S(1)} collective-permute-done((bf16[144,2048]{1,0:T(8,128)(2,1)S(1)}, bf16[144,2048]{1,0:T(8,128)(2,1)S(1)}, u32[]{:S(2)}, u32[]{:S(2)}) %collective-permute-start.60) | collective-permute-done | bytes 589856 | tf_op jit(solution)/shard_map/ppermute | solution.py:1070
  609.9 3.4 collective-permute-start.68
  613.3 6.7 %unpack.3 = f32[1024,2048]{1,0:T(8,128)} custom-call(s32[6]{0:T(128)} %stack.28.info_ref, bf16[4,2,2,64,2048]{4,3,2,1,0:T(8,128)(2,1)} %bitcast.37), custom_call_target="tpu_custom_call" | custom-call | tf_op jit(solution)/shard_map/unpack/pallas_call | solution.py:376
  620.0 4.2 place.1
  624.3 5.0 collective-permute-done.68.refs_7_
  630.0 3.8 unpack_up.1
  633.8 3.2 last.1
  (322 shorter events, 121.8 us)
Async XLA Ops:
  7.2 54.9 %all-gather.8.cloned.1.call-start = ((), (), s32[]{:S(2)}) async-start(), calls=%async_computation.2 | async-start | bytes 1515520 | tf_op jit(solution)/shard_map/all_gather | solution.py:1150
  8.5 18.1 %collective-permute-start = (bf16[256,512]{1,0:T(8,128)(2,1)S(1)}, bf16[256,512]{1,0:T(8,128)(2,1)S(1)}, u32[]{:S(2)}, u32[]{:S(2)}) collective-permute-start(bf16[256,512]{1,0:T(8,128)(2,1)S(1)} %get-tuple-element.313), channel_id=1, source_target_pairs={{0,1},{1,2},{2,3},{3,0},{4,5},{5,6},{6,7},{7,4},{8,9},{9,10},{10,1... | collective-permute-start | bytes 786440 | tf_op jit(solution)/shard_map/ppermute | solution.py:1070
  8.6 33.4 %collective-permute-start.1 = (bf16[256,512]{1,0:T(8,128)(2,1)S(1)}, bf16[256,512]{1,0:T(8,128)(2,1)S(1)}, u32[]{:S(2)}, u32[]{:S(2)}) collective-permute-start(bf16[256,512]{1,0:T(8,128)(2,1)S(1)} %get-tuple-element.315), channel_id=1, source_target_pairs={{0,2},{1,3},{2,0},{3,1},{4,6},{5,7},{6,4},{7,5},{8,10},{9,11},{10,... | collective-permute-start | bytes 786440 | tf_op jit(solution)/shard_map/ppermute | solution.py:1070
  9.9 32.8 %collective-permute-start.2 = (bf16[256,512]{1,0:T(8,128)(2,1)S(1)}, bf16[256,512]{1,0:T(8,128)(2,1)}, u32[]{:S(2)}, u32[]{:S(2)}) collective-permute-start(bf16[256,512]{1,0:T(8,128)(2,1)S(1)} %get-tuple-element.312), channel_id=1, source_target_pairs={{0,3},{1,0},{2,1},{3,2},{4,7},{5,4},{6,5},{7,6},{8,11},{9,8},{10,9... | collective-permute-start | bytes 786440 | tf_op jit(solution)/shard_map/ppermute | solution.py:1070
  17.9 131.1 %reduce-scatter.3.cloned.1.call-start = ((), (), s32[]{:S(2)}) async-start(), calls=%async_computation.3 | async-start | bytes 2949120 | tf_op jit(solution)/shard_map/reduce_scatter | solution.py:1166
  24.2 23.6 %collective-permute-start.4 = (bf16[576,512]{1,0:T(8,128)(2,1)}, bf16[576,512]{1,0:T(8,128)(2,1)S(1)}, u32[]{:S(2)}, u32[]{:S(2)}) collective-permute-start(bf16[576,512]{1,0:T(8,128)(2,1)} %turn.1.refs_0_), channel_id=1, source_target_pairs={{0,8},{4,12},{8,0},{12,4},{16,24},{20,28},{24,16},{28,20},{1,9},{5... | collective-permute-start | bytes 1769480 | tf_op jit(solution)/shard_map/ppermute | solution.py:1059
  25.4 22.4 %collective-permute-start.5 = (bf16[576,512]{1,0:T(8,128)(2,1)}, bf16[576,512]{1,0:T(8,128)(2,1)}, u32[]{:S(2)}, u32[]{:S(2)}) collective-permute-start(bf16[576,512]{1,0:T(8,128)(2,1)} %turn.1.refs_0_), channel_id=1, source_target_pairs={{0,16},{4,20},{8,24},{12,28},{16,0},{20,4},{24,8},{28,12},{1,17},{... | collective-permute-start | bytes 1769480 | tf_op jit(solution)/shard_map/ppermute | solution.py:1059
  51.2 16.0 %collective-permute-start.8 = (bf16[576,512]{1,0:T(8,128)(2,1)S(1)}, bf16[576,512]{1,0:T(8,128)(2,1)}, u32[]{:S(2)}, u32[]{:S(2)}) collective-permute-start(bf16[576,512]{1,0:T(8,128)(2,1)S(1)} %copy-done.9), channel_id=1, source_target_pairs={{0,4},{4,0},{8,12},{12,8},{16,20},{20,16},{24,28},{28,24},{1,5},{5... | collective-permute-start | bytes 1769480 | tf_op jit(solution)/shard_map/ppermute | solution.py:1059
  90.3 111.5 %all-gather.10.cloned.1.call-start = ((), (), s32[]{:S(2)}) async-start(), calls=%async_computation.4 | async-start | bytes 2949120 | tf_op jit(solution)/shard_map/all_gather | solution.py:1185
  152.3 127.7 %reduce-scatter.5.cloned.1.call-start = ((), (), s32[]{:S(2)}) async-start(), calls=%async_computation.5 | async-start | bytes 2949120 | tf_op jit(solution)/shard_map/reduce_scatter | solution.py:1194
  201.8 28.4 %collective-permute-start.16 = (bf16[512,256]{1,0:T(8,128)(2,1)}, bf16[512,256]{1,0:T(8,128)(2,1)}, u32[]{:S(2)}, u32[]{:S(2)}) collective-permute-start(bf16[512,256]{1,0:T(8,128)(2,1)} %get-tuple-element.186), channel_id=1, source_target_pairs={{0,1},{1,2},{2,3},{3,0},{4,5},{5,6},{6,7},{7,4},{8,9},{9,10},{10,1... | collective-permute-start | bytes 786440 | tf_op jit(solution)/shard_map/ppermute | solution.py:1070
  204.2 26.0 %collective-permute-start.17 = (bf16[512,256]{1,0:T(8,128)(2,1)}, bf16[512,256]{1,0:T(8,128)(2,1)}, u32[]{:S(2)}, u32[]{:S(2)}) collective-permute-start(bf16[512,256]{1,0:T(8,128)(2,1)} %get-tuple-element.187), channel_id=1, source_target_pairs={{0,2},{1,3},{2,0},{3,1},{4,6},{5,7},{6,4},{7,5},{8,10},{9,11},{10,... | collective-permute-start | bytes 786440 | tf_op jit(solution)/shard_map/ppermute | solution.py:1070
  204.3 25.9 %collective-permute-start.18 = (bf16[512,256]{1,0:T(8,128)(2,1)S(1)}, bf16[512,256]{1,0:T(8,128)(2,1)}, u32[]{:S(2)}, u32[]{:S(2)}) collective-permute-start(bf16[512,256]{1,0:T(8,128)(2,1)S(1)} %get-tuple-element.188), channel_id=1, source_target_pairs={{0,3},{1,0},{2,1},{3,2},{4,7},{5,4},{6,5},{7,6},{8,11},{9,8},{10,9... | collective-permute-start | bytes 786440 | tf_op jit(solution)/shard_map/ppermute | solution.py:1070
  231.5 101.6 %all-gather.12.cloned.1.call-start = ((), (), s32[]{:S(2)}) async-start(), calls=%async_computation.6 | async-start | bytes 2949120 | tf_op jit(solution)/shard_map/all_gather | solution.py:1208
  266.2 48.5 %collective-permute-start.22 = (bf16[256,4224]{1,0:T(8,128)(2,1)}, bf16[256,4224]{1,0:T(8,128)(2,1)S(1)}, u32[]{:S(2)}, u32[]{:S(2)}) collective-permute-start(bf16[256,4224]{1,0:T(8,128)(2,1)} %get-tuple-element.193), channel_id=1, source_target_pairs={{0,8},{4,12},{8,0},{12,4},{16,24},{20,28},{24,16},{28,20},{1,9},{5... | collective-permute-start | bytes 6488072 | tf_op jit(solution)/shard_map/ppermute | solution.py:1059
  267.4 48.2 %collective-permute-start.23 = (bf16[256,4224]{1,0:T(8,128)(2,1)}, bf16[256,4224]{1,0:T(8,128)(2,1)}, u32[]{:S(2)}, u32[]{:S(2)}) collective-permute-start(bf16[256,4224]{1,0:T(8,128)(2,1)} %get-tuple-element.203), channel_id=1, source_target_pairs={{0,16},{4,20},{8,24},{12,28},{16,0},{20,4},{24,8},{28,12},{1,17},{... | collective-permute-start | bytes 6488072 | tf_op jit(solution)/shard_map/ppermute | solution.py:1059
  283.7 278.3 %all-gather.14.cloned.1.call-start = ((), (), s32[]{:S(2)}) async-start(), calls=%async_computation.8 | async-start | bytes 19464192 | tf_op jit(solution)/shard_map/all_gather | solution.py:1220
  333.6 25.6 %collective-permute-start.25 = (bf16[128,4224]{1,0:T(8,128)(2,1)}, bf16[128,4224]{1,0:T(8,128)(2,1)S(1)}, u32[]{:S(2)}, u32[]{:S(2)}) collective-permute-start(bf16[128,4224]{1,0:T(8,128)(2,1)} %get-tuple-element.204), channel_id=1, source_target_pairs={{0,16},{4,20},{8,24},{12,28},{16,0},{20,4},{24,8},{28,12},{1,17},{... | collective-permute-start | bytes 3244040 | tf_op jit(solution)/shard_map/ppermute | solution.py:1059
  335.0 25.3 %collective-permute-start.26 = (bf16[128,4224]{1,0:T(8,128)(2,1)}, bf16[128,4224]{1,0:T(8,128)(2,1)S(1)}, u32[]{:S(2)}, u32[]{:S(2)}) collective-permute-start(bf16[128,4224]{1,0:T(8,128)(2,1)} %get-tuple-element.212), channel_id=1, source_target_pairs={{0,8},{4,12},{8,0},{12,4},{16,24},{20,28},{24,16},{28,20},{1,9},{5... | collective-permute-start | bytes 3244040 | tf_op jit(solution)/shard_map/ppermute | solution.py:1059
  366.4 246.9 %all-gather.16.cloned.1.call-start = ((), (), s32[]{:S(2)}) async-start(), calls=%async_computation.9 | async-start | bytes 4718592 | tf_op jit(solution)/shard_map/all_gather | solution.py:1257
  366.4 23.2 %collective-permute-start.27 = (bf16[144,2048]{1,0:T(8,128)(2,1)}, bf16[144,2048]{1,0:T(8,128)(2,1)S(1)}, u32[]{:S(2)}, u32[]{:S(2)}) collective-permute-start(bf16[144,2048]{1,0:T(8,128)(2,1)} %get-tuple-element.225), channel_id=1, source_target_pairs={{0,1},{1,2},{2,3},{3,0},{4,5},{5,6},{6,7},{7,4},{8,9},{9,10},{10,1... | collective-permute-start | bytes 1769480 | tf_op jit(solution)/shard_map/ppermute | solution.py:1070
  368.9 50.4 %collective-permute-start.28 = (bf16[144,2048]{1,0:T(8,128)(2,1)}, bf16[144,2048]{1,0:T(8,128)(2,1)S(1)}, u32[]{:S(2)}, u32[]{:S(2)}) collective-permute-start(bf16[144,2048]{1,0:T(8,128)(2,1)} %get-tuple-element.226), channel_id=1, source_target_pairs={{0,2},{1,3},{2,0},{3,1},{4,6},{5,7},{6,4},{7,5},{8,10},{9,11},{10,... | collective-permute-start | bytes 1769480 | tf_op jit(solution)/shard_map/ppermute | solution.py:1070
  369.0 50.4 %collective-permute-start.29 = (bf16[144,2048]{1,0:T(8,128)(2,1)}, bf16[144,2048]{1,0:T(8,128)(2,1)S(1)}, u32[]{:S(2)}, u32[]{:S(2)}) collective-permute-start(bf16[144,2048]{1,0:T(8,128)(2,1)} %get-tuple-element.227), channel_id=1, source_target_pairs={{0,3},{1,0},{2,1},{3,2},{4,7},{5,4},{6,5},{7,6},{8,11},{9,8},{10,9... | collective-permute-start | bytes 1769480 | tf_op jit(solution)/shard_map/ppermute | solution.py:1070
  369.3 50.1 %collective-permute-start.30 = (bf16[128,2048]{1,0:T(8,128)(2,1)}, bf16[128,2048]{1,0:T(8,128)(2,1)S(1)}, u32[]{:S(2)}, u32[]{:S(2)}) collective-permute-start(bf16[128,2048]{1,0:T(8,128)(2,1)} %get-tuple-element.208), channel_id=1, source_target_pairs={{0,8},{4,12},{8,0},{12,4},{16,24},{20,28},{24,16},{28,20},{1,9},{5... | collective-permute-start | bytes 1572872 | tf_op jit(solution)/shard_map/ppermute | solution.py:1059
  370.5 48.9 %collective-permute-start.31 = (bf16[128,2048]{1,0:T(8,128)(2,1)}, bf16[128,2048]{1,0:T(8,128)(2,1)S(1)}, u32[]{:S(2)}, u32[]{:S(2)}) collective-permute-start(bf16[128,2048]{1,0:T(8,128)(2,1)} %get-tuple-element.228), channel_id=1, source_target_pairs={{0,16},{4,20},{8,24},{12,28},{16,0},{20,4},{24,8},{28,12},{1,17},{... | collective-permute-start | bytes 1572872 | tf_op jit(solution)/shard_map/ppermute | solution.py:1059
  432.8 28.9 %collective-permute-start.37 = (bf16[2,288,512]{2,1,0:T(8,128)(2,1)}, bf16[2,288,512]{2,1,0:T(8,128)(2,1)S(1)}, u32[]{:S(2)}, u32[]{:S(2)}) collective-permute-start(bf16[2,288,512]{2,1,0:T(8,128)(2,1)} %get-tuple-element.235), channel_id=1, source_target_pairs={{0,8},{4,12},{8,0},{12,4},{16,24},{20,28},{24,16},{28,20},{1,9},{5... | collective-permute-start | bytes 1769480 | tf_op jit(solution)/shard_map/ppermute | solution.py:1059
  434.1 27.8 %collective-permute-start.38 = (bf16[2,288,512]{2,1,0:T(8,128)(2,1)}, bf16[2,288,512]{2,1,0:T(8,128)(2,1)S(1)}, u32[]{:S(2)}, u32[]{:S(2)}) collective-permute-start(bf16[2,288,512]{2,1,0:T(8,128)(2,1)} %get-tuple-element.245), channel_id=1, source_target_pairs={{0,16},{4,20},{8,24},{12,28},{16,0},{20,4},{24,8},{28,12},{1,17},{... | collective-permute-start | bytes 1769480 | tf_op jit(solution)/shard_map/ppermute | solution.py:1059
  434.9 26.8 %collective-permute-start.35 = (bf16[144,1024]{1,0:T(8,128)(2,1)S(1)}, bf16[144,1024]{1,0:T(8,128)(2,1)S(1)}, u32[]{:S(2)}, u32[]{:S(2)}) collective-permute-start(bf16[144,1024]{1,0:T(8,128)(2,1)S(1)} %copy-done.65), channel_id=1, source_target_pairs={{0,2},{1,3},{2,0},{3,1},{4,6},{5,7},{6,4},{7,5},{8,10},{9,11},{10,... | collective-permute-start | bytes 884744 | tf_op jit(solution)/shard_map/ppermute | solution.py:1070
  436.2 25.5 %collective-permute-start.36 = (bf16[144,1024]{1,0:T(8,128)(2,1)S(1)}, bf16[144,1024]{1,0:T(8,128)(2,1)S(1)}, u32[]{:S(2)}, u32[]{:S(2)}) collective-permute-start(bf16[144,1024]{1,0:T(8,128)(2,1)S(1)} %copy-done.64), channel_id=1, source_target_pairs={{0,3},{1,0},{2,1},{3,2},{4,7},{5,4},{6,5},{7,6},{8,11},{9,8},{10,9... | collective-permute-start | bytes 884744 | tf_op jit(solution)/shard_map/ppermute | solution.py:1070
  470.7 25.4 %collective-permute-start.39 = (bf16[160,1024]{1,0:T(8,128)(2,1)S(1)}, bf16[160,1024]{1,0:T(8,128)(2,1)S(1)}, u32[]{:S(2)}, u32[]{:S(2)}) collective-permute-start(bf16[160,1024]{1,0:T(8,128)(2,1)S(1)} %copy-done.15), channel_id=1, source_target_pairs={{0,1},{1,2},{2,3},{3,0},{4,5},{5,6},{6,7},{7,4},{8,9},{9,10},{10,1... | collective-permute-start | bytes 983048 | tf_op jit(solution)/shard_map/ppermute | solution.py:1070
  470.7 30.1 %collective-permute-start.40 = (bf16[160,1024]{1,0:T(8,128)(2,1)S(1)}, bf16[160,1024]{1,0:T(8,128)(2,1)S(1)}, u32[]{:S(2)}, u32[]{:S(2)}) collective-permute-start(bf16[160,1024]{1,0:T(8,128)(2,1)S(1)} %copy-done.15), channel_id=1, source_target_pairs={{0,2},{1,3},{2,0},{3,1},{4,6},{5,7},{6,4},{7,5},{8,10},{9,11},{10,... | collective-permute-start | bytes 983048 | tf_op jit(solution)/shard_map/ppermute | solution.py:1070
  485.2 16.9 %collective-permute-start.41 = (bf16[160,1024]{1,0:T(8,128)(2,1)S(1)}, bf16[160,1024]{1,0:T(8,128)(2,1)S(1)}, u32[]{:S(2)}, u32[]{:S(2)}) collective-permute-start(bf16[160,1024]{1,0:T(8,128)(2,1)S(1)} %copy-done.15), channel_id=1, source_target_pairs={{0,3},{1,0},{2,1},{3,2},{4,7},{5,4},{6,5},{7,6},{8,11},{9,8},{10,9... | collective-permute-start | bytes 983048 | tf_op jit(solution)/shard_map/ppermute | solution.py:1070
  496.1 23.4 %collective-permute-start.51 = (bf16[64,2048]{1,0:T(8,128)(2,1)S(1)}, bf16[64,2048]{1,0:T(8,128)(2,1)S(1)}, u32[]{:S(2)}, u32[]{:S(2)}) collective-permute-start(bf16[64,2048]{1,0:T(8,128)(2,1)S(1)} %copy-done.67), channel_id=1, source_target_pairs={{0,16},{4,20},{8,24},{12,28},{16,0},{20,4},{24,8},{28,12},{1,17},{... | collective-permute-start | bytes 786440 | tf_op jit(solution)/shard_map/ppermute | solution.py:1059
  500.8 18.7 %collective-permute-start.52 = (bf16[64,2048]{1,0:T(8,128)(2,1)S(1)}, bf16[64,2048]{1,0:T(8,128)(2,1)S(1)}, u32[]{:S(2)}, u32[]{:S(2)}) collective-permute-start(bf16[64,2048]{1,0:T(8,128)(2,1)S(1)} %copy-done.66), channel_id=1, source_target_pairs={{0,8},{4,12},{8,0},{12,4},{16,24},{20,28},{24,16},{28,20},{1,9},{5... | collective-permute-start | bytes 786440 | tf_op jit(solution)/shard_map/ppermute | solution.py:1059
  523.1 110.7 %all-reduce.2.cloned.1.call-start = ((), (), s32[]{:S(2)}) async-start(), calls=%async_computation.7 | async-start | bytes 3162112 | tf_op jit(solution)/shard_map/psum | solution.py:1265
  523.9 15.9 %collective-permute-start.54 = (bf16[144,512]{1,0:T(8,128)(2,1)}, bf16[144,512]{1,0:T(8,128)(2,1)S(1)}, u32[]{:S(2)}, u32[]{:S(2)}) collective-permute-start(bf16[144,512]{1,0:T(8,128)(2,1)} %kv_back.1.refs_4_), channel_id=1, source_target_pairs={{0,2},{1,3},{2,0},{3,1},{4,6},{5,7},{6,4},{7,5},{8,10},{9,11},{10,... | collective-permute-start | bytes 442376 | tf_op jit(solution)/shard_map/ppermute | solution.py:1070
  527.0 24.7 %collective-permute-start.56 = (bf16[2,16,1024]{2,1,0:T(8,128)(2,1)S(1)}, bf16[2,16,1024]{2,1,0:T(8,128)(2,1)S(1)}, u32[]{:S(2)}, u32[]{:S(2)}) collective-permute-start(bf16[2,16,1024]{2,1,0:T(8,128)(2,1)S(1)} %copy-done.72), channel_id=1, source_target_pairs={{0,1},{1,2},{2,3},{3,0},{4,5},{5,6},{6,7},{7,4},{8,9},{9,10},{10,1... | collective-permute-start | bytes 196616 | tf_op jit(solution)/shard_map/ppermute | solution.py:1070
  528.8 22.8 %collective-permute-start.57 = (bf16[2,16,1024]{2,1,0:T(8,128)(2,1)S(1)}, bf16[2,16,1024]{2,1,0:T(8,128)(2,1)S(1)}, u32[]{:S(2)}, u32[]{:S(2)}) collective-permute-start(bf16[2,16,1024]{2,1,0:T(8,128)(2,1)S(1)} %copy-done.71), channel_id=1, source_target_pairs={{0,2},{1,3},{2,0},{3,1},{4,6},{5,7},{6,4},{7,5},{8,10},{9,11},{10,... | collective-permute-start | bytes 196616 | tf_op jit(solution)/shard_map/ppermute | solution.py:1070
  528.9 22.8 %collective-permute-start.58 = (bf16[2,16,1024]{2,1,0:T(8,128)(2,1)S(1)}, bf16[2,16,1024]{2,1,0:T(8,128)(2,1)S(1)}, u32[]{:S(2)}, u32[]{:S(2)}) collective-permute-start(bf16[2,16,1024]{2,1,0:T(8,128)(2,1)S(1)} %copy-done.70), channel_id=1, source_target_pairs={{0,3},{1,0},{2,1},{3,2},{4,7},{5,4},{6,5},{7,6},{8,11},{9,8},{10,9... | collective-permute-start | bytes 196616 | tf_op jit(solution)/shard_map/ppermute | solution.py:1070
  554.6 27.8 %collective-permute-start.59 = (bf16[144,2048]{1,0:T(8,128)(2,1)S(1)}, bf16[144,2048]{1,0:T(8,128)(2,1)S(1)}, u32[]{:S(2)}, u32[]{:S(2)}) collective-permute-start(bf16[144,2048]{1,0:T(8,128)(2,1)S(1)} %copy-done.8), channel_id=1, source_target_pairs={{0,1},{1,2},{2,3},{3,0},{4,5},{5,6},{6,7},{7,4},{8,9},{9,10},{10,1... | collective-permute-start | bytes 1769480 | tf_op jit(solution)/shard_map/ppermute | solution.py:1070
  554.6 54.9 %collective-permute-start.60 = (bf16[144,2048]{1,0:T(8,128)(2,1)S(1)}, bf16[144,2048]{1,0:T(8,128)(2,1)S(1)}, u32[]{:S(2)}, u32[]{:S(2)}) collective-permute-start(bf16[144,2048]{1,0:T(8,128)(2,1)S(1)} %copy-done.8), channel_id=1, source_target_pairs={{0,2},{1,3},{2,0},{3,1},{4,6},{5,7},{6,4},{7,5},{8,10},{9,11},{10,... | collective-permute-start | bytes 1769480 | tf_op jit(solution)/shard_map/ppermute | solution.py:1070
  558.6 51.3 %collective-permute-start.61 = (bf16[144,2048]{1,0:T(8,128)(2,1)S(1)}, bf16[144,2048]{1,0:T(8,128)(2,1)S(1)}, u32[]{:S(2)}, u32[]{:S(2)}) collective-permute-start(bf16[144,2048]{1,0:T(8,128)(2,1)S(1)} %copy-done.8), channel_id=1, source_target_pairs={{0,3},{1,0},{2,1},{3,2},{4,7},{5,4},{6,5},{7,6},{8,11},{9,8},{10,9... | collective-permute-start | bytes 1769480 | tf_op jit(solution)/shard_map/ppermute | solution.py:1070
  560.0 20.4 %collective-permute-start.62 = (bf16[2,64,1024]{2,1,0:T(8,128)(2,1)}, bf16[2,64,1024]{2,1,0:T(8,128)(2,1)S(1)}, u32[]{:S(2)}, u32[]{:S(2)}) collective-permute-start(bf16[2,64,1024]{2,1,0:T(8,128)(2,1)} %pack_up.1.refs_0_), channel_id=1, source_target_pairs={{0,4},{4,0},{8,12},{12,8},{16,20},{20,16},{24,28},{28,24},{1,5},{5... | collective-permute-start | bytes 786440 | tf_op jit(solution)/shard_map/ppermute | solution.py:1059
  561.6 20.1 %collective-permute-start.63 = (bf16[2,64,1024]{2,1,0:T(8,128)(2,1)}, bf16[2,64,1024]{2,1,0:T(8,128)(2,1)S(1)}, u32[]{:S(2)}, u32[]{:S(2)}) collective-permute-start(bf16[2,64,1024]{2,1,0:T(8,128)(2,1)} %pack_up.1.refs_0_), channel_id=1, source_target_pairs={{0,8},{4,12},{8,0},{12,4},{16,24},{20,28},{24,16},{28,20},{1,9},{5... | collective-permute-start | bytes 786440 | tf_op jit(solution)/shard_map/ppermute | solution.py:1059
  580.4 43.9 %collective-permute-start.64 = (bf16[2,64,1024]{2,1,0:T(8,128)(2,1)S(1)}, bf16[2,64,1024]{2,1,0:T(8,128)(2,1)S(1)}, u32[]{:S(2)}, u32[]{:S(2)}) collective-permute-start(bf16[2,64,1024]{2,1,0:T(8,128)(2,1)S(1)} %copy-done.20), channel_id=1, source_target_pairs={{0,12},{4,8},{8,4},{12,0},{16,28},{20,24},{24,20},{28,16},{1,13},{... | collective-permute-start | bytes 786440 | tf_op jit(solution)/shard_map/ppermute | solution.py:1059
  581.7 42.5 %collective-permute-start.65 = (bf16[2,64,1024]{2,1,0:T(8,128)(2,1)S(1)}, bf16[2,64,1024]{2,1,0:T(8,128)(2,1)}, u32[]{:S(2)}, u32[]{:S(2)}) collective-permute-start(bf16[2,64,1024]{2,1,0:T(8,128)(2,1)S(1)} %copy-done.20), channel_id=1, source_target_pairs={{0,16},{4,20},{8,24},{12,28},{16,0},{20,4},{24,8},{28,12},{1,17},{... | collective-permute-start | bytes 786440 | tf_op jit(solution)/shard_map/ppermute | solution.py:1059
  582.4 41.9 %collective-permute-start.66 = (bf16[2,64,1024]{2,1,0:T(8,128)(2,1)S(1)}, bf16[2,64,1024]{2,1,0:T(8,128)(2,1)}, u32[]{:S(2)}, u32[]{:S(2)}) collective-permute-start(bf16[2,64,1024]{2,1,0:T(8,128)(2,1)S(1)} %copy-done.20), channel_id=1, source_target_pairs={{0,20},{4,16},{8,28},{12,24},{16,4},{20,0},{24,12},{28,8},{1,21},{... | collective-permute-start | bytes 786440 | tf_op jit(solution)/shard_map/ppermute | solution.py:1059
  609.9 19.4 %collective-permute-start.68 = (bf16[2,64,1024]{2,1,0:T(8,128)(2,1)S(1)}, bf16[2,64,1024]{2,1,0:T(8,128)(2,1)S(1)}, u32[]{:S(2)}, u32[]{:S(2)}) collective-permute-start(bf16[2,64,1024]{2,1,0:T(8,128)(2,1)S(1)} %copy-done.20), channel_id=1, source_target_pairs={{0,28},{4,24},{8,20},{12,16},{16,12},{20,8},{24,4},{28,0},{1,29},{... | collective-permute-start | bytes 786440 | tf_op jit(solution)/shard_map/ppermute | solution.py:1059
  (102 other events, 992.6 us)
Sparse Core Ops, SparseCore 0:
  18.0 38.4 all-gather.7
  90.4 58.5 reduce-scatter.2
  152.5 49.2 all-gather.9
  231.6 48.3 reduce-scatter.4
  283.8 49.2 all-gather.11
  366.5 113.4 all-gather.13
  523.2 38.0 all-gather.15
  565.2 65.7 all-reduce.1

commit v4 on v3

--- a/solution.py
+++ b/solution.py
@@ -870,28 +870,43 @@
     return call(pack_up_kernel, [((2, rows * len(ups), cols), BF)], ups, "pack_up", prefetch=info)[0]
 
 
-def layer_kernel(info_ref, residual_ref, *refs):
-    parts, out_ref = refs[:-1], refs[-1]
-    out_ref[...] = (residual_ref[...] + sum(part[...].astype(F32) for part in parts)).astype(BF)
+def layer_kernel(info_ref, residual_ref, feed_ref, left_ref, right_ref):
+    half = left_ref.shape[1]
+    out = (residual_ref[...] + feed_ref[...].astype(F32)).astype(BF)
+    left_ref[...] = out[:, :half]
+    right_ref[...] = out[:, half:]
+
+
+def layer_halves(info, residual, feed):
+    rows, model = residual.shape
+    return call(
+        layer_kernel, [((rows, model // 2), BF)] * 2, (residual, feed), "layer", prefetch=info
+    )
 
 
 def place_kernel(info_ref, *refs):
-    parts, out_ref = refs[:-1], refs[-1]
-    for s, part in enumerate(parts):
-        pl.when(pl.program_id(0) == s)(lambda part=part: out_ref.__setitem__(..., part[...]))
-
-
-def place(info, parts):
-    rows, cols = parts[0].shape
-    ranks = len(parts)
+    out_ref = refs[-1]
+    half = out_ref.shape[1] // 2
+    for s in range(len(refs) // 2):
+
+        @pl.when(pl.program_id(0) == s)
+        def _(s=s):
+            out_ref[:, :half] = refs[2 * s][...]
+            out_ref[:, half:] = refs[2 * s + 1][...]
+
+
+def place(info, lefts, rights):
+    rows, cols = lefts[0].shape
+    ranks = len(lefts)
+    parts = [part for pair in zip(lefts, rights) for part in pair]
     return call(
         place_kernel,
-        [((ranks * rows, cols), BF)],
+        [((ranks * rows, 2 * cols), BF)],
         parts,
         "place",
         grid=(ranks,),
-        in_specs=[once((rows, cols), lambda i, w: (0, 0))] * ranks,
-        out_specs=[pl.BlockSpec((rows, cols), lambda i, w: (behind(w, i, ranks), 0))],
+        in_specs=[once((rows, cols), lambda i, w: (0, 0))] * len(parts),
+        out_specs=[pl.BlockSpec((rows, 2 * cols), lambda i, w: (behind(w, i, ranks), 0))],
         prefetch=info,
     )[0]
 
@@ -1193,7 +1208,7 @@
     hidden_low, grad_both, grad_mid_part = after((hidden_low, grad_both, grad_mid_part), downs)
     grad_mid = lax.psum_scatter(grad_mid_part, "rank", scatter_dimension=0, tiled=True)
     both_pair, hidden_pair = swap(grad_both, 0), swap(hidden_low, 0)
-    feed_parts = matmul(info, hidden_low, down_weight, parts=ranks)
+    feed_part = matmul(info, hidden_low, down_weight)
     feed_width = gate_weight.shape[1]
     send_first, send_last, keep_first, keep_last = pair_products(
         info,
@@ -1214,25 +1229,35 @@
     last, first = both(arrays[1], arrays[0])
     grad_branch = after(grad_branch, arrays[0])
     grad_attn = matmul(info, grad_branch, out_weight, True)
-    branch_pair = swap(grad_branch, 0)
+    third = row_count // 3
+    branch_pair = jnp.concatenate(
+        [swap(grad_branch[i * third : (i + 1) * third], 0) for i in range(3)], 0
+    )
     outs = pair_products(info, [(attn_low, attn_pair, grad_branch, branch_pair)], up_cols)
     feed_piece = fold_last(info, (arrays[2], first, arrays[3], last), 4)
     feed_whole = lax.all_gather(feed_piece, "seq", axis=0, tiled=False)
-    feed_sums = rings(after(feed_parts, grad_branch))
+    feed_sum = lax.psum_scatter(
+        after(feed_part, arrays[0]), "rank", scatter_dimension=0, tiled=True
+    )
     first, last = both(outs[0], outs[1])
     grad_query, near, far = attend_back(
         in_order(info), query, grad_attn, attn_vals, log_total, cosine, sine, kv_all,
         start_rows, index_rows, True,
     )
-    grad_query, near, far = after((grad_query, near, far), feed_sums, first, last)
+    (grad_query, near, far), feed_sum = lax.optimization_barrier(
+        (after((grad_query, near, far), first, last), feed_sum)
+    )
     Order.last = grad_query
 
-    latent_grads = rings(latent_parts(info, grad_query, up_own, up_other, ranks))
-    query_pair = swap(grad_query, 0)
-    arrays = fold_near(info, near, swap(far, 0))
-    kv_first, kv_last = both(arrays[0], arrays[1])
+    far, query_pair = swap(far, 0), swap(grad_query, 0)
     outs = [two(array) for array in (outs[2], first, outs[3], last)]
     outs = fold_first(info, outs, 1)
+    last, first = both(outs[1], outs[0])
+    latent_grads = rings(latent_parts(info, grad_query, up_own, up_other, ranks))
+    arrays = fold_near(info, near, far)
+    out_piece = fold_last(info, (outs[2], first, outs[3], last), 1)
+    out_whole = lax.all_gather(out_piece, "seq", axis=0, tiled=False)
+    kv_first, kv_last = both(*after(arrays[:2], out_piece))
     ups = pair_products(info, [(latent_cut, latent_pair, grad_query, query_pair)], up_cols)
     wait(latent_grads, kv_first, kv_last)
 
@@ -1240,21 +1265,16 @@
     latent_blocks = rings([latent_own] * ranks)
     arrays = fold_first(info, (arrays[2], kv_first, arrays[3], kv_last), 1)
     kv_last, kv_first = both(arrays[1], arrays[0])
-    last, first = both(*in_order((outs[1], outs[0])))
     kv_sums = rings(fold_kv(info, (arrays[2], kv_first, arrays[3], kv_last), ranks))
     ups_first, ups_last = both(*in_order(ups[:2]))
     ups = fold_first(info, [two(array) for array in (ups[2], ups_first, ups[3], ups_last)], 1)
     ups_last, ups_first = both(ups[1], ups[0])
-    layer_own = call(
-        layer_kernel, [(residual.shape, BF)], (residual, *feed_sums), "layer", prefetch=info
-    )[0]
+    layer_left, layer_right = layer_halves(info, residual, feed_sum)
     joined, *latent_blocks = lax.optimization_barrier((info, *latent_blocks))
 
     ups = rings(fold_up(joined, (ups[2], ups_first, ups[3], ups_last), ranks))
     kv_own = kv_back(info, cosine, sine, kv_sums)
     kv_blocks = rings([kv_own] * ranks)
-    out_piece = fold_last(info, (outs[2], first, outs[3], last), 1)
-    out_whole = lax.all_gather(out_piece, "seq", axis=0, tiled=False)
     wait(kv_blocks)
 
     grad_in, small, latent_cols, grad_kv = input_back(
@@ -1264,15 +1284,16 @@
     last = last_products(info, normed_low, latent_cols, grad_kv, small, ranks)
     last = lax.psum(last, "seq")
     up_piece = pack_up(info, ups)
-    layer_blocks = rings([in_order(layer_own)] * ranks)
+    lefts = rings([in_order(layer_left)] * ranks)
     up_pieces = [up_piece] + [exchange(in_order(up_piece), mask) for mask in (1, 2)]
     shape = gate_weight.shape
     grad_gate, grad_up, grad_down = unpack(
         info, feed_whole, store_feed, (shape, shape, shape[::-1]), (0, 0, 1)
     )
+    rights = rings([in_order(layer_right)] * ranks)
     up_pieces += [exchange(in_order(up_piece), mask) for mask in range(3, 8)]
     grad_out = unpack(info, out_whole, store_same, [out_weight.shape], [0])[0]
-    layer_out = place(info, layer_blocks)
+    layer_out = place(info, lefts, rights)
     grad_q_up = unpack_up(info, up_pieces, q_up.shape)
     grad_q_down, grad_kv_weight, small = call(
         last_kernel,

time: 658 us -> 647 us (0.983)
  waiting for transfers between devices: 291 us -> 253 us
  starting transfers between devices: 68.4 us -> 90.7 us
    ppermute x27, waiting for transfers between devices: 107 us -> 62.7 us  [ring(): lax.ppermute(value, 'rank', [(i, (i + shift) % ranks) for i in range(rank...]
    ppermute x42 -> x44, starting transfers between devices: 40.9 us -> 65.1 us  [exchange(): return lax.ppermute(value, 'seq', [(i, i ^ mask) for i in range(count)])]
    ppermute x42 -> x44, waiting for transfers between devices: 66.1 us -> 71.5 us  [exchange(): return lax.ppermute(value, 'seq', [(i, i ^ mask) for i in range(count)])]
    unnamed x150 -> x148, local copies, waits for them, and re-layouts: 22.6 us -> 21.4 us
  transfers between devices with their start and end apart: 77 -> 80, of which waited for: 24 -> 23; matrix products, arithmetic and copies ran while one was open for 3% -> 4% of each run, Pallas kernels for 30% -> 31%
where the time goes in v4:
time: 647 us; the launch traced here: 637 us
  waiting for transfers between devices  253 us (39%)
  Pallas kernels  229 us (35%)
  starting transfers between devices  90.7 us (14%)
  local copies, waits for them, and re-layouts  35.6 us (6%)
  between operations  15 us (2%)
  matrix products  6.98 us (1%)
  other arithmetic  6.52 us (1%)
    pallas_call x22, Pallas kernels, placed_call(): pl.pallas_call(kernel, grid_spec=pltpu.PrefetchScalarGridSpec(num_scalar_...  142 us
    ppermute x44, waiting for transfers between devices, exchange(): return lax.ppermute(value, 'seq', [(i, i ^ mask) for i in range(count)])  71.5 us
    ppermute x44, starting transfers between devices, exchange(): return lax.ppermute(value, 'seq', [(i, i ^ mask) for i in range(count)])  65.1 us
    ppermute x27, waiting for transfers between devices, ring(): lax.ppermute(value, 'rank', [(i, (i + shift) % ranks) for i in range(rank...  62.7 us
    all_gather x1, waiting for transfers between devices, per_device_fast(): mid_low = lax.all_gather(mid_own, 'rank', axis=0, tiled=True)  49.4 us
    reduce_scatter x1, waiting for transfers between devices, per_device_fast(): lax.psum_scatter(branch_part, 'rank', scatter_dimension=0, tiled=True)  46.6 us
    pallas_call x10, Pallas kernels, placed_call(): pl.pallas_call(kernel, in_specs=[pl.BlockSpec(memory_space=pltpu.SMEM)] +...  31.9 us
    ppermute x27, starting transfers between devices, ring(): lax.ppermute(value, 'rank', [(i, (i + shift) % ranks) for i in range(rank...  24.5 us
  transfers between devices with their start and end apart: 80, of which 23 were waited for; matrix products, arithmetic and copies ran while one was open for 4% of the time, Pallas kernels for 31%

profile of v4, /device:TPU:25, one launch (start us, length us, event | category | flops | bytes accessed | tf_op | source)
XLA Modules:
  0.0 636.9 jit_solution(14813832324734958751)
XLA Ops:
  10.7 7.2 %project.1 = (bf16[576,2048]{1,0:T(8,128)(2,1)}, f32[576,128]{1,0:T(8,128)}, f32[576,512]{1,0:T(8,128)}, bf16[592,256]{1,0:T(8,128)(2,1)}) custom-call(s32[6]{0:T(128)} %stack.29.info_ref, bf16[576,2048]{1,0:T(8,128)(2,1)} %tokens_ref.4, f32[1,2048]{1,0:T(1,128)} %bitcast.48, bf16[2048,256]{1,0:T(8,128)(2,1)} %down_ref.1, bf16[2048,512]{1,0:T(8,128)(2,1)} %kv_weight_ref.3, ...), custom_call_target="tpu_custom_call" | custom-call | tf_op jit(solution)/shard_map/project/pallas_call | solution.py:376
  26.6 15.4 %collective-permute-done.1 = bf16[256,512]{1,0:T(8,128)(2,1)S(1)} collective-permute-done((bf16[256,512]{1,0:T(8,128)(2,1)S(1)}, bf16[256,512]{1,0:T(8,128)(2,1)S(1)}, u32[]{:S(2)}, u32[]{:S(2)}) %collective-permute-start.1) | collective-permute-done | bytes 262176 | tf_op jit(solution)/shard_map/ppermute | solution.py:1085
  43.8 3.9 collective-permute-start.3
  51.8 4.8 collective-permute-done.6.refs_3_
  62.2 5.1 queries.1
  68.2 15.8 %attend.1 = (bf16[2304,256]{1,0:T(8,128)(2,1)}, f32[576,1024]{1,0:T(8,128)}, bf16[576,1024]{1,0:T(8,128)(2,1)}, f32[1,2304]{1,0:T(1,128)}, bf16[4608,512]{1,0:T(8,128)(2,1)}) custom-call(s32[6]{0:T(128)} %stack.28.info_ref, f32[576,1024]{1,0:T(8,128)} %get-tuple-element.170.pre_ref, f32[576,128]{1,0:T(8,128)} %get-tuple-element.324.cos_ref, ...), custom_call_target="tpu_custom_call" | custom-call | tf_op jit(solution)/shard_map/attend/pallas_call | solution.py:169
  83.9 6.4 %matmul.3 = bf16[576,2048]{1,0:T(8,128)(2,1)} custom-call(s32[6]{0:T(128)} %stack.28.info_ref, bf16[576,1024]{1,0:T(8,128)(2,1)} %get-tuple-element.173.left_ref.refs_0_, bf16[1024,2048]{1,0:T(8,128)(2,1)} %right_ref.5), custom_call_target="tpu_custom_call" | custom-call | tf_op jit(solution)/shard_map/matmul/pallas_call | solution.py:376
  95.4 7.0 %fusion.2.grad_ref = f32[576,1408]{1,0:T(8,128)S(1)} fusion(bf16[576,2048]{1,0:T(8,128)(2,1)} %out_grad_ref.1, bf16[1408,2048]{1,0:T(8,128)(2,1)} %right_ref.4), kind=kOutput, calls=%fused_computation.20 | convolution fusion | flops 3321888768 | bytes 11370496 | tf_op jit(solution)/shard_map/dot_general | solution.py:46
  102.4 46.6 %reduce-scatter.4.cloned.1.call-done.branch_ref = bf16[144,2048]{1,0:T(8,128)(2,1)} async-done(((bf16[576,2048]{1,0:T(8,128)(2,1)}), bf16[144,2048]{1,0:T(8,128)(2,1)}) %reduce-scatter.4.cloned.1.call-update) | async-done | bytes 589840 | tf_op jit(solution)/shard_map/reduce_scatter | solution.py:1181
  149.1 3.3 mid_norm.1
  152.5 49.4 %all-gather.10.cloned.1.call-done.mid_ref.refs_0_ = bf16[576,2048]{1,0:T(8,128)(2,1)} async-done(((bf16[144,2048]{1,0:T(8,128)(2,1)}), bf16[576,2048]{1,0:T(8,128)(2,1)}) %all-gather.10.cloned.1.call-update) | async-done | bytes 2359312 | tf_op jit(solution)/shard_map/all_gather | solution.py:1200
  206.2 19.7 %feed_forward.1 = (bf16[576,1408]{1,0:T(8,128)(2,1)S(1)}, bf16[576,2816]{1,0:T(8,128)(2,1)S(1)}, bf16[576,2048]{1,0:T(8,128)(2,1)S(1)}) custom-call(bf16[576,2048]{1,0:T(8,128)(2,1)S(1)} %copy-done, f32[576,1408]{1,0:T(8,128)S(1)} %fusion.2.grad_ref, bf16[2048,1408]{1,0:T(8,128)(2,1)} %gate_ref.1, bf16[2048,1408]{1,0:T(8,128)(2,1)} %up_ref.1), custom_call_target="tpu_custom_call" | custom-call | flops 2000000000 | tf_op jit(solution)/shard_map/feed_forward/pallas_call | solution.py:322
  233.1 8.0 %matmul.4 = bf16[576,2048]{1,0:T(8,128)(2,1)} custom-call(s32[6]{0:T(128)} %stack.28.info_ref, bf16[576,1408]{1,0:T(8,128)(2,1)} %copy-done.2, bf16[1408,2048]{1,0:T(8,128)(2,1)} %right_ref.4), custom_call_target="tpu_custom_call" | custom-call | tf_op jit(solution)/shard_map/matmul/pallas_call | solution.py:376
  242.8 22.1 %pair_products.3 = (bf16[256,4224]{1,0:T(8,128)(2,1)}, bf16[256,4224]{1,0:T(8,128)(2,1)}, bf16[256,4224]{1,0:T(8,128)(2,1)}, bf16[256,4224]{1,0:T(8,128)(2,1)}) custom-call(s32[6]{0:T(128)} %stack.28.info_ref, bf16[576,2048]{1,0:T(8,128)(2,1)} %all-gather.10.cloned.1.call-done.mid_ref.refs_0_, bf16[576,2048]{1,0:T(8,128)(2,1)} %collective-permute-done.19.refs_1_, ...), custom_call_target="tpu_custom_call" | custom-call | tf_op jit(solution)/shard_map/pair_products/pallas_call | solution.py:376
  267.3 12.8 %reduce-scatter.6.cloned.1.call-done.grad_ref = bf16[144,2048]{1,0:T(8,128)(2,1)} async-done(((bf16[576,2048]{1,0:T(8,128)(2,1)}), bf16[144,2048]{1,0:T(8,128)(2,1)}) %reduce-scatter.6.cloned.1.call-update) | async-done | bytes 589840 | tf_op jit(solution)/shard_map/reduce_scatter | solution.py:1209
  280.1 3.7 mid_back.1
  283.8 29.7 %collective-permute-done.22 = bf16[256,4224]{1,0:T(8,128)(2,1)S(1)} collective-permute-done((bf16[256,4224]{1,0:T(8,128)(2,1)}, bf16[256,4224]{1,0:T(8,128)(2,1)S(1)}, u32[]{:S(2)}, u32[]{:S(2)}) %collective-permute-start.22) | collective-permute-done | bytes 2162720 | tf_op jit(solution)/shard_map/ppermute | solution.py:1074
  314.9 6.7 %fold_first.4 = (bf16[128,4224]{1,0:T(8,128)(2,1)}, bf16[128,4224]{1,0:T(8,128)(2,1)}, bf16[128,4224]{1,0:T(8,128)(2,1)}, bf16[128,4224]{1,0:T(8,128)(2,1)}) custom-call(s32[6]{0:T(128)} %stack.28.info_ref, bf16[2,128,4224]{2,1,0:T(8,128)(2,1)} %bitcast.54, bf16[2,128,4224]{2,1,0:T(8,128)(2,1)} %bitcast.56, bf16[2,128,4224]{2,1,0:T(8,128)(2,1)} %bitcast.55, ...), custom_call_target="tpu_custom_call" | custom-call | flops 999999995904 | tf_op jit(solution)/shard_map/fold_first/pallas_call | solution.py:376
  324.2 9.0 %all-gather.12.cloned.1.call-done.left_ref.refs_2_.branch_ref = bf16[576,2048]{1,0:T(8,128)(2,1)} async-done(((bf16[144,2048]{1,0:T(8,128)(2,1)}), bf16[576,2048]{1,0:T(8,128)(2,1)}) %all-gather.12.cloned.1.call-update) | async-done | bytes 2359312 | tf_op jit(solution)/shard_map/all_gather | solution.py:1223
  336.2 6.6 %matmul.5.grad_ref = bf16[576,1024]{1,0:T(8,128)(2,1)} custom-call(s32[6]{0:T(128)} %stack.28.info_ref, bf16[576,2048]{1,0:T(8,128)(2,1)} %all-gather.12.cloned.1.call-done.left_ref.refs_2_.branch_ref, bf16[1024,2048]{1,0:T(8,128)(2,1)} %right_ref.5), custom_call_target="tpu_custom_call" | custom-call | tf_op jit(solution)/shard_map/matmul/pallas_call | solution.py:376
  344.5 7.5 %pair_products.4 = (bf16[128,2048]{1,0:T(8,128)(2,1)}, bf16[128,2048]{1,0:T(8,128)(2,1)}, bf16[128,2048]{1,0:T(8,128)(2,1)}, bf16[128,2048]{1,0:T(8,128)(2,1)}) custom-call(s32[6]{0:T(128)} %stack.28.info_ref, bf16[576,1024]{1,0:T(8,128)(2,1)} %get-tuple-element.173.left_ref.refs_0_, bf16[576,1024]{1,0:T(8,128)(2,1)} %collective-permute-done.14.refs_1_, ...), custom_call_target="tpu_custom_call" | custom-call | tf_op jit(solution)/shard_map/pair_products/pallas_call | solution.py:376
  353.4 5.2 fold_last.2
  362.8 19.5 %attend_back.1 = (bf16[576,1024]{1,0:T(8,128)(2,1)}, bf16[2,4,288,512]{3,2,1,0:T(8,128)(2,1)}, bf16[2,4,288,512]{3,2,1,0:T(8,128)(2,1)}) custom-call(s32[6]{0:T(128)} %stack.28.info_ref, bf16[2304,256]{1,0:T(8,128)(2,1)} %get-tuple-element.213.query_ref, bf16[576,1024]{1,0:T(8,128)(2,1)} %matmul.5.grad_ref, f32[576,1024]{1,0:T(8,128)} %get-tuple-element.214.out_ref, ...), custom_call_target="tpu_custom_call" | custom-call | tf_op jit(solution)/shard_map/attend_back/pallas_call | solution.py:271
  384.0 3.3 fold_first.5
  387.3 13.3 %collective-permute-start.32 = (bf16[64,2048]{1,0:T(8,128)(2,1)}, bf16[64,2048]{1,0:T(8,128)(2,1)S(1)}, u32[]{:S(2)}, u32[]{:S(2)}) collective-permute-start(bf16[64,2048]{1,0:T(8,128)(2,1)} %get-tuple-element.229), channel_id=1, source_target_pairs={{0,16},{4,20},{8,24},{12,28},{16,0},{20,4},{24,8},{28,12},{1,17},{... | collective-permute-start | bytes 786440 | tf_op jit(solution)/shard_map/ppermute | solution.py:1074
  400.6 8.0 %collective-permute-start.33 = (bf16[64,2048]{1,0:T(8,128)(2,1)}, bf16[64,2048]{1,0:T(8,128)(2,1)S(1)}, u32[]{:S(2)}, u32[]{:S(2)}) collective-permute-start(bf16[64,2048]{1,0:T(8,128)(2,1)} %get-tuple-element.239), channel_id=1, source_target_pairs={{0,8},{4,12},{8,0},{12,4},{16,24},{20,28},{24,16},{28,20},{1,9},{5... | collective-permute-start | bytes 786440 | tf_op jit(solution)/shard_map/ppermute | solution.py:1074
  408.6 4.4 latent_parts.1
  414.4 5.4 fold_near.1
  430.6 5.5 pair_products.5
  436.1 19.0 %collective-permute-done.36.refs_2_ = bf16[144,1024]{1,0:T(8,128)(2,1)S(1)} collective-permute-done((bf16[144,1024]{1,0:T(8,128)(2,1)S(1)}, bf16[144,1024]{1,0:T(8,128)(2,1)S(1)}, u32[]{:S(2)}, u32[]{:S(2)}) %collective-permute-start.36) | collective-permute-done | bytes 294944 | tf_op jit(solution)/shard_map/ppermute | solution.py:1085
  456.0 3.2 latent_back.1.refs_0_
  459.3 3.7 fold_first.6
  467.4 10.6 %collective-permute-done.43.got_first = bf16[288,512]{1,0:T(8,128)(2,1)S(1)} collective-permute-done((bf16[288,512]{1,0:T(8,128)(2,1)}, bf16[288,512]{1,0:T(8,128)(2,1)S(1)}, u32[]{:S(2)}, u32[]{:S(2)}) %collective-permute-start.43) | collective-permute-done | bytes 294944 | tf_op jit(solution)/shard_map/ppermute | solution.py:1074
  482.6 12.5 %collective-permute-done.45 = bf16[128,1024]{1,0:T(8,128)(2,1)S(1)} collective-permute-done((bf16[128,1024]{1,0:T(8,128)(2,1)S(1)}, bf16[128,1024]{1,0:T(8,128)(2,1)S(1)}, u32[]{:S(2)}, u32[]{:S(2)}) %collective-permute-start.45) | collective-permute-done | bytes 262176 | tf_op jit(solution)/shard_map/ppermute | solution.py:1074
  511.6 2.9 collective-permute-start.52
  518.4 9.7 %collective-permute-done.53.refs_6_ = bf16[144,512]{1,0:T(8,128)(2,1)S(1)} collective-permute-done((bf16[144,512]{1,0:T(8,128)(2,1)}, bf16[144,512]{1,0:T(8,128)(2,1)S(1)}, u32[]{:S(2)}, u32[]{:S(2)}) %collective-permute-start.53) | collective-permute-done | bytes 147488 | tf_op jit(solution)/shard_map/ppermute | solution.py:1085
  528.8 6.6 %input_back.1 = (f32[576,512]{1,0:T(8,128)}, bf16[16,256]{1,0:T(8,128)(2,1)}, bf16[576,256]{1,0:T(8,128)(2,1)}, bf16[576,512]{1,0:T(8,128)(2,1)}) custom-call(s32[6]{0:T(128)} %stack.28.info_ref, bf16[576,2048]{1,0:T(8,128)(2,1)} %tokens_ref.4, bf16[576,2048]{1,0:T(8,128)(2,1)} %all-gather.12.cloned.1.call-done.left_ref.refs_2_.branch_ref, ...), custom_call_target="tpu_custom_call" | custom-call | tf_op jit(solution)/shard_map/input_back/pallas_call | solution.py:376
  535.4 4.6 last_products.1
  542.9 5.3 collective-permute-start.64
  551.4 18.4 %unpack.2 = (f32[2048,1408]{1,0:T(8,128)}, f32[2048,1408]{1,0:T(8,128)}, f32[1408,2048]{1,0:T(8,128)}) custom-call(s32[6]{0:T(128)} %stack.28.info_ref, bf16[4,2,2,128,4224]{4,3,2,1,0:T(8,128)(2,1)} %bitcast.34), custom_call_target="tpu_custom_call" | custom-call | tf_op jit(solution)/shard_map/unpack/pallas_call | solution.py:376
  572.3 3.4 collective-permute-start.66
  581.4 16.3 %collective-permute-done.61.refs_5_ = bf16[144,1024]{1,0:T(8,128)(2,1)S(1)} collective-permute-done((bf16[144,1024]{1,0:T(8,128)(2,1)S(1)}, bf16[144,1024]{1,0:T(8,128)(2,1)S(1)}, u32[]{:S(2)}, u32[]{:S(2)}) %collective-permute-start.61) | collective-permute-done | bytes 294944 | tf_op jit(solution)/shard_map/ppermute | solution.py:1085
  598.3 3.0 collective-permute-start.70
  601.3 6.7 %unpack.3 = f32[1024,2048]{1,0:T(8,128)} custom-call(s32[6]{0:T(128)} %stack.28.info_ref, bf16[4,2,2,64,2048]{4,3,2,1,0:T(8,128)(2,1)} %bitcast.37), custom_call_target="tpu_custom_call" | custom-call | tf_op jit(solution)/shard_map/unpack/pallas_call | solution.py:376
  608.1 4.2 place.1
  612.3 6.1 collective-permute-done.70.refs_7_
  619.2 3.8 unpack_up.1
  623.0 3.2 last.1
  (329 shorter events, 123.6 us)
Async XLA Ops:
  7.2 55.0 %all-gather.8.cloned.1.call-start = ((), (), s32[]{:S(2)}) async-start(), calls=%async_computation.3 | async-start | bytes 1515520 | tf_op jit(solution)/shard_map/all_gather | solution.py:1165
  8.5 18.1 %collective-permute-start = (bf16[256,512]{1,0:T(8,128)(2,1)S(1)}, bf16[256,512]{1,0:T(8,128)(2,1)S(1)}, u32[]{:S(2)}, u32[]{:S(2)}) collective-permute-start(bf16[256,512]{1,0:T(8,128)(2,1)S(1)} %get-tuple-element.316), channel_id=1, source_target_pairs={{0,1},{1,2},{2,3},{3,0},{4,5},{5,6},{6,7},{7,4},{8,9},{9,10},{10,1... | collective-permute-start | bytes 786440 | tf_op jit(solution)/shard_map/ppermute | solution.py:1085
  8.6 33.4 %collective-permute-start.1 = (bf16[256,512]{1,0:T(8,128)(2,1)S(1)}, bf16[256,512]{1,0:T(8,128)(2,1)S(1)}, u32[]{:S(2)}, u32[]{:S(2)}) collective-permute-start(bf16[256,512]{1,0:T(8,128)(2,1)S(1)} %get-tuple-element.318), channel_id=1, source_target_pairs={{0,2},{1,3},{2,0},{3,1},{4,6},{5,7},{6,4},{7,5},{8,10},{9,11},{10,... | collective-permute-start | bytes 786440 | tf_op jit(solution)/shard_map/ppermute | solution.py:1085
  9.9 32.8 %collective-permute-start.2 = (bf16[256,512]{1,0:T(8,128)(2,1)S(1)}, bf16[256,512]{1,0:T(8,128)(2,1)}, u32[]{:S(2)}, u32[]{:S(2)}) collective-permute-start(bf16[256,512]{1,0:T(8,128)(2,1)S(1)} %get-tuple-element.315), channel_id=1, source_target_pairs={{0,3},{1,0},{2,1},{3,2},{4,7},{5,4},{6,5},{7,6},{8,11},{9,8},{10,9... | collective-permute-start | bytes 786440 | tf_op jit(solution)/shard_map/ppermute | solution.py:1085
  17.9 131.2 %reduce-scatter.4.cloned.1.call-start = ((), (), s32[]{:S(2)}) async-start(), calls=%async_computation.4 | async-start | bytes 2949120 | tf_op jit(solution)/shard_map/reduce_scatter | solution.py:1181
  24.2 23.6 %collective-permute-start.4 = (bf16[576,512]{1,0:T(8,128)(2,1)}, bf16[576,512]{1,0:T(8,128)(2,1)S(1)}, u32[]{:S(2)}, u32[]{:S(2)}) collective-permute-start(bf16[576,512]{1,0:T(8,128)(2,1)} %turn.1.refs_0_), channel_id=1, source_target_pairs={{0,8},{4,12},{8,0},{12,4},{16,24},{20,28},{24,16},{28,20},{1,9},{5... | collective-permute-start | bytes 1769480 | tf_op jit(solution)/shard_map/ppermute | solution.py:1074
  25.4 22.4 %collective-permute-start.5 = (bf16[576,512]{1,0:T(8,128)(2,1)}, bf16[576,512]{1,0:T(8,128)(2,1)}, u32[]{:S(2)}, u32[]{:S(2)}) collective-permute-start(bf16[576,512]{1,0:T(8,128)(2,1)} %turn.1.refs_0_), channel_id=1, source_target_pairs={{0,16},{4,20},{8,24},{12,28},{16,0},{20,4},{24,8},{28,12},{1,17},{... | collective-permute-start | bytes 1769480 | tf_op jit(solution)/shard_map/ppermute | solution.py:1074
  90.4 111.5 %all-gather.10.cloned.1.call-start = ((), (), s32[]{:S(2)}) async-start(), calls=%async_computation.5 | async-start | bytes 2949120 | tf_op jit(solution)/shard_map/all_gather | solution.py:1200
  152.4 127.7 %reduce-scatter.6.cloned.1.call-start = ((), (), s32[]{:S(2)}) async-start(), calls=%async_computation.6 | async-start | bytes 2949120 | tf_op jit(solution)/shard_map/reduce_scatter | solution.py:1209
  201.8 28.4 %collective-permute-start.16 = (bf16[512,256]{1,0:T(8,128)(2,1)}, bf16[512,256]{1,0:T(8,128)(2,1)}, u32[]{:S(2)}, u32[]{:S(2)}) collective-permute-start(bf16[512,256]{1,0:T(8,128)(2,1)} %get-tuple-element.186), channel_id=1, source_target_pairs={{0,1},{1,2},{2,3},{3,0},{4,5},{5,6},{6,7},{7,4},{8,9},{9,10},{10,1... | collective-permute-start | bytes 786440 | tf_op jit(solution)/shard_map/ppermute | solution.py:1085
  204.3 26.0 %collective-permute-start.17 = (bf16[512,256]{1,0:T(8,128)(2,1)}, bf16[512,256]{1,0:T(8,128)(2,1)}, u32[]{:S(2)}, u32[]{:S(2)}) collective-permute-start(bf16[512,256]{1,0:T(8,128)(2,1)} %get-tuple-element.187), channel_id=1, source_target_pairs={{0,2},{1,3},{2,0},{3,1},{4,6},{5,7},{6,4},{7,5},{8,10},{9,11},{10,... | collective-permute-start | bytes 786440 | tf_op jit(solution)/shard_map/ppermute | solution.py:1085
  204.3 25.9 %collective-permute-start.18 = (bf16[512,256]{1,0:T(8,128)(2,1)S(1)}, bf16[512,256]{1,0:T(8,128)(2,1)}, u32[]{:S(2)}, u32[]{:S(2)}) collective-permute-start(bf16[512,256]{1,0:T(8,128)(2,1)S(1)} %get-tuple-element.188), channel_id=1, source_target_pairs={{0,3},{1,0},{2,1},{3,2},{4,7},{5,4},{6,5},{7,6},{8,11},{9,8},{10,9... | collective-permute-start | bytes 786440 | tf_op jit(solution)/shard_map/ppermute | solution.py:1085
  231.6 101.6 %all-gather.12.cloned.1.call-start = ((), (), s32[]{:S(2)}) async-start(), calls=%async_computation.7 | async-start | bytes 2949120 | tf_op jit(solution)/shard_map/all_gather | solution.py:1223
  264.9 48.6 %collective-permute-start.22 = (bf16[256,4224]{1,0:T(8,128)(2,1)}, bf16[256,4224]{1,0:T(8,128)(2,1)S(1)}, u32[]{:S(2)}, u32[]{:S(2)}) collective-permute-start(bf16[256,4224]{1,0:T(8,128)(2,1)} %get-tuple-element.192), channel_id=1, source_target_pairs={{0,8},{4,12},{8,0},{12,4},{16,24},{20,28},{24,16},{28,20},{1,9},{5... | collective-permute-start | bytes 6488072 | tf_op jit(solution)/shard_map/ppermute | solution.py:1074
  266.1 48.2 %collective-permute-start.23 = (bf16[256,4224]{1,0:T(8,128)(2,1)}, bf16[256,4224]{1,0:T(8,128)(2,1)}, u32[]{:S(2)}, u32[]{:S(2)}) collective-permute-start(bf16[256,4224]{1,0:T(8,128)(2,1)} %get-tuple-element.202), channel_id=1, source_target_pairs={{0,16},{4,20},{8,24},{12,28},{16,0},{20,4},{24,8},{28,12},{1,17},{... | collective-permute-start | bytes 6488072 | tf_op jit(solution)/shard_map/ppermute | solution.py:1074
  283.8 99.7 %reduce-scatter.8.cloned.1.call-start = ((), (), s32[]{:S(2)}) async-start(), calls=%async_computation.8 | async-start | bytes 2949120 | tf_op jit(solution)/shard_map/reduce_scatter | solution.py:1239
  321.5 229.9 %all-gather.14.cloned.1.call-start = ((), (), s32[]{:S(2)}) async-start(), calls=%async_computation.10 | async-start | bytes 19464192 | tf_op jit(solution)/shard_map/all_gather | solution.py:1238
  321.8 30.3 %collective-permute-start.27 = (bf16[128,4224]{1,0:T(8,128)(2,1)}, bf16[128,4224]{1,0:T(8,128)(2,1)S(1)}, u32[]{:S(2)}, u32[]{:S(2)}) collective-permute-start(bf16[128,4224]{1,0:T(8,128)(2,1)} %get-tuple-element.203), channel_id=1, source_target_pairs={{0,16},{4,20},{8,24},{12,28},{16,0},{20,4},{24,8},{28,12},{1,17},{... | collective-permute-start | bytes 3244040 | tf_op jit(solution)/shard_map/ppermute | solution.py:1074
  323.0 29.0 %collective-permute-start.28 = (bf16[128,4224]{1,0:T(8,128)(2,1)S(1)}, bf16[128,4224]{1,0:T(8,128)(2,1)S(1)}, u32[]{:S(2)}, u32[]{:S(2)}) collective-permute-start(bf16[128,4224]{1,0:T(8,128)(2,1)S(1)} %copy-done.64), channel_id=1, source_target_pairs={{0,8},{4,12},{8,0},{12,4},{16,24},{20,28},{24,16},{28,20},{1,9},{5... | collective-permute-start | bytes 3244040 | tf_op jit(solution)/shard_map/ppermute | solution.py:1074
  358.6 242.7 %all-gather.16.cloned.1.call-start = ((), (), s32[]{:S(2)}) async-start(), calls=%async_computation.11 | async-start | bytes 4718592 | tf_op jit(solution)/shard_map/all_gather | solution.py:1259
  358.7 23.6 %collective-permute-start.29 = (bf16[128,2048]{1,0:T(8,128)(2,1)S(1)}, bf16[128,2048]{1,0:T(8,128)(2,1)S(1)}, u32[]{:S(2)}, u32[]{:S(2)}) collective-permute-start(bf16[128,2048]{1,0:T(8,128)(2,1)S(1)} %copy-done.66), channel_id=1, source_target_pairs={{0,8},{4,12},{8,0},{12,4},{16,24},{20,28},{24,16},{28,20},{1,9},{5... | collective-permute-start | bytes 1572872 | tf_op jit(solution)/shard_map/ppermute | solution.py:1074
  360.2 22.1 %collective-permute-start.30 = (bf16[128,2048]{1,0:T(8,128)(2,1)S(1)}, bf16[128,2048]{1,0:T(8,128)(2,1)S(1)}, u32[]{:S(2)}, u32[]{:S(2)}) collective-permute-start(bf16[128,2048]{1,0:T(8,128)(2,1)S(1)} %copy-done.65), channel_id=1, source_target_pairs={{0,16},{4,20},{8,24},{12,28},{16,0},{20,4},{24,8},{28,12},{1,17},{... | collective-permute-start | bytes 1572872 | tf_op jit(solution)/shard_map/ppermute | solution.py:1074
  383.5 29.5 %collective-permute-start.31 = (bf16[2,4,288,512]{3,2,1,0:T(8,128)(2,1)}, bf16[2,4,288,512]{3,2,1,0:T(8,128)(2,1)S(1)}, u32[]{:S(2)}, u32[]{:S(2)}) collective-permute-start(bf16[2,4,288,512]{3,2,1,0:T(8,128)(2,1)} %get-tuple-element.234), channel_id=1, source_target_pairs={{0,4},{4,0},{8,12},{12,8},{16,20},{20,16},{24,28},{28,24},{1,5},{5... | collective-permute-start | bytes 7077896 | tf_op jit(solution)/shard_map/ppermute | solution.py:1074
  387.3 32.5 %collective-permute-start.32 = (bf16[64,2048]{1,0:T(8,128)(2,1)}, bf16[64,2048]{1,0:T(8,128)(2,1)S(1)}, u32[]{:S(2)}, u32[]{:S(2)}) collective-permute-start(bf16[64,2048]{1,0:T(8,128)(2,1)} %get-tuple-element.229), channel_id=1, source_target_pairs={{0,16},{4,20},{8,24},{12,28},{16,0},{20,4},{24,8},{28,12},{1,17},{... | collective-permute-start | bytes 786440 | tf_op jit(solution)/shard_map/ppermute | solution.py:1074
  400.6 20.7 %collective-permute-start.33 = (bf16[64,2048]{1,0:T(8,128)(2,1)}, bf16[64,2048]{1,0:T(8,128)(2,1)S(1)}, u32[]{:S(2)}, u32[]{:S(2)}) collective-permute-start(bf16[64,2048]{1,0:T(8,128)(2,1)} %get-tuple-element.239), channel_id=1, source_target_pairs={{0,8},{4,12},{8,0},{12,4},{16,24},{20,28},{24,16},{28,20},{1,9},{5... | collective-permute-start | bytes 786440 | tf_op jit(solution)/shard_map/ppermute | solution.py:1074
  424.8 198.2 %all-reduce.2.cloned.1.call-start = ((), (), s32[]{:S(2)}) async-start(), calls=%async_computation.9 | async-start | bytes 3162112 | tf_op jit(solution)/shard_map/psum | solution.py:1285
  425.3 29.8 %collective-permute-start.38 = (bf16[2,288,512]{2,1,0:T(8,128)(2,1)}, bf16[2,288,512]{2,1,0:T(8,128)(2,1)S(1)}, u32[]{:S(2)}, u32[]{:S(2)}) collective-permute-start(bf16[2,288,512]{2,1,0:T(8,128)(2,1)} %get-tuple-element.246), channel_id=1, source_target_pairs={{0,8},{4,12},{8,0},{12,4},{16,24},{20,28},{24,16},{28,20},{1,9},{5... | collective-permute-start | bytes 1769480 | tf_op jit(solution)/shard_map/ppermute | solution.py:1074
  427.0 28.2 %collective-permute-start.39 = (bf16[2,288,512]{2,1,0:T(8,128)(2,1)}, bf16[2,288,512]{2,1,0:T(8,128)(2,1)S(1)}, u32[]{:S(2)}, u32[]{:S(2)}) collective-permute-start(bf16[2,288,512]{2,1,0:T(8,128)(2,1)} %get-tuple-element.247), channel_id=1, source_target_pairs={{0,16},{4,20},{8,24},{12,28},{16,0},{20,4},{24,8},{28,12},{1,17},{... | collective-permute-start | bytes 1769480 | tf_op jit(solution)/shard_map/ppermute | solution.py:1074
  429.6 25.6 %collective-permute-start.36 = (bf16[144,1024]{1,0:T(8,128)(2,1)S(1)}, bf16[144,1024]{1,0:T(8,128)(2,1)S(1)}, u32[]{:S(2)}, u32[]{:S(2)}) collective-permute-start(bf16[144,1024]{1,0:T(8,128)(2,1)S(1)} %copy-done.68), channel_id=1, source_target_pairs={{0,2},{1,3},{2,0},{3,1},{4,6},{5,7},{6,4},{7,5},{8,10},{9,11},{10,... | collective-permute-start | bytes 884744 | tf_op jit(solution)/shard_map/ppermute | solution.py:1085
  429.6 25.5 %collective-permute-start.37 = (bf16[144,1024]{1,0:T(8,128)(2,1)S(1)}, bf16[144,1024]{1,0:T(8,128)(2,1)S(1)}, u32[]{:S(2)}, u32[]{:S(2)}) collective-permute-start(bf16[144,1024]{1,0:T(8,128)(2,1)S(1)} %copy-done.67), channel_id=1, source_target_pairs={{0,3},{1,0},{2,1},{3,2},{4,7},{5,4},{6,5},{7,6},{8,11},{9,8},{10,9... | collective-permute-start | bytes 884744 | tf_op jit(solution)/shard_map/ppermute | solution.py:1085
  464.4 18.3 %collective-permute-start.40 = (bf16[160,1024]{1,0:T(8,128)(2,1)S(1)}, bf16[160,1024]{1,0:T(8,128)(2,1)S(1)}, u32[]{:S(2)}, u32[]{:S(2)}) collective-permute-start(bf16[160,1024]{1,0:T(8,128)(2,1)S(1)} %copy-done.12), channel_id=1, source_target_pairs={{0,1},{1,2},{2,3},{3,0},{4,5},{5,6},{6,7},{7,4},{8,9},{9,10},{10,1... | collective-permute-start | bytes 983048 | tf_op jit(solution)/shard_map/ppermute | solution.py:1085
  464.4 36.0 %collective-permute-start.41 = (bf16[160,1024]{1,0:T(8,128)(2,1)S(1)}, bf16[160,1024]{1,0:T(8,128)(2,1)S(1)}, u32[]{:S(2)}, u32[]{:S(2)}) collective-permute-start(bf16[160,1024]{1,0:T(8,128)(2,1)S(1)} %copy-done.12), channel_id=1, source_target_pairs={{0,2},{1,3},{2,0},{3,1},{4,6},{5,7},{6,4},{7,5},{8,10},{9,11},{10,... | collective-permute-start | bytes 983048 | tf_op jit(solution)/shard_map/ppermute | solution.py:1085
  466.0 34.8 %collective-permute-start.42 = (bf16[160,1024]{1,0:T(8,128)(2,1)S(1)}, bf16[160,1024]{1,0:T(8,128)(2,1)S(1)}, u32[]{:S(2)}, u32[]{:S(2)}) collective-permute-start(bf16[160,1024]{1,0:T(8,128)(2,1)S(1)} %copy-done.12), channel_id=1, source_target_pairs={{0,3},{1,0},{2,1},{3,2},{4,7},{5,4},{6,5},{7,6},{8,11},{9,8},{10,9... | collective-permute-start | bytes 983048 | tf_op jit(solution)/shard_map/ppermute | solution.py:1085
  482.6 25.0 %collective-permute-start.49 = (bf16[144,512]{1,0:T(8,128)(2,1)}, bf16[144,512]{1,0:T(8,128)(2,1)S(1)}, u32[]{:S(2)}, u32[]{:S(2)}) collective-permute-start(bf16[144,512]{1,0:T(8,128)(2,1)} %get-tuple-element.278), channel_id=1, source_target_pairs={{0,1},{1,2},{2,3},{3,0},{4,5},{5,6},{6,7},{7,4},{8,9},{9,10},{10,1... | collective-permute-start | bytes 442376 | tf_op jit(solution)/shard_map/ppermute | solution.py:1085
  514.9 25.1 %collective-permute-start.55 = (bf16[2,16,1024]{2,1,0:T(8,128)(2,1)}, bf16[2,16,1024]{2,1,0:T(8,128)(2,1)S(1)}, u32[]{:S(2)}, u32[]{:S(2)}) collective-permute-start(bf16[2,16,1024]{2,1,0:T(8,128)(2,1)} %get-tuple-element.293), channel_id=1, source_target_pairs={{0,1},{1,2},{2,3},{3,0},{4,5},{5,6},{6,7},{7,4},{8,9},{9,10},{10,1... | collective-permute-start | bytes 196616 | tf_op jit(solution)/shard_map/ppermute | solution.py:1085
  517.8 22.2 %collective-permute-start.56 = (bf16[2,16,1024]{2,1,0:T(8,128)(2,1)}, bf16[2,16,1024]{2,1,0:T(8,128)(2,1)S(1)}, u32[]{:S(2)}, u32[]{:S(2)}) collective-permute-start(bf16[2,16,1024]{2,1,0:T(8,128)(2,1)} %get-tuple-element.294), channel_id=1, source_target_pairs={{0,2},{1,3},{2,0},{3,1},{4,6},{5,7},{6,4},{7,5},{8,10},{9,11},{10,... | collective-permute-start | bytes 196616 | tf_op jit(solution)/shard_map/ppermute | solution.py:1085
  518.4 21.6 %collective-permute-start.57 = (bf16[2,16,1024]{2,1,0:T(8,128)(2,1)}, bf16[2,16,1024]{2,1,0:T(8,128)(2,1)S(1)}, u32[]{:S(2)}, u32[]{:S(2)}) collective-permute-start(bf16[2,16,1024]{2,1,0:T(8,128)(2,1)} %get-tuple-element.295), channel_id=1, source_target_pairs={{0,3},{1,0},{2,1},{3,2},{4,7},{5,4},{6,5},{7,6},{8,11},{9,8},{10,9... | collective-permute-start | bytes 196616 | tf_op jit(solution)/shard_map/ppermute | solution.py:1085
  542.9 28.8 %collective-permute-start.58 = (bf16[144,1024]{1,0:T(8,128)(2,1)S(1)}, bf16[144,1024]{1,0:T(8,128)(2,1)S(1)}, u32[]{:S(2)}, u32[]{:S(2)}) collective-permute-start(bf16[144,1024]{1,0:T(8,128)(2,1)S(1)} %copy-done.25), channel_id=1, source_target_pairs={{0,1},{1,2},{2,3},{3,0},{4,5},{5,6},{6,7},{7,4},{8,9},{9,10},{10,1... | collective-permute-start | bytes 884744 | tf_op jit(solution)/shard_map/ppermute | solution.py:1085
  542.9 26.8 %collective-permute-start.64 = (bf16[2,64,1024]{2,1,0:T(8,128)(2,1)}, bf16[2,64,1024]{2,1,0:T(8,128)(2,1)S(1)}, u32[]{:S(2)}, u32[]{:S(2)}) collective-permute-start(bf16[2,64,1024]{2,1,0:T(8,128)(2,1)} %pack_up.1.refs_0_), channel_id=1, source_target_pairs={{0,4},{4,0},{8,12},{12,8},{16,20},{20,16},{24,28},{28,24},{1,5},{5... | collective-permute-start | bytes 786440 | tf_op jit(solution)/shard_map/ppermute | solution.py:1074
  548.3 23.4 %collective-permute-start.65 = (bf16[2,64,1024]{2,1,0:T(8,128)(2,1)}, bf16[2,64,1024]{2,1,0:T(8,128)(2,1)S(1)}, u32[]{:S(2)}, u32[]{:S(2)}) collective-permute-start(bf16[2,64,1024]{2,1,0:T(8,128)(2,1)} %pack_up.1.refs_0_), channel_id=1, source_target_pairs={{0,8},{4,12},{8,0},{12,4},{16,24},{20,28},{24,16},{28,20},{1,9},{5... | collective-permute-start | bytes 786440 | tf_op jit(solution)/shard_map/ppermute | solution.py:1074
  548.3 24.0 %collective-permute-start.60 = (bf16[144,1024]{1,0:T(8,128)(2,1)S(1)}, bf16[144,1024]{1,0:T(8,128)(2,1)S(1)}, u32[]{:S(2)}, u32[]{:S(2)}) collective-permute-start(bf16[144,1024]{1,0:T(8,128)(2,1)S(1)} %copy-done.25), channel_id=1, source_target_pairs={{0,2},{1,3},{2,0},{3,1},{4,6},{5,7},{6,4},{7,5},{8,10},{9,11},{10,... | collective-permute-start | bytes 884744 | tf_op jit(solution)/shard_map/ppermute | solution.py:1085
  549.7 25.9 %collective-permute-start.62 = (bf16[144,1024]{1,0:T(8,128)(2,1)S(1)}, bf16[144,1024]{1,0:T(8,128)(2,1)S(1)}, u32[]{:S(2)}, u32[]{:S(2)}) collective-permute-start(bf16[144,1024]{1,0:T(8,128)(2,1)S(1)} %copy-done.25), channel_id=1, source_target_pairs={{0,3},{1,0},{2,1},{3,2},{4,7},{5,4},{6,5},{7,6},{8,11},{9,8},{10,9... | collective-permute-start | bytes 884744 | tf_op jit(solution)/shard_map/ppermute | solution.py:1085
  571.7 25.9 %collective-permute-start.61 = (bf16[144,1024]{1,0:T(8,128)(2,1)S(1)}, bf16[144,1024]{1,0:T(8,128)(2,1)S(1)}, u32[]{:S(2)}, u32[]{:S(2)}) collective-permute-start(bf16[144,1024]{1,0:T(8,128)(2,1)S(1)} %copy-done.26), channel_id=1, source_target_pairs={{0,2},{1,3},{2,0},{3,1},{4,6},{5,7},{6,4},{7,5},{8,10},{9,11},{10,... | collective-permute-start | bytes 884744 | tf_op jit(solution)/shard_map/ppermute | solution.py:1085
  571.7 26.6 %collective-permute-start.63 = (bf16[144,1024]{1,0:T(8,128)(2,1)S(1)}, bf16[144,1024]{1,0:T(8,128)(2,1)S(1)}, u32[]{:S(2)}, u32[]{:S(2)}) collective-permute-start(bf16[144,1024]{1,0:T(8,128)(2,1)S(1)} %copy-done.26), channel_id=1, source_target_pairs={{0,3},{1,0},{2,1},{3,2},{4,7},{5,4},{6,5},{7,6},{8,11},{9,8},{10,9... | collective-permute-start | bytes 884744 | tf_op jit(solution)/shard_map/ppermute | solution.py:1085
  572.3 40.0 %collective-permute-start.66 = (bf16[2,64,1024]{2,1,0:T(8,128)(2,1)S(1)}, bf16[2,64,1024]{2,1,0:T(8,128)(2,1)S(1)}, u32[]{:S(2)}, u32[]{:S(2)}) collective-permute-start(bf16[2,64,1024]{2,1,0:T(8,128)(2,1)S(1)} %copy-done.17), channel_id=1, source_target_pairs={{0,12},{4,8},{8,4},{12,0},{16,28},{20,24},{24,20},{28,16},{1,13},{... | collective-permute-start | bytes 786440 | tf_op jit(solution)/shard_map/ppermute | solution.py:1074
  575.7 36.6 %collective-permute-start.67 = (bf16[2,64,1024]{2,1,0:T(8,128)(2,1)S(1)}, bf16[2,64,1024]{2,1,0:T(8,128)(2,1)S(1)}, u32[]{:S(2)}, u32[]{:S(2)}) collective-permute-start(bf16[2,64,1024]{2,1,0:T(8,128)(2,1)S(1)} %copy-done.17), channel_id=1, source_target_pairs={{0,16},{4,20},{8,24},{12,28},{16,0},{20,4},{24,8},{28,12},{1,17},{... | collective-permute-start | bytes 786440 | tf_op jit(solution)/shard_map/ppermute | solution.py:1074
  578.8 33.5 %collective-permute-start.68 = (bf16[2,64,1024]{2,1,0:T(8,128)(2,1)S(1)}, bf16[2,64,1024]{2,1,0:T(8,128)(2,1)}, u32[]{:S(2)}, u32[]{:S(2)}) collective-permute-start(bf16[2,64,1024]{2,1,0:T(8,128)(2,1)S(1)} %copy-done.17), channel_id=1, source_target_pairs={{0,20},{4,16},{8,28},{12,24},{16,4},{20,0},{24,12},{28,8},{1,21},{... | collective-permute-start | bytes 786440 | tf_op jit(solution)/shard_map/ppermute | solution.py:1074
  598.3 20.1 %collective-permute-start.70 = (bf16[2,64,1024]{2,1,0:T(8,128)(2,1)S(1)}, bf16[2,64,1024]{2,1,0:T(8,128)(2,1)S(1)}, u32[]{:S(2)}, u32[]{:S(2)}) collective-permute-start(bf16[2,64,1024]{2,1,0:T(8,128)(2,1)S(1)} %copy-done.17), channel_id=1, source_target_pairs={{0,28},{4,24},{8,20},{12,16},{16,12},{20,8},{24,4},{28,0},{1,29},{... | collective-permute-start | bytes 786440 | tf_op jit(solution)/shard_map/ppermute | solution.py:1074
  (104 other events, 1061.4 us)
Sparse Core Ops, SparseCore 0:
  18.0 38.4 all-gather.7
  90.5 58.5 reduce-scatter.3
  152.5 49.2 all-gather.9
  231.7 48.3 reduce-scatter.5
  283.9 49.2 all-gather.11
  336.0 47.5 reduce-scatter.7
  385.4 118.1 all-gather.13
  506.0 36.0 all-gather.15
  548.4 64.2 all-reduce.1

commit v5 on v4

--- a/solution.py
+++ b/solution.py
@@ -72,11 +72,13 @@
 
 
 def attend_kernel(
-    size, tile, heads, places, info_ref, pre_ref, cos_ref, sin_ref, first_ref, *refs
+    size, tile, heads, places, wide, info_ref, pre_ref, cos_ref, sin_ref, first_ref, *refs
 ):
-    pieces_in = refs[: len(places)]
-    query_ref, out_ref, low_ref, log_ref, kv_ref = refs[len(places) : len(places) + 5]
-    max_ref, sum_ref, acc_ref, scores_ref, start_ref, index_ref, sems = refs[len(places) + 5 :]
+    pieces_in, refs = refs[: len(places)], refs[len(places) :]
+    if wide:
+        weight_in, refs = refs[0], refs[1:]
+    query_ref, out_ref, low_ref, log_ref, kv_ref = refs[:5]
+    max_ref, sum_ref, acc_ref, scores_ref, start_ref, index_ref, sems = refs[5 + wide : 12 + wide]
     tokens = pre_ref.shape[0]
     copies = []
     for n, (mask, offset) in enumerate(places):
@@ -85,6 +87,10 @@
         copies.append(pltpu.make_async_copy(pieces_in[n], kv_ref.at[rows, :], sems.at[n]))
     for copy in copies:
         copy.start()
+    if wide:
+        branch_ref, weight_ref, weight_sem = refs[5], refs[13], refs[14]
+        weight_copy = pltpu.make_async_copy(weight_in, weight_ref, weight_sem)
+        weight_copy.start()
     width = kv_ref.shape[1] // 2
     half = width // 2
     lanes = max_ref.shape[1]
@@ -154,21 +160,34 @@
             low_ref[rows, cols] = part.astype(BF)
             at = stop
 
+    if wide:
+        weight_copy.wait()
+
+        def branch(i, carry):
+            cols = pl.ds(pl.multiple_of(i * 512, 512), 512)
+            branch_ref[:, cols] = dense(low_ref[...], weight_ref[:, cols]).astype(BF)
+            return carry
+
+        lax.fori_loop(0, branch_ref.shape[1] // 512, branch, None)
+
 
 def in_vmem(count):
     return [pl.BlockSpec(memory_space=pltpu.VMEM) for _ in range(count)]
 
 
-def attend(info, query_pre, cosine, sine, start, pieces):
+def attend(info, query_pre, cosine, sine, start, pieces, weight=None):
     tokens, all_heads = query_pre.shape
     width = pieces[0][0].shape[1] // 2
     keys = sum(piece[0].shape[0] for piece in pieces)
     rows = tokens * (all_heads // width)
-    size, tile = key_block(keys, 1536), row_tile(rows)
+    size = key_block(keys, 1536)
+    tile = rows // 2 if rows % 256 == 0 else row_tile(rows)
+    wide = weight is not None
+    branch = [((tokens, weight.shape[1]), BF)] if wide else []
     start = jnp.broadcast_to(start[:, None], (tokens, LANES))
     return pl.pallas_call(
         functools.partial(
-            attend_kernel, size, tile, all_heads // width, [piece[1:] for piece in pieces]
+            attend_kernel, size, tile, all_heads // width, [piece[1:] for piece in pieces], wide
         ),
         out_shape=(
             jax.ShapeDtypeStruct((rows, width), BF),
@@ -176,11 +195,12 @@
             jax.ShapeDtypeStruct((tokens, all_heads), BF),
             jax.ShapeDtypeStruct((1, rows), F32),
             jax.ShapeDtypeStruct((keys, 2 * width), BF),
+            *[jax.ShapeDtypeStruct(*out) for out in branch],
         ),
         in_specs=[pl.BlockSpec(memory_space=pltpu.SMEM)]
         + in_vmem(4)
-        + [pl.BlockSpec(memory_space=pl.ANY)] * len(pieces),
-        out_specs=tuple(in_vmem(5)),
+        + [pl.BlockSpec(memory_space=pl.ANY)] * (len(pieces) + wide),
+        out_specs=tuple(in_vmem(5 + wide)),
         scratch_shapes=[
             pltpu.VMEM((tile, LANES), F32),
             pltpu.VMEM((tile, LANES), F32),
@@ -189,11 +209,12 @@
             pltpu.VMEM((rows, LANES), I32),
             pltpu.VMEM((rows, LANES), I32),
             pltpu.SemaphoreType.DMA((len(pieces),)),
-        ],
+        ]
+        + ([pltpu.VMEM(weight.shape, BF), pltpu.SemaphoreType.DMA(())] if wide else []),
         compiler_params=pltpu.CompilerParams(vmem_limit_bytes=56 * 2**20),
         cost_estimate=brief(0),
         name="attend",
-    )(info, query_pre, cosine, sine, start, *[piece[0] for piece in pieces])
+    )(info, query_pre, cosine, sine, start, *[piece[0] for piece in pieces], *([weight] if wide else []))
 
 
 def attend_back_kernel(
@@ -1172,12 +1193,11 @@
     pieces += [(swap(array, 0), mask ^ 1, offset) for array, mask, offset in pieces]
 
     latent_low, recip_c, gain_all, query_pre = queries(place_info, latent_all, up_own, up_other)
-    query, attn_vals, attn_low, log_total, kv_all = attend(
-        in_order(info), query_pre, cosine, sine, start, pieces
+    query, attn_vals, attn_low, log_total, kv_all, branch_part = attend(
+        in_order(info), query_pre, cosine, sine, start, pieces, out_weight
     )
     Order.last = attn_low
 
-    branch_part = matmul(info, attn_low, out_weight)
     branch = lax.psum_scatter(branch_part, "rank", scatter_dimension=0, tiled=True)
     grad_hidden = dense_nt(after(out_grad, branch_part), down_weight)
     out_grad_pair = swap(after(out_grad, branch_part), 0)

time: 647 us -> 642 us (level)
    pallas_call x22 -> x21, Pallas kernels: 142 us -> 136 us  [placed_call(): pl.pallas_call(kernel, grid_spec=pltpu.PrefetchScalarGridSpec(num_scalar_...]
where the time goes in v5:
time: 642 us; the launch traced here: 631 us
  waiting for transfers between devices  257 us (40%)
  Pallas kernels  223 us (35%)
  starting transfers between devices  87.2 us (14%)
  local copies, waits for them, and re-layouts  35.7 us (6%)
  between operations  15 us (2%)
  matrix products  6.97 us (1%)
  other arithmetic  6.52 us (1%)
    pallas_call x21, Pallas kernels, placed_call(): pl.pallas_call(kernel, grid_spec=pltpu.PrefetchScalarGridSpec(num_scalar_...  136 us
    ppermute x44, waiting for transfers between devices, exchange(): return lax.ppermute(value, 'seq', [(i, i ^ mask) for i in range(count)])  71.7 us
    ppermute x27, waiting for transfers between devices, ring(): lax.ppermute(value, 'rank', [(i, (i + shift) % ranks) for i in range(rank...  62.6 us
    ppermute x44, starting transfers between devices, exchange(): return lax.ppermute(value, 'seq', [(i, i ^ mask) for i in range(count)])  61.8 us
    all_gather x1, waiting for transfers between devices, per_device_fast(): mid_low = lax.all_gather(mid_own, 'rank', axis=0, tiled=True)  49.4 us
    reduce_scatter x1, waiting for transfers between devices, per_device_fast(): lax.psum_scatter(branch_part, 'rank', scatter_dimension=0, tiled=True)  46.3 us
    pallas_call x10, Pallas kernels, placed_call(): pl.pallas_call(kernel, in_specs=[pl.BlockSpec(memory_space=pltpu.SMEM)] +...  31.6 us
    ppermute x27, starting transfers between devices, ring(): lax.ppermute(value, 'rank', [(i, (i + shift) % ranks) for i in range(rank...  24.2 us
  transfers between devices with their start and end apart: 80, of which 23 were waited for; matrix products, arithmetic and copies ran while one was open for 4% of the time, Pallas kernels for 31%

profile of v5, /device:TPU:25, one launch (start us, length us, event | category | flops | bytes accessed | tf_op | source)
XLA Modules:
  0.0 630.9 jit_solution(15025692156445026594)
XLA Ops:
  10.7 7.2 %project.1 = (bf16[576,2048]{1,0:T(8,128)(2,1)}, f32[576,128]{1,0:T(8,128)}, f32[576,512]{1,0:T(8,128)}, bf16[592,256]{1,0:T(8,128)(2,1)}) custom-call(s32[6]{0:T(128)} %stack.29.info_ref, bf16[576,2048]{1,0:T(8,128)(2,1)} %tokens_ref.4, f32[1,2048]{1,0:T(1,128)} %bitcast.48, bf16[2048,256]{1,0:T(8,128)(2,1)} %down_ref.1, bf16[2048,512]{1,0:T(8,128)(2,1)} %kv_weight_ref.3, ...), custom_call_target="tpu_custom_call" | custom-call | tf_op jit(solution)/shard_map/project/pallas_call | solution.py:397
  26.6 15.4 %collective-permute-done.1 = bf16[256,512]{1,0:T(8,128)(2,1)S(1)} collective-permute-done((bf16[256,512]{1,0:T(8,128)(2,1)S(1)}, bf16[256,512]{1,0:T(8,128)(2,1)S(1)}, u32[]{:S(2)}, u32[]{:S(2)}) %collective-permute-start.1) | collective-permute-done | bytes 262176 | tf_op jit(solution)/shard_map/ppermute | solution.py:1106
  43.8 3.9 collective-permute-start.3
  51.8 4.8 collective-permute-done.6.refs_3_
  62.2 5.1 queries.1
  68.2 20.1 %attend.1 = (bf16[2304,256]{1,0:T(8,128)(2,1)}, f32[576,1024]{1,0:T(8,128)}, bf16[576,1024]{1,0:T(8,128)(2,1)}, f32[1,2304]{1,0:T(1,128)}, bf16[4608,512]{1,0:T(8,128)(2,1)}, /*index=5*/bf16[576,2048]{1,0:T(8,128)(2,1)}) custom-call(s32[6]{0:T(128)} %stack.28.info_ref, f32[576,1024]{1,0:T(8,128)} %get-tuple-element.170.pre_ref, ...), custom_call_target="tpu_custom_call" | custom-call | tf_op jit(solution)/shard_map/attend/pallas_call | solution.py:188
  93.3 7.0 %fusion.2.grad_ref = f32[576,1408]{1,0:T(8,128)S(1)} fusion(bf16[576,2048]{1,0:T(8,128)(2,1)} %out_grad_ref.1, bf16[1408,2048]{1,0:T(8,128)(2,1)} %right_ref.2), kind=kOutput, calls=%fused_computation.20 | convolution fusion | flops 3321888768 | bytes 11370496 | tf_op jit(solution)/shard_map/dot_general | solution.py:46
  100.4 46.3 %reduce-scatter.4.cloned.1.call-done.branch_ref = bf16[144,2048]{1,0:T(8,128)(2,1)} async-done(((bf16[576,2048]{1,0:T(8,128)(2,1)}), bf16[144,2048]{1,0:T(8,128)(2,1)}) %reduce-scatter.4.cloned.1.call-update) | async-done | bytes 589840 | tf_op jit(solution)/shard_map/reduce_scatter | solution.py:1201
  146.6 3.3 mid_norm.1
  150.0 49.4 %all-gather.10.cloned.1.call-done.mid_ref.refs_0_ = bf16[576,2048]{1,0:T(8,128)(2,1)} async-done(((bf16[144,2048]{1,0:T(8,128)(2,1)}), bf16[576,2048]{1,0:T(8,128)(2,1)}) %all-gather.10.cloned.1.call-update) | async-done | bytes 2359312 | tf_op jit(solution)/shard_map/all_gather | solution.py:1220
  203.8 19.7 %feed_forward.1 = (bf16[576,1408]{1,0:T(8,128)(2,1)S(1)}, bf16[576,2816]{1,0:T(8,128)(2,1)S(1)}, bf16[576,2048]{1,0:T(8,128)(2,1)S(1)}) custom-call(bf16[576,2048]{1,0:T(8,128)(2,1)S(1)} %copy-done, f32[576,1408]{1,0:T(8,128)S(1)} %fusion.2.grad_ref, bf16[2048,1408]{1,0:T(8,128)(2,1)} %gate_ref.1, bf16[2048,1408]{1,0:T(8,128)(2,1)} %up_ref.1), custom_call_target="tpu_custom_call" | custom-call | flops 2000000000 | tf_op jit(solution)/shard_map/feed_forward/pallas_call | solution.py:343
  230.7 8.0 %matmul.2 = bf16[576,2048]{1,0:T(8,128)(2,1)} custom-call(s32[6]{0:T(128)} %stack.28.info_ref, bf16[576,1408]{1,0:T(8,128)(2,1)} %copy-done.2, bf16[1408,2048]{1,0:T(8,128)(2,1)} %right_ref.2), custom_call_target="tpu_custom_call" | custom-call | tf_op jit(solution)/shard_map/matmul/pallas_call | solution.py:397
  240.4 22.2 %pair_products.3 = (bf16[256,4224]{1,0:T(8,128)(2,1)}, bf16[256,4224]{1,0:T(8,128)(2,1)}, bf16[256,4224]{1,0:T(8,128)(2,1)}, bf16[256,4224]{1,0:T(8,128)(2,1)}) custom-call(s32[6]{0:T(128)} %stack.28.info_ref, bf16[576,2048]{1,0:T(8,128)(2,1)} %all-gather.10.cloned.1.call-done.mid_ref.refs_0_, bf16[576,2048]{1,0:T(8,128)(2,1)} %collective-permute-done.19.refs_1_, ...), custom_call_target="tpu_custom_call" | custom-call | tf_op jit(solution)/shard_map/pair_products/pallas_call | solution.py:397
  264.9 12.7 %reduce-scatter.6.cloned.1.call-done.grad_ref = bf16[144,2048]{1,0:T(8,128)(2,1)} async-done(((bf16[576,2048]{1,0:T(8,128)(2,1)}), bf16[144,2048]{1,0:T(8,128)(2,1)}) %reduce-scatter.6.cloned.1.call-update) | async-done | bytes 589840 | tf_op jit(solution)/shard_map/reduce_scatter | solution.py:1229
  277.7 3.6 mid_back.1
  281.4 29.8 %collective-permute-done.22 = bf16[256,4224]{1,0:T(8,128)(2,1)S(1)} collective-permute-done((bf16[256,4224]{1,0:T(8,128)(2,1)}, bf16[256,4224]{1,0:T(8,128)(2,1)S(1)}, u32[]{:S(2)}, u32[]{:S(2)}) %collective-permute-start.22) | collective-permute-done | bytes 2162720 | tf_op jit(solution)/shard_map/ppermute | solution.py:1095
  312.5 6.7 %fold_first.4 = (bf16[128,4224]{1,0:T(8,128)(2,1)}, bf16[128,4224]{1,0:T(8,128)(2,1)}, bf16[128,4224]{1,0:T(8,128)(2,1)}, bf16[128,4224]{1,0:T(8,128)(2,1)}) custom-call(s32[6]{0:T(128)} %stack.28.info_ref, bf16[2,128,4224]{2,1,0:T(8,128)(2,1)} %bitcast.54, bf16[2,128,4224]{2,1,0:T(8,128)(2,1)} %bitcast.56, bf16[2,128,4224]{2,1,0:T(8,128)(2,1)} %bitcast.55, ...), custom_call_target="tpu_custom_call" | custom-call | flops 999999995904 | tf_op jit(solution)/shard_map/fold_first/pallas_call | solution.py:397
  321.8 9.0 %all-gather.12.cloned.1.call-done.left_ref.refs_2_.branch_ref = bf16[576,2048]{1,0:T(8,128)(2,1)} async-done(((bf16[144,2048]{1,0:T(8,128)(2,1)}), bf16[576,2048]{1,0:T(8,128)(2,1)}) %all-gather.12.cloned.1.call-update) | async-done | bytes 2359312 | tf_op jit(solution)/shard_map/all_gather | solution.py:1243
  333.7 6.6 %matmul.3.grad_ref = bf16[576,1024]{1,0:T(8,128)(2,1)} custom-call(s32[6]{0:T(128)} %stack.28.info_ref, bf16[576,2048]{1,0:T(8,128)(2,1)} %all-gather.12.cloned.1.call-done.left_ref.refs_2_.branch_ref, bf16[1024,2048]{1,0:T(8,128)(2,1)} %right_ref.3), custom_call_target="tpu_custom_call" | custom-call | tf_op jit(solution)/shard_map/matmul/pallas_call | solution.py:397
  342.0 7.6 %pair_products.4 = (bf16[128,2048]{1,0:T(8,128)(2,1)}, bf16[128,2048]{1,0:T(8,128)(2,1)}, bf16[128,2048]{1,0:T(8,128)(2,1)}, bf16[128,2048]{1,0:T(8,128)(2,1)}) custom-call(s32[6]{0:T(128)} %stack.28.info_ref, bf16[576,1024]{1,0:T(8,128)(2,1)} %get-tuple-element.173.refs_0_, bf16[576,1024]{1,0:T(8,128)(2,1)} %collective-permute-done.14.refs_1_, ...), custom_call_target="tpu_custom_call" | custom-call | tf_op jit(solution)/shard_map/pair_products/pallas_call | solution.py:397
  351.0 5.2 fold_last.2
  360.3 15.9 %attend_back.1 = (bf16[576,1024]{1,0:T(8,128)(2,1)}, bf16[2,4,288,512]{3,2,1,0:T(8,128)(2,1)}, bf16[2,4,288,512]{3,2,1,0:T(8,128)(2,1)}) custom-call(s32[6]{0:T(128)} %stack.28.info_ref, bf16[2304,256]{1,0:T(8,128)(2,1)} %get-tuple-element.213.query_ref, bf16[576,1024]{1,0:T(8,128)(2,1)} %matmul.3.grad_ref, f32[576,1024]{1,0:T(8,128)} %get-tuple-element.214.out_ref, ...), custom_call_target="tpu_custom_call" | custom-call | tf_op jit(solution)/shard_map/attend_back/pallas_call | solution.py:292
  376.2 4.8 reduce-scatter.8.cloned.1.call-done.feed_ref
  381.5 3.3 fold_first.5
  384.9 9.9 %collective-permute-start.32 = (bf16[64,2048]{1,0:T(8,128)(2,1)}, bf16[64,2048]{1,0:T(8,128)(2,1)S(1)}, u32[]{:S(2)}, u32[]{:S(2)}) collective-permute-start(bf16[64,2048]{1,0:T(8,128)(2,1)} %get-tuple-element.229), channel_id=1, source_target_pairs={{0,16},{4,20},{8,24},{12,28},{16,0},{20,4},{24,8},{28,12},{1,17},{... | collective-permute-start | bytes 786440 | tf_op jit(solution)/shard_map/ppermute | solution.py:1095
  394.8 7.9 %collective-permute-start.33 = (bf16[64,2048]{1,0:T(8,128)(2,1)}, bf16[64,2048]{1,0:T(8,128)(2,1)S(1)}, u32[]{:S(2)}, u32[]{:S(2)}) collective-permute-start(bf16[64,2048]{1,0:T(8,128)(2,1)} %get-tuple-element.239), channel_id=1, source_target_pairs={{0,8},{4,12},{8,0},{12,4},{16,24},{20,28},{24,16},{28,20},{1,9},{5... | collective-permute-start | bytes 786440 | tf_op jit(solution)/shard_map/ppermute | solution.py:1095
  402.7 4.4 latent_parts.1
  408.5 5.4 fold_near.1
  424.6 5.5 pair_products.5
  430.1 19.0 %collective-permute-done.36.refs_2_ = bf16[144,1024]{1,0:T(8,128)(2,1)S(1)} collective-permute-done((bf16[144,1024]{1,0:T(8,128)(2,1)S(1)}, bf16[144,1024]{1,0:T(8,128)(2,1)S(1)}, u32[]{:S(2)}, u32[]{:S(2)}) %collective-permute-start.36) | collective-permute-done | bytes 294944 | tf_op jit(solution)/shard_map/ppermute | solution.py:1106
  450.0 3.2 latent_back.1.refs_0_
  453.2 3.6 fold_first.6
  461.4 10.4 %collective-permute-done.43.got_first = bf16[288,512]{1,0:T(8,128)(2,1)S(1)} collective-permute-done((bf16[288,512]{1,0:T(8,128)(2,1)}, bf16[288,512]{1,0:T(8,128)(2,1)S(1)}, u32[]{:S(2)}, u32[]{:S(2)}) %collective-permute-start.43) | collective-permute-done | bytes 294944 | tf_op jit(solution)/shard_map/ppermute | solution.py:1095
  476.7 12.4 %collective-permute-done.45 = bf16[128,1024]{1,0:T(8,128)(2,1)S(1)} collective-permute-done((bf16[128,1024]{1,0:T(8,128)(2,1)S(1)}, bf16[128,1024]{1,0:T(8,128)(2,1)S(1)}, u32[]{:S(2)}, u32[]{:S(2)}) %collective-permute-start.45) | collective-permute-done | bytes 262176 | tf_op jit(solution)/shard_map/ppermute | solution.py:1095
  508.7 2.9 collective-permute-start.55
  512.2 9.7 %collective-permute-done.53.refs_6_ = bf16[144,512]{1,0:T(8,128)(2,1)S(1)} collective-permute-done((bf16[144,512]{1,0:T(8,128)(2,1)}, bf16[144,512]{1,0:T(8,128)(2,1)S(1)}, u32[]{:S(2)}, u32[]{:S(2)}) %collective-permute-start.53) | collective-permute-done | bytes 147488 | tf_op jit(solution)/shard_map/ppermute | solution.py:1106
  522.6 6.8 %input_back.1 = (f32[576,512]{1,0:T(8,128)}, bf16[16,256]{1,0:T(8,128)(2,1)}, bf16[576,256]{1,0:T(8,128)(2,1)}, bf16[576,512]{1,0:T(8,128)(2,1)}) custom-call(s32[6]{0:T(128)} %stack.28.info_ref, bf16[576,2048]{1,0:T(8,128)(2,1)} %tokens_ref.4, bf16[576,2048]{1,0:T(8,128)(2,1)} %all-gather.12.cloned.1.call-done.left_ref.refs_2_.branch_ref, ...), custom_call_target="tpu_custom_call" | custom-call | tf_op jit(solution)/shard_map/input_back/pallas_call | solution.py:397
  529.5 4.6 last_products.1
  537.0 5.1 collective-permute-start.64
  545.5 18.4 %unpack.2 = (f32[2048,1408]{1,0:T(8,128)}, f32[2048,1408]{1,0:T(8,128)}, f32[1408,2048]{1,0:T(8,128)}) custom-call(s32[6]{0:T(128)} %stack.28.info_ref, bf16[4,2,2,128,4224]{4,3,2,1,0:T(8,128)(2,1)} %bitcast.34), custom_call_target="tpu_custom_call" | custom-call | tf_op jit(solution)/shard_map/unpack/pallas_call | solution.py:397
  566.3 3.2 collective-permute-start.66
  575.3 16.4 %collective-permute-done.61.refs_5_ = bf16[144,1024]{1,0:T(8,128)(2,1)S(1)} collective-permute-done((bf16[144,1024]{1,0:T(8,128)(2,1)S(1)}, bf16[144,1024]{1,0:T(8,128)(2,1)S(1)}, u32[]{:S(2)}, u32[]{:S(2)}) %collective-permute-start.61) | collective-permute-done | bytes 294944 | tf_op jit(solution)/shard_map/ppermute | solution.py:1106
  592.2 2.9 collective-permute-start.70
  595.1 6.7 %unpack.3 = f32[1024,2048]{1,0:T(8,128)} custom-call(s32[6]{0:T(128)} %stack.28.info_ref, bf16[4,2,2,64,2048]{4,3,2,1,0:T(8,128)(2,1)} %bitcast.37), custom_call_target="tpu_custom_call" | custom-call | tf_op jit(solution)/shard_map/unpack/pallas_call | solution.py:397
  601.9 4.2 place.1
  606.2 6.2 collective-permute-done.70.refs_7_
  613.1 3.8 unpack_up.1
  616.9 3.2 last.1
  (328 shorter events, 122.6 us)
Async XLA Ops:
  7.2 55.0 %all-gather.8.cloned.1.call-start = ((), (), s32[]{:S(2)}) async-start(), calls=%async_computation.3 | async-start | bytes 1515520 | tf_op jit(solution)/shard_map/all_gather | solution.py:1186
  8.5 18.1 %collective-permute-start = (bf16[256,512]{1,0:T(8,128)(2,1)S(1)}, bf16[256,512]{1,0:T(8,128)(2,1)S(1)}, u32[]{:S(2)}, u32[]{:S(2)}) collective-permute-start(bf16[256,512]{1,0:T(8,128)(2,1)S(1)} %get-tuple-element.316), channel_id=1, source_target_pairs={{0,1},{1,2},{2,3},{3,0},{4,5},{5,6},{6,7},{7,4},{8,9},{9,10},{10,1... | collective-permute-start | bytes 786440 | tf_op jit(solution)/shard_map/ppermute | solution.py:1106
  8.6 33.4 %collective-permute-start.1 = (bf16[256,512]{1,0:T(8,128)(2,1)S(1)}, bf16[256,512]{1,0:T(8,128)(2,1)S(1)}, u32[]{:S(2)}, u32[]{:S(2)}) collective-permute-start(bf16[256,512]{1,0:T(8,128)(2,1)S(1)} %get-tuple-element.318), channel_id=1, source_target_pairs={{0,2},{1,3},{2,0},{3,1},{4,6},{5,7},{6,4},{7,5},{8,10},{9,11},{10,... | collective-permute-start | bytes 786440 | tf_op jit(solution)/shard_map/ppermute | solution.py:1106
  9.9 32.8 %collective-permute-start.2 = (bf16[256,512]{1,0:T(8,128)(2,1)S(1)}, bf16[256,512]{1,0:T(8,128)(2,1)}, u32[]{:S(2)}, u32[]{:S(2)}) collective-permute-start(bf16[256,512]{1,0:T(8,128)(2,1)S(1)} %get-tuple-element.315), channel_id=1, source_target_pairs={{0,3},{1,0},{2,1},{3,2},{4,7},{5,4},{6,5},{7,6},{8,11},{9,8},{10,9... | collective-permute-start | bytes 786440 | tf_op jit(solution)/shard_map/ppermute | solution.py:1106
  17.9 128.7 %reduce-scatter.4.cloned.1.call-start = ((), (), s32[]{:S(2)}) async-start(), calls=%async_computation.4 | async-start | bytes 2949120 | tf_op jit(solution)/shard_map/reduce_scatter | solution.py:1201
  24.2 23.6 %collective-permute-start.4 = (bf16[576,512]{1,0:T(8,128)(2,1)}, bf16[576,512]{1,0:T(8,128)(2,1)S(1)}, u32[]{:S(2)}, u32[]{:S(2)}) collective-permute-start(bf16[576,512]{1,0:T(8,128)(2,1)} %turn.1.refs_0_), channel_id=1, source_target_pairs={{0,8},{4,12},{8,0},{12,4},{16,24},{20,28},{24,16},{28,20},{1,9},{5... | collective-permute-start | bytes 1769480 | tf_op jit(solution)/shard_map/ppermute | solution.py:1095
  25.4 22.4 %collective-permute-start.5 = (bf16[576,512]{1,0:T(8,128)(2,1)}, bf16[576,512]{1,0:T(8,128)(2,1)}, u32[]{:S(2)}, u32[]{:S(2)}) collective-permute-start(bf16[576,512]{1,0:T(8,128)(2,1)} %turn.1.refs_0_), channel_id=1, source_target_pairs={{0,16},{4,20},{8,24},{12,28},{16,0},{20,4},{24,8},{28,12},{1,17},{... | collective-permute-start | bytes 1769480 | tf_op jit(solution)/shard_map/ppermute | solution.py:1095
  88.3 111.1 %all-gather.10.cloned.1.call-start = ((), (), s32[]{:S(2)}) async-start(), calls=%async_computation.5 | async-start | bytes 2949120 | tf_op jit(solution)/shard_map/all_gather | solution.py:1220
  150.0 127.7 %reduce-scatter.6.cloned.1.call-start = ((), (), s32[]{:S(2)}) async-start(), calls=%async_computation.6 | async-start | bytes 2949120 | tf_op jit(solution)/shard_map/reduce_scatter | solution.py:1229
  199.4 28.4 %collective-permute-start.16 = (bf16[512,256]{1,0:T(8,128)(2,1)}, bf16[512,256]{1,0:T(8,128)(2,1)}, u32[]{:S(2)}, u32[]{:S(2)}) collective-permute-start(bf16[512,256]{1,0:T(8,128)(2,1)} %get-tuple-element.186), channel_id=1, source_target_pairs={{0,1},{1,2},{2,3},{3,0},{4,5},{5,6},{6,7},{7,4},{8,9},{9,10},{10,1... | collective-permute-start | bytes 786440 | tf_op jit(solution)/shard_map/ppermute | solution.py:1106
  201.8 26.0 %collective-permute-start.17 = (bf16[512,256]{1,0:T(8,128)(2,1)}, bf16[512,256]{1,0:T(8,128)(2,1)}, u32[]{:S(2)}, u32[]{:S(2)}) collective-permute-start(bf16[512,256]{1,0:T(8,128)(2,1)} %get-tuple-element.187), channel_id=1, source_target_pairs={{0,2},{1,3},{2,0},{3,1},{4,6},{5,7},{6,4},{7,5},{8,10},{9,11},{10,... | collective-permute-start | bytes 786440 | tf_op jit(solution)/shard_map/ppermute | solution.py:1106
  201.9 25.9 %collective-permute-start.18 = (bf16[512,256]{1,0:T(8,128)(2,1)S(1)}, bf16[512,256]{1,0:T(8,128)(2,1)}, u32[]{:S(2)}, u32[]{:S(2)}) collective-permute-start(bf16[512,256]{1,0:T(8,128)(2,1)S(1)} %get-tuple-element.188), channel_id=1, source_target_pairs={{0,3},{1,0},{2,1},{3,2},{4,7},{5,4},{6,5},{7,6},{8,11},{9,8},{10,9... | collective-permute-start | bytes 786440 | tf_op jit(solution)/shard_map/ppermute | solution.py:1106
  229.2 101.6 %all-gather.12.cloned.1.call-start = ((), (), s32[]{:S(2)}) async-start(), calls=%async_computation.7 | async-start | bytes 2949120 | tf_op jit(solution)/shard_map/all_gather | solution.py:1243
  262.6 48.6 %collective-permute-start.22 = (bf16[256,4224]{1,0:T(8,128)(2,1)}, bf16[256,4224]{1,0:T(8,128)(2,1)S(1)}, u32[]{:S(2)}, u32[]{:S(2)}) collective-permute-start(bf16[256,4224]{1,0:T(8,128)(2,1)} %get-tuple-element.192), channel_id=1, source_target_pairs={{0,8},{4,12},{8,0},{12,4},{16,24},{20,28},{24,16},{28,20},{1,9},{5... | collective-permute-start | bytes 6488072 | tf_op jit(solution)/shard_map/ppermute | solution.py:1095
  263.7 48.2 %collective-permute-start.23 = (bf16[256,4224]{1,0:T(8,128)(2,1)}, bf16[256,4224]{1,0:T(8,128)(2,1)}, u32[]{:S(2)}, u32[]{:S(2)}) collective-permute-start(bf16[256,4224]{1,0:T(8,128)(2,1)} %get-tuple-element.202), channel_id=1, source_target_pairs={{0,16},{4,20},{8,24},{12,28},{16,0},{20,4},{24,8},{28,12},{1,17},{... | collective-permute-start | bytes 6488072 | tf_op jit(solution)/shard_map/ppermute | solution.py:1095
  281.3 99.7 %reduce-scatter.8.cloned.1.call-start = ((), (), s32[]{:S(2)}) async-start(), calls=%async_computation.8 | async-start | bytes 2949120 | tf_op jit(solution)/shard_map/reduce_scatter | solution.py:1259
  319.2 226.3 %all-gather.14.cloned.1.call-start = ((), (), s32[]{:S(2)}) async-start(), calls=%async_computation.10 | async-start | bytes 19464192 | tf_op jit(solution)/shard_map/all_gather | solution.py:1258
  319.4 30.2 %collective-permute-start.27 = (bf16[128,4224]{1,0:T(8,128)(2,1)}, bf16[128,4224]{1,0:T(8,128)(2,1)S(1)}, u32[]{:S(2)}, u32[]{:S(2)}) collective-permute-start(bf16[128,4224]{1,0:T(8,128)(2,1)} %get-tuple-element.203), channel_id=1, source_target_pairs={{0,16},{4,20},{8,24},{12,28},{16,0},{20,4},{24,8},{28,12},{1,17},{... | collective-permute-start | bytes 3244040 | tf_op jit(solution)/shard_map/ppermute | solution.py:1095
  320.7 29.0 %collective-permute-start.28 = (bf16[128,4224]{1,0:T(8,128)(2,1)S(1)}, bf16[128,4224]{1,0:T(8,128)(2,1)S(1)}, u32[]{:S(2)}, u32[]{:S(2)}) collective-permute-start(bf16[128,4224]{1,0:T(8,128)(2,1)S(1)} %copy-done.64), channel_id=1, source_target_pairs={{0,8},{4,12},{8,0},{12,4},{16,24},{20,28},{24,16},{28,20},{1,9},{5... | collective-permute-start | bytes 3244040 | tf_op jit(solution)/shard_map/ppermute | solution.py:1095
  356.2 239.0 %all-gather.16.cloned.1.call-start = ((), (), s32[]{:S(2)}) async-start(), calls=%async_computation.11 | async-start | bytes 4718592 | tf_op jit(solution)/shard_map/all_gather | solution.py:1279
  356.2 20.0 %collective-permute-start.29 = (bf16[128,2048]{1,0:T(8,128)(2,1)S(1)}, bf16[128,2048]{1,0:T(8,128)(2,1)S(1)}, u32[]{:S(2)}, u32[]{:S(2)}) collective-permute-start(bf16[128,2048]{1,0:T(8,128)(2,1)S(1)} %copy-done.66), channel_id=1, source_target_pairs={{0,8},{4,12},{8,0},{12,4},{16,24},{20,28},{24,16},{28,20},{1,9},{5... | collective-permute-start | bytes 1572872 | tf_op jit(solution)/shard_map/ppermute | solution.py:1095
  357.7 18.5 %collective-permute-start.30 = (bf16[128,2048]{1,0:T(8,128)(2,1)S(1)}, bf16[128,2048]{1,0:T(8,128)(2,1)S(1)}, u32[]{:S(2)}, u32[]{:S(2)}) collective-permute-start(bf16[128,2048]{1,0:T(8,128)(2,1)S(1)} %copy-done.65), channel_id=1, source_target_pairs={{0,16},{4,20},{8,24},{12,28},{16,0},{20,4},{24,8},{28,12},{1,17},{... | collective-permute-start | bytes 1572872 | tf_op jit(solution)/shard_map/ppermute | solution.py:1095
  381.1 26.0 %collective-permute-start.31 = (bf16[2,4,288,512]{3,2,1,0:T(8,128)(2,1)}, bf16[2,4,288,512]{3,2,1,0:T(8,128)(2,1)S(1)}, u32[]{:S(2)}, u32[]{:S(2)}) collective-permute-start(bf16[2,4,288,512]{3,2,1,0:T(8,128)(2,1)} %get-tuple-element.234), channel_id=1, source_target_pairs={{0,4},{4,0},{8,12},{12,8},{16,20},{20,16},{24,28},{28,24},{1,5},{5... | collective-permute-start | bytes 7077896 | tf_op jit(solution)/shard_map/ppermute | solution.py:1095
  384.9 29.1 %collective-permute-start.32 = (bf16[64,2048]{1,0:T(8,128)(2,1)}, bf16[64,2048]{1,0:T(8,128)(2,1)S(1)}, u32[]{:S(2)}, u32[]{:S(2)}) collective-permute-start(bf16[64,2048]{1,0:T(8,128)(2,1)} %get-tuple-element.229), channel_id=1, source_target_pairs={{0,16},{4,20},{8,24},{12,28},{16,0},{20,4},{24,8},{28,12},{1,17},{... | collective-permute-start | bytes 786440 | tf_op jit(solution)/shard_map/ppermute | solution.py:1095
  394.8 20.6 %collective-permute-start.33 = (bf16[64,2048]{1,0:T(8,128)(2,1)}, bf16[64,2048]{1,0:T(8,128)(2,1)S(1)}, u32[]{:S(2)}, u32[]{:S(2)}) collective-permute-start(bf16[64,2048]{1,0:T(8,128)(2,1)} %get-tuple-element.239), channel_id=1, source_target_pairs={{0,8},{4,12},{8,0},{12,4},{16,24},{20,28},{24,16},{28,20},{1,9},{5... | collective-permute-start | bytes 786440 | tf_op jit(solution)/shard_map/ppermute | solution.py:1095
  418.9 198.0 %all-reduce.2.cloned.1.call-start = ((), (), s32[]{:S(2)}) async-start(), calls=%async_computation.9 | async-start | bytes 3162112 | tf_op jit(solution)/shard_map/psum | solution.py:1305
  419.5 29.7 %collective-permute-start.38 = (bf16[2,288,512]{2,1,0:T(8,128)(2,1)}, bf16[2,288,512]{2,1,0:T(8,128)(2,1)S(1)}, u32[]{:S(2)}, u32[]{:S(2)}) collective-permute-start(bf16[2,288,512]{2,1,0:T(8,128)(2,1)} %get-tuple-element.246), channel_id=1, source_target_pairs={{0,8},{4,12},{8,0},{12,4},{16,24},{20,28},{24,16},{28,20},{1,9},{5... | collective-permute-start | bytes 1769480 | tf_op jit(solution)/shard_map/ppermute | solution.py:1095
  421.1 28.0 %collective-permute-start.39 = (bf16[2,288,512]{2,1,0:T(8,128)(2,1)}, bf16[2,288,512]{2,1,0:T(8,128)(2,1)S(1)}, u32[]{:S(2)}, u32[]{:S(2)}) collective-permute-start(bf16[2,288,512]{2,1,0:T(8,128)(2,1)} %get-tuple-element.247), channel_id=1, source_target_pairs={{0,16},{4,20},{8,24},{12,28},{16,0},{20,4},{24,8},{28,12},{1,17},{... | collective-permute-start | bytes 1769480 | tf_op jit(solution)/shard_map/ppermute | solution.py:1095
  423.5 25.6 %collective-permute-start.36 = (bf16[144,1024]{1,0:T(8,128)(2,1)S(1)}, bf16[144,1024]{1,0:T(8,128)(2,1)S(1)}, u32[]{:S(2)}, u32[]{:S(2)}) collective-permute-start(bf16[144,1024]{1,0:T(8,128)(2,1)S(1)} %copy-done.68), channel_id=1, source_target_pairs={{0,2},{1,3},{2,0},{3,1},{4,6},{5,7},{6,4},{7,5},{8,10},{9,11},{10,... | collective-permute-start | bytes 884744 | tf_op jit(solution)/shard_map/ppermute | solution.py:1106
  423.6 25.5 %collective-permute-start.37 = (bf16[144,1024]{1,0:T(8,128)(2,1)S(1)}, bf16[144,1024]{1,0:T(8,128)(2,1)S(1)}, u32[]{:S(2)}, u32[]{:S(2)}) collective-permute-start(bf16[144,1024]{1,0:T(8,128)(2,1)S(1)} %copy-done.67), channel_id=1, source_target_pairs={{0,3},{1,0},{2,1},{3,2},{4,7},{5,4},{6,5},{7,6},{8,11},{9,8},{10,9... | collective-permute-start | bytes 884744 | tf_op jit(solution)/shard_map/ppermute | solution.py:1106
  458.3 18.3 %collective-permute-start.40 = (bf16[160,1024]{1,0:T(8,128)(2,1)S(1)}, bf16[160,1024]{1,0:T(8,128)(2,1)S(1)}, u32[]{:S(2)}, u32[]{:S(2)}) collective-permute-start(bf16[160,1024]{1,0:T(8,128)(2,1)S(1)} %copy-done.12), channel_id=1, source_target_pairs={{0,1},{1,2},{2,3},{3,0},{4,5},{5,6},{6,7},{7,4},{8,9},{9,10},{10,1... | collective-permute-start | bytes 983048 | tf_op jit(solution)/shard_map/ppermute | solution.py:1106
  458.3 36.0 %collective-permute-start.41 = (bf16[160,1024]{1,0:T(8,128)(2,1)S(1)}, bf16[160,1024]{1,0:T(8,128)(2,1)S(1)}, u32[]{:S(2)}, u32[]{:S(2)}) collective-permute-start(bf16[160,1024]{1,0:T(8,128)(2,1)S(1)} %copy-done.12), channel_id=1, source_target_pairs={{0,2},{1,3},{2,0},{3,1},{4,6},{5,7},{6,4},{7,5},{8,10},{9,11},{10,... | collective-permute-start | bytes 983048 | tf_op jit(solution)/shard_map/ppermute | solution.py:1106
  459.9 34.7 %collective-permute-start.42 = (bf16[160,1024]{1,0:T(8,128)(2,1)S(1)}, bf16[160,1024]{1,0:T(8,128)(2,1)S(1)}, u32[]{:S(2)}, u32[]{:S(2)}) collective-permute-start(bf16[160,1024]{1,0:T(8,128)(2,1)S(1)} %copy-done.12), channel_id=1, source_target_pairs={{0,3},{1,0},{2,1},{3,2},{4,7},{5,4},{6,5},{7,6},{8,11},{9,8},{10,9... | collective-permute-start | bytes 983048 | tf_op jit(solution)/shard_map/ppermute | solution.py:1106
  476.7 24.9 %collective-permute-start.49 = (bf16[144,512]{1,0:T(8,128)(2,1)}, bf16[144,512]{1,0:T(8,128)(2,1)S(1)}, u32[]{:S(2)}, u32[]{:S(2)}) collective-permute-start(bf16[144,512]{1,0:T(8,128)(2,1)} %get-tuple-element.278), channel_id=1, source_target_pairs={{0,1},{1,2},{2,3},{3,0},{4,5},{5,6},{6,7},{7,4},{8,9},{9,10},{10,1... | collective-permute-start | bytes 442376 | tf_op jit(solution)/shard_map/ppermute | solution.py:1106
  508.7 25.3 %collective-permute-start.55 = (bf16[2,16,1024]{2,1,0:T(8,128)(2,1)}, bf16[2,16,1024]{2,1,0:T(8,128)(2,1)S(1)}, u32[]{:S(2)}, u32[]{:S(2)}) collective-permute-start(bf16[2,16,1024]{2,1,0:T(8,128)(2,1)} %get-tuple-element.293), channel_id=1, source_target_pairs={{0,1},{1,2},{2,3},{3,0},{4,5},{5,6},{6,7},{7,4},{8,9},{9,10},{10,1... | collective-permute-start | bytes 196616 | tf_op jit(solution)/shard_map/ppermute | solution.py:1106
  511.6 22.4 %collective-permute-start.56 = (bf16[2,16,1024]{2,1,0:T(8,128)(2,1)}, bf16[2,16,1024]{2,1,0:T(8,128)(2,1)S(1)}, u32[]{:S(2)}, u32[]{:S(2)}) collective-permute-start(bf16[2,16,1024]{2,1,0:T(8,128)(2,1)} %get-tuple-element.294), channel_id=1, source_target_pairs={{0,2},{1,3},{2,0},{3,1},{4,6},{5,7},{6,4},{7,5},{8,10},{9,11},{10,... | collective-permute-start | bytes 196616 | tf_op jit(solution)/shard_map/ppermute | solution.py:1106
  512.2 21.8 %collective-permute-start.57 = (bf16[2,16,1024]{2,1,0:T(8,128)(2,1)}, bf16[2,16,1024]{2,1,0:T(8,128)(2,1)S(1)}, u32[]{:S(2)}, u32[]{:S(2)}) collective-permute-start(bf16[2,16,1024]{2,1,0:T(8,128)(2,1)} %get-tuple-element.295), channel_id=1, source_target_pairs={{0,3},{1,0},{2,1},{3,2},{4,7},{5,4},{6,5},{7,6},{8,11},{9,8},{10,9... | collective-permute-start | bytes 196616 | tf_op jit(solution)/shard_map/ppermute | solution.py:1106
  537.0 28.8 %collective-permute-start.58 = (bf16[144,1024]{1,0:T(8,128)(2,1)S(1)}, bf16[144,1024]{1,0:T(8,128)(2,1)S(1)}, u32[]{:S(2)}, u32[]{:S(2)}) collective-permute-start(bf16[144,1024]{1,0:T(8,128)(2,1)S(1)} %copy-done.25), channel_id=1, source_target_pairs={{0,1},{1,2},{2,3},{3,0},{4,5},{5,6},{6,7},{7,4},{8,9},{9,10},{10,1... | collective-permute-start | bytes 884744 | tf_op jit(solution)/shard_map/ppermute | solution.py:1106
  537.0 26.8 %collective-permute-start.64 = (bf16[2,64,1024]{2,1,0:T(8,128)(2,1)}, bf16[2,64,1024]{2,1,0:T(8,128)(2,1)S(1)}, u32[]{:S(2)}, u32[]{:S(2)}) collective-permute-start(bf16[2,64,1024]{2,1,0:T(8,128)(2,1)} %pack_up.1.refs_0_), channel_id=1, source_target_pairs={{0,4},{4,0},{8,12},{12,8},{16,20},{20,16},{24,28},{28,24},{1,5},{5... | collective-permute-start | bytes 786440 | tf_op jit(solution)/shard_map/ppermute | solution.py:1095
  542.1 23.7 %collective-permute-start.65 = (bf16[2,64,1024]{2,1,0:T(8,128)(2,1)}, bf16[2,64,1024]{2,1,0:T(8,128)(2,1)S(1)}, u32[]{:S(2)}, u32[]{:S(2)}) collective-permute-start(bf16[2,64,1024]{2,1,0:T(8,128)(2,1)} %pack_up.1.refs_0_), channel_id=1, source_target_pairs={{0,8},{4,12},{8,0},{12,4},{16,24},{20,28},{24,16},{28,20},{1,9},{5... | collective-permute-start | bytes 786440 | tf_op jit(solution)/shard_map/ppermute | solution.py:1095
  542.3 24.0 %collective-permute-start.60 = (bf16[144,1024]{1,0:T(8,128)(2,1)S(1)}, bf16[144,1024]{1,0:T(8,128)(2,1)S(1)}, u32[]{:S(2)}, u32[]{:S(2)}) collective-permute-start(bf16[144,1024]{1,0:T(8,128)(2,1)S(1)} %copy-done.25), channel_id=1, source_target_pairs={{0,2},{1,3},{2,0},{3,1},{4,6},{5,7},{6,4},{7,5},{8,10},{9,11},{10,... | collective-permute-start | bytes 884744 | tf_op jit(solution)/shard_map/ppermute | solution.py:1106
  543.8 25.7 %collective-permute-start.62 = (bf16[144,1024]{1,0:T(8,128)(2,1)S(1)}, bf16[144,1024]{1,0:T(8,128)(2,1)S(1)}, u32[]{:S(2)}, u32[]{:S(2)}) collective-permute-start(bf16[144,1024]{1,0:T(8,128)(2,1)S(1)} %copy-done.25), channel_id=1, source_target_pairs={{0,3},{1,0},{2,1},{3,2},{4,7},{5,4},{6,5},{7,6},{8,11},{9,8},{10,9... | collective-permute-start | bytes 884744 | tf_op jit(solution)/shard_map/ppermute | solution.py:1106
  565.8 25.9 %collective-permute-start.61 = (bf16[144,1024]{1,0:T(8,128)(2,1)S(1)}, bf16[144,1024]{1,0:T(8,128)(2,1)S(1)}, u32[]{:S(2)}, u32[]{:S(2)}) collective-permute-start(bf16[144,1024]{1,0:T(8,128)(2,1)S(1)} %copy-done.26), channel_id=1, source_target_pairs={{0,2},{1,3},{2,0},{3,1},{4,6},{5,7},{6,4},{7,5},{8,10},{9,11},{10,... | collective-permute-start | bytes 884744 | tf_op jit(solution)/shard_map/ppermute | solution.py:1106
  565.8 26.4 %collective-permute-start.63 = (bf16[144,1024]{1,0:T(8,128)(2,1)S(1)}, bf16[144,1024]{1,0:T(8,128)(2,1)S(1)}, u32[]{:S(2)}, u32[]{:S(2)}) collective-permute-start(bf16[144,1024]{1,0:T(8,128)(2,1)S(1)} %copy-done.26), channel_id=1, source_target_pairs={{0,3},{1,0},{2,1},{3,2},{4,7},{5,4},{6,5},{7,6},{8,11},{9,8},{10,9... | collective-permute-start | bytes 884744 | tf_op jit(solution)/shard_map/ppermute | solution.py:1106
  566.3 39.8 %collective-permute-start.66 = (bf16[2,64,1024]{2,1,0:T(8,128)(2,1)S(1)}, bf16[2,64,1024]{2,1,0:T(8,128)(2,1)S(1)}, u32[]{:S(2)}, u32[]{:S(2)}) collective-permute-start(bf16[2,64,1024]{2,1,0:T(8,128)(2,1)S(1)} %copy-done.17), channel_id=1, source_target_pairs={{0,12},{4,8},{8,4},{12,0},{16,28},{20,24},{24,20},{28,16},{1,13},{... | collective-permute-start | bytes 786440 | tf_op jit(solution)/shard_map/ppermute | solution.py:1095
  569.5 36.6 %collective-permute-start.67 = (bf16[2,64,1024]{2,1,0:T(8,128)(2,1)S(1)}, bf16[2,64,1024]{2,1,0:T(8,128)(2,1)S(1)}, u32[]{:S(2)}, u32[]{:S(2)}) collective-permute-start(bf16[2,64,1024]{2,1,0:T(8,128)(2,1)S(1)} %copy-done.17), channel_id=1, source_target_pairs={{0,16},{4,20},{8,24},{12,28},{16,0},{20,4},{24,8},{28,12},{1,17},{... | collective-permute-start | bytes 786440 | tf_op jit(solution)/shard_map/ppermute | solution.py:1095
  572.4 33.7 %collective-permute-start.68 = (bf16[2,64,1024]{2,1,0:T(8,128)(2,1)S(1)}, bf16[2,64,1024]{2,1,0:T(8,128)(2,1)}, u32[]{:S(2)}, u32[]{:S(2)}) collective-permute-start(bf16[2,64,1024]{2,1,0:T(8,128)(2,1)S(1)} %copy-done.17), channel_id=1, source_target_pairs={{0,20},{4,16},{8,28},{12,24},{16,4},{20,0},{24,12},{28,8},{1,21},{... | collective-permute-start | bytes 786440 | tf_op jit(solution)/shard_map/ppermute | solution.py:1095
  592.2 20.1 %collective-permute-start.70 = (bf16[2,64,1024]{2,1,0:T(8,128)(2,1)S(1)}, bf16[2,64,1024]{2,1,0:T(8,128)(2,1)S(1)}, u32[]{:S(2)}, u32[]{:S(2)}) collective-permute-start(bf16[2,64,1024]{2,1,0:T(8,128)(2,1)S(1)} %copy-done.17), channel_id=1, source_target_pairs={{0,28},{4,24},{8,20},{12,16},{16,12},{20,8},{24,4},{28,0},{1,29},{... | collective-permute-start | bytes 786440 | tf_op jit(solution)/shard_map/ppermute | solution.py:1095
  (104 other events, 1066.0 us)
Sparse Core Ops, SparseCore 0:
  18.0 38.4 all-gather.7
  88.4 58.1 reduce-scatter.3
  150.1 49.2 all-gather.9
  229.3 48.3 reduce-scatter.5
  281.4 49.2 all-gather.11
  333.5 47.5 reduce-scatter.7
  383.0 115.4 all-gather.13
  500.9 37.4 all-gather.15
  542.5 64.0 all-reduce.1

commit v6 on v5

--- a/solution.py
+++ b/solution.py
@@ -77,8 +77,9 @@
     pieces_in, refs = refs[: len(places)], refs[len(places) :]
     if wide:
         weight_in, refs = refs[0], refs[1:]
-    query_ref, out_ref, low_ref, log_ref, kv_ref = refs[:5]
+    query_out, out_ref, low_ref, log_ref, kv_out = refs[:5]
     max_ref, sum_ref, acc_ref, scores_ref, start_ref, index_ref, sems = refs[5 + wide : 12 + wide]
+    query_ref, kv_ref, out_sems = refs[12 + wide : 15 + wide]
     tokens = pre_ref.shape[0]
     copies = []
     for n, (mask, offset) in enumerate(places):
@@ -88,7 +89,7 @@
     for copy in copies:
         copy.start()
     if wide:
-        branch_ref, weight_ref, weight_sem = refs[5], refs[13], refs[14]
+        branch_ref, weight_ref, weight_sem = refs[5], refs[16], refs[17]
         weight_copy = pltpu.make_async_copy(weight_in, weight_ref, weight_sem)
         weight_copy.start()
     width = kv_ref.shape[1] // 2
@@ -104,8 +105,12 @@
         query_ref[rows, half:] = (front * sine + back * cosine).astype(BF)
         start_ref[rows, :] = first_ref[...]
         index_ref[rows, :] = info_ref[0] + lax.broadcasted_iota(I32, (tokens, lanes), 0)
+    query_copy = pltpu.make_async_copy(query_ref, query_out, out_sems.at[0])
+    query_copy.start()
     for copy in copies:
         copy.wait()
+    kv_copy = pltpu.make_async_copy(kv_ref, kv_out, out_sems.at[1])
+    kv_copy.start()
     pieces = [slice(n * lanes, (n + 1) * lanes) for n in range(size // lanes)]
     for i in range(heads * tokens // tile):
         r = slice(i * tile, (i + 1) * tile)
@@ -160,6 +165,8 @@
             low_ref[rows, cols] = part.astype(BF)
             at = stop
 
+    query_copy.wait()
+    kv_copy.wait()
     if wide:
         weight_copy.wait()
 
@@ -200,7 +207,12 @@
         in_specs=[pl.BlockSpec(memory_space=pltpu.SMEM)]
         + in_vmem(4)
         + [pl.BlockSpec(memory_space=pl.ANY)] * (len(pieces) + wide),
-        out_specs=tuple(in_vmem(5 + wide)),
+        out_specs=(
+            pl.BlockSpec(memory_space=pltpu.HBM),
+            *in_vmem(3),
+            pl.BlockSpec(memory_space=pltpu.HBM),
+            *in_vmem(int(wide)),
+        ),
         scratch_shapes=[
             pltpu.VMEM((tile, LANES), F32),
             pltpu.VMEM((tile, LANES), F32),
@@ -209,6 +221,9 @@
             pltpu.VMEM((rows, LANES), I32),
             pltpu.VMEM((rows, LANES), I32),
             pltpu.SemaphoreType.DMA((len(pieces),)),
+            pltpu.VMEM((rows, width), BF),
+            pltpu.VMEM((keys, 2 * width), BF),
+            pltpu.SemaphoreType.DMA((2,)),
         ]
         + ([pltpu.VMEM(weight.shape, BF), pltpu.SemaphoreType.DMA(())] if wide else []),
         compiler_params=pltpu.CompilerParams(vmem_limit_bytes=56 * 2**20),

time: 642 us -> 642 us (level)
  transfers between devices with their start and end apart: 80 -> 80, of which waited for: 23 -> 23; matrix products, arithmetic and copies ran while one was open for 4% -> 4% of each run, Pallas kernels for 31% -> 32%
where the time goes in v6:
time: 642 us; the launch traced here: 632 us
  waiting for transfers between devices  253 us (39%)
  Pallas kernels  224 us (35%)
  starting transfers between devices  90.7 us (14%)
  local copies, waits for them, and re-layouts  35.6 us (6%)
  between operations  15 us (2%)
  matrix products  6.97 us (1%)
  other arithmetic  6.52 us (1%)
    pallas_call x21, Pallas kernels, placed_call(): pl.pallas_call(kernel, grid_spec=pltpu.PrefetchScalarGridSpec(num_scalar_...  135 us
    ppermute x44, waiting for transfers between devices, exchange(): return lax.ppermute(value, 'seq', [(i, i ^ mask) for i in range(count)])  71.6 us
    ppermute x44, starting transfers between devices, exchange(): return lax.ppermute(value, 'seq', [(i, i ^ mask) for i in range(count)])  65 us
    ppermute x27, waiting for transfers between devices, ring(): lax.ppermute(value, 'rank', [(i, (i + shift) % ranks) for i in range(rank...  62.7 us
    all_gather x1, waiting for transfers between devices, per_device_fast(): mid_low = lax.all_gather(mid_own, 'rank', axis=0, tiled=True)  49.4 us
    reduce_scatter x1, waiting for transfers between devices, per_device_fast(): lax.psum_scatter(branch_part, 'rank', scatter_dimension=0, tiled=True)  46.2 us
    pallas_call x10, Pallas kernels, placed_call(): pl.pallas_call(kernel, in_specs=[pl.BlockSpec(memory_space=pltpu.SMEM)] +...  31.8 us
    ppermute x27, starting transfers between devices, ring(): lax.ppermute(value, 'rank', [(i, (i + shift) % ranks) for i in range(rank...  24.5 us
  transfers between devices with their start and end apart: 80, of which 23 were waited for; matrix products, arithmetic and copies ran while one was open for 4% of the time, Pallas kernels for 32%

profile of v6, /device:TPU:25, one launch (start us, length us, event | category | flops | bytes accessed | tf_op | source)
XLA Modules:
  0.0 631.8 jit_solution(18355927003216536505)
XLA Ops:
  10.7 7.2 %project.1 = (bf16[576,2048]{1,0:T(8,128)(2,1)}, f32[576,128]{1,0:T(8,128)}, f32[576,512]{1,0:T(8,128)}, bf16[592,256]{1,0:T(8,128)(2,1)}) custom-call(s32[6]{0:T(128)} %stack.29.info_ref, bf16[576,2048]{1,0:T(8,128)(2,1)} %tokens_ref.4, f32[1,2048]{1,0:T(1,128)} %bitcast.48, bf16[2048,256]{1,0:T(8,128)(2,1)} %down_ref.1, bf16[2048,512]{1,0:T(8,128)(2,1)} %kv_weight_ref.3, ...), custom_call_target="tpu_custom_call" | custom-call | tf_op jit(solution)/shard_map/project/pallas_call | solution.py:412
  26.6 15.4 %collective-permute-done.1 = bf16[256,512]{1,0:T(8,128)(2,1)S(1)} collective-permute-done((bf16[256,512]{1,0:T(8,128)(2,1)S(1)}, bf16[256,512]{1,0:T(8,128)(2,1)S(1)}, u32[]{:S(2)}, u32[]{:S(2)}) %collective-permute-start.1) | collective-permute-done | bytes 262176 | tf_op jit(solution)/shard_map/ppermute | solution.py:1121
  43.8 3.9 collective-permute-start.3
  51.8 4.8 collective-permute-done.6.refs_3_
  62.2 5.1 queries.1
  68.2 17.4 %attend.1 = (bf16[2304,256]{1,0:T(8,128)(2,1)}, f32[576,1024]{1,0:T(8,128)}, bf16[576,1024]{1,0:T(8,128)(2,1)}, f32[1,2304]{1,0:T(1,128)}, bf16[4608,512]{1,0:T(8,128)(2,1)}, /*index=5*/bf16[576,2048]{1,0:T(8,128)(2,1)}) custom-call(s32[6]{0:T(128)} %stack.28.info_ref, f32[576,1024]{1,0:T(8,128)} %get-tuple-element.170.pre_ref, ...), custom_call_target="tpu_custom_call" | custom-call | tf_op jit(solution)/shard_map/attend/pallas_call | solution.py:195
  90.7 7.0 %fusion.2.grad_ref = f32[576,1408]{1,0:T(8,128)S(1)} fusion(bf16[576,2048]{1,0:T(8,128)(2,1)} %out_grad_ref.1, bf16[1408,2048]{1,0:T(8,128)(2,1)} %right_ref.2), kind=kOutput, calls=%fused_computation.20 | convolution fusion | flops 3321888768 | bytes 11370496 | tf_op jit(solution)/shard_map/dot_general | solution.py:46
  97.7 46.2 %reduce-scatter.4.cloned.1.call-done.branch_ref = bf16[144,2048]{1,0:T(8,128)(2,1)} async-done(((bf16[576,2048]{1,0:T(8,128)(2,1)}), bf16[144,2048]{1,0:T(8,128)(2,1)}) %reduce-scatter.4.cloned.1.call-update) | async-done | bytes 589840 | tf_op jit(solution)/shard_map/reduce_scatter | solution.py:1216
  143.9 3.3 mid_norm.1
  147.3 49.4 %all-gather.10.cloned.1.call-done.mid_ref.refs_0_ = bf16[576,2048]{1,0:T(8,128)(2,1)} async-done(((bf16[144,2048]{1,0:T(8,128)(2,1)}), bf16[576,2048]{1,0:T(8,128)(2,1)}) %all-gather.10.cloned.1.call-update) | async-done | bytes 2359312 | tf_op jit(solution)/shard_map/all_gather | solution.py:1235
  201.1 19.7 %feed_forward.1 = (bf16[576,1408]{1,0:T(8,128)(2,1)S(1)}, bf16[576,2816]{1,0:T(8,128)(2,1)S(1)}, bf16[576,2048]{1,0:T(8,128)(2,1)S(1)}) custom-call(bf16[576,2048]{1,0:T(8,128)(2,1)S(1)} %copy-done, f32[576,1408]{1,0:T(8,128)S(1)} %fusion.2.grad_ref, bf16[2048,1408]{1,0:T(8,128)(2,1)} %gate_ref.1, bf16[2048,1408]{1,0:T(8,128)(2,1)} %up_ref.1), custom_call_target="tpu_custom_call" | custom-call | flops 2000000000 | tf_op jit(solution)/shard_map/feed_forward/pallas_call | solution.py:358
  228.0 8.0 %matmul.2 = bf16[576,2048]{1,0:T(8,128)(2,1)} custom-call(s32[6]{0:T(128)} %stack.28.info_ref, bf16[576,1408]{1,0:T(8,128)(2,1)} %copy-done.2, bf16[1408,2048]{1,0:T(8,128)(2,1)} %right_ref.2), custom_call_target="tpu_custom_call" | custom-call | tf_op jit(solution)/shard_map/matmul/pallas_call | solution.py:412
  237.7 22.2 %pair_products.3 = (bf16[256,4224]{1,0:T(8,128)(2,1)}, bf16[256,4224]{1,0:T(8,128)(2,1)}, bf16[256,4224]{1,0:T(8,128)(2,1)}, bf16[256,4224]{1,0:T(8,128)(2,1)}) custom-call(s32[6]{0:T(128)} %stack.28.info_ref, bf16[576,2048]{1,0:T(8,128)(2,1)} %all-gather.10.cloned.1.call-done.mid_ref.refs_0_, bf16[576,2048]{1,0:T(8,128)(2,1)} %collective-permute-done.19.refs_1_, ...), custom_call_target="tpu_custom_call" | custom-call | tf_op jit(solution)/shard_map/pair_products/pallas_call | solution.py:412
  262.2 12.7 %reduce-scatter.6.cloned.1.call-done.grad_ref = bf16[144,2048]{1,0:T(8,128)(2,1)} async-done(((bf16[576,2048]{1,0:T(8,128)(2,1)}), bf16[144,2048]{1,0:T(8,128)(2,1)}) %reduce-scatter.6.cloned.1.call-update) | async-done | bytes 589840 | tf_op jit(solution)/shard_map/reduce_scatter | solution.py:1244
  274.9 3.6 mid_back.1
  278.7 29.8 %collective-permute-done.22 = bf16[256,4224]{1,0:T(8,128)(2,1)S(1)} collective-permute-done((bf16[256,4224]{1,0:T(8,128)(2,1)}, bf16[256,4224]{1,0:T(8,128)(2,1)S(1)}, u32[]{:S(2)}, u32[]{:S(2)}) %collective-permute-start.22) | collective-permute-done | bytes 2162720 | tf_op jit(solution)/shard_map/ppermute | solution.py:1110
  309.8 6.7 %fold_first.4 = (bf16[128,4224]{1,0:T(8,128)(2,1)}, bf16[128,4224]{1,0:T(8,128)(2,1)}, bf16[128,4224]{1,0:T(8,128)(2,1)}, bf16[128,4224]{1,0:T(8,128)(2,1)}) custom-call(s32[6]{0:T(128)} %stack.28.info_ref, bf16[2,128,4224]{2,1,0:T(8,128)(2,1)} %bitcast.54, bf16[2,128,4224]{2,1,0:T(8,128)(2,1)} %bitcast.56, bf16[2,128,4224]{2,1,0:T(8,128)(2,1)} %bitcast.55, ...), custom_call_target="tpu_custom_call" | custom-call | flops 999999995904 | tf_op jit(solution)/shard_map/fold_first/pallas_call | solution.py:412
  319.1 9.0 %all-gather.12.cloned.1.call-done.left_ref.refs_2_.branch_ref = bf16[576,2048]{1,0:T(8,128)(2,1)} async-done(((bf16[144,2048]{1,0:T(8,128)(2,1)}), bf16[576,2048]{1,0:T(8,128)(2,1)}) %all-gather.12.cloned.1.call-update) | async-done | bytes 2359312 | tf_op jit(solution)/shard_map/all_gather | solution.py:1258
  331.0 6.6 %matmul.3.grad_ref = bf16[576,1024]{1,0:T(8,128)(2,1)} custom-call(s32[6]{0:T(128)} %stack.28.info_ref, bf16[576,2048]{1,0:T(8,128)(2,1)} %all-gather.12.cloned.1.call-done.left_ref.refs_2_.branch_ref, bf16[1024,2048]{1,0:T(8,128)(2,1)} %right_ref.3), custom_call_target="tpu_custom_call" | custom-call | tf_op jit(solution)/shard_map/matmul/pallas_call | solution.py:412
  339.3 7.6 %pair_products.4 = (bf16[128,2048]{1,0:T(8,128)(2,1)}, bf16[128,2048]{1,0:T(8,128)(2,1)}, bf16[128,2048]{1,0:T(8,128)(2,1)}, bf16[128,2048]{1,0:T(8,128)(2,1)}) custom-call(s32[6]{0:T(128)} %stack.28.info_ref, bf16[576,1024]{1,0:T(8,128)(2,1)} %get-tuple-element.173.refs_0_, bf16[576,1024]{1,0:T(8,128)(2,1)} %collective-permute-done.14.refs_1_, ...), custom_call_target="tpu_custom_call" | custom-call | tf_op jit(solution)/shard_map/pair_products/pallas_call | solution.py:412
  348.2 5.2 fold_last.2
  357.6 19.5 %attend_back.1 = (bf16[576,1024]{1,0:T(8,128)(2,1)}, bf16[2,4,288,512]{3,2,1,0:T(8,128)(2,1)}, bf16[2,4,288,512]{3,2,1,0:T(8,128)(2,1)}) custom-call(s32[6]{0:T(128)} %stack.28.info_ref, bf16[2304,256]{1,0:T(8,128)(2,1)} %get-tuple-element.213.query_ref, bf16[576,1024]{1,0:T(8,128)(2,1)} %matmul.3.grad_ref, f32[576,1024]{1,0:T(8,128)} %get-tuple-element.214.out_ref, ...), custom_call_target="tpu_custom_call" | custom-call | tf_op jit(solution)/shard_map/attend_back/pallas_call | solution.py:307
  378.8 3.3 fold_first.5
  382.1 13.3 %collective-permute-start.32 = (bf16[64,2048]{1,0:T(8,128)(2,1)}, bf16[64,2048]{1,0:T(8,128)(2,1)S(1)}, u32[]{:S(2)}, u32[]{:S(2)}) collective-permute-start(bf16[64,2048]{1,0:T(8,128)(2,1)} %get-tuple-element.229), channel_id=1, source_target_pairs={{0,16},{4,20},{8,24},{12,28},{16,0},{20,4},{24,8},{28,12},{1,17},{... | collective-permute-start | bytes 786440 | tf_op jit(solution)/shard_map/ppermute | solution.py:1110
  395.4 8.0 %collective-permute-start.33 = (bf16[64,2048]{1,0:T(8,128)(2,1)}, bf16[64,2048]{1,0:T(8,128)(2,1)S(1)}, u32[]{:S(2)}, u32[]{:S(2)}) collective-permute-start(bf16[64,2048]{1,0:T(8,128)(2,1)} %get-tuple-element.239), channel_id=1, source_target_pairs={{0,8},{4,12},{8,0},{12,4},{16,24},{20,28},{24,16},{28,20},{1,9},{5... | collective-permute-start | bytes 786440 | tf_op jit(solution)/shard_map/ppermute | solution.py:1110
  403.4 4.4 latent_parts.1
  409.2 5.4 fold_near.1
  425.5 5.5 pair_products.5
  431.0 19.0 %collective-permute-done.36.refs_2_ = bf16[144,1024]{1,0:T(8,128)(2,1)S(1)} collective-permute-done((bf16[144,1024]{1,0:T(8,128)(2,1)S(1)}, bf16[144,1024]{1,0:T(8,128)(2,1)S(1)}, u32[]{:S(2)}, u32[]{:S(2)}) %collective-permute-start.36) | collective-permute-done | bytes 294944 | tf_op jit(solution)/shard_map/ppermute | solution.py:1121
  450.8 3.2 latent_back.1.refs_0_
  454.1 3.7 fold_first.6
  462.2 10.6 %collective-permute-done.43.got_first = bf16[288,512]{1,0:T(8,128)(2,1)S(1)} collective-permute-done((bf16[288,512]{1,0:T(8,128)(2,1)}, bf16[288,512]{1,0:T(8,128)(2,1)S(1)}, u32[]{:S(2)}, u32[]{:S(2)}) %collective-permute-start.43) | collective-permute-done | bytes 294944 | tf_op jit(solution)/shard_map/ppermute | solution.py:1110
  477.5 12.5 %collective-permute-done.45 = bf16[128,1024]{1,0:T(8,128)(2,1)S(1)} collective-permute-done((bf16[128,1024]{1,0:T(8,128)(2,1)S(1)}, bf16[128,1024]{1,0:T(8,128)(2,1)S(1)}, u32[]{:S(2)}, u32[]{:S(2)}) %collective-permute-start.45) | collective-permute-done | bytes 262176 | tf_op jit(solution)/shard_map/ppermute | solution.py:1110
  506.4 2.9 collective-permute-start.52
  509.7 2.9 collective-permute-start.55
  513.2 9.7 %collective-permute-done.53.refs_6_ = bf16[144,512]{1,0:T(8,128)(2,1)S(1)} collective-permute-done((bf16[144,512]{1,0:T(8,128)(2,1)}, bf16[144,512]{1,0:T(8,128)(2,1)S(1)}, u32[]{:S(2)}, u32[]{:S(2)}) %collective-permute-start.53) | collective-permute-done | bytes 147488 | tf_op jit(solution)/shard_map/ppermute | solution.py:1121
  523.6 6.6 %input_back.1 = (f32[576,512]{1,0:T(8,128)}, bf16[16,256]{1,0:T(8,128)(2,1)}, bf16[576,256]{1,0:T(8,128)(2,1)}, bf16[576,512]{1,0:T(8,128)(2,1)}) custom-call(s32[6]{0:T(128)} %stack.28.info_ref, bf16[576,2048]{1,0:T(8,128)(2,1)} %tokens_ref.4, bf16[576,2048]{1,0:T(8,128)(2,1)} %all-gather.12.cloned.1.call-done.left_ref.refs_2_.branch_ref, ...), custom_call_target="tpu_custom_call" | custom-call | tf_op jit(solution)/shard_map/input_back/pallas_call | solution.py:412
  530.2 4.6 last_products.1
  537.7 5.3 collective-permute-start.64
  546.2 18.4 %unpack.2 = (f32[2048,1408]{1,0:T(8,128)}, f32[2048,1408]{1,0:T(8,128)}, f32[1408,2048]{1,0:T(8,128)}) custom-call(s32[6]{0:T(128)} %stack.28.info_ref, bf16[4,2,2,128,4224]{4,3,2,1,0:T(8,128)(2,1)} %bitcast.34), custom_call_target="tpu_custom_call" | custom-call | tf_op jit(solution)/shard_map/unpack/pallas_call | solution.py:412
  567.1 3.4 collective-permute-start.66
  576.2 16.2 %collective-permute-done.61.refs_5_ = bf16[144,1024]{1,0:T(8,128)(2,1)S(1)} collective-permute-done((bf16[144,1024]{1,0:T(8,128)(2,1)S(1)}, bf16[144,1024]{1,0:T(8,128)(2,1)S(1)}, u32[]{:S(2)}, u32[]{:S(2)}) %collective-permute-start.61) | collective-permute-done | bytes 294944 | tf_op jit(solution)/shard_map/ppermute | solution.py:1121
  593.2 3.0 collective-permute-start.70
  596.1 6.7 %unpack.3 = f32[1024,2048]{1,0:T(8,128)} custom-call(s32[6]{0:T(128)} %stack.28.info_ref, bf16[4,2,2,64,2048]{4,3,2,1,0:T(8,128)(2,1)} %bitcast.37), custom_call_target="tpu_custom_call" | custom-call | tf_op jit(solution)/shard_map/unpack/pallas_call | solution.py:412
  602.9 4.2 place.1
  607.2 6.1 collective-permute-done.70.refs_7_
  614.0 3.8 unpack_up.1
  617.8 3.2 last.1
  (328 shorter events, 120.7 us)
Async XLA Ops:
  7.2 55.0 %all-gather.8.cloned.1.call-start = ((), (), s32[]{:S(2)}) async-start(), calls=%async_computation.3 | async-start | bytes 1515520 | tf_op jit(solution)/shard_map/all_gather | solution.py:1201
  8.5 18.1 %collective-permute-start = (bf16[256,512]{1,0:T(8,128)(2,1)S(1)}, bf16[256,512]{1,0:T(8,128)(2,1)S(1)}, u32[]{:S(2)}, u32[]{:S(2)}) collective-permute-start(bf16[256,512]{1,0:T(8,128)(2,1)S(1)} %get-tuple-element.316), channel_id=1, source_target_pairs={{0,1},{1,2},{2,3},{3,0},{4,5},{5,6},{6,7},{7,4},{8,9},{9,10},{10,1... | collective-permute-start | bytes 786440 | tf_op jit(solution)/shard_map/ppermute | solution.py:1121
  8.6 33.4 %collective-permute-start.1 = (bf16[256,512]{1,0:T(8,128)(2,1)S(1)}, bf16[256,512]{1,0:T(8,128)(2,1)S(1)}, u32[]{:S(2)}, u32[]{:S(2)}) collective-permute-start(bf16[256,512]{1,0:T(8,128)(2,1)S(1)} %get-tuple-element.318), channel_id=1, source_target_pairs={{0,2},{1,3},{2,0},{3,1},{4,6},{5,7},{6,4},{7,5},{8,10},{9,11},{10,... | collective-permute-start | bytes 786440 | tf_op jit(solution)/shard_map/ppermute | solution.py:1121
  9.9 32.8 %collective-permute-start.2 = (bf16[256,512]{1,0:T(8,128)(2,1)S(1)}, bf16[256,512]{1,0:T(8,128)(2,1)}, u32[]{:S(2)}, u32[]{:S(2)}) collective-permute-start(bf16[256,512]{1,0:T(8,128)(2,1)S(1)} %get-tuple-element.315), channel_id=1, source_target_pairs={{0,3},{1,0},{2,1},{3,2},{4,7},{5,4},{6,5},{7,6},{8,11},{9,8},{10,9... | collective-permute-start | bytes 786440 | tf_op jit(solution)/shard_map/ppermute | solution.py:1121
  17.9 126.0 %reduce-scatter.4.cloned.1.call-start = ((), (), s32[]{:S(2)}) async-start(), calls=%async_computation.4 | async-start | bytes 2949120 | tf_op jit(solution)/shard_map/reduce_scatter | solution.py:1216
  24.2 23.6 %collective-permute-start.4 = (bf16[576,512]{1,0:T(8,128)(2,1)}, bf16[576,512]{1,0:T(8,128)(2,1)S(1)}, u32[]{:S(2)}, u32[]{:S(2)}) collective-permute-start(bf16[576,512]{1,0:T(8,128)(2,1)} %turn.1.refs_0_), channel_id=1, source_target_pairs={{0,8},{4,12},{8,0},{12,4},{16,24},{20,28},{24,16},{28,20},{1,9},{5... | collective-permute-start | bytes 1769480 | tf_op jit(solution)/shard_map/ppermute | solution.py:1110
  25.4 22.4 %collective-permute-start.5 = (bf16[576,512]{1,0:T(8,128)(2,1)}, bf16[576,512]{1,0:T(8,128)(2,1)}, u32[]{:S(2)}, u32[]{:S(2)}) collective-permute-start(bf16[576,512]{1,0:T(8,128)(2,1)} %turn.1.refs_0_), channel_id=1, source_target_pairs={{0,16},{4,20},{8,24},{12,28},{16,0},{20,4},{24,8},{28,12},{1,17},{... | collective-permute-start | bytes 1769480 | tf_op jit(solution)/shard_map/ppermute | solution.py:1110
  85.6 111.0 %all-gather.10.cloned.1.call-start = ((), (), s32[]{:S(2)}) async-start(), calls=%async_computation.5 | async-start | bytes 2949120 | tf_op jit(solution)/shard_map/all_gather | solution.py:1235
  147.3 127.7 %reduce-scatter.6.cloned.1.call-start = ((), (), s32[]{:S(2)}) async-start(), calls=%async_computation.6 | async-start | bytes 2949120 | tf_op jit(solution)/shard_map/reduce_scatter | solution.py:1244
  196.7 28.4 %collective-permute-start.16 = (bf16[512,256]{1,0:T(8,128)(2,1)}, bf16[512,256]{1,0:T(8,128)(2,1)}, u32[]{:S(2)}, u32[]{:S(2)}) collective-permute-start(bf16[512,256]{1,0:T(8,128)(2,1)} %get-tuple-element.186), channel_id=1, source_target_pairs={{0,1},{1,2},{2,3},{3,0},{4,5},{5,6},{6,7},{7,4},{8,9},{9,10},{10,1... | collective-permute-start | bytes 786440 | tf_op jit(solution)/shard_map/ppermute | solution.py:1121
  199.1 26.0 %collective-permute-start.17 = (bf16[512,256]{1,0:T(8,128)(2,1)}, bf16[512,256]{1,0:T(8,128)(2,1)}, u32[]{:S(2)}, u32[]{:S(2)}) collective-permute-start(bf16[512,256]{1,0:T(8,128)(2,1)} %get-tuple-element.187), channel_id=1, source_target_pairs={{0,2},{1,3},{2,0},{3,1},{4,6},{5,7},{6,4},{7,5},{8,10},{9,11},{10,... | collective-permute-start | bytes 786440 | tf_op jit(solution)/shard_map/ppermute | solution.py:1121
  199.2 25.9 %collective-permute-start.18 = (bf16[512,256]{1,0:T(8,128)(2,1)S(1)}, bf16[512,256]{1,0:T(8,128)(2,1)}, u32[]{:S(2)}, u32[]{:S(2)}) collective-permute-start(bf16[512,256]{1,0:T(8,128)(2,1)S(1)} %get-tuple-element.188), channel_id=1, source_target_pairs={{0,3},{1,0},{2,1},{3,2},{4,7},{5,4},{6,5},{7,6},{8,11},{9,8},{10,9... | collective-permute-start | bytes 786440 | tf_op jit(solution)/shard_map/ppermute | solution.py:1121
  226.4 101.6 %all-gather.12.cloned.1.call-start = ((), (), s32[]{:S(2)}) async-start(), calls=%async_computation.7 | async-start | bytes 2949120 | tf_op jit(solution)/shard_map/all_gather | solution.py:1258
  259.9 48.6 %collective-permute-start.22 = (bf16[256,4224]{1,0:T(8,128)(2,1)}, bf16[256,4224]{1,0:T(8,128)(2,1)S(1)}, u32[]{:S(2)}, u32[]{:S(2)}) collective-permute-start(bf16[256,4224]{1,0:T(8,128)(2,1)} %get-tuple-element.192), channel_id=1, source_target_pairs={{0,8},{4,12},{8,0},{12,4},{16,24},{20,28},{24,16},{28,20},{1,9},{5... | collective-permute-start | bytes 6488072 | tf_op jit(solution)/shard_map/ppermute | solution.py:1110
  261.0 48.2 %collective-permute-start.23 = (bf16[256,4224]{1,0:T(8,128)(2,1)}, bf16[256,4224]{1,0:T(8,128)(2,1)}, u32[]{:S(2)}, u32[]{:S(2)}) collective-permute-start(bf16[256,4224]{1,0:T(8,128)(2,1)} %get-tuple-element.202), channel_id=1, source_target_pairs={{0,16},{4,20},{8,24},{12,28},{16,0},{20,4},{24,8},{28,12},{1,17},{... | collective-permute-start | bytes 6488072 | tf_op jit(solution)/shard_map/ppermute | solution.py:1110
  278.6 99.7 %reduce-scatter.8.cloned.1.call-start = ((), (), s32[]{:S(2)}) async-start(), calls=%async_computation.8 | async-start | bytes 2949120 | tf_op jit(solution)/shard_map/reduce_scatter | solution.py:1274
  316.5 229.8 %all-gather.14.cloned.1.call-start = ((), (), s32[]{:S(2)}) async-start(), calls=%async_computation.10 | async-start | bytes 19464192 | tf_op jit(solution)/shard_map/all_gather | solution.py:1273
  316.7 30.2 %collective-permute-start.27 = (bf16[128,4224]{1,0:T(8,128)(2,1)}, bf16[128,4224]{1,0:T(8,128)(2,1)S(1)}, u32[]{:S(2)}, u32[]{:S(2)}) collective-permute-start(bf16[128,4224]{1,0:T(8,128)(2,1)} %get-tuple-element.203), channel_id=1, source_target_pairs={{0,16},{4,20},{8,24},{12,28},{16,0},{20,4},{24,8},{28,12},{1,17},{... | collective-permute-start | bytes 3244040 | tf_op jit(solution)/shard_map/ppermute | solution.py:1110
  317.9 29.0 %collective-permute-start.28 = (bf16[128,4224]{1,0:T(8,128)(2,1)S(1)}, bf16[128,4224]{1,0:T(8,128)(2,1)S(1)}, u32[]{:S(2)}, u32[]{:S(2)}) collective-permute-start(bf16[128,4224]{1,0:T(8,128)(2,1)S(1)} %copy-done.64), channel_id=1, source_target_pairs={{0,8},{4,12},{8,0},{12,4},{16,24},{20,28},{24,16},{28,20},{1,9},{5... | collective-permute-start | bytes 3244040 | tf_op jit(solution)/shard_map/ppermute | solution.py:1110
  353.4 242.7 %all-gather.16.cloned.1.call-start = ((), (), s32[]{:S(2)}) async-start(), calls=%async_computation.11 | async-start | bytes 4718592 | tf_op jit(solution)/shard_map/all_gather | solution.py:1294
  353.5 23.6 %collective-permute-start.29 = (bf16[128,2048]{1,0:T(8,128)(2,1)S(1)}, bf16[128,2048]{1,0:T(8,128)(2,1)S(1)}, u32[]{:S(2)}, u32[]{:S(2)}) collective-permute-start(bf16[128,2048]{1,0:T(8,128)(2,1)S(1)} %copy-done.66), channel_id=1, source_target_pairs={{0,8},{4,12},{8,0},{12,4},{16,24},{20,28},{24,16},{28,20},{1,9},{5... | collective-permute-start | bytes 1572872 | tf_op jit(solution)/shard_map/ppermute | solution.py:1110
  355.0 22.1 %collective-permute-start.30 = (bf16[128,2048]{1,0:T(8,128)(2,1)S(1)}, bf16[128,2048]{1,0:T(8,128)(2,1)S(1)}, u32[]{:S(2)}, u32[]{:S(2)}) collective-permute-start(bf16[128,2048]{1,0:T(8,128)(2,1)S(1)} %copy-done.65), channel_id=1, source_target_pairs={{0,16},{4,20},{8,24},{12,28},{16,0},{20,4},{24,8},{28,12},{1,17},{... | collective-permute-start | bytes 1572872 | tf_op jit(solution)/shard_map/ppermute | solution.py:1110
  378.4 29.5 %collective-permute-start.31 = (bf16[2,4,288,512]{3,2,1,0:T(8,128)(2,1)}, bf16[2,4,288,512]{3,2,1,0:T(8,128)(2,1)S(1)}, u32[]{:S(2)}, u32[]{:S(2)}) collective-permute-start(bf16[2,4,288,512]{3,2,1,0:T(8,128)(2,1)} %get-tuple-element.234), channel_id=1, source_target_pairs={{0,4},{4,0},{8,12},{12,8},{16,20},{20,16},{24,28},{28,24},{1,5},{5... | collective-permute-start | bytes 7077896 | tf_op jit(solution)/shard_map/ppermute | solution.py:1110
  382.1 32.5 %collective-permute-start.32 = (bf16[64,2048]{1,0:T(8,128)(2,1)}, bf16[64,2048]{1,0:T(8,128)(2,1)S(1)}, u32[]{:S(2)}, u32[]{:S(2)}) collective-permute-start(bf16[64,2048]{1,0:T(8,128)(2,1)} %get-tuple-element.229), channel_id=1, source_target_pairs={{0,16},{4,20},{8,24},{12,28},{16,0},{20,4},{24,8},{28,12},{1,17},{... | collective-permute-start | bytes 786440 | tf_op jit(solution)/shard_map/ppermute | solution.py:1110
  395.4 20.7 %collective-permute-start.33 = (bf16[64,2048]{1,0:T(8,128)(2,1)}, bf16[64,2048]{1,0:T(8,128)(2,1)S(1)}, u32[]{:S(2)}, u32[]{:S(2)}) collective-permute-start(bf16[64,2048]{1,0:T(8,128)(2,1)} %get-tuple-element.239), channel_id=1, source_target_pairs={{0,8},{4,12},{8,0},{12,4},{16,24},{20,28},{24,16},{28,20},{1,9},{5... | collective-permute-start | bytes 786440 | tf_op jit(solution)/shard_map/ppermute | solution.py:1110
  419.6 198.2 %all-reduce.2.cloned.1.call-start = ((), (), s32[]{:S(2)}) async-start(), calls=%async_computation.9 | async-start | bytes 3162112 | tf_op jit(solution)/shard_map/psum | solution.py:1320
  420.1 29.8 %collective-permute-start.38 = (bf16[2,288,512]{2,1,0:T(8,128)(2,1)}, bf16[2,288,512]{2,1,0:T(8,128)(2,1)S(1)}, u32[]{:S(2)}, u32[]{:S(2)}) collective-permute-start(bf16[2,288,512]{2,1,0:T(8,128)(2,1)} %get-tuple-element.246), channel_id=1, source_target_pairs={{0,8},{4,12},{8,0},{12,4},{16,24},{20,28},{24,16},{28,20},{1,9},{5... | collective-permute-start | bytes 1769480 | tf_op jit(solution)/shard_map/ppermute | solution.py:1110
  421.8 28.2 %collective-permute-start.39 = (bf16[2,288,512]{2,1,0:T(8,128)(2,1)}, bf16[2,288,512]{2,1,0:T(8,128)(2,1)S(1)}, u32[]{:S(2)}, u32[]{:S(2)}) collective-permute-start(bf16[2,288,512]{2,1,0:T(8,128)(2,1)} %get-tuple-element.247), channel_id=1, source_target_pairs={{0,16},{4,20},{8,24},{12,28},{16,0},{20,4},{24,8},{28,12},{1,17},{... | collective-permute-start | bytes 1769480 | tf_op jit(solution)/shard_map/ppermute | solution.py:1110
  424.4 25.6 %collective-permute-start.36 = (bf16[144,1024]{1,0:T(8,128)(2,1)S(1)}, bf16[144,1024]{1,0:T(8,128)(2,1)S(1)}, u32[]{:S(2)}, u32[]{:S(2)}) collective-permute-start(bf16[144,1024]{1,0:T(8,128)(2,1)S(1)} %copy-done.68), channel_id=1, source_target_pairs={{0,2},{1,3},{2,0},{3,1},{4,6},{5,7},{6,4},{7,5},{8,10},{9,11},{10,... | collective-permute-start | bytes 884744 | tf_op jit(solution)/shard_map/ppermute | solution.py:1121
  424.5 25.5 %collective-permute-start.37 = (bf16[144,1024]{1,0:T(8,128)(2,1)S(1)}, bf16[144,1024]{1,0:T(8,128)(2,1)S(1)}, u32[]{:S(2)}, u32[]{:S(2)}) collective-permute-start(bf16[144,1024]{1,0:T(8,128)(2,1)S(1)} %copy-done.67), channel_id=1, source_target_pairs={{0,3},{1,0},{2,1},{3,2},{4,7},{5,4},{6,5},{7,6},{8,11},{9,8},{10,9... | collective-permute-start | bytes 884744 | tf_op jit(solution)/shard_map/ppermute | solution.py:1121
  459.2 18.3 %collective-permute-start.40 = (bf16[160,1024]{1,0:T(8,128)(2,1)S(1)}, bf16[160,1024]{1,0:T(8,128)(2,1)S(1)}, u32[]{:S(2)}, u32[]{:S(2)}) collective-permute-start(bf16[160,1024]{1,0:T(8,128)(2,1)S(1)} %copy-done.12), channel_id=1, source_target_pairs={{0,1},{1,2},{2,3},{3,0},{4,5},{5,6},{6,7},{7,4},{8,9},{9,10},{10,1... | collective-permute-start | bytes 983048 | tf_op jit(solution)/shard_map/ppermute | solution.py:1121
  459.2 36.0 %collective-permute-start.41 = (bf16[160,1024]{1,0:T(8,128)(2,1)S(1)}, bf16[160,1024]{1,0:T(8,128)(2,1)S(1)}, u32[]{:S(2)}, u32[]{:S(2)}) collective-permute-start(bf16[160,1024]{1,0:T(8,128)(2,1)S(1)} %copy-done.12), channel_id=1, source_target_pairs={{0,2},{1,3},{2,0},{3,1},{4,6},{5,7},{6,4},{7,5},{8,10},{9,11},{10,... | collective-permute-start | bytes 983048 | tf_op jit(solution)/shard_map/ppermute | solution.py:1121
  460.8 34.8 %collective-permute-start.42 = (bf16[160,1024]{1,0:T(8,128)(2,1)S(1)}, bf16[160,1024]{1,0:T(8,128)(2,1)S(1)}, u32[]{:S(2)}, u32[]{:S(2)}) collective-permute-start(bf16[160,1024]{1,0:T(8,128)(2,1)S(1)} %copy-done.12), channel_id=1, source_target_pairs={{0,3},{1,0},{2,1},{3,2},{4,7},{5,4},{6,5},{7,6},{8,11},{9,8},{10,9... | collective-permute-start | bytes 983048 | tf_op jit(solution)/shard_map/ppermute | solution.py:1121
  477.5 25.0 %collective-permute-start.49 = (bf16[144,512]{1,0:T(8,128)(2,1)}, bf16[144,512]{1,0:T(8,128)(2,1)S(1)}, u32[]{:S(2)}, u32[]{:S(2)}) collective-permute-start(bf16[144,512]{1,0:T(8,128)(2,1)} %get-tuple-element.278), channel_id=1, source_target_pairs={{0,1},{1,2},{2,3},{3,0},{4,5},{5,6},{6,7},{7,4},{8,9},{9,10},{10,1... | collective-permute-start | bytes 442376 | tf_op jit(solution)/shard_map/ppermute | solution.py:1121
  509.7 25.1 %collective-permute-start.55 = (bf16[2,16,1024]{2,1,0:T(8,128)(2,1)}, bf16[2,16,1024]{2,1,0:T(8,128)(2,1)S(1)}, u32[]{:S(2)}, u32[]{:S(2)}) collective-permute-start(bf16[2,16,1024]{2,1,0:T(8,128)(2,1)} %get-tuple-element.293), channel_id=1, source_target_pairs={{0,1},{1,2},{2,3},{3,0},{4,5},{5,6},{6,7},{7,4},{8,9},{9,10},{10,1... | collective-permute-start | bytes 196616 | tf_op jit(solution)/shard_map/ppermute | solution.py:1121
  512.6 22.2 %collective-permute-start.56 = (bf16[2,16,1024]{2,1,0:T(8,128)(2,1)}, bf16[2,16,1024]{2,1,0:T(8,128)(2,1)S(1)}, u32[]{:S(2)}, u32[]{:S(2)}) collective-permute-start(bf16[2,16,1024]{2,1,0:T(8,128)(2,1)} %get-tuple-element.294), channel_id=1, source_target_pairs={{0,2},{1,3},{2,0},{3,1},{4,6},{5,7},{6,4},{7,5},{8,10},{9,11},{10,... | collective-permute-start | bytes 196616 | tf_op jit(solution)/shard_map/ppermute | solution.py:1121
  513.2 21.6 %collective-permute-start.57 = (bf16[2,16,1024]{2,1,0:T(8,128)(2,1)}, bf16[2,16,1024]{2,1,0:T(8,128)(2,1)S(1)}, u32[]{:S(2)}, u32[]{:S(2)}) collective-permute-start(bf16[2,16,1024]{2,1,0:T(8,128)(2,1)} %get-tuple-element.295), channel_id=1, source_target_pairs={{0,3},{1,0},{2,1},{3,2},{4,7},{5,4},{6,5},{7,6},{8,11},{9,8},{10,9... | collective-permute-start | bytes 196616 | tf_op jit(solution)/shard_map/ppermute | solution.py:1121
  537.7 28.8 %collective-permute-start.58 = (bf16[144,1024]{1,0:T(8,128)(2,1)S(1)}, bf16[144,1024]{1,0:T(8,128)(2,1)S(1)}, u32[]{:S(2)}, u32[]{:S(2)}) collective-permute-start(bf16[144,1024]{1,0:T(8,128)(2,1)S(1)} %copy-done.25), channel_id=1, source_target_pairs={{0,1},{1,2},{2,3},{3,0},{4,5},{5,6},{6,7},{7,4},{8,9},{9,10},{10,1... | collective-permute-start | bytes 884744 | tf_op jit(solution)/shard_map/ppermute | solution.py:1121
  537.7 26.8 %collective-permute-start.64 = (bf16[2,64,1024]{2,1,0:T(8,128)(2,1)}, bf16[2,64,1024]{2,1,0:T(8,128)(2,1)S(1)}, u32[]{:S(2)}, u32[]{:S(2)}) collective-permute-start(bf16[2,64,1024]{2,1,0:T(8,128)(2,1)} %pack_up.1.refs_0_), channel_id=1, source_target_pairs={{0,4},{4,0},{8,12},{12,8},{16,20},{20,16},{24,28},{28,24},{1,5},{5... | collective-permute-start | bytes 786440 | tf_op jit(solution)/shard_map/ppermute | solution.py:1110
  543.1 23.4 %collective-permute-start.65 = (bf16[2,64,1024]{2,1,0:T(8,128)(2,1)}, bf16[2,64,1024]{2,1,0:T(8,128)(2,1)S(1)}, u32[]{:S(2)}, u32[]{:S(2)}) collective-permute-start(bf16[2,64,1024]{2,1,0:T(8,128)(2,1)} %pack_up.1.refs_0_), channel_id=1, source_target_pairs={{0,8},{4,12},{8,0},{12,4},{16,24},{20,28},{24,16},{28,20},{1,9},{5... | collective-permute-start | bytes 786440 | tf_op jit(solution)/shard_map/ppermute | solution.py:1110
  543.1 24.0 %collective-permute-start.60 = (bf16[144,1024]{1,0:T(8,128)(2,1)S(1)}, bf16[144,1024]{1,0:T(8,128)(2,1)S(1)}, u32[]{:S(2)}, u32[]{:S(2)}) collective-permute-start(bf16[144,1024]{1,0:T(8,128)(2,1)S(1)} %copy-done.25), channel_id=1, source_target_pairs={{0,2},{1,3},{2,0},{3,1},{4,6},{5,7},{6,4},{7,5},{8,10},{9,11},{10,... | collective-permute-start | bytes 884744 | tf_op jit(solution)/shard_map/ppermute | solution.py:1121
  544.6 25.9 %collective-permute-start.62 = (bf16[144,1024]{1,0:T(8,128)(2,1)S(1)}, bf16[144,1024]{1,0:T(8,128)(2,1)S(1)}, u32[]{:S(2)}, u32[]{:S(2)}) collective-permute-start(bf16[144,1024]{1,0:T(8,128)(2,1)S(1)} %copy-done.25), channel_id=1, source_target_pairs={{0,3},{1,0},{2,1},{3,2},{4,7},{5,4},{6,5},{7,6},{8,11},{9,8},{10,9... | collective-permute-start | bytes 884744 | tf_op jit(solution)/shard_map/ppermute | solution.py:1121
  566.5 25.9 %collective-permute-start.61 = (bf16[144,1024]{1,0:T(8,128)(2,1)S(1)}, bf16[144,1024]{1,0:T(8,128)(2,1)S(1)}, u32[]{:S(2)}, u32[]{:S(2)}) collective-permute-start(bf16[144,1024]{1,0:T(8,128)(2,1)S(1)} %copy-done.26), channel_id=1, source_target_pairs={{0,2},{1,3},{2,0},{3,1},{4,6},{5,7},{6,4},{7,5},{8,10},{9,11},{10,... | collective-permute-start | bytes 884744 | tf_op jit(solution)/shard_map/ppermute | solution.py:1121
  566.6 26.6 %collective-permute-start.63 = (bf16[144,1024]{1,0:T(8,128)(2,1)S(1)}, bf16[144,1024]{1,0:T(8,128)(2,1)S(1)}, u32[]{:S(2)}, u32[]{:S(2)}) collective-permute-start(bf16[144,1024]{1,0:T(8,128)(2,1)S(1)} %copy-done.26), channel_id=1, source_target_pairs={{0,3},{1,0},{2,1},{3,2},{4,7},{5,4},{6,5},{7,6},{8,11},{9,8},{10,9... | collective-permute-start | bytes 884744 | tf_op jit(solution)/shard_map/ppermute | solution.py:1121
  567.1 40.0 %collective-permute-start.66 = (bf16[2,64,1024]{2,1,0:T(8,128)(2,1)S(1)}, bf16[2,64,1024]{2,1,0:T(8,128)(2,1)S(1)}, u32[]{:S(2)}, u32[]{:S(2)}) collective-permute-start(bf16[2,64,1024]{2,1,0:T(8,128)(2,1)S(1)} %copy-done.17), channel_id=1, source_target_pairs={{0,12},{4,8},{8,4},{12,0},{16,28},{20,24},{24,20},{28,16},{1,13},{... | collective-permute-start | bytes 786440 | tf_op jit(solution)/shard_map/ppermute | solution.py:1110
  570.5 36.6 %collective-permute-start.67 = (bf16[2,64,1024]{2,1,0:T(8,128)(2,1)S(1)}, bf16[2,64,1024]{2,1,0:T(8,128)(2,1)S(1)}, u32[]{:S(2)}, u32[]{:S(2)}) collective-permute-start(bf16[2,64,1024]{2,1,0:T(8,128)(2,1)S(1)} %copy-done.17), channel_id=1, source_target_pairs={{0,16},{4,20},{8,24},{12,28},{16,0},{20,4},{24,8},{28,12},{1,17},{... | collective-permute-start | bytes 786440 | tf_op jit(solution)/shard_map/ppermute | solution.py:1110
  573.6 33.5 %collective-permute-start.68 = (bf16[2,64,1024]{2,1,0:T(8,128)(2,1)S(1)}, bf16[2,64,1024]{2,1,0:T(8,128)(2,1)}, u32[]{:S(2)}, u32[]{:S(2)}) collective-permute-start(bf16[2,64,1024]{2,1,0:T(8,128)(2,1)S(1)} %copy-done.17), channel_id=1, source_target_pairs={{0,20},{4,16},{8,28},{12,24},{16,4},{20,0},{24,12},{28,8},{1,21},{... | collective-permute-start | bytes 786440 | tf_op jit(solution)/shard_map/ppermute | solution.py:1110
  593.2 20.1 %collective-permute-start.70 = (bf16[2,64,1024]{2,1,0:T(8,128)(2,1)S(1)}, bf16[2,64,1024]{2,1,0:T(8,128)(2,1)S(1)}, u32[]{:S(2)}, u32[]{:S(2)}) collective-permute-start(bf16[2,64,1024]{2,1,0:T(8,128)(2,1)S(1)} %copy-done.17), channel_id=1, source_target_pairs={{0,28},{4,24},{8,20},{12,16},{16,12},{20,8},{24,4},{28,0},{1,29},{... | collective-permute-start | bytes 786440 | tf_op jit(solution)/shard_map/ppermute | solution.py:1110
  (104 other events, 1061.4 us)
Sparse Core Ops, SparseCore 0:
  18.0 38.4 all-gather.7
  85.8 58.1 reduce-scatter.3
  147.4 49.2 all-gather.9
  226.6 48.3 reduce-scatter.5
  278.7 49.2 all-gather.11
  330.8 47.5 reduce-scatter.7
  380.2 118.1 all-gather.13
  500.9 36.0 all-gather.15
  543.2 64.2 all-reduce.1
